TPU v7x, 32 devices: a whole 2x2x4 slice. The times are simulated.
32 devices in a mesh: grp: 2 (over x), seq: 16 (over z, y, core).
Axes of the slice: x: 2, y: 2, z: 4, core: 2. Of those that a mesh axis runs over, the one named last changes fastest.
Arguments:
- inputs: bfloat16 [2, 2048, 1536], P('grp', 'seq'), may hold values from -6 to 6
- cotangent: bfloat16 [2, 2048, 1536], P('grp', 'seq'), may hold values from -6 to 6
- block_ids: int32 [2, 2048], P('grp'), may hold values from 0 to 15, never falling along the last dimension, each value on 1 to 256 neighbouring positions
- piece_order: int32 [16], replicated, may hold values from 0 to 15, each once
- w_query: bfloat16 [1536, 1536], P('seq'), may hold values from -0.15625 to 0.15625
- w_key: bfloat16 [1536, 768], P('seq'), may hold values from -0.15625 to 0.15625
- w_value: bfloat16 [1536, 768], P('seq'), may hold values from -0.15625 to 0.15625
- w_out: bfloat16 [1536, 1536], P('seq'), may hold values from -3.5 to 3.5
- w_gate: bfloat16 [1536, 4096], P('seq'), may hold values from -0.15625 to 0.15625
- w_up: bfloat16 [1536, 4096], P('seq'), may hold values from -0.15625 to 0.15625
- w_down: bfloat16 [4096, 1536], P('seq'), may hold values from -0.09375 to 0.09375
- gain_attn: bfloat16 [1536], P('seq'), may hold values from 0.5 to 1.5
- gain_mlp: bfloat16 [1536], P('seq'), may hold values from 0.5 to 1.5
Outputs:
- output: bfloat16 [2, 2048, 1536], P('grp', 'seq')
- grad_inputs: bfloat16 [2, 2048, 1536], P('grp', 'seq')
- grad_w_query: float32 [1536, 1536], P('seq')
- grad_w_key: float32 [1536, 768], P('seq')
- grad_w_value: float32 [1536, 768], P('seq')
- grad_w_out: float32 [1536, 1536], P('seq')
- grad_w_gate: float32 [1536, 4096], P('seq')
- grad_w_up: float32 [1536, 4096], P('seq')
- grad_w_down: float32 [4096, 1536], P('seq')
- grad_gain_attn: float32 [1536], P('seq')
- grad_gain_mlp: float32 [1536], P('seq')
Inputs may be any that keep to these rules, and one draw needn't show every extreme that they name: `block_ids`: along each sequence's positions the block numbers never fall; each block covers 1 to 256 positions, and some block covers exactly 256. `piece_order`: each number appears once.
All inputs are finite; a program needn't handle non-finite values.
Results may differ from a plain program's by a relative error of at most 0.019.
Values may be sent and summed in bfloat16 or wider, within the bound.
No kernel may reach another device: no remote copies, remote signals or barrier semaphores. Data moves between devices by JAX's collectives and lax.ppermute only.
A program may use at most 384 MiB of HBM per device.

v0:
```python
import jax
import jax.numpy as jnp
from jax import lax
from jax.sharding import PartitionSpec as P

HEADS = 16
KV_HEADS = 8
HEAD_DIM = 96


eps_norm = 1e-05
rope_base = 100000.0
masked_score = -1e30


def rms_scale(rows_in):
    return lax.rsqrt(jnp.mean(rows_in * rows_in, axis=-1, keepdims=True) + eps_norm)


def norm_back(grad_normed, rows_in, row_scale, gain_row):
    normed = rows_in * row_scale
    grad_gain = jnp.sum(grad_normed * normed, axis=0)
    scaled_grad = grad_normed * gain_row
    grad_rows = row_scale * (
        scaled_grad - normed * jnp.mean(scaled_grad * normed, axis=-1, keepdims=True)
    )
    return (grad_rows, grad_gain)


def rotary_tables(positions, head_dim):
    half_dim = head_dim // 2
    frequency = rope_base ** (-jnp.arange(half_dim, dtype=jnp.float32) * 2.0 / head_dim)
    angles = positions.astype(jnp.float32)[:, None] * frequency[None, :]
    return (jnp.cos(angles)[:, None, :], jnp.sin(angles)[:, None, :])


def rotate(vectors, cosine_table, sine_table):
    half_dim = vectors.shape[-1] // 2
    front_half = vectors[..., :half_dim]
    back_half = vectors[..., half_dim:]
    return jnp.concatenate(
        [
            front_half * cosine_table - back_half * sine_table,
            back_half * cosine_table + front_half * sine_table,
        ],
        axis=-1,
    )


def unrotate(grads, cosine_table, sine_table):
    half_dim = grads.shape[-1] // 2
    front_half = grads[..., :half_dim]
    back_half = grads[..., half_dim:]
    return jnp.concatenate(
        [
            front_half * cosine_table + back_half * sine_table,
            back_half * cosine_table - front_half * sine_table,
        ],
        axis=-1,
    )


def over_rows(left, right):
    return lax.dot_general(
        left, right, (((0,), (0,)), ((), ())), preferred_element_type=jnp.float32
    )


def times_back(left, right):
    return lax.dot_general(
        left, right, (((1,), (1,)), ((), ())), preferred_element_type=jnp.float32
    )


def key_block_rows(key_count):
    block_rows = min(key_count, 1024)
    return block_rows


def masked_scores(query_part, key_part, query_blocks, key_blocks, score_scale):
    scores = (
        jnp.einsum("qkgd,tkd->kgqt", query_part, key_part, preferred_element_type=jnp.float32)
        * score_scale
    )
    allowed = key_blocks[None, None, None, :] <= query_blocks[None, None, :, None]
    return jnp.where(allowed, scores, masked_score)


def forward_block(running, query_part, query_blocks, key_part, value_part, key_blocks, score_scale):
    row_max, row_sum, running_sum = running
    scores = masked_scores(query_part, key_part, query_blocks, key_blocks, score_scale)
    new_max = jnp.maximum(row_max, jnp.max(scores, axis=-1))
    likely = jnp.exp(scores - new_max[..., None])
    fading = jnp.exp(row_max - new_max)
    row_sum = row_sum * fading + jnp.sum(likely, axis=-1)
    running_sum = running_sum * fading[..., None] + jnp.einsum(
        "kgqt,tkd->kgqd",
        likely.astype(jnp.bfloat16),
        value_part,
        preferred_element_type=jnp.float32,
    )
    return (new_max, row_sum, running_sum)


def backward_block(
    grad_query,
    query_part,
    query_blocks,
    key_part,
    value_part,
    key_blocks,
    log_total,
    grad_heads,
    delta_rows,
    score_scale,
):
    scores = masked_scores(query_part, key_part, query_blocks, key_blocks, score_scale)
    chance = jnp.exp(scores - log_total[..., None])
    grad_value = jnp.einsum(
        "kgqt,kgqd->tkd",
        chance.astype(jnp.bfloat16),
        grad_heads,
        preferred_element_type=jnp.float32,
    )
    grad_chance = jnp.einsum(
        "kgqd,tkd->kgqt", grad_heads, value_part, preferred_element_type=jnp.float32
    )
    grad_scores = (chance * (grad_chance - delta_rows[..., None])).astype(jnp.bfloat16)
    grad_query = (
        grad_query
        + jnp.einsum("kgqt,tkd->kgqd", grad_scores, key_part, preferred_element_type=jnp.float32)
        * score_scale
    )
    grad_key = (
        jnp.einsum("kgqt,qkgd->tkd", grad_scores, query_part, preferred_element_type=jnp.float32)
        * score_scale
    )
    return (grad_query, grad_key, grad_value)


def local(
    inputs,
    cotangent,
    block_ids,
    piece_order,
    w_query,
    w_key,
    w_value,
    w_out,
    w_gate,
    w_up,
    w_down,
    gain_attn,
    gain_mlp,
):
    shards = (w_query, w_key, w_value, w_out, w_gate, w_up, w_down, gain_attn, gain_mlp)
    (
        full_query,
        full_key,
        full_value,
        full_out,
        full_gate,
        full_up,
        full_down,
        gain_one,
        gain_two,
    ) = (
        lax.all_gather(shards[0], "seq", axis=0, tiled=True),
        lax.all_gather(shards[1], "seq", axis=0, tiled=True),
        lax.all_gather(shards[2], "seq", axis=0, tiled=True),
        lax.all_gather(shards[3], "seq", axis=0, tiled=True),
        lax.all_gather(shards[4], "seq", axis=0, tiled=True),
        lax.all_gather(shards[5], "seq", axis=0, tiled=True),
        lax.all_gather(shards[6], "seq", axis=0, tiled=True),
        lax.all_gather(shards[7], "seq", axis=0, tiled=True),
        lax.all_gather(shards[8], "seq", axis=0, tiled=True),
    )
    seq_count, tok_rows, model_width = inputs.shape
    row_count = seq_count * tok_rows
    head_count = HEADS
    kv_heads = KV_HEADS
    head_dim = HEAD_DIM
    groups = head_count // kv_heads
    kv_width = kv_heads * head_dim
    q_width = head_count * head_dim
    score_scale = head_dim ** (-0.5)
    own_first = jnp.take(piece_order, lax.axis_index("seq")) * tok_rows
    local_pos = own_first + jnp.arange(tok_rows, dtype=jnp.int32)
    cosine_table, sine_table = rotary_tables(local_pos, head_dim)
    query_blk = jnp.take(block_ids, local_pos, axis=1)

    def key_positions(key_count):
        stored = jnp.arange(key_count, dtype=jnp.int32)
        return jnp.take(piece_order, stored // tok_rows) * tok_rows + stored % tok_rows

    residual = inputs.reshape(row_count, model_width).astype(jnp.float32)
    gain_first = gain_one.astype(jnp.float32)
    gain_second = gain_two.astype(jnp.float32)
    scale_first = rms_scale(residual)
    normed_attn = (residual * scale_first * gain_first).astype(jnp.bfloat16)
    query_pre = jnp.dot(normed_attn, full_query, preferred_element_type=jnp.float32)
    key_pre = jnp.dot(normed_attn, full_key, preferred_element_type=jnp.float32)
    value_pre = jnp.dot(normed_attn, full_value, preferred_element_type=jnp.float32)
    queries = rotate(
        query_pre.reshape(seq_count, tok_rows, head_count, head_dim), cosine_table, sine_table
    ).astype(jnp.bfloat16)
    key_rot = rotate(
        key_pre.reshape(seq_count, tok_rows, kv_heads, head_dim), cosine_table, sine_table
    ).astype(jnp.bfloat16)
    values = value_pre.astype(jnp.bfloat16)
    kv_local = jnp.concatenate(
        [
            key_rot.reshape(seq_count, tok_rows, kv_width),
            values.reshape(seq_count, tok_rows, kv_width),
        ],
        axis=2,
    )
    query_grouped = queries.reshape(seq_count, tok_rows, kv_heads, groups, head_dim)
    start_max = jnp.full((seq_count, kv_heads, groups, tok_rows), masked_score, jnp.float32)
    start_sum = jnp.zeros((seq_count, kv_heads, groups, tok_rows), jnp.float32)
    start_acc = jnp.zeros((seq_count, kv_heads, groups, tok_rows, head_dim), jnp.float32)
    state_in = (start_max, start_sum, start_acc)
    key_piece = lax.all_gather(kv_local, "seq", axis=1, tiled=True)
    key_count = key_piece.shape[1]
    block_rows = key_block_rows(key_count)
    key_pos = key_positions(key_count)
    member = 0
    key_blk = jnp.take(block_ids[member], key_pos).reshape(key_count // block_rows, block_rows)
    kv_rows = key_piece[member].reshape(key_count // block_rows, block_rows, 2 * kv_width)
    own_query = query_grouped[member]
    own_blocks = query_blk[member]

    def forward_key_step(running, block_in):
        kv_block, blk_block = block_in
        key_part = kv_block[:, :kv_width].reshape(block_rows, kv_heads, head_dim)
        value_part = kv_block[:, kv_width:].reshape(block_rows, kv_heads, head_dim)
        running = forward_block(
            running, own_query, own_blocks, key_part, value_part, blk_block, score_scale
        )
        return (running, None)

    running, unused = lax.scan(
        forward_key_step,
        (state_in[0][member], state_in[1][member], state_in[2][member]),
        (kv_rows, key_blk),
    )
    results = [running]
    row_max = jnp.stack([entry[0] for entry in results])
    row_sum = jnp.stack([entry[1] for entry in results])
    running_sum = jnp.stack([entry[2] for entry in results])
    log_total = row_max + jnp.log(row_sum)
    attention = running_sum / row_sum[..., None]
    attended = (
        jnp.transpose(attention, (0, 3, 1, 2, 4)).reshape(row_count, q_width).astype(jnp.bfloat16)
    )
    middle = residual + jnp.dot(attended, full_out, preferred_element_type=jnp.float32)
    scale_second = rms_scale(middle)
    normed_mlp = (middle * scale_second * gain_second).astype(jnp.bfloat16)
    gate_value = jnp.dot(normed_mlp, full_gate, preferred_element_type=jnp.float32)
    upward = jnp.dot(normed_mlp, full_up, preferred_element_type=jnp.float32)
    sigmoid_gate = jax.nn.sigmoid(gate_value)
    hidden = (gate_value * sigmoid_gate * upward).astype(jnp.bfloat16)
    output = (middle + jnp.dot(hidden, full_down, preferred_element_type=jnp.float32)).astype(
        jnp.bfloat16
    )
    (
        full_query,
        full_key,
        full_value,
        full_out,
        full_gate,
        full_up,
        full_down,
        gain_one,
        gain_two,
    ) = (
        lax.all_gather(shards[0], "seq", axis=0, tiled=True),
        lax.all_gather(shards[1], "seq", axis=0, tiled=True),
        lax.all_gather(shards[2], "seq", axis=0, tiled=True),
        lax.all_gather(shards[3], "seq", axis=0, tiled=True),
        lax.all_gather(shards[4], "seq", axis=0, tiled=True),
        lax.all_gather(shards[5], "seq", axis=0, tiled=True),
        lax.all_gather(shards[6], "seq", axis=0, tiled=True),
        lax.all_gather(shards[7], "seq", axis=0, tiled=True),
        lax.all_gather(shards[8], "seq", axis=0, tiled=True),
    )
    gain_first = gain_one.astype(jnp.float32)
    gain_second = gain_two.astype(jnp.float32)
    upstream = cotangent.reshape(row_count, model_width)
    grad_down = over_rows(hidden, upstream)
    grad_hidden = times_back(upstream, full_down)
    grad_gate = (
        grad_hidden * upward * sigmoid_gate * (1.0 + gate_value * (1.0 - sigmoid_gate))
    ).astype(jnp.bfloat16)
    grad_upward = (grad_hidden * gate_value * sigmoid_gate).astype(jnp.bfloat16)
    grad_w_gate = over_rows(normed_mlp, grad_gate)
    grad_w_up = over_rows(normed_mlp, grad_upward)
    grad_normed_mlp = times_back(grad_gate, full_gate) + times_back(grad_upward, full_up)
    grad_mid_norm, grad_gain_mlp = norm_back(grad_normed_mlp, middle, scale_second, gain_second)
    grad_middle = upstream.astype(jnp.float32) + grad_mid_norm
    grad_middle_low = grad_middle.astype(jnp.bfloat16)
    grad_w_out = over_rows(attended, grad_middle_low)
    grad_attended = times_back(grad_middle_low, full_out).astype(jnp.bfloat16)
    grad_heads = jnp.transpose(
        grad_attended.reshape(seq_count, tok_rows, kv_heads, groups, head_dim), (0, 2, 3, 1, 4)
    )
    delta_rows = jnp.sum(grad_heads.astype(jnp.float32) * attention, axis=-1)
    start_query = jnp.zeros((seq_count, kv_heads, groups, tok_rows, head_dim), jnp.float32)
    start_kv = jnp.zeros((seq_count, block_ids.shape[1], 2 * kv_width), jnp.float32)
    state_in = (start_query, start_kv)
    key_piece = lax.all_gather(kv_local, "seq", axis=1, tiled=True)
    key_count = key_piece.shape[1]
    backward_block_rows = key_block_rows(key_count)
    key_pos = key_positions(key_count)
    member = 0
    key_blk = jnp.take(block_ids[member], key_pos).reshape(
        key_count // backward_block_rows, backward_block_rows
    )
    kv_rows = key_piece[member].reshape(
        key_count // backward_block_rows, backward_block_rows, 2 * kv_width
    )
    backward_own_query = query_grouped[member]
    backward_own_blocks = query_blk[member]
    own_total = log_total[member]
    own_grads = grad_heads[member]
    own_delta = delta_rows[member]

    def backward_key_step(grad_query, block_in):
        kv_block, blk_block = block_in
        key_part = kv_block[:, :kv_width].reshape(backward_block_rows, kv_heads, head_dim)
        value_part = kv_block[:, kv_width:].reshape(backward_block_rows, kv_heads, head_dim)
        result = backward_block(
            grad_query,
            backward_own_query,
            backward_own_blocks,
            key_part,
            value_part,
            blk_block,
            own_total,
            own_grads,
            own_delta,
            score_scale,
        )
        return (result[0], (result[1], result[2]))

    grad_query, key_grads = lax.scan(backward_key_step, state_in[0][member], (kv_rows, key_blk))
    fresh = jnp.concatenate(
        [key_grads[0].reshape(key_count, kv_width), key_grads[1].reshape(key_count, kv_width)],
        axis=1,
    )
    query_grads = [grad_query]
    kv_grads = [fresh]
    grad_query_all = jnp.stack(query_grads)
    grad_kv_all = jnp.stack(kv_grads)
    grad_kv_own = lax.psum_scatter(grad_kv_all, "seq", scatter_dimension=1, tiled=True)
    grad_query_rows = jnp.transpose(grad_query_all, (0, 3, 1, 2, 4)).reshape(
        seq_count, tok_rows, head_count, head_dim
    )
    grad_query_pre = (
        unrotate(grad_query_rows, cosine_table, sine_table)
        .reshape(row_count, q_width)
        .astype(jnp.bfloat16)
    )
    grad_key_rows = grad_kv_own[:, :, :kv_width].reshape(seq_count, tok_rows, kv_heads, head_dim)
    grad_key_pre = (
        unrotate(grad_key_rows, cosine_table, sine_table)
        .reshape(row_count, kv_width)
        .astype(jnp.bfloat16)
    )
    grad_value_pre = grad_kv_own[:, :, kv_width:].reshape(row_count, kv_width).astype(jnp.bfloat16)
    grad_w_query = over_rows(normed_attn, grad_query_pre)
    grad_w_key = over_rows(normed_attn, grad_key_pre)
    grad_w_value = over_rows(normed_attn, grad_value_pre)
    grad_normed_attn = (
        times_back(grad_query_pre, full_query)
        + times_back(grad_key_pre, full_key)
        + times_back(grad_value_pre, full_value)
    )
    grad_in_norm, grad_gain_attn = norm_back(grad_normed_attn, residual, scale_first, gain_first)
    grad_inputs = (
        (grad_middle + grad_in_norm).astype(jnp.bfloat16).reshape(seq_count, tok_rows, model_width)
    )
    terms = (
        grad_w_query,
        grad_w_key,
        grad_w_value,
        grad_w_out,
        grad_w_gate,
        grad_w_up,
        grad_down,
        grad_gain_attn,
        grad_gain_mlp,
    )
    shares = (
        lax.psum_scatter(terms[0], "seq", scatter_dimension=0, tiled=True),
        lax.psum_scatter(terms[1], "seq", scatter_dimension=0, tiled=True),
        lax.psum_scatter(terms[2], "seq", scatter_dimension=0, tiled=True),
        lax.psum_scatter(terms[3], "seq", scatter_dimension=0, tiled=True),
        lax.psum_scatter(terms[4], "seq", scatter_dimension=0, tiled=True),
        lax.psum_scatter(terms[5], "seq", scatter_dimension=0, tiled=True),
        lax.psum_scatter(terms[6], "seq", scatter_dimension=0, tiled=True),
        lax.psum_scatter(terms[7], "seq", scatter_dimension=0, tiled=True),
        lax.psum_scatter(terms[8], "seq", scatter_dimension=0, tiled=True),
    )
    totals = (
        lax.psum(shares[0].astype(jnp.bfloat16), "grp").astype(jnp.float32),
        lax.psum(shares[1].astype(jnp.bfloat16), "grp").astype(jnp.float32),
        lax.psum(shares[2].astype(jnp.bfloat16), "grp").astype(jnp.float32),
        lax.psum(shares[3].astype(jnp.bfloat16), "grp").astype(jnp.float32),
        lax.psum(shares[4].astype(jnp.bfloat16), "grp").astype(jnp.float32),
        lax.psum(shares[5].astype(jnp.bfloat16), "grp").astype(jnp.float32),
        lax.psum(shares[6].astype(jnp.bfloat16), "grp").astype(jnp.float32),
        lax.psum(shares[7].astype(jnp.bfloat16), "grp").astype(jnp.float32),
        lax.psum(shares[8].astype(jnp.bfloat16), "grp").astype(jnp.float32),
    )
    return (
        output.reshape(seq_count, tok_rows, model_width),
        grad_inputs,
        totals[0],
        totals[1],
        totals[2],
        totals[3],
        totals[4],
        totals[5],
        totals[6],
        totals[7],
        totals[8],
    )


def solution(mesh):
    return jax.shard_map(
        local,
        mesh=mesh,
        in_specs=(
            P("grp", "seq", None),
            P("grp", "seq", None),
            P("grp", None),
            P(),
            P("seq", None),
            P("seq", None),
            P("seq", None),
            P("seq", None),
            P("seq", None),
            P("seq", None),
            P("seq", None),
            P("seq"),
            P("seq"),
        ),
        out_specs=(
            P("grp", "seq", None),
            P("grp", "seq", None),
            P("seq", None),
            P("seq", None),
            P("seq", None),
            P("seq", None),
            P("seq", None),
            P("seq", None),
            P("seq", None),
            P("seq"),
            P("seq"),
        ),
        check_vma=False,
    )
```

profile of v0, /device:TPU:0, one launch (start us, length us, event | category | flops | bytes accessed | tf_op | source)
XLA Modules:
  0.0 2285.1 jit_solution(9417412373605997588)
XLA Ops:
  13.2 35.9 %all-reduce.5 = (bf16[1536]{0:T(1024)(128)(2,1)S(1)}, bf16[1536]{0:T(1024)(128)(2,1)S(1)}) all-reduce(bf16[1536]{0:T(1024)(128)(2,1)S(1)} %dynamic-update-slice.1, bf16[1536]{0:T(1024)(128)(2,1)S(1)} %dynamic-update-slice.2), channel_id=1, replica_groups=mesh['grp'=2,'seq'=16] {'seq'}, use_global_device_ids=true, to_apply=%add | all-reduce | flops 3072 | bytes 12288
  59.2 39.5 %all-gather.11.cloned.1.call-done = bf16[1536,768]{1,0:T(8,128)(2,1)} async-done(((bf16[96,768]{1,0:T(8,128)(2,1)}), bf16[1536,768]{1,0:T(8,128)(2,1)}) %all-gather.11.cloned.1.call-update) | async-done | bytes 2359312 | tf_op jit(solution)/shard_map/all_gather | solution.py:170
  104.5 10.3 broadcast_clamp_fusion
  114.9 11.8 gather_fusion.1
  126.6 10.3 and_select_fusion
  139.3 14.0 all-gather.15.cloned.1.call-done
  153.3 6.7 copy.52
  159.9 3.9 convolution_bitcast_fusion
  164.0 52.4 %all-gather.13.cloned.1.call-done = bf16[1,2048,1536]{2,1,0:T(8,128)(2,1)} async-done(((bf16[1,128,1536]{2,1,0:T(8,128)(2,1)}), bf16[1,2048,1536]{2,1,0:T(8,128)(2,1)}) %all-gather.13.cloned.1.call-update) | async-done | bytes 6291472 | tf_op jit(solution)/shard_map/all_gather | solution.py:223
  216.4 8.7 copy.53
  225.1 32.9 %while.31 = (s32[]{:T(128)}, f32[8,2,128]{2,1,0:T(2,128)S(1)}, f32[8,2,128]{2,1,0:T(2,128)S(1)}, f32[8,2,128,96]{2,3,1,0:T(8,128)S(1)}, s32[2,1024]{1,0:T(2,128)...) while((s32[]{:T(128)}, f32[8,2,128]{2,1,0:T(2,128)S(1)}, ...), condition=%wide.region_4.7_spmd.clone, body=%wide.region_1.6_spmd.clone.sunk | while | flops 829106176 | bytes 77083280 | solution.py:242
  228.5 4.8 fusion.188
  233.4 5.2 fusion.190
  244.9 4.8 fusion.188
  249.7 5.3 fusion.190
  260.1 10.3 all-gather.17.cloned.1.call-done
  270.4 3.2 multiply_reduce_fusion.2
  274.5 97.4 %all-gather.19.cloned.1.call-done = bf16[1536,4096]{1,0:T(8,128)(2,1)} async-done(((bf16[96,4096]{1,0:T(8,128)(2,1)}), bf16[1536,4096]{1,0:T(8,128)(2,1)}) %all-gather.19.cloned.1.call-update) | async-done | bytes 12582928 | tf_op jit(solution)/shard_map/all_gather | solution.py:172
  371.9 7.7 fusion.109
  379.6 93.6 %all-gather.21.cloned.1.call-done = bf16[1536,4096]{1,0:T(8,128)(2,1)} async-done(((bf16[96,4096]{1,0:T(8,128)(2,1)}), bf16[1536,4096]{1,0:T(8,128)(2,1)}) %all-gather.21.cloned.1.call-update) | async-done | bytes 12582928 | tf_op jit(solution)/shard_map/all_gather | solution.py:173
  473.2 7.8 fusion.110
  481.0 93.5 %all-gather.23.cloned.1.call-done = bf16[4096,1536]{1,0:T(8,128)(2,1)} async-done(((bf16[256,1536]{1,0:T(8,128)(2,1)}), bf16[4096,1536]{1,0:T(8,128)(2,1)}) %all-gather.23.cloned.1.call-update) | async-done | bytes 12582928 | tf_op jit(solution)/shard_map/all_gather | solution.py:174
  574.4 11.7 multiply_convert_fusion
  586.2 9.3 fusion.111
  595.5 7.1 multiply_reduce_fusion
  604.1 4.3 convolution_convert_fusion
  611.1 277.9 %while.32 = (s32[]{:T(128)}, f32[8,2,128,96]{2,3,1,0:T(8,128)}, f32[2,1024,8,96]{1,0,3,2:T(2,128)}, f32[2,1024,8,96]{1,0,3,2:T(2,128)}, s32[2,1024]{1,0:T(2,128)...) while((s32[]{:T(128)}, f32[8,2,128,96]{2,3,1,0:T(8,128)}, ...), condition=%wide.region_9.12_spmd.clone, body=%wide.region_8.11_spmd.clone.sunk | while | flops 2035744768 | bytes 141038384 | solution.py:346
  618.7 5.4 fusion.205
  624.1 4.1 fusion.206
  629.6 3.2 copy.83
  632.9 54.2 %dynamic_update_slice.11 = f32[2,1024,8,96]{1,0,3,2:T(2,128)} dynamic-update-slice(f32[2,1024,8,96]{1,0,3,2:T(2,128)} %get-tuple-element.529, f32[1,1024,8,96]{1,0,3,2:T(1,128)S(1)} %copy.83, s32[]{:T(128)} %get-tuple-element.527, s32[]{:T(128)} %constant.129.clone.1..sunk.1, s32[]{:T(128)} %constant.129.clone.1..sunk.1, s32[]{:T(128)} %constant.129.clone.1..sunk.1) | dynamic-update-slice | bytes 6291460 | tf_op jit(solution)/shard_map/while/body/jit(dynamic_update_index_in_dim)/dynamic_update_slice | solution.py:346
  687.1 5.5 fusion.208
  692.6 3.2 copy.84
  695.8 54.2 %dynamic_update_slice.12 = f32[2,1024,8,96]{1,0,3,2:T(2,128)} dynamic-update-slice(f32[2,1024,8,96]{1,0,3,2:T(2,128)} %get-tuple-element.530, f32[1,1024,8,96]{1,0,3,2:T(1,128)S(1)} %copy.84, s32[]{:T(128)} %get-tuple-element.527, s32[]{:T(128)} %constant.129.clone.1..sunk.1, s32[]{:T(128)} %constant.129.clone.1..sunk.1, s32[]{:T(128)} %constant.129.clone.1..sunk.1) | dynamic-update-slice | bytes 6291460 | tf_op jit(solution)/shard_map/while/body/jit(dynamic_update_index_in_dim)/dynamic_update_slice | solution.py:346
  757.3 5.4 fusion.205
  762.7 4.3 fusion.206
  768.4 3.2 copy.83
  771.7 54.2 %dynamic_update_slice.11 = f32[2,1024,8,96]{1,0,3,2:T(2,128)} dynamic-update-slice(f32[2,1024,8,96]{1,0,3,2:T(2,128)} %get-tuple-element.529, f32[1,1024,8,96]{1,0,3,2:T(1,128)S(1)} %copy.83, s32[]{:T(128)} %get-tuple-element.527, s32[]{:T(128)} %constant.129.clone.1..sunk.1, s32[]{:T(128)} %constant.129.clone.1..sunk.1, s32[]{:T(128)} %constant.129.clone.1..sunk.1) | dynamic-update-slice | bytes 6291460 | tf_op jit(solution)/shard_map/while/body/jit(dynamic_update_index_in_dim)/dynamic_update_slice | solution.py:346
  825.8 5.5 fusion.208
  831.4 3.2 copy.84
  834.6 54.2 %dynamic_update_slice.12 = f32[2,1024,8,96]{1,0,3,2:T(2,128)} dynamic-update-slice(f32[2,1024,8,96]{1,0,3,2:T(2,128)} %get-tuple-element.530, f32[1,1024,8,96]{1,0,3,2:T(1,128)S(1)} %copy.84, s32[]{:T(128)} %get-tuple-element.527, s32[]{:T(128)} %constant.129.clone.1..sunk.1, s32[]{:T(128)} %constant.129.clone.1..sunk.1, s32[]{:T(128)} %constant.129.clone.1..sunk.1) | dynamic-update-slice | bytes 6291460 | tf_op jit(solution)/shard_map/while/body/jit(dynamic_update_index_in_dim)/dynamic_update_slice | solution.py:346
  889.0 8.6 copy.79
  897.6 5.7 copy.80
  903.4 11.4 maximum_bitcast_fusion
  916.8 5.7 fusion.58
  923.8 6.0 fusion.67
  929.9 118.0 %reduce-scatter.9.cloned.1.call-done = f32[1,128,1536]{1,2,0:T(8,128)} async-done(((f32[1,2048,1536]{1,2,0:T(8,128)}), f32[1,128,1536]{1,2,0:T(8,128)}) %reduce-scatter.9.cloned.1.call-update) | async-done | bytes 786448 | tf_op jit(solution)/shard_map/reduce_scatter | solution.py:355
  1049.0 3.0 fusion.62
  1052.3 4.2 fusion.60
  1056.5 12.8 fusion.113
  1070.6 10.2 fusion.114
  1082.2 10.2 fusion.52
  1092.5 69.8 %reduce-scatter.11.cloned.1.call-done = f32[96,1536]{1,0:T(8,128)} async-done(((f32[1536,1536]{1,0:T(8,128)}), f32[96,1536]{1,0:T(8,128)}) %reduce-scatter.11.cloned.1.call-update) | async-done | bytes 589840 | tf_op jit(solution)/shard_map/reduce_scatter | solution.py:395
  1164.1 114.0 %reduce-scatter.17.cloned.1.call-done = f32[96,1536]{1,0:T(8,128)} async-done(((f32[1536,1536]{1,0:T(8,128)}), f32[96,1536]{1,0:T(8,128)}) %reduce-scatter.17.cloned.1.call-update) | async-done | bytes 589840 | tf_op jit(solution)/shard_map/reduce_scatter | solution.py:398
  1279.9 77.2 %reduce-scatter.13.cloned.1.call-done = f32[96,768]{1,0:T(8,128)} async-done(((f32[1536,768]{1,0:T(8,128)}), f32[96,768]{1,0:T(8,128)}) %reduce-scatter.13.cloned.1.call-update) | async-done | bytes 294928 | tf_op jit(solution)/shard_map/reduce_scatter | solution.py:396
  1358.8 77.3 %reduce-scatter.15.cloned.1.call-done = f32[96,768]{1,0:T(8,128)} async-done(((f32[1536,768]{1,0:T(8,128)}), f32[96,768]{1,0:T(8,128)}) %reduce-scatter.15.cloned.1.call-update) | async-done | bytes 294928 | tf_op jit(solution)/shard_map/reduce_scatter | solution.py:397
  1437.8 245.4 %reduce-scatter.19.cloned.1.call-done = f32[96,4096]{1,0:T(8,128)} async-done(((f32[1536,4096]{1,0:T(8,128)}), f32[96,4096]{1,0:T(8,128)}) %reduce-scatter.19.cloned.1.call-update) | async-done | bytes 1572880 | tf_op jit(solution)/shard_map/reduce_scatter | solution.py:399
  1685.6 244.5 %reduce-scatter.21.cloned.1.call-done = f32[96,4096]{1,0:T(8,128)} async-done(((f32[1536,4096]{1,0:T(8,128)}), f32[96,4096]{1,0:T(8,128)}) %reduce-scatter.21.cloned.1.call-update) | async-done | bytes 1572880 | tf_op jit(solution)/shard_map/reduce_scatter | solution.py:400
  1932.4 244.5 %reduce-scatter.23.cloned.1.call-done = f32[256,1536]{1,0:T(8,128)} async-done(((f32[4096,1536]{1,0:T(8,128)}), f32[256,1536]{1,0:T(8,128)}) %reduce-scatter.23.cloned.1.call-update) | async-done | bytes 1572880 | tf_op jit(solution)/shard_map/reduce_scatter | solution.py:401
  2180.1 4.0 fusion.112
  2184.1 8.3 fusion.31
  2195.2 59.5 %all-reduce.4 = (bf16[1536]{0:T(1024)(128)(2,1)S(1)}, bf16[1536]{0:T(1024)(128)(2,1)S(1)}) all-reduce(f32[1536]{0:T(1024)S(1)} %get-tuple-element.255, f32[1536]{0:T(1024)S(1)} %copy-done.44), channel_id=10, replica_groups=mesh['grp'=2,'seq'=16] {'seq'}, use_global_device_ids=true, to_apply=%region_27.30.clone | all-reduce | flops 3072 | bytes 18432
  2254.8 5.0 all-reduce.6
  2261.9 7.0 all-reduce.10.cloned.1.call-done
  (241 shorter events, 95.5 us)
Async XLA Ops:
  7.2 107.7 %copy-start = (s32[1,2048]{1,0:T(1,128)S(1)}, s32[1,2048]{1,0:T(1,128)}, u32[]{:S(2)}) copy-start(s32[1,2048]{1,0:T(1,128)} %param.23) | copy-start | bytes 24580
  7.2 50.9 %copy-start.6 = (bf16[1,128,1536]{2,1,0:T(8,128)(2,1)S(1)}, bf16[1,128,1536]{2,1,0:T(8,128)(2,1)}, u32[]{:S(2)}) copy-start(bf16[1,128,1536]{2,1,0:T(8,128)(2,1)} %param.21) | copy-start | bytes 1179652
  7.2 48.1 %all-gather.9.cloned.1.call-start = ((), (), s32[]{:S(2)}) async-start(), calls=%async_computation.8 | async-start | bytes 2506752 | tf_op jit(solution)/shard_map/all_gather | solution.py:169
  7.9 90.8 %all-gather.11.cloned.1.call-start = ((), (), s32[]{:S(2)}) async-start(), calls=%async_computation.9 | async-start | bytes 2506752 | tf_op jit(solution)/shard_map/all_gather | solution.py:170
  8.7 144.6 %all-gather.15.cloned.1.call-start = ((), (), s32[]{:S(2)}) async-start(), calls=%async_computation.11 | async-start | bytes 5013504 | tf_op jit(solution)/shard_map/all_gather | solution.py:168
  9.4 207.0 %all-gather.13.cloned.1.call-start = ((), (), s32[]{:S(2)}) async-start(), calls=%async_computation.10 | async-start | bytes 6684672 | tf_op jit(solution)/shard_map/all_gather | solution.py:223
  49.1 110.8 %copy-start.30 = (f32[1536]{0:T(1024)}, f32[1536]{0:T(1024)S(1)}, u32[]{:S(2)}) copy-start(f32[1536]{0:T(1024)S(1)} %convert_element_type.208) | copy-start | bytes 18436
  53.0 107.0 %copy-start.42 = (f32[128]{0:T(128)}, f32[128]{0:T(128)S(1)}, u32[]{:S(2)}) copy-start(f32[128]{0:T(128)S(1)} %add_rsqrt_fusion.1) | copy-start | bytes 1540
  53.1 110.7 %copy-start.33 = (f32[128,48]{0,1:T(8,128)}, f32[128,48]{0,1:T(8,128)S(1)}, u32[]{:S(2)}) copy-start(f32[128,48]{0,1:T(8,128)S(1)} %get-tuple-element.327) | copy-start | bytes 73732
  53.2 110.7 %copy-start.35 = (f32[128,48]{0,1:T(8,128)}, f32[128,48]{0,1:T(8,128)S(1)}, u32[]{:S(2)}) copy-start(f32[128,48]{0,1:T(8,128)S(1)} %get-tuple-element.328) | copy-start | bytes 73732
  101.8 168.7 %all-gather.17.cloned.1.call-start = ((), (), s32[]{:S(2)}) async-start(), calls=%async_computation.12 | async-start | bytes 5013504 | tf_op jit(solution)/shard_map/all_gather | solution.py:171
  102.4 269.6 %all-gather.19.cloned.1.call-start = ((), (), s32[]{:S(2)}) async-start(), calls=%async_computation.13 | async-start | bytes 13369344 | tf_op jit(solution)/shard_map/all_gather | solution.py:172
  102.9 370.2 %all-gather.21.cloned.1.call-start = ((), (), s32[]{:S(2)}) async-start(), calls=%async_computation.14 | async-start | bytes 13369344 | tf_op jit(solution)/shard_map/all_gather | solution.py:173
  103.7 470.8 %all-gather.23.cloned.1.call-start = ((), (), s32[]{:S(2)}) async-start(), calls=%async_computation.15 | async-start | bytes 13369344 | tf_op jit(solution)/shard_map/all_gather | solution.py:174
  104.4 943.4 %reduce-scatter.9.cloned.1.call-start = ((), (), s32[]{:S(2)}) async-start(), calls=%async_computation.16 | async-start | bytes 13369344 | tf_op jit(solution)/shard_map/reduce_scatter | solution.py:355
  233.4 5.8 copy-start.2
  249.7 5.9 copy-start.2
  258.0 16.3 copy-start.41
  260.1 14.2 copy-start.18
  273.7 328.9 %copy-start.8 = (f32[128,1536]{1,0:T(8,128)}, f32[128,1536]{1,0:T(8,128)S(1)}, u32[]{:S(2)}) copy-start(f32[128,1536]{1,0:T(8,128)S(1)} %get-tuple-element.349) | copy-start | bytes 2359300
  274.5 198.7 %copy-start.10 = (bf16[128,1536]{1,0:T(8,128)(2,1)}, bf16[128,1536]{1,0:T(8,128)(2,1)S(1)}, u32[]{:S(2)}) copy-start(bf16[128,1536]{1,0:T(8,128)(2,1)S(1)} %multiply_convert_fusion.3) | copy-start | bytes 1179652
  379.6 194.8 %copy-start.28 = (bf16[1,128,1536]{2,1,0:T(8,128)(2,1)S(1)}, bf16[1,128,1536]{2,1,0:T(8,128)(2,1)}, u32[]{:S(2)}) copy-start(bf16[1,128,1536]{2,1,0:T(8,128)(2,1)} %param.22) | copy-start | bytes 1179652
  586.2 9.3 copy-start.5
  602.6 6.8 copy-start.24
  604.1 6.9 copy-start.12
  614.0 4.7 copy-start.45
  614.0 4.7 copy-start.46
  615.3 3.3 copy-start.4
  616.2 2.5 copy-start.22
  624.1 4.1 copy-start.3
  632.9 54.2 %copy-start.47 = (f32[1,8,2,128]{3,2,1,0:T(2,128)S(1)}, f32[1,8,2,128]{3,2,1,0:T(2,128)}, u32[]{:S(2)}) copy-start(f32[1,8,2,128]{3,2,1,0:T(2,128)} %get-tuple-element.548) | copy-start | bytes 24580 | tf_op jit(solution)/shard_map/while
  752.5 4.7 copy-start.45
  752.6 4.7 copy-start.46
  753.9 3.3 copy-start.4
  754.8 2.5 copy-start.22
  762.7 4.3 copy-start.3
  771.7 54.2 %copy-start.47 = (f32[1,8,2,128]{3,2,1,0:T(2,128)S(1)}, f32[1,8,2,128]{3,2,1,0:T(2,128)}, u32[]{:S(2)}) copy-start(f32[1,8,2,128]{3,2,1,0:T(2,128)} %get-tuple-element.548) | copy-start | bytes 24580 | tf_op jit(solution)/shard_map/while
  889.0 8.7 copy-start.16
  914.7 2.0 copy-start.7
  914.7 2.0 copy-start.31
  914.7 2.0 copy-start.43
  914.8 247.6 %reduce-scatter.11.cloned.1.call-start = ((), (), s32[]{:S(2)}) async-start(), calls=%async_computation.17 | async-start | bytes 10027008 | tf_op jit(solution)/shard_map/reduce_scatter | solution.py:395
  922.5 355.7 %reduce-scatter.17.cloned.1.call-start = ((), (), s32[]{:S(2)}) async-start(), calls=%async_computation.20 | async-start | bytes 10027008 | tf_op jit(solution)/shard_map/reduce_scatter | solution.py:398
  929.8 427.3 %reduce-scatter.13.cloned.1.call-start = ((), (), s32[]{:S(2)}) async-start(), calls=%async_computation.18 | async-start | bytes 5013504 | tf_op jit(solution)/shard_map/reduce_scatter | solution.py:396
  1049.0 3.0 copy-start.25
  1052.0 4.5 copy-start.11
  1052.0 4.5 copy-start.21
  1052.0 384.2 %reduce-scatter.15.cloned.1.call-start = ((), (), s32[]{:S(2)}) async-start(), calls=%async_computation.19 | async-start | bytes 5013504 | tf_op jit(solution)/shard_map/reduce_scatter | solution.py:397
  1056.5 626.7 %reduce-scatter.19.cloned.1.call-start = ((), (), s32[]{:S(2)}) async-start(), calls=%async_computation.21 | async-start | bytes 26738688 | tf_op jit(solution)/shard_map/reduce_scatter | solution.py:399
  1069.4 860.7 %reduce-scatter.21.cloned.1.call-start = ((), (), s32[]{:S(2)}) async-start(), calls=%async_computation.22 | async-start | bytes 26738688 | tf_op jit(solution)/shard_map/reduce_scatter | solution.py:400
  1080.9 1096.0 %reduce-scatter.23.cloned.1.call-start = ((), (), s32[]{:S(2)}) async-start(), calls=%async_computation.23 | async-start | bytes 26738688 | tf_op jit(solution)/shard_map/reduce_scatter | solution.py:401
  1092.4 1176.4 %all-reduce.10.cloned.1.call-start = ((), (), s32[]{:S(2)}) async-start(), calls=%async_computation.24 | async-start | bytes 6488064 | tf_op jit(solution)/shard_map/psum | solution.py:406
  2179.3 4.7 copy-start.9
  2184.1 8.4 copy-start.14
  2184.1 8.4 copy-start.26
  2184.1 9.3 copy-start.27
  2192.5 1.7 copy-start.15
  2192.5 2.7 copy-start.44
  2268.8 5.0 copy-start.32
  2268.8 6.3 copy-start.38
  2268.8 7.2 copy-start.37
  2268.8 8.0 copy-start.40
  2268.8 8.8 copy-start.39
  2268.9 9.5 copy-start.1
  (8 other events, 8.8 us)
Sparse Core Ops, SparseCore 0:
  10.3 44.9 all-gather.8
  57.6 41.1 all-gather.10
  101.1 52.1 all-gather.14
  156.0 60.4 all-gather.12
  218.6 51.8 all-gather.16
  272.6 99.3 all-gather.18
  374.2 98.9 all-gather.20
  475.5 98.9 all-gather.22
  914.9 132.9 reduce-scatter.8
  1051.8 110.4 reduce-scatter.10
  1167.0 111.1 reduce-scatter.16
  1281.8 75.2 reduce-scatter.12
  1361.5 74.5 reduce-scatter.14
  1440.1 243.0 reduce-scatter.18
  1687.1 242.8 reduce-scatter.20
  1934.0 242.8 reduce-scatter.22
  2180.7 88.1 all-reduce.9
where the time goes:
time: 2310 us; the launch traced here: 2290 us
  waiting for transfers between devices  1610 us (70%)
  local copies, waits for them, and re-layouts  305 us (13%)
  matrix products  174 us (8%)
  blocking collectives  100 us (4%)
  other arithmetic  81.8 us (4%)
    reduce_scatter x1, waiting for transfers between devices, local(): lax.psum_scatter(terms[4], 'seq', scatter_dimension=0, tiled=True)  245 us
    reduce_scatter x1, waiting for transfers between devices, local(): lax.psum_scatter(terms[6], 'seq', scatter_dimension=0, tiled=True)  245 us
    reduce_scatter x1, waiting for transfers between devices, local(): lax.psum_scatter(terms[5], 'seq', scatter_dimension=0, tiled=True)  244 us
    dynamic_update_slice x8, local copies, waits for them, and re-layouts, local(): lax.scan(backward_key_step, state_in[0][member], (kv_rows, key_blk))  230 us
    reduce_scatter x1, waiting for transfers between devices, local(): lax.psum_scatter(grad_kv_all, 'seq', scatter_dimension=1, tiled=True)  118 us
    reduce_scatter x1, waiting for transfers between devices, local(): lax.psum_scatter(terms[3], 'seq', scatter_dimension=0, tiled=True)  114 us
    all_gather x1, waiting for transfers between devices, local(): lax.all_gather(shards[4], 'seq', axis=0, tiled=True)  97.4 us
    unnamed x2, blocking collectives  95.3 us
  transfers between devices with their start and end apart: 17, of which 17 were waited for; matrix products, arithmetic and copies ran while one was open for 9% of the time, Pallas kernels for 0%

commit v1 on v0

--- a/solution.py
+++ b/solution.py
@@ -1,6 +1,10 @@
+import functools
+
 import jax
 import jax.numpy as jnp
 from jax import lax
+from jax.experimental import pallas as pl
+from jax.experimental.pallas import tpu as pltpu
 from jax.sharding import PartitionSpec as P
 
 HEADS = 16
@@ -138,7 +142,584 @@
     return (grad_query, grad_key, grad_value)
 
 
-def local(
+BIT_X, BIT_ZH, BIT_ZL, BIT_Y, BIT_C = 16, 8, 4, 2, 1
+DEVICES = 32
+AXES = ("grp", "seq")
+SQUARE = ((64, (BIT_X, BIT_Y, BIT_C)), (64, (BIT_Y, BIT_X, BIT_C)))
+CUBE = (
+    (48, (BIT_X, BIT_Y, BIT_ZL, BIT_C)),
+    (48, (BIT_Y, BIT_ZL, BIT_X, BIT_C)),
+    (32, (BIT_ZL, BIT_X, BIT_Y, BIT_C)),
+)
+VMEM_LIMIT = 48 * 1024 * 1024
+
+
+def swap(value, mask, sends=None):
+    pairs = [(i, i ^ mask) for i in range(DEVICES) if sends is None or sends(i)]
+    return lax.ppermute(value, AXES, pairs)
+
+
+def bit_of(index, mask):
+    return 1 if index & mask else 0
+
+
+def gather_rows(rows, parts):
+    first, gathered = 0, []
+    for count, order in parts:
+        held = rows[first : first + count]
+        for mask in order:
+            held = jnp.concatenate([held, swap(held, mask)], axis=0)
+        gathered.append(held)
+        first += count
+    return gathered
+
+
+def scatter_rows(pieces, parts):
+    totals = []
+    for held, (count, order) in zip(pieces, parts):
+        for mask in reversed(order):
+            half = held.shape[0] // 2
+            arrived = swap(held[half:], mask)
+            total = held[:half].astype(jnp.float32) + arrived.astype(jnp.float32)
+            held = total if half == count else total.astype(jnp.bfloat16)
+        totals.append(held)
+    return jnp.concatenate(totals, axis=0)
+
+
+def z_of(index):
+    return (index // 4) % 4
+
+
+def line_gather(value, z_index):
+    below, above = [], []
+    rising, falling = value, value
+    for step in range(3):
+        rising = lax.ppermute(
+            rising, AXES, [(i, i + 4) for i in range(DEVICES) if step <= z_of(i) < 3]
+        )
+        falling = lax.ppermute(
+            falling, AXES, [(i, i - 4) for i in range(DEVICES) if 0 < z_of(i) <= 3 - step]
+        )
+        below.append(rising)
+        above.append(falling)
+    slots = jnp.stack([below[2], below[1], below[0], value, above[0], above[1], above[2]])
+    return lax.dynamic_slice_in_dim(slots, 3 - z_index, 4, axis=0)
+
+
+def line_scatter(terms, z_index):
+    def term_for(z_to):
+        return lax.dynamic_index_in_dim(terms, jnp.clip(z_to, 0, 3), 0, keepdims=False)
+
+    rising, falling = None, None
+    for step in (3, 2, 1):
+        up, down = term_for(z_index + step), term_for(z_index - step)
+        if rising is not None:
+            up = (up.astype(jnp.float32) + rising.astype(jnp.float32)).astype(jnp.bfloat16)
+            down = (down.astype(jnp.float32) + falling.astype(jnp.float32)).astype(jnp.bfloat16)
+        rising = lax.ppermute(
+            up, AXES, [(i, i + 4) for i in range(DEVICES) if z_of(i) + step <= 3]
+        )
+        falling = lax.ppermute(
+            down, AXES, [(i, i - 4) for i in range(DEVICES) if z_of(i) - step >= 0]
+        )
+    own = term_for(z_index).astype(jnp.float32)
+    return own + rising.astype(jnp.float32) + falling.astype(jnp.float32)
+
+
+def trade_blocks(blocks, masks):
+    for count, mask in enumerate(masks):
+        axis = count
+        keep = lax.index_in_dim(blocks, 0, axis, keepdims=False)
+        send = lax.index_in_dim(blocks, 1, axis, keepdims=False)
+        blocks = jnp.stack([keep, swap(send, mask)])
+    return blocks
+
+
+def permute_blocks(table, blocks, out_dtype):
+    count = table.shape[0]
+    rows, columns = blocks.shape[1:]
+
+    def body(table_ref, in_ref, out_ref):
+        out_ref[...] = in_ref[...].astype(out_dtype)
+
+    return pl.pallas_call(
+        body,
+        out_shape=jax.ShapeDtypeStruct((count, rows, columns), out_dtype),
+        grid_spec=pltpu.PrefetchScalarGridSpec(
+            num_scalar_prefetch=1,
+            grid=(count,),
+            in_specs=[pl.BlockSpec((1, rows, columns), lambda i, t: (t[i], 0, 0))],
+            out_specs=pl.BlockSpec((1, rows, columns), lambda i, t: (i, 0, 0)),
+        ),
+    )(table, blocks)
+
+
+def pick_columns(table, first, second, gain_rows, width):
+    count, rows = table.shape[0], first.shape[0]
+
+    def body(table_ref, first_ref, second_ref, gain_ref, out_ref):
+        gain = gain_ref[...]
+        out_ref[0, :, :width] = (first_ref[...].astype(jnp.float32) * gain).astype(jnp.bfloat16)
+        out_ref[0, :, width:] = (second_ref[...].astype(jnp.float32) * gain).astype(jnp.bfloat16)
+
+    return pl.pallas_call(
+        body,
+        out_shape=jax.ShapeDtypeStruct((count, rows, 2 * width), jnp.bfloat16),
+        grid_spec=pltpu.PrefetchScalarGridSpec(
+            num_scalar_prefetch=1,
+            grid=(count,),
+            in_specs=[
+                pl.BlockSpec((rows, width), lambda i, t: (0, t[i])),
+                pl.BlockSpec((rows, width), lambda i, t: (0, t[i])),
+                pl.BlockSpec((rows, 1), lambda i, t: (0, 0)),
+            ],
+            out_specs=pl.BlockSpec((1, rows, 2 * width), lambda i, t: (i, 0, 0)),
+        ),
+    )(table, first, second, gain_rows)
+
+
+def spread_columns(table, blocks, gain_rows, width):
+    count, rows = table.shape[0], blocks.shape[1]
+
+    def body(table_ref, in_ref, gain_ref, first_ref, second_ref):
+        gain = gain_ref[...]
+        first_ref[...] = in_ref[0, :, :width].astype(jnp.float32) * gain
+        second_ref[...] = in_ref[0, :, width:].astype(jnp.float32) * gain
+
+    return pl.pallas_call(
+        body,
+        out_shape=[jax.ShapeDtypeStruct((rows, count * width), jnp.float32)] * 2,
+        grid_spec=pltpu.PrefetchScalarGridSpec(
+            num_scalar_prefetch=1,
+            grid=(count,),
+            in_specs=[
+                pl.BlockSpec((1, rows, 2 * width), lambda i, t: (t[i], 0, 0)),
+                pl.BlockSpec((rows, 1), lambda i, t: (0, 0)),
+            ],
+            out_specs=[pl.BlockSpec((rows, width), lambda i, t: (0, i))] * 2,
+        ),
+    )(table, blocks, gain_rows)
+
+
+def attend_forward(queries, keys, values, query_blk, key_blk, score_scale):
+    seqs, heads, rows, depth = queries.shape
+    key_count = keys.shape[1]
+    tile = 256
+
+    def body(q_ref, k_ref, v_ref, qb_ref, kb_ref, out_ref, total_ref):
+        scores = times_back(q_ref[0, 0], k_ref[0]) * score_scale
+        scores = jnp.where(kb_ref[0] <= qb_ref[0], scores, masked_score)
+        top = jnp.max(scores, axis=-1, keepdims=True)
+        likely = jnp.exp(scores - top)
+        row_sum = jnp.sum(likely, axis=-1, keepdims=True)
+        mixed = jnp.dot(
+            likely.astype(jnp.bfloat16), v_ref[0], preferred_element_type=jnp.float32
+        )
+        out_ref[0, 0] = mixed / row_sum
+        total_ref[0, 0] = top + jnp.log(row_sum)
+
+    q_spec = pl.BlockSpec((1, 1, tile, depth), lambda s, h, t: (s, h, t, 0))
+    k_spec = pl.BlockSpec((1, key_count, depth), lambda s, h, t: (s, 0, 0))
+    return pl.pallas_call(
+        body,
+        out_shape=[
+            jax.ShapeDtypeStruct((seqs, heads, rows, depth), jnp.float32),
+            jax.ShapeDtypeStruct((seqs, heads, rows, 1), jnp.float32),
+        ],
+        grid=(seqs, heads, rows // tile),
+        in_specs=[
+            q_spec,
+            k_spec,
+            k_spec,
+            pl.BlockSpec((1, tile, 1), lambda s, h, t: (s, t, 0)),
+            pl.BlockSpec((1, 1, key_count), lambda s, h, t: (s, 0, 0)),
+        ],
+        out_specs=[
+            q_spec,
+            pl.BlockSpec((1, 1, tile, 1), lambda s, h, t: (s, h, t, 0)),
+        ],
+        compiler_params=pltpu.CompilerParams(vmem_limit_bytes=VMEM_LIMIT),
+        cost_estimate=pl.CostEstimate(
+            flops=4 * seqs * heads * rows * key_count * depth,
+            bytes_accessed=8 * 1024 * 1024,
+            transcendentals=seqs * heads * rows * key_count,
+        ),
+    )(queries, keys, values, query_blk, key_blk)
+
+
+def attend_backward(
+    queries, keys, values, attention, grad_heads, totals, query_blk, key_blk, score_scale
+):
+    seqs, heads, rows, depth = queries.shape
+    key_count = keys.shape[1]
+    tile = 256
+
+    def body(
+        q_ref, k_ref, v_ref, a_ref, g_ref, total_ref, qb_ref, kb_ref, dq_ref, dk_ref, dv_ref
+    ):
+        first = (pl.program_id(1) == 0) & (pl.program_id(2) == 0)
+
+        @pl.when(first)
+        def _():
+            dk_ref[...] = jnp.zeros_like(dk_ref)
+            dv_ref[...] = jnp.zeros_like(dv_ref)
+
+        grads = g_ref[0, 0]
+        delta = jnp.sum(grads.astype(jnp.float32) * a_ref[0, 0], axis=-1, keepdims=True)
+        scores = times_back(q_ref[0, 0], k_ref[0]) * score_scale
+        scores = jnp.where(kb_ref[0] <= qb_ref[0], scores, masked_score)
+        chance = jnp.exp(scores - total_ref[0, 0])
+        dv_ref[0] += over_rows(chance.astype(jnp.bfloat16), grads)
+        grad_chance = times_back(grads, v_ref[0])
+        grad_scores = (chance * (grad_chance - delta)).astype(jnp.bfloat16)
+        dq_ref[0, 0] = (
+            jnp.dot(grad_scores, k_ref[0], preferred_element_type=jnp.float32) * score_scale
+        )
+        dk_ref[0] += over_rows(grad_scores, q_ref[0, 0]) * score_scale
+
+    q_spec = pl.BlockSpec((1, 1, tile, depth), lambda s, h, t: (s, h, t, 0))
+    k_spec = pl.BlockSpec((1, key_count, depth), lambda s, h, t: (s, 0, 0))
+    return pl.pallas_call(
+        body,
+        out_shape=[
+            jax.ShapeDtypeStruct((seqs, heads, rows, depth), jnp.float32),
+            jax.ShapeDtypeStruct((seqs, key_count, depth), jnp.float32),
+            jax.ShapeDtypeStruct((seqs, key_count, depth), jnp.float32),
+        ],
+        grid=(seqs, heads, rows // tile),
+        in_specs=[
+            q_spec,
+            k_spec,
+            k_spec,
+            q_spec,
+            q_spec,
+            pl.BlockSpec((1, 1, tile, 1), lambda s, h, t: (s, h, t, 0)),
+            pl.BlockSpec((1, tile, 1), lambda s, h, t: (s, t, 0)),
+            pl.BlockSpec((1, 1, key_count), lambda s, h, t: (s, 0, 0)),
+        ],
+        out_specs=[q_spec, k_spec, k_spec],
+        compiler_params=pltpu.CompilerParams(vmem_limit_bytes=VMEM_LIMIT),
+        cost_estimate=pl.CostEstimate(
+            flops=10 * seqs * heads * rows * key_count * depth,
+            bytes_accessed=16 * 1024 * 1024,
+            transcendentals=seqs * heads * rows * key_count,
+        ),
+    )(queries, keys, values, attention, grad_heads, totals, query_blk, key_blk)
+
+
+def by_sequence(parts):
+    width = parts[0].shape[1]
+    first = parts[0].reshape(2, 2, 2, 64, width).transpose(2, 1, 0, 3, 4)
+    second = parts[1].reshape(2, 2, 2, 64, width).transpose(1, 2, 0, 3, 4)
+    return jnp.stack([first, second], axis=3).reshape(2, 512, width)
+
+
+def by_arrival(rows):
+    width = rows.shape[2]
+    split = rows.reshape(2, 2, 2, 2, 64, width)
+    first = split[:, :, :, 0].transpose(2, 1, 0, 3, 4).reshape(512, width)
+    second = split[:, :, :, 1].transpose(2, 0, 1, 3, 4).reshape(512, width)
+    return [first, second]
+
+
+def rotate_wide(rows, cosine, sine, heads):
+    return rotate(
+        rows.reshape(2, 512, heads, HEAD_DIM), cosine[None, :, None], sine[None, :, None]
+    )
+
+
+def unrotate_wide(rows, cosine, sine, heads):
+    return unrotate(
+        rows.reshape(2, 512, heads, HEAD_DIM), cosine[None, :, None], sine[None, :, None]
+    )
+
+
+def cube_plan(
+    inputs,
+    cotangent,
+    block_ids,
+    piece_order,
+    w_query,
+    w_key,
+    w_value,
+    w_out,
+    w_gate,
+    w_up,
+    w_down,
+    gain_attn,
+    gain_mlp,
+):
+    low, wide = jnp.bfloat16, jnp.float32
+    x = lax.axis_index("grp")
+    seq_at = lax.axis_index("seq")
+    z = seq_at // 4
+    zh, zl, y, c = (seq_at >> 3) & 1, (seq_at >> 2) & 1, (seq_at >> 1) & 1, seq_at & 1
+    pair = [(a, b) for a in (0, 1) for b in (0, 1)]
+    score_scale = HEAD_DIM ** (-0.5)
+    gain_rows_attn = gain_attn.astype(wide)[:, None]
+    gain_rows_mlp = gain_mlp.astype(wide)[:, None]
+
+    residual = inputs[0].astype(wide)
+    scale_first = rms_scale(residual)
+    normed_first = residual * scale_first
+    normed_parts = gather_rows(normed_first.astype(low), SQUARE)
+
+    packed = jnp.concatenate(
+        [w_query.reshape(96, 8, 192), w_key.reshape(96, 8, 96), w_value.reshape(96, 8, 96)],
+        axis=2,
+    )
+    packed = (packed.astype(wide) * gain_rows_attn[:, :, None]).astype(low).transpose(1, 0, 2)
+    near = jnp.stack([(x ^ c ^ jc) * 4 + (c ^ jc) * 2 + (y ^ jy) for jc, jy in pair])
+    wanted = permute_blocks(near, packed, low).reshape(2, 2, 96, 384)
+    traded = trade_blocks(wanted, (BIT_C, BIT_Y))
+    heads_rows = line_gather(traded.reshape(4, 96, 384), z).reshape(16, 96, 384)
+    natural = jnp.stack(
+        [zz * 4 + (yy ^ y) * 2 + (cc ^ c) for zz in range(4) for yy, cc in pair]
+    )
+    w_heads = permute_blocks(natural, heads_rows, low).reshape(1536, 384)
+
+    def owns_out(i):
+        return bit_of(i, BIT_ZL) == bit_of(i, BIT_X) ^ bit_of(i, BIT_ZH)
+
+    out_owner = zl == x ^ zh
+    side = x ^ zh
+    near_block = swap(w_out, BIT_ZL, owns_out)
+    near_block = jnp.where(out_owner, w_out, near_block)
+    far_block = swap(near_block, BIT_ZH)
+    kept_block = jnp.where(c == side, near_block, far_block)
+    sent_block = jnp.where(c == side, far_block, near_block)
+    other_block = swap(sent_block, BIT_C)
+    w_out_heads = jnp.where(
+        c == 0,
+        jnp.concatenate([kept_block, other_block], axis=0),
+        jnp.concatenate([other_block, kept_block], axis=0),
+    )
+
+    wanted_mlp = jnp.stack(
+        [
+            (x ^ c ^ jc) * 8 + (zl ^ jl) * 4 + (y ^ jy) * 2 + (c ^ jc)
+            for jc in (0, 1)
+            for jy, jl in pair
+        ]
+    )
+    picked = pick_columns(wanted_mlp, w_gate, w_up, gain_rows_mlp, 256)
+    traded = trade_blocks(picked.reshape(2, 2, 2, 96, 512), (BIT_C, BIT_Y, BIT_ZL))
+    near_rows = traded.reshape(8, 96, 512)
+    all_rows = jnp.concatenate([near_rows, swap(near_rows, BIT_ZH)], axis=0)
+    natural_mlp = seq_at ^ jnp.arange(16, dtype=jnp.int32)
+    w_both = permute_blocks(natural_mlp, all_rows, low).reshape(1536, 512)
+
+    def owns_down(i):
+        return bit_of(i, BIT_X) ^ bit_of(i, BIT_C) == bit_of(i, BIT_ZH)
+
+    down_owner = (x ^ c) == zh
+    w_rows = jnp.where(down_owner, w_down, swap(w_down, BIT_ZH, owns_down))
+
+    grads_parts = gather_rows(cotangent[0], CUBE)
+
+    pieces = jnp.stack(
+        [piece_order[zz * 4 + (y ^ jy) * 2 + (c ^ jc)] for zz in range(4) for jy, jc in pair]
+    )
+    own_pieces = lax.dynamic_slice_in_dim(pieces, z * 4, 4)
+    own_pos = (own_pieces[:, None] * 128 + jnp.arange(128, dtype=jnp.int32)[None, :]).reshape(512)
+    frequency = rope_base ** (-jnp.arange(HEAD_DIM // 2, dtype=wide) * 2.0 / HEAD_DIM)
+    angles = own_pos.astype(wide)[:, None] * frequency[None, :]
+    cosine, sine = jnp.cos(angles), jnp.sin(angles)
+    ids = jnp.concatenate([block_ids, swap(block_ids, BIT_X)], axis=0).reshape(2, 16, 128)
+    chosen = (pieces[:, None] == jnp.arange(16, dtype=jnp.int32)[None, :]).astype(wide)
+    key_blk = jnp.einsum(
+        "kp,spr->skr", chosen, ids.astype(wide), precision=lax.Precision.HIGHEST
+    )
+    query_blk = lax.dynamic_slice_in_dim(key_blk, z * 4, 4, axis=1).reshape(2, 512, 1)
+    key_blk = key_blk.reshape(2, 1, 2048)
+
+    projected = by_sequence(
+        [jnp.dot(part, w_heads, preferred_element_type=wide) for part in normed_parts]
+    )
+    turned = rotate_wide(projected[:, :, :288], cosine, sine, 3).astype(low)
+    queries = turned[:, :, :2].transpose(0, 2, 1, 3)
+    own_keys = turned[:, :, 2]
+    own_values = projected[:, :, 288:].astype(low)
+    sent_kv = jnp.concatenate(
+        [own_keys[0], own_keys[1], own_values[0], own_values[1]], axis=1
+    )
+    all_kv = line_gather(sent_kv, z).reshape(2048, 4, HEAD_DIM).transpose(1, 0, 2)
+    keys, values = all_kv[:2], all_kv[2:]
+    attention, totals = attend_forward(
+        queries, keys, values, query_blk, key_blk, score_scale
+    )
+    attended = by_arrival(attention.astype(low).transpose(0, 2, 1, 3).reshape(2, 512, 192))
+    mixed = scatter_rows(
+        [
+            jnp.dot(part, w_out_heads, preferred_element_type=wide).astype(low)
+            for part in attended
+        ],
+        SQUARE,
+    )
+    middle = residual + mixed
+
+    scale_second = rms_scale(middle)
+    normed_second = middle * scale_second
+    mlp_parts = gather_rows(normed_second.astype(low), CUBE)
+    out_terms, back_terms, grad_both_terms, grad_down_terms = [], [], [], []
+    for rows, grads in zip(mlp_parts, grads_parts):
+        both = jnp.dot(rows, w_both, preferred_element_type=wide)
+        gate, up = both[:, :256], both[:, 256:]
+        bend = jax.nn.sigmoid(gate)
+        hidden = (gate * bend * up).astype(low)
+        grad_hidden = times_back(grads, w_rows)
+        grad_gate = (grad_hidden * up * bend * (1.0 + gate * (1.0 - bend))).astype(low)
+        grad_up = (grad_hidden * gate * bend).astype(low)
+        grad_both = jnp.concatenate([grad_gate, grad_up], axis=1)
+        back_terms.append(times_back(grad_both, w_both).astype(low))
+        out_terms.append(jnp.dot(hidden, w_rows, preferred_element_type=wide).astype(low))
+        grad_both_terms.append(over_rows(rows, grad_both))
+        grad_down_terms.append(over_rows(hidden, grads))
+    scaled_second = scatter_rows(back_terms, CUBE)
+    output = (middle + scatter_rows(out_terms, CUBE)).astype(low)
+    upstream = cotangent[0].astype(wide)
+    grad_middle = upstream + scale_second * (
+        scaled_second
+        - normed_second * jnp.mean(scaled_second * normed_second, axis=-1, keepdims=True)
+    )
+
+    middle_parts = gather_rows(grad_middle.astype(low), SQUARE)
+    grad_attended = by_sequence([times_back(part, w_out_heads).astype(low) for part in middle_parts])
+    grad_heads = grad_attended.reshape(2, 512, 2, HEAD_DIM).transpose(0, 2, 1, 3)
+    grad_out_heads = sum(
+        over_rows(left, right) for left, right in zip(attended, middle_parts)
+    )
+    grad_queries, grad_keys, grad_values = attend_backward(
+        queries,
+        keys,
+        values,
+        attention,
+        grad_heads,
+        totals,
+        query_blk,
+        key_blk,
+        score_scale,
+    )
+    kv_terms = jnp.concatenate(
+        [grad_keys[0], grad_keys[1], grad_values[0], grad_values[1]], axis=1
+    ).astype(low)
+    kv_own = line_scatter(kv_terms.reshape(4, 512, 384), z)
+    kv_own = kv_own.reshape(512, 2, 2, HEAD_DIM)
+    grad_key_pre = unrotate_wide(kv_own[:, 0].transpose(1, 0, 2), cosine, sine, 1)
+    grad_value_pre = kv_own[:, 1].transpose(1, 0, 2)
+    grad_query_pre = unrotate_wide(grad_queries.transpose(0, 2, 1, 3), cosine, sine, 2)
+    grad_heads_pre = jnp.concatenate(
+        [
+            grad_query_pre.reshape(2, 512, 192),
+            grad_key_pre.reshape(2, 512, 96),
+            grad_value_pre,
+        ],
+        axis=2,
+    ).astype(low)
+    pre_parts = by_arrival(grad_heads_pre)
+    scaled_first = scatter_rows(
+        [times_back(part, w_heads).astype(low) for part in pre_parts], SQUARE
+    )
+    grad_inputs = grad_middle + scale_first * (
+        scaled_first
+        - normed_first * jnp.mean(scaled_first * normed_first, axis=-1, keepdims=True)
+    )
+
+    grad_heads_w = sum(over_rows(left, right) for left, right in zip(normed_parts, pre_parts))
+    away = jnp.stack(
+        [zz * 4 + (y ^ jy) * 2 + (c ^ jc) for zz in range(4) for jc, jy in pair]
+    )
+    terms = permute_blocks(away, grad_heads_w.reshape(16, 96, 384), low)
+    mine = line_scatter(terms.reshape(4, 4, 96, 384), z).astype(low)
+    held = trade_blocks(mine.reshape(2, 2, 96, 384), (BIT_C, BIT_Y)).reshape(4, 96, 384)
+    held = jnp.concatenate([held, swap(held, BIT_X)], axis=0)
+    home = jnp.stack(
+        [
+            (k2 ^ k1 ^ x) * 4 + (k0 ^ y) * 2 + (k1 ^ c)
+            for k2 in (0, 1)
+            for k1, k0 in pair
+        ]
+    )
+    raw = permute_blocks(home, held, wide).transpose(1, 0, 2)
+    own_heads = packed_rows(w_query, w_key, w_value)
+    grad_gain_attn = jnp.sum(raw * own_heads, axis=(1, 2))
+    raw = raw * gain_rows_attn[:, :, None]
+    grad_w_query = raw[:, :, :192].reshape(96, 1536)
+    grad_w_key = raw[:, :, 192:288].reshape(96, 768)
+    grad_w_value = raw[:, :, 288:].reshape(96, 768)
+
+    first_half, second_half = grad_out_heads[:96].astype(low), grad_out_heads[96:].astype(low)
+    kept = jnp.where(c == 0, first_half, second_half)
+    arrived = swap(jnp.where(c == 0, second_half, first_half), BIT_C)
+    stays = jnp.where(c == side, kept, arrived)
+    leaves = jnp.where(c == side, arrived, kept)
+    total = (stays.astype(wide) + swap(leaves, BIT_ZH).astype(wide)).astype(low)
+    total = total.astype(wide) + swap(total, BIT_ZL, lambda i: not owns_out(i)).astype(wide)
+    grad_w_out = jnp.where(
+        out_owner, total, swap(total.astype(low), BIT_X, owns_out).astype(wide)
+    )
+
+    grad_down = sum(grad_down_terms)
+    total = grad_down + swap(
+        grad_down.astype(low), BIT_ZH, lambda i: not owns_down(i)
+    ).astype(wide)
+    grad_w_down = jnp.where(
+        down_owner, total, swap(total.astype(low), BIT_X, owns_down).astype(wide)
+    )
+
+    grad_both_w = sum(grad_both_terms)
+    away_mlp = jnp.stack(
+        [
+            seq_at ^ (jh * 8 + jl * 4 + jy * 2 + jc)
+            for jh in (0, 1)
+            for jc in (0, 1)
+            for jy, jl in pair
+        ]
+    )
+    terms = permute_blocks(away_mlp, grad_both_w.reshape(16, 96, 512), low)
+    arrived = swap(terms[8:], BIT_ZH)
+    mine = (terms[:8].astype(wide) + arrived.astype(wide)).astype(low)
+    held = trade_blocks(mine.reshape(2, 2, 2, 96, 512), (BIT_C, BIT_Y, BIT_ZL))
+    held = held.reshape(8, 96, 512)
+    held = jnp.concatenate([held, swap(held, BIT_X)], axis=0)
+    home_mlp = jnp.stack(
+        [
+            (h ^ cc ^ x) * 8 + (ll ^ zl) * 4 + (yy ^ y) * 2 + (cc ^ c)
+            for h in (0, 1)
+            for ll in (0, 1)
+            for yy, cc in pair
+        ]
+    )
+    grad_w_gate, grad_w_up = spread_columns(home_mlp, held, gain_rows_mlp, 256)
+    grad_gain_mlp = (
+        jnp.sum(
+            grad_w_gate * w_gate.astype(wide) + grad_w_up * w_up.astype(wide), axis=1
+        )
+        / gain_rows_mlp[:, 0]
+    )
+    return (
+        output[None],
+        grad_inputs.astype(low)[None],
+        grad_w_query,
+        grad_w_key,
+        grad_w_value,
+        grad_w_out,
+        grad_w_gate,
+        grad_w_up,
+        grad_w_down,
+        grad_gain_attn,
+        grad_gain_mlp,
+    )
+
+
+def packed_rows(w_query, w_key, w_value):
+    return jnp.concatenate(
+        [w_query.reshape(96, 8, 192), w_key.reshape(96, 8, 96), w_value.reshape(96, 8, 96)],
+        axis=2,
+    ).astype(jnp.float32)
+
+
+def ring_plan(
     inputs,
     cotangent,
     block_ids,
@@ -429,6 +1010,9 @@
 
 
 def solution(mesh):
+    local = ring_plan
+    if (mesh.shape["grp"], mesh.shape["seq"]) == (2, 16):
+        local = cube_plan
     return jax.shard_map(
         local,
         mesh=mesh,

time: 2310 us -> 761 us (0.33)
  waiting for transfers between devices: 1610 us -> 279 us
  local copies, waits for them, and re-layouts: 305 us -> 96.4 us
  starting transfers between devices: 0.89 us -> 151 us
  matrix products: 174 us -> 52.8 us
  blocking collectives: 100 us -> 0 us
  Pallas kernels: 0 us -> 96.5 us
    reduce_scatter x8 -> x0, waiting for transfers between devices: 1190 us -> none  [the longest x1 245 us: local(): lax.psum_scatter(terms[4], 'seq', scatter_dimension=0, tiled=True)]
    all_gather x8 -> x0, waiting for transfers between devices: 403 us -> none  [the longest x1 97.4 us: local(): lax.all_gather(shards[4], 'seq', axis=0, tiled=True)]
    ppermute x0 -> x121, waiting for transfers between devices: none -> 279 us  [the longest x97 199 us: swap(): return lax.ppermute(value, AXES, pairs)]
    dynamic_update_slice x8 -> x0, local copies, waits for them, and re-layouts: 230 us -> none  [local(): lax.scan(backward_key_step, state_in[0][member], (kv_rows, key_blk))]
    ppermute x0 -> x121, starting transfers between devices: none -> 151 us  [the longest x97 101 us: swap(): return lax.ppermute(value, AXES, pairs)]
    pallas_call x0 -> x10, Pallas kernels: none -> 96.5 us  [the longest x6 50.1 us: permute_blocks(): pl.pallas_call(body, out_shape=jax.ShapeDtypeStruct((count, rows, columns...]
    unnamed x2 -> x0, blocking collectives: 95.3 us -> none
    dot_general x21 -> x11, matrix products: 83.8 us -> 12.3 us  [the longest x3 4.04 us: cube_plan(): both = jnp.dot(rows, w_both, preferred_element_type=wide)]
  transfers between devices with their start and end apart: 17 -> 121, of which waited for: 17 -> 53; matrix products, arithmetic and copies ran while one was open for 9% -> 23% of each run, Pallas kernels for 0% -> 7%
where the time goes in v1:
time: 761 us; the launch traced here: 750 us
  waiting for transfers between devices  279 us (37%)
  starting transfers between devices  151 us (20%)
  Pallas kernels  96.5 us (13%)
  local copies, waits for them, and re-layouts  96.4 us (13%)
  other arithmetic  70.3 us (9%)
  matrix products  52.8 us (7%)
    ppermute x97, waiting for transfers between devices, swap(): return lax.ppermute(value, AXES, pairs)  199 us
    ppermute x97, starting transfers between devices, swap(): return lax.ppermute(value, AXES, pairs)  101 us
    pallas_call x6, Pallas kernels, permute_blocks(): pl.pallas_call(body, out_shape=jax.ShapeDtypeStruct((count, rows, columns...  50.1 us
    ppermute x6, waiting for transfers between devices, line_gather(): lax.ppermute(falling, AXES, [(i, i - 4) for i in range(DEVICES) if 0 < z_...  41.3 us
    unnamed x331, local copies, waits for them, and re-layouts  31.7 us
    dot_general x10, matrix products, over_rows(): lax.dot_general(left, right, (((0,), (0,)), ((), ())), preferred_element_...  23.3 us
    ppermute x6, starting transfers between devices, line_scatter(): lax.ppermute(up, AXES, [(i, i + 4) for i in range(DEVICES) if z_of(i) + s...  23.2 us
    ppermute x6, waiting for transfers between devices, line_scatter(): lax.ppermute(up, AXES, [(i, i + 4) for i in range(DEVICES) if z_of(i) + s...  21.7 us
  transfers between devices with their start and end apart: 121, of which 53 were waited for; matrix products, arithmetic and copies ran while one was open for 23% of the time, Pallas kernels for 7%

profile of v1, /device:TPU:0, one launch (start us, length us, event | category | flops | bytes accessed | tf_op | source)
XLA Modules:
  0.0 749.6 jit_solution(11656941571875215421)
XLA Ops:
  2.7 5.9 shard_map.215
  14.0 3.9 shard_map.212
  20.1 3.0 collective-permute-start.11
  28.0 10.3 %stack.403 = s32[16]{0:T(128)S(1)} concatenate(s32[1]{0:T(128)} %get-tuple-element.136, s32[1]{0:T(128)} %get-tuple-element.135, s32[1]{0:T(128)} %get-tuple-element.134, s32[1]{0:T(128)} %get-tuple-element.133, s32[1]{0:T(128)} %get-tuple-element.132, s32[1]{0:T(128)} %get-tuple-element.131, s32[1]{0:T(128)} %get-tuple-element.130, s32[1]{0:T(128)} %get-tuple-element.129, ...), dimensions={0} | concatenate | bytes 128 | tf_op jit(solution)/shard_map/stack | solution.py:520
  49.6 4.4 collective-permute-done.67
  56.2 3.5 collective-permute-start.21
  67.3 3.8 collective-permute-done.76
  75.1 6.8 collective-permute-done.68
  81.8 4.4 collective-permute-start.5
  89.5 8.5 %collective-permute-done.22 = bf16[96,1536]{1,0:T(8,128)(2,1)S(1)} collective-permute-done((bf16[96,1536]{1,0:T(8,128)(2,1)S(1)}, bf16[96,1536]{1,0:T(8,128)(2,1)S(1)}, u32[]{:S(2)}, u32[]{:S(2)}) %collective-permute-start.22) | collective-permute-done | bytes 294944 | tf_op jit(solution)/shard_map/ppermute | solution.py:159
  104.2 8.6 %collective-permute-start.69 = (bf16[192,1536]{1,0:T(8,128)(2,1)}, bf16[192,1536]{1,0:T(8,128)(2,1)}, u32[]{:S(2)}, u32[]{:S(2)}) collective-permute-start(bf16[192,1536]{1,0:T(8,128)(2,1)} %pad_maximum_fusion.28), channel_id=1, source_target_pairs={{0,16},{1,17},{2,18},{3,19},{4,20},{5,21},{6,22},{7,23},{8,24},{9,... | collective-permute-start | bytes 1769480 | tf_op jit(solution)/shard_map/ppermute | solution.py:159
  115.2 7.9 %collective-permute-start.61 = (bf16[192,1536]{1,0:T(8,128)(2,1)}, bf16[192,1536]{1,0:T(8,128)(2,1)}, u32[]{:S(2)}, u32[]{:S(2)}) collective-permute-start(bf16[192,1536]{1,0:T(8,128)(2,1)} %pad_maximum_fusion.27), channel_id=1, source_target_pairs={{0,4},{1,5},{2,6},{3,7},{4,0},{5,1},{6,2},{7,3},{8,12},{9,13},{10,... | collective-permute-start | bytes 1769480 | tf_op jit(solution)/shard_map/ppermute | solution.py:159
  127.0 8.2 %collective-permute-done.9 = bf16[4,96,384]{2,1,0:T(8,128)(2,1)S(1)} collective-permute-done((bf16[4,96,384]{2,1,0:T(8,128)(2,1)S(1)}, bf16[4,96,384]{2,1,0:T(8,128)(2,1)S(1)}, u32[]{:S(2)}, u32[]{:S(2)}) %collective-permute-start.9) | collective-permute-done | bytes 294944 | tf_op jit(solution)/shard_map/ppermute | solution.py:200
  137.0 9.5 %collective-permute-done.10 = bf16[4,96,384]{2,1,0:T(8,128)(2,1)S(1)} collective-permute-done((bf16[4,96,384]{2,1,0:T(8,128)(2,1)S(1)}, bf16[4,96,384]{2,1,0:T(8,128)(2,1)S(1)}, u32[]{:S(2)}, u32[]{:S(2)}) %collective-permute-start.10) | collective-permute-done | bytes 294944 | tf_op jit(solution)/shard_map/ppermute | solution.py:200
  147.7 9.9 %shard_map.213 = bf16[16,96,384]{2,1,0:T(8,128)(2,1)} custom-call(s32[16]{0:T(128)} %stack.383.table_ref, bf16[16,96,384]{2,1,0:T(8,128)(2,1)} %bitcast.431), custom_call_target="tpu_custom_call" | custom-call | tf_op jit(solution)/shard_map/pallas_call | solution.py:245
  174.1 4.0 collective-permute-start.14
  200.2 19.9 %collective-permute-done.37 = bf16[8,96,512]{2,1,0:T(8,128)(2,1)S(1)} collective-permute-done((bf16[8,96,512]{2,1,0:T(8,128)(2,1)S(1)}, bf16[8,96,512]{2,1,0:T(8,128)(2,1)S(1)}, u32[]{:S(2)}, u32[]{:S(2)}) %collective-permute-start.37) | collective-permute-done | bytes 786464 | tf_op jit(solution)/shard_map/ppermute | solution.py:159
  221.4 10.0 %shard_map.216 = bf16[16,96,512]{2,1,0:T(8,128)(2,1)} custom-call(s32[16]{0:T(128)} %iota_xor_fusion.table_ref, bf16[16,96,512]{2,1,0:T(8,128)(2,1)} %pad_maximum_fusion.3.in_ref), custom_call_target="tpu_custom_call" | custom-call | tf_op jit(solution)/shard_map/pallas_call | solution.py:245
  231.4 9.1 %collective-permute-done.18 = bf16[512,384]{1,0:T(8,128)(2,1)S(1)} collective-permute-done((bf16[512,384]{1,0:T(8,128)(2,1)}, bf16[512,384]{1,0:T(8,128)(2,1)S(1)}, u32[]{:S(2)}, u32[]{:S(2)}) %collective-permute-start.18) | collective-permute-done | bytes 393248 | tf_op jit(solution)/shard_map/ppermute | solution.py:200
  244.5 11.8 %collective-permute-done.19 = bf16[512,384]{1,0:T(8,128)(2,1)S(1)} collective-permute-done((bf16[512,384]{1,0:T(8,128)(2,1)S(1)}, bf16[512,384]{1,0:T(8,128)(2,1)S(1)}, u32[]{:S(2)}, u32[]{:S(2)}) %collective-permute-start.19) | collective-permute-done | bytes 393248 | tf_op jit(solution)/shard_map/ppermute | solution.py:200
  257.7 4.1 reshape.365
  262.3 10.0 %shard_map.214 = (f32[2,2,512,96]{3,2,1,0:T(8,128)S(1)}, f32[2,2,512,1]{3,2,1,0:T(8,128)S(1)}) custom-call(bf16[2,2,512,96]{3,2,1,0:T(8,128)(2,1)S(1)} %fusion.41.q_ref, bf16[2,2048,96]{2,1,0:T(8,128)(2,1)S(1)} %get-tuple-element.32.k_ref, bf16[2,2048,96]{2,1,0:T(8,128)(2,1)S(1)} %get-tuple-element.31.v_ref, f32[2,512,1]{2,1,0:T(8,128)S(1)} %reshape.366.qb_ref, ...), custom_call_target="tpu_custom_call" | custom-call | flops 1610612736 | bytes 8388608 | tf_op jit(solution)/shard_map/pallas_call | solution.py:323
  284.8 10.2 %collective-permute-done.28 = bf16[128,1536]{1,0:T(8,128)(2,1)S(1)} collective-permute-done((bf16[128,1536]{1,0:T(8,128)(2,1)S(1)}, bf16[128,1536]{1,0:T(8,128)(2,1)S(1)}, u32[]{:S(2)}, u32[]{:S(2)}) %collective-permute-start.28) | collective-permute-done | bytes 393248 | tf_op jit(solution)/shard_map/ppermute | solution.py:159
  297.3 3.9 collective-permute-done.29
  317.2 4.1 collective-permute-done.31
  321.7 4.1 collective-permute-done.53
  327.8 3.5 collective-permute-done.32
  340.9 3.2 fusion.110
  363.9 3.2 fusion
  370.4 10.4 %shard_map.220 = bf16[16,96,512]{2,1,0:T(8,128)(2,1)} custom-call(s32[16]{0:T(128)} %stack.477.table_ref, f32[16,96,512]{2,1,0:T(8,128)} %bitcast.419), custom_call_target="tpu_custom_call" | custom-call | tf_op jit(solution)/shard_map/pallas_call | solution.py:245
  391.3 9.1 %collective-permute-done.80 = bf16[128,1536]{1,0:T(8,128)(2,1)S(1)} collective-permute-done((bf16[128,1536]{1,0:T(8,128)(2,1)S(1)}, bf16[128,1536]{1,0:T(8,128)(2,1)S(1)}, u32[]{:S(2)}, u32[]{:S(2)}) %collective-permute-start.80) | collective-permute-done | bytes 393248 | tf_op jit(solution)/shard_map/ppermute | solution.py:159
  401.4 9.5 %collective-permute-done.56 = bf16[128,1536]{1,0:T(8,128)(2,1)S(1)} collective-permute-done((bf16[128,1536]{1,0:T(8,128)(2,1)S(1)}, bf16[128,1536]{1,0:T(8,128)(2,1)S(1)}, u32[]{:S(2)}, u32[]{:S(2)}) %collective-permute-start.56) | collective-permute-done | bytes 393248 | tf_op jit(solution)/shard_map/ppermute | solution.py:159
  411.7 4.8 collective-permute-done.81
  417.3 4.9 collective-permute-done.57
  422.5 4.4 collective-permute-done.82
  427.8 3.7 collective-permute-done.58
  433.8 20.5 %collective-permute-done.119 = bf16[256,1536]{1,0:T(8,128)(2,1)S(1)} collective-permute-done((bf16[256,1536]{1,0:T(8,128)(2,1)S(1)}, bf16[256,1536]{1,0:T(8,128)(2,1)S(1)}, u32[]{:S(2)}, u32[]{:S(2)}) %collective-permute-start.119) | collective-permute-done | bytes 786464 | tf_op jit(solution)/shard_map/ppermute | solution.py:159
  466.1 9.1 %collective-permute-done.116 = bf16[2,2,96,512]{3,2,0,1:T(8,128)(2,1)S(1)} collective-permute-done((bf16[2,2,96,512]{3,2,0,1:T(8,128)(2,1)S(1)}, bf16[2,2,96,512]{3,2,0,1:T(8,128)(2,1)S(1)}, u32[]{:S(2)}, u32[]{:S(2)}) %collective-permute-start.116) | collective-permute-done | bytes 393248 | tf_op jit(solution)/shard_map/ppermute | solution.py:159
  478.8 4.1 collective-permute-done.72
  487.4 3.4 collective-permute-done.48
  493.8 6.1 collective-permute-done.117
  501.5 4.7 collective-permute-done.73
  513.1 7.5 %collective-permute-done.66 = bf16[48,1536]{1,0:T(8,128)(2,1)S(1)} collective-permute-done((bf16[48,1536]{1,0:T(8,128)(2,1)S(1)}, bf16[48,1536]{1,0:T(8,128)(2,1)S(1)}, u32[]{:S(2)}, u32[]{:S(2)}) %collective-permute-start.66) | collective-permute-done | bytes 147488 | tf_op jit(solution)/shard_map/ppermute | solution.py:159
  529.7 4.6 collective-permute-done.83
  545.3 11.0 %shard_map.221 = (f32[96,4096]{1,0:T(8,128)}, f32[96,4096]{1,0:T(8,128)}) custom-call(s32[16]{0:T(128)} %stack.460.table_ref, bf16[16,96,512]{2,1,0:T(8,128)(2,1)} %pad_maximum_fusion.7.in_ref, f32[96,1]{1,0:T(8,128)} %copy.54.gain_ref), custom_call_target="tpu_custom_call" | custom-call | tf_op jit(solution)/shard_map/pallas_call | solution.py:289
  556.3 3.1 add_reduce_fusion
  569.5 19.5 %shard_map.217 = (f32[2,2,512,96]{3,2,1,0:T(8,128)S(1)}, f32[2,2048,96]{2,1,0:T(8,128)}, f32[2,2048,96]{2,1,0:T(8,128)}) custom-call(bf16[2,2,512,96]{3,2,1,0:T(8,128)(2,1)S(1)} %copy-done.5, bf16[2,2048,96]{2,1,0:T(8,128)(2,1)S(1)} %copy-done.1, bf16[2,2048,96]{2,1,0:T(8,128)(2,1)S(1)} %get-tuple-element.31.v_ref, ...), custom_call_target="tpu_custom_call" | custom-call | flops 4026531840 | bytes 16777216 | tf_op jit(solution)/shard_map/pallas_call | solution.py:382
  606.6 4.0 collective-permute-start.89
  613.0 7.1 collective-permute-done.89
  620.2 4.4 collective-permute-start.90
  628.4 5.6 collective-permute-done.90
  638.5 6.9 collective-permute-start.113
  652.6 3.3 collective-permute-done.91
  655.9 5.6 collective-permute-done.94
  666.0 3.6 convolution_add_fusion.1
  669.7 10.1 %shard_map.218 = bf16[16,96,384]{2,1,0:T(8,128)(2,1)} custom-call(s32[16]{0:T(128)} %stack.439.table_ref, f32[16,96,384]{2,1,0:T(8,128)} %bitcast.439), custom_call_target="tpu_custom_call" | custom-call | tf_op jit(solution)/shard_map/pallas_call | solution.py:245
  680.9 4.0 collective-permute-start.101
  689.7 4.4 collective-permute-start.102
  695.2 3.0 collective-permute-done.102
  699.1 5.0 collective-permute-start.103
  708.8 7.7 %collective-permute-done.106 = bf16[4,96,384]{2,1,0:T(8,128)(2,1)S(1)} collective-permute-done((bf16[4,96,384]{2,1,0:T(8,128)(2,1)S(1)}, bf16[4,96,384]{2,1,0:T(8,128)(2,1)S(1)}, u32[]{:S(2)}, u32[]{:S(2)}) %collective-permute-start.106) | collective-permute-done | bytes 294944 | tf_op jit(solution)/shard_map/ppermute | solution.py:222
  721.1 3.6 collective-permute-done.100
  730.8 5.4 collective-permute-done.109
  737.1 5.8 shard_map.219
  (807 shorter events, 315.0 us)
Async XLA Ops:
  10.7 62.7 %collective-permute-start.34 = (bf16[2,2,96,512]{3,2,1,0:T(8,128)(2,1)}, bf16[2,2,96,512]{3,2,1,0:T(8,128)(2,1)}, u32[]{:S(2)}, u32[]{:S(2)}) collective-permute-start(bf16[2,2,96,512]{3,2,1,0:T(8,128)(2,1)} %bitcast.87), channel_id=1, source_target_pairs={{0,1},{1,0},{2,3},{3,2},{4,5},{5,4},{6,7},{7,6},{8,9},{9,8},{10,11... | collective-permute-start | bytes 1179656 | tf_op jit(solution)/shard_map/ppermute | solution.py:159
  19.6 36.5 %collective-permute-start.3 = (bf16[2,96,384]{2,1,0:T(8,128)(2,1)}, bf16[2,96,384]{2,1,0:T(8,128)(2,1)}, u32[]{:S(2)}, u32[]{:S(2)}) collective-permute-start(bf16[2,96,384]{2,1,0:T(8,128)(2,1)} %get-tuple-element.119), channel_id=1, source_target_pairs={{0,1},{1,0},{2,3},{3,2},{4,5},{5,4},{6,7},{7,6},{8,9},{9,8},{10,11... | collective-permute-start | bytes 442376 | tf_op jit(solution)/shard_map/ppermute | solution.py:159
  20.1 44.3 %collective-permute-start.11 = (bf16[64,1536]{1,0:T(8,128)(2,1)S(1)}, bf16[64,1536]{1,0:T(8,128)(2,1)S(1)}, u32[]{:S(2)}, u32[]{:S(2)}) collective-permute-start(bf16[64,1536]{1,0:T(8,128)(2,1)S(1)} %get-tuple-element.109), channel_id=1, source_target_pairs={{0,2},{1,3},{2,0},{3,1},{4,6},{5,7},{6,4},{7,5},{8,10},{9,11},{10,... | collective-permute-start | bytes 589832 | tf_op jit(solution)/shard_map/ppermute | solution.py:159
  23.1 41.4 %collective-permute-start = (bf16[64,1536]{1,0:T(8,128)(2,1)S(1)}, bf16[64,1536]{1,0:T(8,128)(2,1)S(1)}, u32[]{:S(2)}, u32[]{:S(2)}) collective-permute-start(bf16[64,1536]{1,0:T(8,128)(2,1)S(1)} %get-tuple-element.108), channel_id=1, source_target_pairs={{0,16},{1,17},{2,18},{3,19},{4,20},{5,21},{6,22},{7,23},{8,24},{9,... | collective-permute-start | bytes 589832 | tf_op jit(solution)/shard_map/ppermute | solution.py:159
  24.6 19.6 %collective-permute-start.20 = (s32[1,2048]{1,0:T(1,128)S(1)}, s32[1,2048]{1,0:T(1,128)S(1)}, u32[]{:S(2)}, u32[]{:S(2)}) collective-permute-start(s32[1,2048]{1,0:T(1,128)S(1)} %copy-done.139), channel_id=1, source_target_pairs={{0,16},{1,17},{2,18},{3,19},{4,20},{5,21},{6,22},{7,23},{8,24},{9,... | collective-permute-start | bytes 24584 | tf_op jit(solution)/shard_map/ppermute | solution.py:159
  60.7 62.4 %collective-permute-start.38 = (bf16[256,1536]{1,0:T(8,128)(2,1)}, bf16[256,1536]{1,0:T(8,128)(2,1)S(1)}, u32[]{:S(2)}, u32[]{:S(2)}) collective-permute-start(bf16[256,1536]{1,0:T(8,128)(2,1)} %param.23), channel_id=1, source_target_pairs={{0,8},{2,10},{4,12},{6,14},{9,1},{11,3},{13,5},{15,7},{17,25},{19,... | collective-permute-start | bytes 2359304 | tf_op jit(solution)/shard_map/ppermute | solution.py:159
  65.2 16.6 %collective-permute-start.68 = (bf16[96,1536]{1,0:T(8,128)(2,1)S(1)}, bf16[96,1536]{1,0:T(8,128)(2,1)S(1)}, u32[]{:S(2)}, u32[]{:S(2)}) collective-permute-start(bf16[96,1536]{1,0:T(8,128)(2,1)S(1)} %pad_maximum_fusion.54), channel_id=1, source_target_pairs={{0,4},{1,5},{2,6},{3,7},{4,0},{5,1},{6,2},{7,3},{8,12},{9,13},{10,... | collective-permute-start | bytes 884744 | tf_op jit(solution)/shard_map/ppermute | solution.py:159
  71.1 16.8 %collective-permute-start.60 = (bf16[96,1536]{1,0:T(8,128)(2,1)S(1)}, bf16[96,1536]{1,0:T(8,128)(2,1)S(1)}, u32[]{:S(2)}, u32[]{:S(2)}) collective-permute-start(bf16[96,1536]{1,0:T(8,128)(2,1)S(1)} %pad_maximum_fusion.53), channel_id=1, source_target_pairs={{0,2},{1,3},{2,0},{3,1},{4,6},{5,7},{6,4},{7,5},{8,10},{9,11},{10,... | collective-permute-start | bytes 884744 | tf_op jit(solution)/shard_map/ppermute | solution.py:159
  71.8 28.4 %collective-permute-start.12 = (bf16[128,1536]{1,0:T(8,128)(2,1)S(1)}, bf16[128,1536]{1,0:T(8,128)(2,1)S(1)}, u32[]{:S(2)}, u32[]{:S(2)}) collective-permute-start(bf16[128,1536]{1,0:T(8,128)(2,1)S(1)} %pad_maximum_fusion.42), channel_id=1, source_target_pairs={{0,16},{1,17},{2,18},{3,19},{4,20},{5,21},{6,22},{7,23},{8,24},{9,... | collective-permute-start | bytes 1179656 | tf_op jit(solution)/shard_map/ppermute | solution.py:159
  73.4 28.7 %collective-permute-start.1 = (bf16[128,1536]{1,0:T(8,128)(2,1)S(1)}, bf16[128,1536]{1,0:T(8,128)(2,1)S(1)}, u32[]{:S(2)}, u32[]{:S(2)}) collective-permute-start(bf16[128,1536]{1,0:T(8,128)(2,1)S(1)} %pad_maximum_fusion.41), channel_id=1, source_target_pairs={{0,2},{1,3},{2,0},{3,1},{4,6},{5,7},{6,4},{7,5},{8,10},{9,11},{10,... | collective-permute-start | bytes 1179656 | tf_op jit(solution)/shard_map/ppermute | solution.py:159
  81.8 22.3 %collective-permute-start.5 = (bf16[4,96,384]{2,1,0:T(8,128)(2,1)S(1)}, bf16[4,96,384]{2,1,0:T(8,128)(2,1)S(1)}, u32[]{:S(2)}, u32[]{:S(2)}) collective-permute-start(bf16[4,96,384]{2,1,0:T(8,128)(2,1)S(1)} %bitcast.458), channel_id=1, source_target_pairs={{0,4},{1,5},{2,6},{3,7},{4,8},{5,9},{6,10},{7,11},{8,12},{9,13},{1... | collective-permute-start | bytes 884744 | tf_op jit(solution)/shard_map/ppermute | solution.py:197
  98.0 17.2 %collective-permute-start.8 = (bf16[4,96,384]{2,1,0:T(8,128)(2,1)S(1)}, bf16[4,96,384]{2,1,0:T(8,128)(2,1)S(1)}, u32[]{:S(2)}, u32[]{:S(2)}) collective-permute-start(bf16[4,96,384]{2,1,0:T(8,128)(2,1)S(1)} %bitcast.459), channel_id=1, source_target_pairs={{4,0},{5,1},{6,2},{7,3},{8,4},{9,5},{10,6},{11,7},{12,8},{13,9},{1... | collective-permute-start | bytes 884744 | tf_op jit(solution)/shard_map/ppermute | solution.py:200
  100.2 12.6 %collective-permute-start.77 = (bf16[128,1536]{1,0:T(8,128)(2,1)S(1)}, bf16[128,1536]{1,0:T(8,128)(2,1)S(1)}, u32[]{:S(2)}, u32[]{:S(2)}) collective-permute-start(bf16[128,1536]{1,0:T(8,128)(2,1)S(1)} %pad_maximum_fusion.45), channel_id=1, source_target_pairs={{0,2},{1,3},{2,0},{3,1},{4,6},{5,7},{6,4},{7,5},{8,10},{9,11},{10,... | collective-permute-start | bytes 1179656 | tf_op jit(solution)/shard_map/ppermute | solution.py:159
  102.1 24.0 %collective-permute-start.35 = (bf16[2,2,96,512]{3,2,0,1:T(8,128)(2,1)S(1)}, bf16[2,2,96,512]{3,2,0,1:T(8,128)(2,1)S(1)}, u32[]{:S(2)}, u32[]{:S(2)}) collective-permute-start(bf16[2,2,96,512]{3,2,0,1:T(8,128)(2,1)S(1)} %get-tuple-element.73), channel_id=1, source_target_pairs={{0,2},{1,3},{2,0},{3,1},{4,6},{5,7},{6,4},{7,5},{8,10},{9,11},{10,... | collective-permute-start | bytes 1179656 | tf_op jit(solution)/shard_map/ppermute | solution.py:159
  104.2 69.9 %collective-permute-start.69 = (bf16[192,1536]{1,0:T(8,128)(2,1)}, bf16[192,1536]{1,0:T(8,128)(2,1)}, u32[]{:S(2)}, u32[]{:S(2)}) collective-permute-start(bf16[192,1536]{1,0:T(8,128)(2,1)} %pad_maximum_fusion.28), channel_id=1, source_target_pairs={{0,16},{1,17},{2,18},{3,19},{4,20},{5,21},{6,22},{7,23},{8,24},{9,... | collective-permute-start | bytes 1769480 | tf_op jit(solution)/shard_map/ppermute | solution.py:159
  115.2 68.2 %collective-permute-start.61 = (bf16[192,1536]{1,0:T(8,128)(2,1)}, bf16[192,1536]{1,0:T(8,128)(2,1)}, u32[]{:S(2)}, u32[]{:S(2)}) collective-permute-start(bf16[192,1536]{1,0:T(8,128)(2,1)} %pad_maximum_fusion.27), channel_id=1, source_target_pairs={{0,4},{1,5},{2,6},{3,7},{4,0},{5,1},{6,2},{7,3},{8,12},{9,13},{10,... | collective-permute-start | bytes 1769480 | tf_op jit(solution)/shard_map/ppermute | solution.py:159
  126.1 31.6 %collective-permute-start.13 = (bf16[256,1536]{1,0:T(8,128)(2,1)}, bf16[256,1536]{1,0:T(8,128)(2,1)}, u32[]{:S(2)}, u32[]{:S(2)}) collective-permute-start(bf16[256,1536]{1,0:T(8,128)(2,1)} %pad_maximum_fusion.13), channel_id=1, source_target_pairs={{0,1},{1,0},{2,3},{3,2},{4,5},{5,4},{6,7},{7,6},{8,9},{9,8},{10,11... | collective-permute-start | bytes 2359304 | tf_op jit(solution)/shard_map/ppermute | solution.py:159
  135.2 25.2 %collective-permute-start.2 = (bf16[256,1536]{1,0:T(8,128)(2,1)}, bf16[256,1536]{1,0:T(8,128)(2,1)}, u32[]{:S(2)}, u32[]{:S(2)}) collective-permute-start(bf16[256,1536]{1,0:T(8,128)(2,1)} %pad_maximum_fusion.12), channel_id=1, source_target_pairs={{0,1},{1,0},{2,3},{3,2},{4,5},{5,4},{6,7},{7,6},{8,9},{9,8},{10,11... | collective-permute-start | bytes 2359304 | tf_op jit(solution)/shard_map/ppermute | solution.py:159
  146.5 127.9 %collective-permute-start.23 = (bf16[96,1536]{1,0:T(8,128)(2,1)}, bf16[96,1536]{1,0:T(8,128)(2,1)}, u32[]{:S(2)}, u32[]{:S(2)}) collective-permute-start(bf16[96,1536]{1,0:T(8,128)(2,1)} %get-tuple-element.89), channel_id=1, source_target_pairs={{0,1},{1,0},{2,3},{3,2},{4,5},{5,4},{6,7},{7,6},{8,9},{9,8},{10,11... | collective-permute-start | bytes 884744 | tf_op jit(solution)/shard_map/ppermute | solution.py:159
  157.6 35.9 %collective-permute-start.78 = (bf16[256,1536]{1,0:T(8,128)(2,1)}, bf16[256,1536]{1,0:T(8,128)(2,1)}, u32[]{:S(2)}, u32[]{:S(2)}) collective-permute-start(bf16[256,1536]{1,0:T(8,128)(2,1)} %pad_maximum_fusion.18), channel_id=1, source_target_pairs={{0,1},{1,0},{2,3},{3,2},{4,5},{5,4},{6,7},{7,6},{8,9},{9,8},{10,11... | collective-permute-start | bytes 2359304 | tf_op jit(solution)/shard_map/ppermute | solution.py:159
  160.4 21.9 %collective-permute-start.36 = (bf16[2,2,96,512]{3,2,1,0:T(8,128)(2,1)}, bf16[2,2,96,512]{3,2,1,0:T(8,128)(2,1)}, u32[]{:S(2)}, u32[]{:S(2)}) collective-permute-start(bf16[2,2,96,512]{3,2,1,0:T(8,128)(2,1)} %get-tuple-element.71), channel_id=1, source_target_pairs={{0,4},{1,5},{2,6},{3,7},{4,0},{5,1},{6,2},{7,3},{8,12},{9,13},{10,... | collective-permute-start | bytes 1179656 | tf_op jit(solution)/shard_map/ppermute | solution.py:159
  174.1 13.5 %collective-permute-start.14 = (bf16[512,384]{1,0:T(8,128)(2,1)S(1)}, bf16[512,384]{1,0:T(8,128)(2,1)S(1)}, u32[]{:S(2)}, u32[]{:S(2)}) collective-permute-start(bf16[512,384]{1,0:T(8,128)(2,1)S(1)} %pad_maximum_fusion.43), channel_id=1, source_target_pairs={{0,4},{1,5},{2,6},{3,7},{4,8},{5,9},{6,10},{7,11},{8,12},{9,13},{1... | collective-permute-start | bytes 1179656 | tf_op jit(solution)/shard_map/ppermute | solution.py:197
  183.4 36.7 %collective-permute-start.37 = (bf16[8,96,512]{2,1,0:T(8,128)(2,1)S(1)}, bf16[8,96,512]{2,1,0:T(8,128)(2,1)S(1)}, u32[]{:S(2)}, u32[]{:S(2)}) collective-permute-start(bf16[8,96,512]{2,1,0:T(8,128)(2,1)S(1)} %bitcast.435), channel_id=1, source_target_pairs={{0,8},{1,9},{2,10},{3,11},{4,12},{5,13},{6,14},{7,15},{8,0},{9,1},... | collective-permute-start | bytes 2359304 | tf_op jit(solution)/shard_map/ppermute | solution.py:159
  183.5 12.7 %collective-permute-start.17 = (bf16[512,384]{1,0:T(8,128)(2,1)S(1)}, bf16[512,384]{1,0:T(8,128)(2,1)}, u32[]{:S(2)}, u32[]{:S(2)}) collective-permute-start(bf16[512,384]{1,0:T(8,128)(2,1)S(1)} %pad_maximum_fusion.43), channel_id=1, source_target_pairs={{4,0},{5,1},{6,2},{7,3},{8,4},{9,5},{10,6},{11,7},{12,8},{13,9},{1... | collective-permute-start | bytes 1179656 | tf_op jit(solution)/shard_map/ppermute | solution.py:200
  193.5 83.7 %collective-permute-start.70 = (bf16[384,1536]{1,0:T(8,128)(2,1)}, bf16[384,1536]{1,0:T(8,128)(2,1)}, u32[]{:S(2)}, u32[]{:S(2)}) collective-permute-start(bf16[384,1536]{1,0:T(8,128)(2,1)} %pad_maximum_fusion.11), channel_id=1, source_target_pairs={{0,1},{1,0},{2,3},{3,2},{4,5},{5,4},{6,7},{7,6},{8,9},{9,8},{10,11... | collective-permute-start | bytes 3538952 | tf_op jit(solution)/shard_map/ppermute | solution.py:159
  196.2 44.4 %collective-permute-start.18 = (bf16[512,384]{1,0:T(8,128)(2,1)}, bf16[512,384]{1,0:T(8,128)(2,1)S(1)}, u32[]{:S(2)}, u32[]{:S(2)}) collective-permute-start(bf16[512,384]{1,0:T(8,128)(2,1)} %collective-permute-done.17), channel_id=1, source_target_pairs={{4,0},{5,1},{6,2},{7,3},{8,4},{9,5},{10,6},{11,7},{20,16},{21,17},... | collective-permute-start | bytes 1179656 | tf_op jit(solution)/shard_map/ppermute | solution.py:200
  197.5 44.3 %collective-permute-start.16 = (bf16[512,384]{1,0:T(8,128)(2,1)}, bf16[512,384]{1,0:T(8,128)(2,1)S(1)}, u32[]{:S(2)}, u32[]{:S(2)}) collective-permute-start(bf16[512,384]{1,0:T(8,128)(2,1)} %collective-permute-done.15), channel_id=1, source_target_pairs={{8,12},{9,13},{10,14},{11,15},{24,28},{25,29},{26,30},{27,31}} | collective-permute-start | bytes 1179656 | tf_op jit(solution)/shard_map/ppermute | solution.py:197
  220.1 61.2 %collective-permute-start.62 = (bf16[384,1536]{1,0:T(8,128)(2,1)}, bf16[384,1536]{1,0:T(8,128)(2,1)}, u32[]{:S(2)}, u32[]{:S(2)}) collective-permute-start(bf16[384,1536]{1,0:T(8,128)(2,1)} %pad_maximum_fusion.10), channel_id=1, source_target_pairs={{0,1},{1,0},{2,3},{3,2},{4,5},{5,4},{6,7},{7,6},{8,9},{9,8},{10,11... | collective-permute-start | bytes 3538952 | tf_op jit(solution)/shard_map/ppermute | solution.py:159
  240.5 15.8 %collective-permute-start.19 = (bf16[512,384]{1,0:T(8,128)(2,1)S(1)}, bf16[512,384]{1,0:T(8,128)(2,1)S(1)}, u32[]{:S(2)}, u32[]{:S(2)}) collective-permute-start(bf16[512,384]{1,0:T(8,128)(2,1)S(1)} %collective-permute-done.18), channel_id=1, source_target_pairs={{4,0},{5,1},{6,2},{7,3},{20,16},{21,17},{22,18},{23,19}} | collective-permute-start | bytes 1179656 | tf_op jit(solution)/shard_map/ppermute | solution.py:200
  327.7 17.4 %collective-permute-start.46 = (bf16[384,1536]{1,0:T(8,128)(2,1)S(1)}, bf16[384,1536]{1,0:T(8,128)(2,1)S(1)}, u32[]{:S(2)}, u32[]{:S(2)}) collective-permute-start(bf16[384,1536]{1,0:T(8,128)(2,1)S(1)} %pad_maximum_fusion.9), channel_id=1, source_target_pairs={{0,1},{1,0},{2,3},{3,2},{4,5},{5,4},{6,7},{7,6},{8,9},{9,8},{10,11... | collective-permute-start | bytes 3538952 | tf_op jit(solution)/shard_map/ppermute | solution.py:159
  331.4 21.5 %collective-permute-start.33 = (bf16[384,1536]{1,0:T(8,128)(2,1)S(1)}, bf16[384,1536]{1,0:T(8,128)(2,1)S(1)}, u32[]{:S(2)}, u32[]{:S(2)}) collective-permute-start(bf16[384,1536]{1,0:T(8,128)(2,1)S(1)} %pad_maximum_fusion.8), channel_id=1, source_target_pairs={{0,1},{1,0},{2,3},{3,2},{4,5},{5,4},{6,7},{7,6},{8,9},{9,8},{10,11... | collective-permute-start | bytes 3538952 | tf_op jit(solution)/shard_map/ppermute | solution.py:159
  338.4 49.0 %collective-permute-start.79 = (bf16[256,1536]{1,0:T(8,128)(2,1)}, bf16[256,1536]{1,0:T(8,128)(2,1)}, u32[]{:S(2)}, u32[]{:S(2)}) collective-permute-start(bf16[256,1536]{1,0:T(8,128)(2,1)} %slice.691), channel_id=1, source_target_pairs={{0,1},{1,0},{2,3},{3,2},{4,5},{5,4},{6,7},{7,6},{8,9},{9,8},{10,11... | collective-permute-start | bytes 2359304 | tf_op jit(solution)/shard_map/ppermute | solution.py:159
  340.6 48.4 %collective-permute-start.55 = (bf16[256,1536]{1,0:T(8,128)(2,1)}, bf16[256,1536]{1,0:T(8,128)(2,1)}, u32[]{:S(2)}, u32[]{:S(2)}) collective-permute-start(bf16[256,1536]{1,0:T(8,128)(2,1)} %slice.667), channel_id=1, source_target_pairs={{0,1},{1,0},{2,3},{3,2},{4,5},{5,4},{6,7},{7,6},{8,9},{9,8},{10,11... | collective-permute-start | bytes 2359304 | tf_op jit(solution)/shard_map/ppermute | solution.py:159
  351.4 103.2 %collective-permute-start.71 = (bf16[384,1536]{1,0:T(8,128)(2,1)}, bf16[384,1536]{1,0:T(8,128)(2,1)}, u32[]{:S(2)}, u32[]{:S(2)}) collective-permute-start(bf16[384,1536]{1,0:T(8,128)(2,1)} %slice.683), channel_id=1, source_target_pairs={{0,1},{1,0},{2,3},{3,2},{4,5},{5,4},{6,7},{7,6},{8,9},{9,8},{10,11... | collective-permute-start | bytes 3538952 | tf_op jit(solution)/shard_map/ppermute | solution.py:159
  360.0 97.8 %collective-permute-start.63 = (bf16[384,1536]{1,0:T(8,128)(2,1)}, bf16[384,1536]{1,0:T(8,128)(2,1)}, u32[]{:S(2)}, u32[]{:S(2)}) collective-permute-start(bf16[384,1536]{1,0:T(8,128)(2,1)} %slice.675), channel_id=1, source_target_pairs={{0,1},{1,0},{2,3},{3,2},{4,5},{5,4},{6,7},{7,6},{8,9},{9,8},{10,11... | collective-permute-start | bytes 3538952 | tf_op jit(solution)/shard_map/ppermute | solution.py:159
  363.7 95.9 %collective-permute-start.47 = (bf16[384,1536]{1,0:T(8,128)(2,1)}, bf16[384,1536]{1,0:T(8,128)(2,1)}, u32[]{:S(2)}, u32[]{:S(2)}) collective-permute-start(bf16[384,1536]{1,0:T(8,128)(2,1)} %slice.656), channel_id=1, source_target_pairs={{0,1},{1,0},{2,3},{3,2},{4,5},{5,4},{6,7},{7,6},{8,9},{9,8},{10,11... | collective-permute-start | bytes 3538952 | tf_op jit(solution)/shard_map/ppermute | solution.py:159
  387.4 46.1 %collective-permute-start.114 = (bf16[8,96,512]{2,1,0:T(8,128)(2,1)S(1)}, bf16[8,96,512]{2,1,0:T(8,128)(2,1)S(1)}, u32[]{:S(2)}, u32[]{:S(2)}) collective-permute-start(bf16[8,96,512]{2,1,0:T(8,128)(2,1)S(1)} %slice.734), channel_id=1, source_target_pairs={{0,8},{1,9},{2,10},{3,11},{4,12},{5,13},{6,14},{7,15},{8,0},{9,1},... | collective-permute-start | bytes 2359304 | tf_op jit(solution)/shard_map/ppermute | solution.py:159
  431.5 22.8 %collective-permute-start.119 = (bf16[256,1536]{1,0:T(8,128)(2,1)S(1)}, bf16[256,1536]{1,0:T(8,128)(2,1)S(1)}, u32[]{:S(2)}, u32[]{:S(2)}) collective-permute-start(bf16[256,1536]{1,0:T(8,128)(2,1)S(1)} %get-tuple-element.138), channel_id=1, source_target_pairs={{1,9},{3,11},{5,13},{7,15},{8,0},{10,2},{12,4},{14,6},{16,24},{18,... | collective-permute-start | bytes 2359304 | tf_op jit(solution)/shard_map/ppermute | solution.py:159
  433.5 31.1 %collective-permute-start.39 = (bf16[384,1536]{1,0:T(8,128)(2,1)S(1)}, bf16[384,1536]{1,0:T(8,128)(2,1)S(1)}, u32[]{:S(2)}, u32[]{:S(2)}) collective-permute-start(bf16[384,1536]{1,0:T(8,128)(2,1)S(1)} %copy-done.105), channel_id=1, source_target_pairs={{0,1},{1,0},{2,3},{3,2},{4,5},{5,4},{6,7},{7,6},{8,9},{9,8},{10,11... | collective-permute-start | bytes 3538952 | tf_op jit(solution)/shard_map/ppermute | solution.py:159
  454.5 22.4 %collective-permute-start.120 = (bf16[256,1536]{1,0:T(8,128)(2,1)S(1)}, bf16[256,1536]{1,0:T(8,128)(2,1)S(1)}, u32[]{:S(2)}, u32[]{:S(2)}) collective-permute-start(bf16[256,1536]{1,0:T(8,128)(2,1)S(1)} %fusion.13), channel_id=1, source_target_pairs={{0,16},{2,18},{4,20},{6,22},{9,25},{11,27},{13,29},{15,31},{17,1},... | collective-permute-start | bytes 2359304 | tf_op jit(solution)/shard_map/ppermute | solution.py:159
  457.8 25.1 %collective-permute-start.72 = (bf16[192,1536]{1,0:T(8,128)(2,1)S(1)}, bf16[192,1536]{1,0:T(8,128)(2,1)S(1)}, u32[]{:S(2)}, u32[]{:S(2)}) collective-permute-start(bf16[192,1536]{1,0:T(8,128)(2,1)S(1)} %slice.685), channel_id=1, source_target_pairs={{0,16},{1,17},{2,18},{3,19},{4,20},{5,21},{6,22},{7,23},{8,24},{9,... | collective-permute-start | bytes 1769480 | tf_op jit(solution)/shard_map/ppermute | solution.py:159
  459.6 26.4 %collective-permute-start.64 = (bf16[192,1536]{1,0:T(8,128)(2,1)S(1)}, bf16[192,1536]{1,0:T(8,128)(2,1)S(1)}, u32[]{:S(2)}, u32[]{:S(2)}) collective-permute-start(bf16[192,1536]{1,0:T(8,128)(2,1)S(1)} %slice.677), channel_id=1, source_target_pairs={{0,4},{1,5},{2,6},{3,7},{4,0},{5,1},{6,2},{7,3},{8,12},{9,13},{10,... | collective-permute-start | bytes 1769480 | tf_op jit(solution)/shard_map/ppermute | solution.py:159
  462.6 28.3 %collective-permute-start.48 = (bf16[192,1536]{1,0:T(8,128)(2,1)S(1)}, bf16[192,1536]{1,0:T(8,128)(2,1)S(1)}, u32[]{:S(2)}, u32[]{:S(2)}) collective-permute-start(bf16[192,1536]{1,0:T(8,128)(2,1)S(1)} %slice.658), channel_id=1, source_target_pairs={{0,16},{1,17},{2,18},{3,19},{4,20},{5,21},{6,22},{7,23},{8,24},{9,... | collective-permute-start | bytes 1769480 | tf_op jit(solution)/shard_map/ppermute | solution.py:159
  475.2 17.1 %collective-permute-start.40 = (bf16[192,1536]{1,0:T(8,128)(2,1)S(1)}, bf16[192,1536]{1,0:T(8,128)(2,1)S(1)}, u32[]{:S(2)}, u32[]{:S(2)}) collective-permute-start(bf16[192,1536]{1,0:T(8,128)(2,1)S(1)} %slice.647), channel_id=1, source_target_pairs={{0,4},{1,5},{2,6},{3,7},{4,0},{5,1},{6,2},{7,3},{8,12},{9,13},{10,... | collective-permute-start | bytes 1769480 | tf_op jit(solution)/shard_map/ppermute | solution.py:159
  477.0 22.9 %collective-permute-start.117 = (bf16[2,2,96,512]{3,2,1,0:T(8,128)(2,1)S(1)}, bf16[2,2,96,512]{3,2,1,0:T(8,128)(2,1)S(1)}, u32[]{:S(2)}, u32[]{:S(2)}) collective-permute-start(bf16[2,2,96,512]{3,2,1,0:T(8,128)(2,1)S(1)} %get-tuple-element.63), channel_id=1, source_target_pairs={{0,4},{1,5},{2,6},{3,7},{4,0},{5,1},{6,2},{7,3},{8,12},{9,13},{10,... | collective-permute-start | bytes 1179656 | tf_op jit(solution)/shard_map/ppermute | solution.py:159
  483.1 23.1 %collective-permute-start.73 = (bf16[96,1536]{1,0:T(8,128)(2,1)S(1)}, bf16[96,1536]{1,0:T(8,128)(2,1)S(1)}, u32[]{:S(2)}, u32[]{:S(2)}) collective-permute-start(bf16[96,1536]{1,0:T(8,128)(2,1)S(1)} %slice.687), channel_id=1, source_target_pairs={{0,4},{1,5},{2,6},{3,7},{4,0},{5,1},{6,2},{7,3},{8,12},{9,13},{10,... | collective-permute-start | bytes 884744 | tf_op jit(solution)/shard_map/ppermute | solution.py:159
  486.2 21.3 %collective-permute-start.65 = (bf16[96,1536]{1,0:T(8,128)(2,1)S(1)}, bf16[96,1536]{1,0:T(8,128)(2,1)S(1)}, u32[]{:S(2)}, u32[]{:S(2)}) collective-permute-start(bf16[96,1536]{1,0:T(8,128)(2,1)S(1)} %slice.679), channel_id=1, source_target_pairs={{0,2},{1,3},{2,0},{3,1},{4,6},{5,7},{6,4},{7,5},{8,10},{9,11},{10,... | collective-permute-start | bytes 884744 | tf_op jit(solution)/shard_map/ppermute | solution.py:159
  491.0 20.1 %collective-permute-start.49 = (bf16[96,1536]{1,0:T(8,128)(2,1)S(1)}, bf16[96,1536]{1,0:T(8,128)(2,1)S(1)}, u32[]{:S(2)}, u32[]{:S(2)}) collective-permute-start(bf16[96,1536]{1,0:T(8,128)(2,1)S(1)} %slice.660), channel_id=1, source_target_pairs={{0,4},{1,5},{2,6},{3,7},{4,0},{5,1},{6,2},{7,3},{8,12},{9,13},{10,... | collective-permute-start | bytes 884744 | tf_op jit(solution)/shard_map/ppermute | solution.py:159
  492.5 30.7 %collective-permute-start.41 = (bf16[96,1536]{1,0:T(8,128)(2,1)S(1)}, bf16[96,1536]{1,0:T(8,128)(2,1)S(1)}, u32[]{:S(2)}, u32[]{:S(2)}) collective-permute-start(bf16[96,1536]{1,0:T(8,128)(2,1)S(1)} %slice.649), channel_id=1, source_target_pairs={{0,2},{1,3},{2,0},{3,1},{4,6},{5,7},{6,4},{7,5},{8,10},{9,11},{10,... | collective-permute-start | bytes 884744 | tf_op jit(solution)/shard_map/ppermute | solution.py:159
  500.0 44.0 %collective-permute-start.118 = (bf16[8,96,512]{2,1,0:T(8,128)(2,1)S(1)}, bf16[8,96,512]{2,1,0:T(8,128)(2,1)S(1)}, u32[]{:S(2)}, u32[]{:S(2)}) collective-permute-start(bf16[8,96,512]{2,1,0:T(8,128)(2,1)S(1)} %bitcast.433), channel_id=1, source_target_pairs={{0,16},{1,17},{2,18},{3,19},{4,20},{5,21},{6,22},{7,23},{8,24},{9,... | collective-permute-start | bytes 2359304 | tf_op jit(solution)/shard_map/ppermute | solution.py:159
  507.6 13.1 %collective-permute-start.66 = (bf16[48,1536]{1,0:T(8,128)(2,1)S(1)}, bf16[48,1536]{1,0:T(8,128)(2,1)S(1)}, u32[]{:S(2)}, u32[]{:S(2)}) collective-permute-start(bf16[48,1536]{1,0:T(8,128)(2,1)S(1)} %slice.681), channel_id=1, source_target_pairs={{0,16},{1,17},{2,18},{3,19},{4,20},{5,21},{6,22},{7,23},{8,24},{9,... | collective-permute-start | bytes 442376 | tf_op jit(solution)/shard_map/ppermute | solution.py:159
  511.2 24.3 %collective-permute-start.50 = (bf16[48,1536]{1,0:T(8,128)(2,1)S(1)}, bf16[48,1536]{1,0:T(8,128)(2,1)S(1)}, u32[]{:S(2)}, u32[]{:S(2)}) collective-permute-start(bf16[48,1536]{1,0:T(8,128)(2,1)S(1)} %slice.662), channel_id=1, source_target_pairs={{0,2},{1,3},{2,0},{3,1},{4,6},{5,7},{6,4},{7,5},{8,10},{9,11},{10,... | collective-permute-start | bytes 442376 | tf_op jit(solution)/shard_map/ppermute | solution.py:159
  523.3 19.9 %collective-permute-start.42 = (bf16[48,1536]{1,0:T(8,128)(2,1)S(1)}, bf16[48,1536]{1,0:T(8,128)(2,1)S(1)}, u32[]{:S(2)}, u32[]{:S(2)}) collective-permute-start(bf16[48,1536]{1,0:T(8,128)(2,1)S(1)} %slice.651), channel_id=1, source_target_pairs={{0,16},{1,17},{2,18},{3,19},{4,20},{5,21},{6,22},{7,23},{8,24},{9,... | collective-permute-start | bytes 442376 | tf_op jit(solution)/shard_map/ppermute | solution.py:159
  539.9 19.5 %collective-permute-start.88 = (bf16[256,1536]{1,0:T(8,128)(2,1)}, bf16[256,1536]{1,0:T(8,128)(2,1)}, u32[]{:S(2)}, u32[]{:S(2)}) collective-permute-start(bf16[256,1536]{1,0:T(8,128)(2,1)} %pad_maximum_fusion.21), channel_id=1, source_target_pairs={{0,1},{1,0},{2,3},{3,2},{4,5},{5,4},{6,7},{7,6},{8,9},{9,8},{10,11... | collective-permute-start | bytes 2359304 | tf_op jit(solution)/shard_map/ppermute | solution.py:159
  543.2 18.4 %collective-permute-start.85 = (bf16[256,1536]{1,0:T(8,128)(2,1)}, bf16[256,1536]{1,0:T(8,128)(2,1)}, u32[]{:S(2)}, u32[]{:S(2)}) collective-permute-start(bf16[256,1536]{1,0:T(8,128)(2,1)} %pad_maximum_fusion.20), channel_id=1, source_target_pairs={{0,1},{1,0},{2,3},{3,2},{4,5},{5,4},{6,7},{7,6},{8,9},{9,8},{10,11... | collective-permute-start | bytes 2359304 | tf_op jit(solution)/shard_map/ppermute | solution.py:159
  606.6 13.5 %collective-permute-start.89 = (bf16[512,384]{0,1:T(8,128)(2,1)S(1)}, bf16[512,384]{0,1:T(8,128)(2,1)S(1)}, u32[]{:S(2)}, u32[]{:S(2)}) collective-permute-start(bf16[512,384]{0,1:T(8,128)(2,1)S(1)} %get-tuple-element.37), channel_id=1, source_target_pairs={{0,4},{1,5},{2,6},{3,7},{16,20},{17,21},{18,22},{19,23}} | collective-permute-start | bytes 1179656 | tf_op jit(solution)/shard_map/ppermute | solution.py:219
  611.7 14.8 %collective-permute-start.111 = (bf16[96,1536]{1,0:T(8,128)(2,1)S(1)}, bf16[96,1536]{1,0:T(8,128)(2,1)S(1)}, u32[]{:S(2)}, u32[]{:S(2)}) collective-permute-start(bf16[96,1536]{1,0:T(8,128)(2,1)S(1)} %broadcast_select_fusion.4), channel_id=1, source_target_pairs={{0,8},{1,9},{2,10},{3,11},{4,12},{5,13},{6,14},{7,15},{8,0},{9,1},... | collective-permute-start | bytes 884744 | tf_op jit(solution)/shard_map/ppermute | solution.py:159
  612.3 16.1 %collective-permute-start.92 = (bf16[512,384]{0,1:T(8,128)(2,1)S(1)}, bf16[512,384]{0,1:T(8,128)(2,1)S(1)}, u32[]{:S(2)}, u32[]{:S(2)}) collective-permute-start(bf16[512,384]{0,1:T(8,128)(2,1)S(1)} %get-tuple-element.38), channel_id=1, source_target_pairs={{12,8},{13,9},{14,10},{15,11},{28,24},{29,25},{30,26},{31,27}} | collective-permute-start | bytes 1179656 | tf_op jit(solution)/shard_map/ppermute | solution.py:222
  620.2 13.7 %collective-permute-start.90 = (bf16[512,384]{0,1:T(8,128)(2,1)S(1)}, bf16[512,384]{0,1:T(8,128)(2,1)S(1)}, u32[]{:S(2)}, u32[]{:S(2)}) collective-permute-start(bf16[512,384]{0,1:T(8,128)(2,1)S(1)} %fusion.29), channel_id=1, source_target_pairs={{0,4},{1,5},{2,6},{3,7},{4,8},{5,9},{6,10},{7,11},{16,20},{17,21},... | collective-permute-start | bytes 1179656 | tf_op jit(solution)/shard_map/ppermute | solution.py:219
  635.0 12.9 %collective-permute-start.93 = (bf16[512,384]{0,1:T(8,128)(2,1)}, bf16[512,384]{0,1:T(8,128)(2,1)}, u32[]{:S(2)}, u32[]{:S(2)}) collective-permute-start(bf16[512,384]{0,1:T(8,128)(2,1)} %get-tuple-element.36), channel_id=1, source_target_pairs={{8,4},{9,5},{10,6},{11,7},{12,8},{13,9},{14,10},{15,11},{24,20},{2... | collective-permute-start | bytes 1179656 | tf_op jit(solution)/shard_map/ppermute | solution.py:222
  649.0 12.5 %collective-permute-start.94 = (bf16[512,384]{0,1:T(8,128)(2,1)S(1)}, bf16[512,384]{0,1:T(8,128)(2,1)S(1)}, u32[]{:S(2)}, u32[]{:S(2)}) collective-permute-start(bf16[512,384]{0,1:T(8,128)(2,1)S(1)} %fusion.28), channel_id=1, source_target_pairs={{4,0},{5,1},{6,2},{7,3},{8,4},{9,5},{10,6},{11,7},{12,8},{13,9},{1... | collective-permute-start | bytes 1179656 | tf_op jit(solution)/shard_map/ppermute | solution.py:222
  686.0 18.1 %collective-permute-start.98 = (bf16[256,1536]{1,0:T(8,128)(2,1)S(1)}, bf16[256,1536]{1,0:T(8,128)(2,1)S(1)}, u32[]{:S(2)}, u32[]{:S(2)}) collective-permute-start(bf16[256,1536]{1,0:T(8,128)(2,1)S(1)} %slice.719), channel_id=1, source_target_pairs={{0,1},{1,0},{2,3},{3,2},{4,5},{5,4},{6,7},{7,6},{8,9},{9,8},{10,11... | collective-permute-start | bytes 2359304 | tf_op jit(solution)/shard_map/ppermute | solution.py:159
  695.2 12.4 %collective-permute-start.95 = (bf16[256,1536]{1,0:T(8,128)(2,1)S(1)}, bf16[256,1536]{1,0:T(8,128)(2,1)S(1)}, u32[]{:S(2)}, u32[]{:S(2)}) collective-permute-start(bf16[256,1536]{1,0:T(8,128)(2,1)S(1)} %slice.712), channel_id=1, source_target_pairs={{0,1},{1,0},{2,3},{3,2},{4,5},{5,4},{6,7},{7,6},{8,9},{9,8},{10,11... | collective-permute-start | bytes 2359304 | tf_op jit(solution)/shard_map/ppermute | solution.py:159
  704.4 12.4 %collective-permute-start.99 = (bf16[128,1536]{1,0:T(8,128)(2,1)S(1)}, bf16[128,1536]{1,0:T(8,128)(2,1)S(1)}, u32[]{:S(2)}, u32[]{:S(2)}) collective-permute-start(bf16[128,1536]{1,0:T(8,128)(2,1)S(1)} %slice.721), channel_id=1, source_target_pairs={{0,16},{1,17},{2,18},{3,19},{4,20},{5,21},{6,22},{7,23},{8,24},{9,... | collective-permute-start | bytes 1179656 | tf_op jit(solution)/shard_map/ppermute | solution.py:159
  (206 other events, 2339.5 us)

commit v2 on v0

--- a/solution.py
+++ b/solution.py
@@ -1,6 +1,10 @@
+import functools
+
 import jax
 import jax.numpy as jnp
 from jax import lax
+from jax.experimental import pallas as pl
+from jax.experimental.pallas import tpu as pltpu
 from jax.sharding import PartitionSpec as P
 
 HEADS = 16
@@ -138,7 +142,1140 @@
     return (grad_query, grad_key, grad_value)
 
 
-def local(
+BIT_X, BIT_ZH, BIT_ZL, BIT_Y, BIT_C = 16, 8, 4, 2, 1
+DEVICES = 32
+AXES = ("grp", "seq")
+THIRDS = (
+    (BIT_X, BIT_Y, BIT_ZL),
+    (BIT_Y, BIT_ZL, BIT_X),
+    (BIT_ZL, BIT_X, BIT_Y),
+)
+HALVES = (
+    (BIT_ZL, BIT_X, BIT_Y),
+    (BIT_ZL, BIT_Y, BIT_X),
+)
+log2_e = 1.4426950408889634
+VMEM_LIMIT = 48 * 1024 * 1024
+low, wide = jnp.bfloat16, jnp.float32
+
+
+def swap(value, mask, sends=None):
+    pairs = [(i, i ^ mask) for i in range(DEVICES) if sends is None or sends(i)]
+    return lax.ppermute(value, AXES, pairs)
+
+
+def bit_of(index, mask):
+    return 1 if index & mask else 0
+
+
+def sync(*values):
+    return lax.optimization_barrier(values)
+
+
+def gather_start(rows, orders):
+    width = rows.shape[1] // len(orders)
+    return [rows[None, :, i * width : (i + 1) * width] for i in range(len(orders))]
+
+
+def gather_next(parts, orders, step):
+    return [
+        jnp.concatenate([held, swap(held, order[step])], axis=0)
+        for held, order in zip(parts, orders)
+    ]
+
+
+def gather_last(parts):
+    return [(held, swap(held, BIT_C)) for held in parts]
+
+
+def scatter_start(pairs):
+    return [(kept, swap(sent, BIT_C)) for kept, sent in pairs]
+
+
+def scatter_next(sums, orders, step):
+    result = []
+    for (kept, arrived), order in zip(sums, orders):
+        half = kept.shape[0] // 2
+        sent = (kept[half:].astype(wide) + arrived[half:].astype(wide)).astype(low)
+        kept = (kept[:half].astype(wide) + arrived[:half].astype(wide)).astype(low)
+        result.append((kept, swap(sent, order[step])))
+    return result
+
+
+def scatter_last(sums):
+    return [kept.astype(wide) + arrived.astype(wide) for kept, arrived in sums]
+
+
+def cube_groups():
+    return [
+        [gx * 16 + zh * 8 + rest for gx in (0, 1) for rest in range(8)] for zh in (0, 1)
+    ]
+
+
+def cube_gather(rows):
+    return lax.all_gather(rows, AXES, axis=0, tiled=True, axis_index_groups=cube_groups())
+
+
+def cube_scatter(rows):
+    return lax.psum_scatter(
+        rows, AXES, scatter_dimension=0, tiled=True, axis_index_groups=cube_groups()
+    )
+
+
+def trade_block(blocks, axis, mask):
+    keep = lax.index_in_dim(blocks, 0, axis, keepdims=False)
+    send = lax.index_in_dim(blocks, 1, axis, keepdims=False)
+    return jnp.stack([keep, swap(send, mask)])
+
+
+def trade_blocks(blocks, masks):
+    for axis, mask in enumerate(masks):
+        keep = lax.index_in_dim(blocks, 0, axis, keepdims=False)
+        send = lax.index_in_dim(blocks, 1, axis, keepdims=False)
+        blocks = jnp.stack([keep, swap(send, mask)])
+    return blocks
+
+
+def block_at(order):
+    place = {BIT_X: 2, BIT_Y: 1, BIT_ZL: 0}
+
+    def find(g):
+        return sum(((g >> place[mask]) & 1) << rank for rank, mask in enumerate(order))
+
+    return find
+
+
+def row_specs(orders, step):
+    width = 1536 // len(orders)
+    specs = []
+    for order in orders:
+        find = block_at(order)
+        for _ in range(2):
+            specs.append(
+                pl.BlockSpec((1, 128, width), lambda *a, find=find: (find(step(*a)), 0, 0))
+            )
+    return specs
+
+
+def row_shapes(orders):
+    width = 1536 // len(orders)
+    return [jax.ShapeDtypeStruct((8, 128, width), low)] * (2 * len(orders))
+
+
+def flat(pairs):
+    return [array for pair in pairs for array in pair]
+
+
+def paired(arrays):
+    return [(arrays[i], arrays[i + 1]) for i in range(0, len(arrays), 2)]
+
+
+def load_rows(refs):
+    return jnp.concatenate(
+        [
+            jnp.concatenate([refs[i][0], refs[i + 1][0]], axis=0)
+            for i in range(0, len(refs), 2)
+        ],
+        axis=1,
+    )
+
+
+def store_rows(refs, rows):
+    width = 1536 // (len(refs) // 2)
+    for i in range(0, len(refs), 2):
+        columns = slice((i // 2) * width, (i // 2 + 1) * width)
+        refs[i][0] = rows[:128, columns].astype(low)
+        refs[i + 1][0] = rows[128:, columns].astype(low)
+
+
+def whole_spec(shape):
+    return pl.BlockSpec(shape, lambda *a: (0,) * len(shape))
+
+
+def kernel_call(body, grid, in_specs, out_specs, out_shape, scratch, flops, moved, args, exps=0):
+    return pl.pallas_call(
+        body,
+        out_shape=out_shape,
+        grid_spec=pltpu.PrefetchScalarGridSpec(
+            num_scalar_prefetch=1,
+            grid=grid,
+            in_specs=in_specs,
+            out_specs=out_specs,
+            scratch_shapes=scratch,
+        ),
+        compiler_params=pltpu.CompilerParams(vmem_limit_bytes=VMEM_LIMIT),
+        cost_estimate=pl.CostEstimate(
+            flops=flops, bytes_accessed=moved, transcendentals=exps
+        ),
+    )(*args)
+
+
+def head_columns(w_query, w_key, w_value, head):
+    shared = w_value if head % 2 else w_key
+    start = (head // 2) * 96
+    return w_query[:, head * 96 : head * 96 + 96], shared[:, start : start + 96]
+
+
+def pick_heads(table, w_query, w_key, w_value, gain_rows):
+    def body(table_ref, q_ref, k_ref, v_ref, gain_ref, out_ref, scr):
+        gain = gain_ref[...]
+        for head in range(16):
+            one, two = head_columns(q_ref, k_ref, v_ref, head)
+            scr[head, :, :96] = (one.astype(wide) * gain).astype(low)
+            scr[head, :, 96:] = (two.astype(wide) * gain).astype(low)
+        for i in range(8):
+            out_ref[i] = scr[table_ref[i]]
+
+    args = (w_query, w_key, w_value, gain_rows)
+    return kernel_call(
+        body,
+        (1,),
+        [whole_spec(a.shape) for a in args],
+        whole_spec((8, 96, 192)),
+        jax.ShapeDtypeStruct((8, 96, 192), low),
+        [pltpu.VMEM((16, 96, 192), low)],
+        0,
+        1024 * 1024,
+        (table, *args),
+    )
+
+
+def pick_columns(table, first, second, gain_rows):
+    rows = first.shape[0]
+
+    def body(table_ref, first_ref, second_ref, gain_ref, out_ref):
+        gain = gain_ref[...]
+        for i in range(8):
+            columns = pl.ds(pl.multiple_of(table_ref[i] * 256, 256), 256)
+            out_ref[i, :, :256] = (first_ref[:, columns].astype(wide) * gain).astype(low)
+            out_ref[i, :, 256:] = (second_ref[:, columns].astype(wide) * gain).astype(low)
+
+    shape = (8, rows, 512)
+    return kernel_call(
+        body,
+        (1,),
+        [whole_spec(first.shape), whole_spec(second.shape), whole_spec(gain_rows.shape)],
+        whole_spec(shape),
+        jax.ShapeDtypeStruct(shape, low),
+        [],
+        0,
+        4 * first.size,
+        (table, first, second, gain_rows),
+    )
+
+
+def assemble_rows(table, *groups):
+    rows, width = groups[0].shape[1:]
+
+    def body(table_ref, *refs):
+        out_ref, i = refs[-1], 0
+        for ref in refs[:-1]:
+            for k in range(ref.shape[0]):
+                start = pl.multiple_of(table_ref[i] * rows, rows)
+                out_ref[pl.ds(start, rows), :] = ref[k]
+                i += 1
+
+    shape = (16 * rows, width)
+    return kernel_call(
+        body,
+        (1,),
+        [whole_spec(group.shape) for group in groups],
+        whole_spec(shape),
+        jax.ShapeDtypeStruct(shape, low),
+        [],
+        0,
+        64 * rows * width,
+        (table, *groups),
+    )
+
+
+def spread_columns(table, near, far, gain_rows, first, second):
+    rows = near.shape[1]
+
+    def body(table_ref, near_ref, far_ref, gain_ref, w1_ref, w2_ref, g1_ref, g2_ref, sum_ref):
+        gain = gain_ref[...]
+        total = jnp.zeros((rows, 256), wide)
+        for i in range(16):
+            source = near_ref if i < 8 else far_ref
+            columns = pl.ds(pl.multiple_of(table_ref[i] * 256, 256), 256)
+            block = source[i % 8].astype(wide)
+            one, two = block[:, :256], block[:, 256:]
+            total += one * w1_ref[:, columns].astype(wide)
+            total += two * w2_ref[:, columns].astype(wide)
+            g1_ref[:, columns] = one * gain
+            g2_ref[:, columns] = two * gain
+        sum_ref[...] = jnp.sum(total, axis=1, keepdims=True)
+
+    return kernel_call(
+        body,
+        (1,),
+        [whole_spec(a.shape) for a in (near, far, gain_rows, first, second)],
+        [whole_spec(first.shape), whole_spec(second.shape), whole_spec((rows, 1))],
+        [
+            jax.ShapeDtypeStruct(first.shape, wide),
+            jax.ShapeDtypeStruct(second.shape, wide),
+            jax.ShapeDtypeStruct((rows, 1), wide),
+        ],
+        [],
+        0,
+        6 * 2 * first.size,
+        (table, near, far, gain_rows, first, second),
+    )
+
+
+def spread_heads(table, near, far, w_query, w_key, w_value, gain_rows):
+    def body(
+        table_ref, near_ref, far_ref, q_ref, k_ref, v_ref, gain_ref, *rest
+    ):
+        gq_ref, gk_ref, gv_ref, sum_ref, scr = rest
+        gain = gain_ref[...]
+        for i in range(16):
+            source = near_ref if i < 8 else far_ref
+            scr[table_ref[i]] = source[i % 8].astype(wide)
+        total = jnp.zeros((96, 96), wide)
+        for head in range(16):
+            one, two = head_columns(q_ref, k_ref, v_ref, head)
+            block = scr[head]
+            first, second = block[:, :96], block[:, 96:]
+            total += first * one.astype(wide) + second * two.astype(wide)
+            gq_ref[:, head * 96 : head * 96 + 96] = first * gain
+            shared = gv_ref if head % 2 else gk_ref
+            start = (head // 2) * 96
+            shared[:, start : start + 96] = second * gain
+        sum_ref[...] = jnp.sum(total, axis=1, keepdims=True)
+
+    args = (near, far, w_query, w_key, w_value, gain_rows)
+    shapes = [w_query.shape, w_key.shape, w_value.shape, (96, 1)]
+    return kernel_call(
+        body,
+        (1,),
+        [whole_spec(a.shape) for a in args],
+        [whole_spec(shape) for shape in shapes],
+        [jax.ShapeDtypeStruct(shape, wide) for shape in shapes],
+        [pltpu.VMEM((16, 96, 192), wide)],
+        0,
+        4 * 1024 * 1024,
+        (table, *args),
+    )
+
+
+def turn(rows, cosine, sine):
+    front, back = rows[:48], rows[48:]
+    return jnp.concatenate([front * cosine - back * sine, back * cosine + front * sine], axis=0)
+
+
+def turn_back(rows, cosine, sine):
+    front, back = rows[:48], rows[48:]
+    return jnp.concatenate([front * cosine + back * sine, back * cosine - front * sine], axis=0)
+
+
+def align_rows(core, rows):
+    turned = jnp.concatenate([rows[128:], rows[:128]], axis=0)
+    return jnp.where(core == 0, rows, turned)
+
+
+def align(core, columns):
+    turned = jnp.concatenate([columns[:, 128:], columns[:, :128]], axis=1)
+    return jnp.where(core == 0, columns, turned)
+
+
+def table_specs():
+    return [pl.BlockSpec((48, 256), lambda g, t: (0, g % 4))] * 4
+
+
+def cube_spec():
+    return pl.BlockSpec((256, 1536), lambda g, t: (t[g], 0))
+
+
+def project(at, normed, w_heads, tables):
+    def body(at_ref, rows_ref, w_ref, cos_ref, sin_ref, cos2_ref, sin2_ref, q_ref, own_ref, wt_scr):
+        @pl.when(pl.program_id(0) == 0)
+        def _():
+            wt_scr[...] = w_ref[...].astype(wide).T.astype(low)
+
+        made = times_back(wt_scr[...], rows_ref[...])
+        q_ref[0] = turn(made[:96], cos_ref[...], sin_ref[...]).astype(low)
+        own_ref[0] = turn(made[96:], cos2_ref[...], sin2_ref[...]).astype(low)
+
+    out_spec = pl.BlockSpec((1, 96, 256), lambda g, t: (g // 4, 0, g % 4))
+    shape = jax.ShapeDtypeStruct((2, 96, 1024), low)
+    return kernel_call(
+        body,
+        (8,),
+        [cube_spec(), whole_spec((1536, 192))] + table_specs(),
+        [out_spec, out_spec],
+        [shape, shape],
+        [pltpu.VMEM((192, 1536), low)],
+        2 * 2048 * 1536 * 192,
+        8 * 1024 * 1024,
+        (at, normed, w_heads, *tables),
+    )
+
+
+def head_specs():
+    kv = pl.BlockSpec((1, 96, 1024), lambda s, t, a: (s, 0, 0))
+    other = pl.BlockSpec((1, 1, 96, 1024), lambda s, t, a: (0, s, 0, 0))
+    other_far = pl.BlockSpec((1, 1, 96, 1024), lambda s, t, a: (1, s, 0, 0))
+    return [kv, kv, other, other_far]
+
+
+def key_and_value(core, own_ref, far_ref, other_ref, other_far_ref):
+    mine = jnp.concatenate([own_ref[0], far_ref[0]], axis=1)
+    theirs = jnp.concatenate([other_ref[0, 0], other_far_ref[0, 0]], axis=1)
+    keyed = core == 0
+    return jnp.where(keyed, mine, theirs), jnp.where(keyed, theirs, mine)
+
+
+def masked(scores, key_column, query_ref, score_scale):
+    return jnp.where(key_column <= query_ref[0], scores * (score_scale * log2_e), masked_score)
+
+
+def attend_forward(at, queries, held, query_blk, key_blk, score_scale):
+    def body(at_ref, q_ref, a_ref, b_ref, c_ref, d_ref, qb_ref, kb_ref, *rest):
+        keep_ref, send_ref, att_ref, total_ref, k_scr, v_scr, kb_scr = rest
+
+        @pl.when(pl.program_id(1) == 0)
+        def _():
+            key_part, value_part = key_and_value(at_ref[8], a_ref, b_ref, c_ref, d_ref)
+            k_scr[...] = key_part.astype(wide).T.astype(low)
+            v_scr[...] = value_part
+            kb_scr[...] = jnp.broadcast_to(kb_ref[0], (128, 2048)).T[:, :1]
+
+        scores = jnp.dot(k_scr[...], q_ref[0], preferred_element_type=wide)
+        scores = masked(scores, kb_scr[...], qb_ref, score_scale)
+        top = jnp.max(scores, axis=0, keepdims=True)
+        likely = jnp.exp2(scores - top)
+        column_sum = jnp.sum(likely, axis=0, keepdims=True)
+        mixed = jnp.dot(v_scr[...], likely.astype(low), preferred_element_type=wide)
+        mixed = mixed / column_sum
+        att_ref[0] = mixed
+        total_ref[0] = top + jnp.log(column_sum) * log2_e
+        mixed = align(at_ref[8], mixed).astype(low)
+        keep_ref[0] = mixed[:, :128]
+        send_ref[0] = mixed[:, 128:]
+
+    q_spec = pl.BlockSpec((1, 96, 256), lambda s, t, a: (s, 0, t))
+    one_spec = pl.BlockSpec((1, 1, 256), lambda s, t, a: (s, 0, t))
+    block_spec = pl.BlockSpec((1, 96, 128), lambda s, t, a: (s * 4 + t, 0, 0))
+    return kernel_call(
+        body,
+        (2, 4),
+        [q_spec]
+        + head_specs()
+        + [one_spec, pl.BlockSpec((1, 1, 2048), lambda s, t, a: (s, 0, 0))],
+        [block_spec, block_spec, q_spec, one_spec],
+        [
+            jax.ShapeDtypeStruct((8, 96, 128), low),
+            jax.ShapeDtypeStruct((8, 96, 128), low),
+            jax.ShapeDtypeStruct((2, 96, 1024), wide),
+            jax.ShapeDtypeStruct((2, 1, 1024), wide),
+        ],
+        [
+            pltpu.VMEM((2048, 96), low),
+            pltpu.VMEM((96, 2048), low),
+            pltpu.VMEM((2048, 1), wide),
+        ],
+        4 * 2 * 1024 * 2048 * 96,
+        12 * 1024 * 1024,
+        (at, queries, *held, query_blk, key_blk),
+        exps=2 * 1024 * 2048,
+    )
+
+
+def out_project(at, blocks, w_full, residual):
+    def body(at_ref, in_ref, w_ref, x_ref, middle_ref, scale_ref, normed_ref, att_ref):
+        for i in range(16):
+            start = pl.multiple_of(at_ref[i] * 96, 96)
+            att_ref[pl.ds(start, 96), :] = in_ref[i]
+        rows = att_ref[...].astype(wide).T.astype(low)
+        middle = x_ref[...] + jnp.dot(rows, w_ref[...], preferred_element_type=wide)
+        scale = rms_scale(middle)
+        middle_ref[...] = middle
+        scale_ref[...] = scale
+        normed_ref[...] = (middle * scale).astype(low)
+
+    shapes = [
+        jax.ShapeDtypeStruct((128, 1536), wide),
+        jax.ShapeDtypeStruct((128, 1), wide),
+        jax.ShapeDtypeStruct((128, 1536), low),
+    ]
+    return kernel_call(
+        body,
+        (1,),
+        [whole_spec(a.shape) for a in (blocks, w_full, residual)],
+        [whole_spec(shape.shape) for shape in shapes],
+        shapes,
+        [pltpu.VMEM((1536, 128), low)],
+        2 * 128 * 1536 * 1536,
+        6 * 1024 * 1024,
+        (at, blocks, w_full, residual),
+    )
+
+
+def out_back(at, grad_out, sums, middle, scale, w_full):
+    def body(at_ref, dy_ref, a_ref, b_ref, c_ref, x_ref, scale_ref, w_ref, *rest):
+        middle_ref, low_ref, keep_ref, send_ref, scr = rest
+        scaled = jnp.concatenate([a_ref[0], b_ref[0], c_ref[0]], axis=1)
+        scale = scale_ref[...]
+        normed = x_ref[...] * scale
+        grad = dy_ref[...].astype(wide) + scale * (
+            scaled - normed * jnp.mean(scaled * normed, axis=-1, keepdims=True)
+        )
+        middle_ref[...] = grad
+        grad = grad.astype(low)
+        low_ref[...] = grad
+        scr[...] = times_back(w_ref[...], grad).astype(low)
+        for i in range(8):
+            start = pl.multiple_of(at_ref[i] * 96, 96)
+            keep_ref[i] = scr[pl.ds(start, 96), :]
+            start = pl.multiple_of(at_ref[8 + i] * 96, 96)
+            send_ref[i] = scr[pl.ds(start, 96), :]
+
+    args = (grad_out, *sums, middle, scale, w_full)
+    shapes = [
+        jax.ShapeDtypeStruct((128, 1536), wide),
+        jax.ShapeDtypeStruct((128, 1536), low),
+        jax.ShapeDtypeStruct((8, 96, 128), low),
+        jax.ShapeDtypeStruct((8, 96, 128), low),
+    ]
+    return kernel_call(
+        body,
+        (1,),
+        [whole_spec(a.shape) for a in args],
+        [whole_spec(shape.shape) for shape in shapes],
+        shapes,
+        [pltpu.VMEM((1536, 128), low)],
+        4 * 128 * 1536 * 1536,
+        14 * 1024 * 1024,
+        (at, *args),
+    )
+
+
+def attend_backward(
+    at, queries, held, query_blk, key_blk, attention, totals, grad_blocks, tables, score_scale
+):
+    def body(at_ref, q_ref, a_ref, b_ref, c_ref, d_ref, qb_ref, kb_ref, *rest):
+        att_ref, total_ref, cos_ref, sin_ref = rest[:4]
+        own_ref, core_ref = rest[4:6]
+        dq_ref, mine_ref, sent_ref = rest[6:9]
+        k_scr, kt_scr, v_scr, dk_scr, dv_scr, kb_scr = rest[9:]
+        tile = pl.program_id(1)
+
+        @pl.when(tile == 0)
+        def _():
+            key_part, value_part = key_and_value(at_ref[8], a_ref, b_ref, c_ref, d_ref)
+            kt_scr[...] = key_part
+            kb_scr[...] = jnp.broadcast_to(kb_ref[0], (128, 2048)).T[:, :1]
+            k_scr[...] = key_part.astype(wide).T.astype(low)
+            v_scr[...] = value_part.astype(wide).T.astype(low)
+            dk_scr[...] = jnp.zeros_like(dk_scr)
+            dv_scr[...] = jnp.zeros_like(dv_scr)
+
+        att = att_ref[0]
+        grad_att = align(
+            at_ref[8], jnp.concatenate([own_ref[0, 0], core_ref[0, 0]], axis=1).astype(wide)
+        ).astype(low)
+        delta = jnp.sum(grad_att.astype(wide) * att, axis=0, keepdims=True)
+        scores = jnp.dot(k_scr[...], q_ref[0], preferred_element_type=wide)
+        scores = masked(scores, kb_scr[...], qb_ref, score_scale)
+        chance = jnp.exp2(scores - total_ref[0])
+        dv_scr[...] += times_back(grad_att, chance.astype(low))
+        grad_chance = jnp.dot(v_scr[...], grad_att, preferred_element_type=wide)
+        grad_scores = (chance * (grad_chance - delta)).astype(low)
+        grad_query = jnp.dot(kt_scr[...], grad_scores, preferred_element_type=wide)
+        dq_ref[0] = turn_back(grad_query * score_scale, cos_ref[...], sin_ref[...]).astype(low)
+        dk_scr[...] += times_back(q_ref[0], grad_scores)
+
+        @pl.when(tile == 3)
+        def _():
+            grad_key = dk_scr[...] * score_scale
+            grad_value = dv_scr[...]
+            keyed = at_ref[8] == 0
+            mine = jnp.where(keyed, grad_key, grad_value)
+            sent = jnp.where(keyed, grad_value, grad_key)
+            mine_ref[0, 0] = mine[:, :1024].astype(low)
+            mine_ref[1, 0] = mine[:, 1024:].astype(low)
+            sent_ref[0, 0] = sent[:, :1024].astype(low)
+            sent_ref[1, 0] = sent[:, 1024:].astype(low)
+
+    q_spec = pl.BlockSpec((1, 96, 256), lambda s, t, a: (s, 0, t))
+    one_spec = pl.BlockSpec((1, 1, 256), lambda s, t, a: (s, 0, t))
+    kv_out = pl.BlockSpec((2, 1, 96, 1024), lambda s, t, a: (0, s, 0, 0))
+    angle = pl.BlockSpec((48, 256), lambda s, t, a: (0, t))
+
+    def block_of(s, t):
+        return (t & 1) * 4 + (t >> 1) * 2 + s
+
+    return kernel_call(
+        body,
+        (2, 4),
+        [q_spec]
+        + head_specs()
+        + [
+            one_spec,
+            pl.BlockSpec((1, 1, 2048), lambda s, t, a: (s, 0, 0)),
+            q_spec,
+            one_spec,
+            angle,
+            angle,
+            pl.BlockSpec((1, 1, 96, 128), lambda s, t, a: (block_of(s, t), 0, 0, 0)),
+            pl.BlockSpec((1, 1, 96, 128), lambda s, t, a: (block_of(s, t), 1, 0, 0)),
+        ],
+        [q_spec, kv_out, kv_out],
+        [
+            jax.ShapeDtypeStruct((2, 96, 1024), low),
+            jax.ShapeDtypeStruct((2, 2, 96, 1024), low),
+            jax.ShapeDtypeStruct((2, 2, 96, 1024), low),
+        ],
+        [
+            pltpu.VMEM((2048, 96), low),
+            pltpu.VMEM((96, 2048), low),
+            pltpu.VMEM((2048, 96), low),
+            pltpu.VMEM((96, 2048), wide),
+            pltpu.VMEM((96, 2048), wide),
+            pltpu.VMEM((2048, 1), wide),
+        ],
+        10 * 2 * 1024 * 2048 * 96,
+        12 * 1024 * 1024,
+        (
+            at,
+            queries,
+            *held,
+            query_blk,
+            key_blk,
+            attention,
+            totals,
+            *tables[:2],
+            grad_blocks,
+            grad_blocks,
+        ),
+        exps=2 * 1024 * 2048,
+    )
+
+
+def head_grads(dq_ref, ds_ref, cos_ref, sin_ref):
+    own = turn_back(ds_ref[0], cos_ref[...], sin_ref[...])
+    return jnp.concatenate([dq_ref[0].astype(wide), own], axis=0)
+
+
+def head_grad_specs():
+    q_spec = pl.BlockSpec((1, 96, 256), lambda g, t: (g // 4, 0, g % 4))
+    return table_specs()[:2] + [q_spec, q_spec]
+
+
+def head_weights(at, normed, tables, grad_queries, grad_own):
+    def body(at_ref, rows_ref, cos_ref, sin_ref, dq_ref, ds_ref, *rest):
+        keep_ref, send_ref, gw_scr, nat_scr = rest
+        g = pl.program_id(0)
+
+        @pl.when(g == 0)
+        def _():
+            gw_scr[...] = jnp.zeros_like(gw_scr)
+
+        both = head_grads(dq_ref, ds_ref, cos_ref, sin_ref)
+        gw_scr[...] += jnp.dot(both.astype(low), rows_ref[...], preferred_element_type=wide)
+
+        @pl.when(g == 7)
+        def _():
+            nat_scr[...] = gw_scr[...].T
+            for i in range(8):
+                start = pl.multiple_of(at_ref[9 + i] * 96, 96)
+                keep_ref[i] = nat_scr[pl.ds(start, 96), :].astype(low)
+                start = pl.multiple_of(at_ref[17 + i] * 96, 96)
+                send_ref[i] = nat_scr[pl.ds(start, 96), :].astype(low)
+
+    blocks = jax.ShapeDtypeStruct((8, 96, 192), low)
+    return kernel_call(
+        body,
+        (8,),
+        [cube_spec()] + head_grad_specs(),
+        [whole_spec((8, 96, 192))] * 2,
+        [blocks, blocks],
+        [pltpu.VMEM((192, 1536), wide), pltpu.VMEM((1536, 192), wide)],
+        2 * 2048 * 1536 * 192,
+        8 * 1024 * 1024,
+        (at, normed, *tables[2:], grad_queries, grad_own),
+    )
+
+
+def project_back(at, w_heads, tables, grad_queries, grad_own):
+    def body(at_ref, w_ref, cos_ref, sin_ref, dq_ref, ds_ref, *rest):
+        outs, wt_scr = rest[:6], rest[6]
+
+        @pl.when(pl.program_id(0) == 0)
+        def _():
+            wt_scr[...] = w_ref[...].astype(wide).T.astype(low)
+
+        both = align(at_ref[8], head_grads(dq_ref, ds_ref, cos_ref, sin_ref))
+        store_rows(outs, jnp.dot(both.T.astype(low), wt_scr[...], preferred_element_type=wide))
+
+    return kernel_call(
+        body,
+        (8,),
+        [whole_spec((1536, 192))] + head_grad_specs(),
+        row_specs(THIRDS, lambda g, t: g),
+        row_shapes(THIRDS),
+        [pltpu.VMEM((192, 1536), low)],
+        2 * 2048 * 1536 * 192,
+        8 * 1024 * 1024,
+        (at, w_heads, *tables[2:], grad_queries, grad_own),
+    )
+
+
+def hidden_back(at, grads, w_rows):
+    def body(at_ref, *refs):
+        rows, (w_ref, out_ref) = refs[:6], refs[6:]
+        out_ref[...] = align_rows(at_ref[8], times_back(load_rows(rows), w_ref[...]))
+
+    return kernel_call(
+        body,
+        (8,),
+        row_specs(THIRDS, lambda g, t: g) + [whole_spec((256, 1536))],
+        pl.BlockSpec((256, 256), lambda g, t: (g, 0)),
+        jax.ShapeDtypeStruct((2048, 256), wide),
+        [],
+        2 * 2048 * 1536 * 256,
+        8 * 1024 * 1024,
+        (at, *flat(grads), w_rows),
+    )
+
+
+def feed_back(at, normed, w_both, grad_hidden):
+    def body(at_ref, rows_ref, w_ref, dh_ref, *rest):
+        outs, (hidden_ref, both_ref, wt_scr) = rest[:6], rest[6:]
+
+        @pl.when(pl.program_id(0) == 0)
+        def _():
+            wt_scr[...] = w_ref[...].astype(wide).T.astype(low)
+
+        both = jnp.dot(rows_ref[...], w_ref[...], preferred_element_type=wide)
+        gate, up = both[:, :256], both[:, 256:]
+        bend = jax.nn.sigmoid(gate)
+        smooth = gate * bend
+        grad_hidden = dh_ref[...]
+        hidden_ref[...] = (smooth * up).astype(low)
+        grad_gate = grad_hidden * up * (bend + smooth * (1.0 - bend))
+        grad_both = jnp.concatenate([grad_gate, grad_hidden * smooth], axis=1).astype(low)
+        both_ref[...] = grad_both
+        grad_both = align_rows(at_ref[8], grad_both.astype(wide)).astype(low)
+        store_rows(outs, jnp.dot(grad_both, wt_scr[...], preferred_element_type=wide))
+
+    return kernel_call(
+        body,
+        (8,),
+        [cube_spec(), whole_spec((1536, 512)), pl.BlockSpec((256, 256), lambda g, t: (g, 0))],
+        row_specs(THIRDS, lambda g, t: g)
+        + [
+            pl.BlockSpec((256, 256), lambda g, t: (g, 0)),
+            pl.BlockSpec((256, 512), lambda g, t: (g, 0)),
+        ],
+        row_shapes(THIRDS)
+        + [
+            jax.ShapeDtypeStruct((2048, 256), low),
+            jax.ShapeDtypeStruct((2048, 512), low),
+        ],
+        [pltpu.VMEM((512, 1536), low)],
+        4 * 2048 * 1536 * 512,
+        18 * 1024 * 1024,
+        (at, normed, w_both, grad_hidden),
+        exps=2048 * 256,
+    )
+
+
+def feed_out(at, hidden, w_rows):
+    def body(at_ref, hidden_ref, w_ref, *outs):
+        made = jnp.dot(hidden_ref[...], w_ref[...], preferred_element_type=wide)
+        store_rows(outs, align_rows(at_ref[8], made))
+
+    return kernel_call(
+        body,
+        (8,),
+        [pl.BlockSpec((256, 256), lambda g, t: (g, 0)), whole_spec((256, 1536))],
+        row_specs(HALVES, lambda g, t: g),
+        row_shapes(HALVES),
+        [],
+        2 * 2048 * 1536 * 256,
+        8 * 1024 * 1024,
+        (at, hidden, w_rows),
+    )
+
+
+def down_weights(at, hidden, grads):
+    def body(at_ref, *refs):
+        rows, (hidden_ref, gw_ref, gw_scr) = refs[:6], refs[6:]
+        g = pl.program_id(0)
+
+        @pl.when(g == 0)
+        def _():
+            gw_scr[...] = jnp.zeros_like(gw_scr)
+
+        held = align_rows(at_ref[8], hidden_ref[...].astype(wide)).astype(low)
+        gw_scr[...] += over_rows(held, load_rows(rows))
+
+        @pl.when(g == 7)
+        def _():
+            gw_ref[...] = gw_scr[...].astype(low)
+
+    return kernel_call(
+        body,
+        (8,),
+        row_specs(THIRDS, lambda g, t: g) + [pl.BlockSpec((256, 256), lambda g, t: (g, 0))],
+        whole_spec((256, 1536)),
+        jax.ShapeDtypeStruct((256, 1536), low),
+        [pltpu.VMEM((256, 1536), wide)],
+        2 * 2048 * 1536 * 256,
+        8 * 1024 * 1024,
+        (at, *flat(grads), hidden),
+    )
+
+
+def out_weights(at, attention, grads):
+    def body(at_ref, att_ref, rows_ref, gw_ref, gw_scr):
+        g = pl.program_id(0)
+
+        @pl.when(g == 0)
+        def _():
+            gw_scr[...] = jnp.zeros_like(gw_scr)
+
+        gw_scr[...] += jnp.dot(
+            att_ref[0].astype(low), rows_ref[...], preferred_element_type=wide
+        )
+
+        @pl.when(g == 7)
+        def _():
+            gw_ref[...] = gw_scr[...].astype(low)
+
+    return kernel_call(
+        body,
+        (8,),
+        [pl.BlockSpec((1, 96, 256), lambda g, t: (g // 4, 0, g % 4)), cube_spec()],
+        whole_spec((96, 1536)),
+        jax.ShapeDtypeStruct((96, 1536), low),
+        [pltpu.VMEM((96, 1536), wide)],
+        2 * 2048 * 1536 * 96,
+        8 * 1024 * 1024,
+        (at, attention, grads),
+    )
+
+
+def feed_weights(at, normed, grad_both):
+    def body(at_ref, rows_ref, both_ref, keep_ref, send_ref, gw_scr, nat_scr):
+        g = pl.program_id(0)
+
+        @pl.when(g == 0)
+        def _():
+            gw_scr[...] = jnp.zeros_like(gw_scr)
+
+        gw_scr[...] += over_rows(both_ref[...], rows_ref[...])
+
+        @pl.when(g == 7)
+        def _():
+            nat_scr[...] = gw_scr[...].T
+            for i in range(8):
+                start = pl.multiple_of(at_ref[9 + i] * 96, 96)
+                keep_ref[i] = nat_scr[pl.ds(start, 96), :].astype(low)
+                start = pl.multiple_of(at_ref[17 + i] * 96, 96)
+                send_ref[i] = nat_scr[pl.ds(start, 96), :].astype(low)
+
+    return kernel_call(
+        body,
+        (8,),
+        [cube_spec(), pl.BlockSpec((256, 512), lambda g, t: (g, 0))],
+        [whole_spec((8, 96, 512))] * 2,
+        [jax.ShapeDtypeStruct((8, 96, 512), low)] * 2,
+        [pltpu.VMEM((512, 1536), wide), pltpu.VMEM((1536, 512), wide)],
+        2 * 2048 * 1536 * 512,
+        14 * 1024 * 1024,
+        (at, normed, grad_both),
+    )
+
+
+def sum_low(left, right):
+    return (left.astype(wide) + right.astype(wide)).astype(low)
+
+
+def cube_plan(
+    inputs,
+    cotangent,
+    block_ids,
+    piece_order,
+    w_query,
+    w_key,
+    w_value,
+    w_out,
+    w_gate,
+    w_up,
+    w_down,
+    gain_attn,
+    gain_mlp,
+):
+    x = lax.axis_index("grp")
+    seq_at = lax.axis_index("seq")
+    zh, c = seq_at >> 3, seq_at & 1
+    score_scale = HEAD_DIM ** (-0.5)
+    gain_rows_attn = gain_attn.astype(wide)[:, None]
+    gain_rows_mlp = gain_mlp.astype(wide)[:, None]
+    eight = jnp.arange(8, dtype=jnp.int32)
+    sixteen = jnp.arange(16, dtype=jnp.int32)
+    cyl = (eight >> 2) + (eight & 2) + ((eight & 1) << 2)
+    place = c.astype(jnp.int32)[None]
+    natural = seq_at ^ sixteen
+
+    def owns_out(i):
+        return bit_of(i, BIT_X) == bit_of(i, BIT_ZH)
+
+    def owns_down(i):
+        return bit_of(i, BIT_X) ^ bit_of(i, BIT_C) == bit_of(i, BIT_ZH)
+
+    def lacks_out(i):
+        return not owns_out(i)
+
+    def lacks_down(i):
+        return not owns_down(i)
+
+    out_owner, down_owner = x == zh, (x ^ c) == zh
+
+    order = ((sixteen & 8)) | ((sixteen & 4) >> 1) | ((sixteen & 2) << 1) | (sixteen & 1)
+    stored = (seq_at & 14) ^ order
+    pieces = jnp.sum(
+        jnp.where(stored[:, None] == sixteen[None, :], piece_order[None, :], 0), axis=1
+    )
+    own_pos = (pieces[:8, None] * 128 + jnp.arange(128, dtype=jnp.int32)[None, :]).reshape(1024)
+    frequency = rope_base ** (-jnp.arange(HEAD_DIM // 2, dtype=wide) * 2.0 / HEAD_DIM)
+    angles = frequency[:, None] * own_pos.astype(wide)[None, :]
+    cosine, sine = jnp.cos(angles), jnp.sin(angles)
+    keyed = c == 0
+    tables = (
+        cosine,
+        sine,
+        jnp.where(keyed, cosine, 1.0),
+        jnp.where(keyed, sine, 0.0),
+    )
+
+    low_zy = ((eight & 1) << 2) | (eight & 2)
+    side_of = x ^ (eight >> 2)
+    spots = jnp.concatenate([side_of * 4 + (((seq_at ^ low_zy) & 7) >> 1), place])
+    spots_rows = jnp.concatenate([spots, natural])
+    head_for = jnp.concatenate(
+        [side_of * 8 + ((seq_at ^ low_zy ^ core) & 7) for core in (0, 1)]
+    )
+
+    residual = inputs[0].astype(wide)
+    scale_first = rms_scale(residual)
+    normed_first = residual * scale_first
+    normed = cube_gather(normed_first.astype(low))
+    head_of = x * 8 + ((seq_at ^ cyl) & 7)
+    heads = pick_heads(head_of, w_query, w_key, w_value, gain_rows_attn)
+    heads = trade_block(heads.reshape(2, 2, 2, 96, 192), 0, BIT_C)
+    heads, w_out_held = sync(heads, w_out)
+    out_near = swap(w_out_held, BIT_ZH, owns_out)
+    heads = trade_block(heads, 1, BIT_Y)
+    heads, ids_held, up_held = sync(heads, block_ids, w_up)
+    heads = trade_block(heads, 2, BIT_ZL)
+    other_ids = swap(ids_held, BIT_X)
+    wanted_mlp = (x ^ ((seq_at ^ cyl) & 1)) * 8 + ((seq_at ^ cyl) & 7)
+    both_blocks = pick_columns(wanted_mlp, w_gate, up_held, gain_rows_mlp)
+    heads, out_near, both_blocks = sync(heads, out_near, both_blocks)
+    heads = heads.reshape(8, 96, 192)
+    heads_far = swap(heads, BIT_ZH)
+    both_blocks = trade_block(both_blocks.reshape(2, 2, 2, 96, 512), 0, BIT_C)
+    both_blocks = trade_block(both_blocks, 1, BIT_Y)
+    w_out_head = jnp.where(out_owner, w_out, out_near)
+    heads, heads_far, both_blocks, w_down_held, tables = sync(
+        heads, heads_far, both_blocks, w_down, tables
+    )
+    w_heads = assemble_rows(natural, heads, heads_far)
+    ids = jnp.concatenate([block_ids, other_ids], axis=0).reshape(2, 16, 128)
+    chosen = (pieces[:, None] == sixteen[None, :]).astype(low)
+    blocks = jnp.einsum(
+        "kp,spr->skr", chosen, ids.astype(low), preferred_element_type=wide
+    ).reshape(2, 1, 2048)
+    query_blk, key_blk = blocks[:, :, :1024], blocks
+    normed, w_heads, both_blocks, w_out_head, query_blk, key_blk, rows_dy = sync(
+        normed, w_heads, both_blocks, w_out_head, query_blk, key_blk, cotangent[0]
+    )
+
+    out_full = cube_gather(w_out_head)
+    grads = gather_next(gather_start(rows_dy, THIRDS), THIRDS, 0)
+    queries, own_part = project(spots, normed, w_heads, tables)
+    queries, own_part, grads, both_blocks = sync(queries, own_part, grads, both_blocks)
+    far_part = swap(own_part, BIT_ZH)
+    grads = gather_next(grads, THIRDS, 1)
+    far_part, grads, both_blocks = sync(far_part, grads, both_blocks)
+    other_parts = swap(jnp.stack([own_part, far_part]), BIT_C)
+    both_blocks = trade_block(both_blocks, 2, BIT_ZL)
+    other_parts, far_part, grads = sync(other_parts, far_part, grads)
+    held = (own_part, far_part, other_parts, other_parts)
+    grads = gather_next(grads, THIRDS, 2)
+    down_near = swap(w_down_held, BIT_ZH, owns_down)
+    keep, send, attention, totals = attend_forward(
+        spots, queries, held, query_blk, key_blk, score_scale
+    )
+    keep, send, attention, totals, both_blocks, grads, out_full = sync(
+        keep, send, attention, totals, both_blocks, grads, out_full
+    )
+
+    near_rows = [both_blocks[0].reshape(4, 96, 512), both_blocks[1].reshape(4, 96, 512)]
+    traded = jnp.stack([keep, swap(send, BIT_C)]).reshape(2, 2, 2, 2, 96, 128)
+    grads = gather_last(grads)
+    traded, grads, down_near, near_rows = sync(traded, grads, down_near, near_rows)
+    far_first = swap(near_rows[0], BIT_ZH)
+    traded = trade_block(traded, 1, BIT_X)
+    traded, near_rows = sync(traded, near_rows)
+    traded = trade_block(traded, 2, BIT_Y)
+    traded, far_first, near_rows = sync(traded, far_first, near_rows)
+    far_second = swap(near_rows[1], BIT_ZH)
+    traded = trade_block(traded, 3, BIT_ZL).reshape(16, 96, 128)
+    traded, residual = sync(traded, residual)
+    lyxc = ((sixteen & 8) >> 1) | ((sixteen & 4) >> 1) | (sixteen & 1)
+    head_from = (x ^ ((sixteen & 2) >> 1)) * 8 + ((seq_at ^ lyxc) & 7)
+    middle, scale_second, rows_second = out_project(head_from, traded, out_full, residual)
+
+    rows_second, middle, scale_second, grads = sync(rows_second, middle, scale_second, grads)
+    normed_mlp = cube_gather(rows_second)
+    w_rows = jnp.where(down_owner, w_down_held, down_near)
+    grad_hidden = hidden_back(spots, grads, w_rows)
+    grad_hidden, far_second = sync(grad_hidden, far_second)
+    w_both = assemble_rows(natural, *near_rows, far_first, far_second)
+    normed_mlp, grad_hidden, w_both = sync(normed_mlp, grad_hidden, w_both)
+    made = feed_back(spots, normed_mlp, w_both, grad_hidden)
+    hidden, grad_both = made[6:]
+    sums = scatter_start(paired(made[:6]))
+    sums, hidden, grad_both = sync(sums, hidden, grad_both)
+    sums = scatter_next(sums, THIRDS, 2)
+    keep_both, send_both = feed_weights(spots_rows, normed_mlp, grad_both)
+    sums, keep_both, send_both = sync(sums, keep_both, send_both)
+    sums = scatter_next(sums, THIRDS, 1)
+    sums, = sync(sums)
+    sums = scatter_next(sums, THIRDS, 0)
+    sums, hidden, send_both = sync(sums, hidden, send_both)
+
+    parts = scatter_last(sums)
+    grad_middle, grad_low, keep, send = out_back(
+        head_for, cotangent[0], parts, middle, scale_second, out_full
+    )
+    grad_middle, grad_low, keep, send, hidden, send_both = sync(
+        grad_middle, grad_low, keep, send, hidden, send_both
+    )
+    middle_rows = cube_gather(grad_low)
+    arrived_first = swap(send_both[:4], BIT_ZH)
+    traded = jnp.stack([keep, swap(send, BIT_C)]).reshape(2, 2, 2, 2, 96, 128)
+    traded, hidden = sync(traded, hidden)
+    out_terms = feed_out(spots, hidden, w_rows)
+    traded = trade_block(traded, 1, BIT_X)
+    traded, out_terms, hidden = sync(traded, out_terms, hidden)
+    grad_down = down_weights(spots, hidden, grads)
+    traded = trade_block(traded, 2, BIT_Y)
+    traded, grad_down, arrived_first, send_both, out_terms = sync(
+        traded, grad_down, arrived_first, send_both, out_terms
+    )
+    arrived_second = swap(send_both[4:], BIT_ZH)
+    traded = trade_block(traded, 3, BIT_ZL).reshape(8, 2, 96, 128)
+    out_sums = scatter_start(paired(out_terms))
+    traded, out_sums = sync(traded, out_sums)
+    out_sums = scatter_next(out_sums, HALVES, 2)
+    made = attend_backward(
+        spots,
+        queries,
+        held,
+        query_blk,
+        key_blk,
+        attention,
+        totals,
+        traded,
+        tables,
+        score_scale,
+    )
+    made, out_sums, arrived_second = sync(made, out_sums, arrived_second)
+    grad_queries, mine, sent = made
+    both_sum = sum_low(keep_both, jnp.concatenate([arrived_first, arrived_second], axis=0))
+    arrived = swap(sent, BIT_C)
+    arrived, both_sum, grad_down = sync(arrived, both_sum, grad_down)
+    far_terms = sum_low(mine[1], arrived[1])
+    far_terms, out_sums, both_sum = sync([far_terms[0], far_terms[1]], out_sums, both_sum)
+    far_first = swap(far_terms[0], BIT_ZH)
+    out_sums = scatter_next(out_sums, HALVES, 1)
+    both_sum = trade_block(both_sum.reshape(2, 2, 2, 96, 512), 0, BIT_ZL)
+    far_first, far_terms, out_sums, both_sum, middle_rows = sync(
+        far_first, far_terms, out_sums, both_sum, middle_rows
+    )
+    far_second = swap(far_terms[1], BIT_ZH)
+    both_sum = trade_block(both_sum, 1, BIT_Y)
+    grad_out_head = out_weights(spots, attention, middle_rows)
+    far_second, both_sum, grad_out_head, out_sums = sync(
+        far_second, both_sum, grad_out_head, out_sums
+    )
+    grad_own = (
+        mine[0].astype(wide)
+        + arrived[0].astype(wide)
+        + jnp.stack([far_first, far_second]).astype(wide)
+    )
+    out_sums = scatter_next(out_sums, HALVES, 0)
+    down_arrived = swap(grad_down, BIT_ZH, lacks_down)
+    both_near = trade_block(both_sum, 2, BIT_C).reshape(8, 96, 512)
+    made = project_back(spots, w_heads, tables, grad_queries, grad_own)
+    sums = scatter_start(paired(made))
+    sums, grad_own, both_near = sync(sums, grad_own, both_near)
+    both_far = swap(both_near, BIT_X)
+    keep_heads, send_heads = head_weights(
+        spots_rows, normed, tables, grad_queries, grad_own
+    )
+    sums = scatter_next(sums, THIRDS, 2)
+    sums, keep_heads, send_heads, out_sums, down_arrived = sync(
+        sums, keep_heads, send_heads, out_sums, down_arrived
+    )
+    heads_first = swap(send_heads, BIT_ZH)
+    output = jnp.concatenate([part[0] for part in scatter_last(out_sums)], axis=1)
+    output = (middle + output).astype(low)
+    down_sum = sum_low(grad_down, down_arrived)
+    sums = scatter_next(sums, THIRDS, 1)
+    sums, output, down_sum, both_far = sync(sums, output, down_sum, both_far)
+    down_far = swap(down_sum, BIT_X, owns_down)
+    sums = scatter_next(sums, THIRDS, 0)
+    sums, heads_first, grad_out_head = sync(sums, heads_first, grad_out_head)
+    out_arrived = swap(grad_out_head, BIT_ZH, lacks_out)
+    heads_sum = sum_low(keep_heads, heads_first)
+    heads_sum = trade_block(heads_sum.reshape(2, 2, 2, 96, 192), 0, BIT_ZL)
+    scaled_first = jnp.concatenate([part[0] for part in scatter_last(sums)], axis=1)
+    grad_inputs = grad_middle + scale_first * (
+        scaled_first
+        - normed_first * jnp.mean(scaled_first * normed_first, axis=-1, keepdims=True)
+    )
+    heads_sum = trade_block(heads_sum, 1, BIT_Y)
+    heads_near = trade_block(heads_sum, 2, BIT_C).reshape(8, 96, 192)
+    heads_near, out_arrived = sync(heads_near, out_arrived)
+    heads_far = swap(heads_near, BIT_X)
+    out_sum = sum_low(grad_out_head, out_arrived)
+    out_far = swap(out_sum, BIT_X, owns_out)
+
+    back = seq_at ^ cyl
+    home = jnp.concatenate([x * 8 + (back & 7), (1 - x) * 8 + (back & 7)])
+    grad_w_query, grad_w_key, grad_w_value, grad_gain_attn = spread_heads(
+        home, heads_near, heads_far, w_query, w_key, w_value, gain_rows_attn
+    )
+    grad_w_out = jnp.where(out_owner, out_sum, out_far).astype(wide)
+    grad_w_down = jnp.where(down_owner, down_sum, down_far).astype(wide)
+    side = (back & 1) ^ x
+    home = jnp.concatenate([side * 8 + (back & 7), (1 - side) * 8 + (back & 7)])
+    grad_w_gate, grad_w_up, grad_gain_mlp = spread_columns(
+        home, both_near, both_far, gain_rows_mlp, w_gate, w_up
+    )
+    return (
+        output[None],
+        grad_inputs.astype(low)[None],
+        grad_w_query,
+        grad_w_key,
+        grad_w_value,
+        grad_w_out,
+        grad_w_gate,
+        grad_w_up,
+        grad_w_down,
+        grad_gain_attn[:, 0],
+        grad_gain_mlp[:, 0],
+    )
+
+
+def ring_plan(
     inputs,
     cotangent,
     block_ids,
@@ -429,6 +1566,9 @@
 
 
 def solution(mesh):
+    local = ring_plan
+    if (mesh.shape["grp"], mesh.shape["seq"]) == (2, 16):
+        local = cube_plan
     return jax.shard_map(
         local,
         mesh=mesh,

time: 2310 us -> 527 us (0.23)
  waiting for transfers between devices: 1610 us -> 238 us
  local copies, waits for them, and re-layouts: 305 us -> 17.2 us
  matrix products: 174 us -> 0.19 us
  Pallas kernels: 0 us -> 119 us
  starting transfers between devices: 0.89 us -> 103 us
  blocking collectives: 100 us -> 0 us
  other arithmetic: 81.8 us -> 31.5 us
    reduce_scatter x8 -> x0, waiting for transfers between devices: 1190 us -> none  [the longest x1 245 us: local(): lax.psum_scatter(terms[4], 'seq', scatter_dimension=0, tiled=True)]
    all_gather x8 -> x4, waiting for transfers between devices: 403 us -> 31 us  [cube_gather(): lax.all_gather(rows, AXES, axis=0, tiled=True, axis_index_groups=cube_gro...]
    dynamic_update_slice x8 -> x0, local copies, waits for them, and re-layouts: 230 us -> none  [local(): lax.scan(backward_key_step, state_in[0][member], (kv_rows, key_blk))]
    ppermute x0 -> x84, waiting for transfers between devices: none -> 207 us  [swap(): return lax.ppermute(value, AXES, pairs)]
    dot_general x35 -> x1, matrix products: 174 us -> 0.19 us  [cube_plan(): jnp.einsum('kp,spr->skr', chosen, ids.astype(low), preferred_element_type...]
    pallas_call x0 -> x19, Pallas kernels: none -> 119 us  [kernel_call(): pl.pallas_call(body, out_shape=out_shape, grid_spec=pltpu.PrefetchScalarG...]
    ppermute x0 -> x84, starting transfers between devices: none -> 103 us  [swap(): return lax.ppermute(value, AXES, pairs)]
    unnamed x2 -> x0, blocking collectives: 95.3 us -> none
  transfers between devices with their start and end apart: 17 -> 88, of which waited for: 17 -> 48; matrix products, arithmetic and copies ran while one was open for 9% -> 6% of each run, Pallas kernels for 0% -> 17%
where the time goes in v2:
time: 527 us; the launch traced here: 525 us
  waiting for transfers between devices  238 us (45%)
  Pallas kernels  119 us (23%)
  starting transfers between devices  103 us (20%)
  other arithmetic  31.5 us (6%)
  local copies, waits for them, and re-layouts  17.2 us (3%)
  between operations  15.8 us (3%)
    ppermute x84, waiting for transfers between devices, swap(): return lax.ppermute(value, AXES, pairs)  207 us
    pallas_call x19, Pallas kernels, kernel_call(): pl.pallas_call(body, out_shape=out_shape, grid_spec=pltpu.PrefetchScalarG...  119 us
    ppermute x84, starting transfers between devices, swap(): return lax.ppermute(value, AXES, pairs)  103 us
    all_gather x4, waiting for transfers between devices, cube_gather(): lax.all_gather(rows, AXES, axis=0, tiled=True, axis_index_groups=cube_gro...  31 us
    unnamed x222, local copies, waits for them, and re-layouts  11.7 us
    convert_element_type x24, other arithmetic, scatter_next(): sent = (kept[half:].astype(wide) + arrived[half:].astype(wide)).astype(low)  10.6 us
  transfers between devices with their start and end apart: 88, of which 48 were waited for; matrix products, arithmetic and copies ran while one was open for 6% of the time, Pallas kernels for 17%

profile of v2, /device:TPU:0, one launch (start us, length us, event | category | flops | bytes accessed | tf_op | source)
XLA Modules:
  0.0 524.8 jit_solution(11648241630320692303)
XLA Ops:
  13.5 3.0 collective-permute-start.1
  17.3 5.2 collective-permute-start.3
  27.0 16.5 %collective-permute-done.2 = bf16[2,2,96,192]{3,2,1,0:T(8,128)(2,1)S(1)} collective-permute-done((bf16[2,2,96,192]{3,2,1,0:T(8,128)(2,1)S(1)}, bf16[2,2,96,192]{3,2,1,0:T(8,128)(2,1)S(1)}, u32[]{:S(2)}, u32[]{:S(2)}) %collective-permute-start.2) | collective-permute-done | bytes 147488 | tf_op jit(solution)/shard_map/ppermute | solution.py:164
  46.8 10.0 %collective-permute-done.6 = bf16[2,2,96,512]{3,2,0,1:T(8,128)(2,1)S(1)} collective-permute-done((bf16[2,2,96,512]{3,2,0,1:T(8,128)(2,1)S(1)}, bf16[2,2,96,512]{3,2,0,1:T(8,128)(2,1)S(1)}, u32[]{:S(2)}, u32[]{:S(2)}) %collective-permute-start.6) | collective-permute-done | bytes 393248 | tf_op jit(solution)/shard_map/ppermute | solution.py:164
  57.7 5.6 %collective-permute-done.4.refs_1_ = bf16[8,96,192]{2,1,0:T(8,128)(2,1)S(1)} collective-permute-done((bf16[8,96,192]{2,1,0:T(8,128)(2,1)S(1)}, bf16[8,96,192]{2,1,0:T(8,128)(2,1)S(1)}, u32[]{:S(2)}, u32[]{:S(2)}) %collective-permute-start.4) | collective-permute-done | bytes 294944 | tf_op jit(solution)/shard_map/ppermute | solution.py:164
  63.9 5.6 %all-gather.5.cloned.1.call-done.rows_ref = bf16[2048,1536]{1,0:T(8,128)(2,1)} async-done(((bf16[128,1536]{1,0:T(8,128)(2,1)}), bf16[2048,1536]{1,0:T(8,128)(2,1)}) %all-gather.5.cloned.1.call-update) | async-done | bytes 6291472 | tf_op jit(solution)/shard_map/all_gather | solution.py:216
  69.7 2.8 collective-permute-start.10
  74.7 8.0 %shard_map.215 = (bf16[2,96,1024]{2,1,0:T(8,128)(2,1)S(1)}, bf16[2,96,1024]{2,1,0:T(8,128)(2,1)S(1)}) custom-call(s32[9]{0:T(128)S(1)} %pad_add_fusion.at_ref, bf16[2048,1536]{1,0:T(8,128)(2,1)} %all-gather.5.cloned.1.call-done.rows_ref, bf16[1536,192]{1,0:T(8,128)(2,1)S(1)} %shard_map.214.w_ref, f32[48,1024]{1,0:T(8,128)S(1)} %get-tuple-element.282.cos_ref.rest_2_, ...), custom_call_target="tpu_custom_call" | custom-call | flops 1207959552 | bytes 8388608 | tf_op jit(solution)/shard_map/pallas_call | solution.py:296
  83.5 2.6 collective-permute-start.11
  87.4 3.1 collective-permute-done.12
  90.6 14.4 %collective-permute-done.13 = bf16[2,128,512]{2,1,0:T(8,128)(2,1)S(1)} collective-permute-done((bf16[2,128,512]{2,1,0:T(8,128)(2,1)S(1)}, bf16[2,128,512]{2,1,0:T(8,128)(2,1)S(1)}, u32[]{:S(2)}, u32[]{:S(2)}) %collective-permute-start.13) | collective-permute-done | bytes 262176 | tf_op jit(solution)/shard_map/ppermute | solution.py:164
  106.4 5.6 %collective-permute-start.16 = (bf16[2,2,96,512]{3,2,1,0:T(8,128)(2,1)S(1)}, bf16[2,2,96,512]{3,2,1,0:T(8,128)(2,1)S(1)}, u32[]{:S(2)}, u32[]{:S(2)}) collective-permute-start(bf16[2,2,96,512]{3,2,1,0:T(8,128)(2,1)S(1)} %get-tuple-element.568), channel_id=1, source_target_pairs={{0,4},{1,5},{2,6},{3,7},{4,0},{5,1},{6,2},{7,3},{8,12},{9,13},{10,... | collective-permute-start | bytes 1179656 | tf_op jit(solution)/shard_map/ppermute | solution.py:164
  112.1 2.1 collective-permute-start.17
  114.7 11.7 %collective-permute-done.16 = bf16[2,2,96,512]{3,2,1,0:T(8,128)(2,1)S(1)} collective-permute-done((bf16[2,2,96,512]{3,2,1,0:T(8,128)(2,1)S(1)}, bf16[2,2,96,512]{3,2,1,0:T(8,128)(2,1)S(1)}, u32[]{:S(2)}, u32[]{:S(2)}) %collective-permute-start.16) | collective-permute-done | bytes 393248 | tf_op jit(solution)/shard_map/ppermute | solution.py:164
  127.3 11.3 %shard_map.216 = (bf16[8,96,128]{2,1,0:T(8,128)(2,1)S(1)}, bf16[8,96,128]{2,1,0:T(8,128)(2,1)S(1)}, f32[2,96,1024]{2,1,0:T(8,128)S(1)}, f32[2,1,1024]{2,1,0:T(1,128)S(1)}) custom-call(s32[9]{0:T(128)S(1)} %pad_add_fusion.at_ref, bf16[2,96,1024]{2,1,0:T(8,128)(2,1)S(1)} %get-tuple-element.288.q_ref, bf16[2,96,1024]{2,1,0:T(8,128)(2,1)S(1)} %get-tuple-element.289.a_ref, ...), custom_call_target="tpu_custom_call" | custom-call | flops 1610612736 | bytes 12582912 | tf_op jit(solution)/shard_map/pallas_call | solution.py:296
  140.5 4.4 collective-permute-start.24
  145.0 1.9 fusion.41
  147.0 7.8 %collective-permute-done.24 = bf16[256,1536]{1,0:T(8,128)(2,1)S(1)} collective-permute-done((bf16[256,1536]{1,0:T(8,128)(2,1)}, bf16[256,1536]{1,0:T(8,128)(2,1)S(1)}, u32[]{:S(2)}, u32[]{:S(2)}) %collective-permute-start.24) | collective-permute-done | bytes 786464 | tf_op jit(solution)/shard_map/ppermute | solution.py:164
  155.3 3.0 collective-permute-start.27
  158.3 2.3 collective-permute-done.25
  162.3 4.1 collective-permute-done.26
  166.4 5.3 %collective-permute-done.27.refs_2_ = bf16[4,96,512]{2,1,0:T(8,128)(2,1)S(1)} collective-permute-done((bf16[4,96,512]{2,1,0:T(8,128)(2,1)S(1)}, bf16[4,96,512]{2,1,0:T(8,128)(2,1)S(1)}, u32[]{:S(2)}, u32[]{:S(2)}) %collective-permute-start.27) | collective-permute-done | bytes 393248 | tf_op jit(solution)/shard_map/ppermute | solution.py:164
  171.8 12.4 %collective-permute-start.28 = (bf16[2,2,2,96,128]{4,3,2,1,0:T(8,128)(2,1)S(1)}, bf16[2,2,2,96,128]{4,3,2,1,0:T(8,128)(2,1)S(1)}, u32[]{:S(2)}, u32[]{:S(2)}) collective-permute-start(bf16[2,2,2,96,128]{4,3,2,1,0:T(8,128)(2,1)S(1)} %get-tuple-element.600), channel_id=1, source_target_pairs={{0,4},{1,5},{2,6},{3,7},{4,0},{5,1},{6,2},{7,3},{8,12},{9,13},{10,... | collective-permute-start | bytes 589832 | tf_op jit(solution)/shard_map/ppermute | solution.py:164
  184.3 5.5 %collective-permute-done.28 = bf16[2,2,2,96,128]{4,3,2,1,0:T(8,128)(2,1)S(1)} collective-permute-done((bf16[2,2,2,96,128]{4,3,2,1,0:T(8,128)(2,1)S(1)}, bf16[2,2,2,96,128]{4,3,2,1,0:T(8,128)(2,1)S(1)}, u32[]{:S(2)}, u32[]{:S(2)}) %collective-permute-start.28) | collective-permute-done | bytes 196640 | tf_op jit(solution)/shard_map/ppermute | solution.py:164
  189.9 3.9 shard_map.217
  199.0 7.6 %shard_map.218.dh_ref = f32[2048,256]{1,0:T(8,128)} custom-call(s32[9]{0:T(128)S(1)} %pad_add_fusion.at_ref, bf16[8,128,512]{2,1,0:T(8,128)(2,1)S(1)} %pad_maximum_fusion.refs_0_, bf16[8,128,512]{2,1,0:T(8,128)(2,1)S(1)} %copy-done.1, bf16[8,128,512]{2,1,0:T(8,128)(2,1)S(1)} %pad_maximum_fusion.1.refs_2_, bf16[8,128,512]{2,1,0:T(8,128)(2,1)S(1)} %copy-done.4, ...), custom_call_target="tpu_custom_call" | custom-call | flops 1610612736 | bytes 8388608 | tf_op jit(solution)/shard_map/pallas_call | solution.py:296
  206.5 9.7 %collective-permute-done.29.refs_3_ = bf16[4,96,512]{2,1,0:T(8,128)(2,1)S(1)} collective-permute-done((bf16[4,96,512]{2,1,0:T(8,128)(2,1)}, bf16[4,96,512]{2,1,0:T(8,128)(2,1)S(1)}, u32[]{:S(2)}, u32[]{:S(2)}) %collective-permute-start.29) | collective-permute-done | bytes 393248 | tf_op jit(solution)/shard_map/ppermute | solution.py:164
  218.1 25.3 %all-gather.9.cloned.1.call-done.rows_ref = bf16[2048,1536]{1,0:T(8,128)(2,1)} async-done(((bf16[128,1536]{1,0:T(8,128)(2,1)}), bf16[2048,1536]{1,0:T(8,128)(2,1)}) %all-gather.9.cloned.1.call-update) | async-done | bytes 6291472 | tf_op jit(solution)/shard_map/all_gather | solution.py:216
  243.4 13.1 %shard_map.220 = (bf16[8,128,512]{2,1,0:T(8,128)(2,1)S(1)}, bf16[8,128,512]{2,1,0:T(8,128)(2,1)S(1)}, bf16[8,128,512]{2,1,0:T(8,128)(2,1)S(1)}, bf16[8,128,512]{...) custom-call(s32[9]{0:T(128)S(1)} %pad_add_fusion.at_ref, ...), custom_call_target="tpu_custom_call" | custom-call | flops 6442450944 | bytes 18874368 | tf_op jit(solution)/shard_map/pallas_call | solution.py:296
  257.3 1.9 collective-permute-done.30
  259.1 3.0 collective-permute-done.31
  265.5 9.5 %shard_map.221 = (bf16[8,96,512]{2,1,0:T(8,128)(2,1)S(1)}, bf16[8,96,512]{2,1,0:T(8,128)(2,1)S(1)}) custom-call(s32[25]{0:T(128)S(1)} %pad_add_fusion.2.at_ref, bf16[2048,1536]{1,0:T(8,128)(2,1)} %all-gather.9.cloned.1.call-done.rows_ref, bf16[2048,512]{1,0:T(8,128)(2,1)S(1)} %copy-done.80), custom_call_target="tpu_custom_call" | custom-call | flops 3221225472 | bytes 14680064 | tf_op jit(solution)/shard_map/pallas_call | solution.py:296
  283.1 2.2 collective-permute-done.36
  291.1 2.0 collective-permute-done.39
  295.7 4.5 shard_map.222
  308.2 5.4 %shard_map.223 = (bf16[8,128,768]{2,1,0:T(8,128)(2,1)S(1)}, bf16[8,128,768]{2,1,0:T(8,128)(2,1)S(1)}, bf16[8,128,768]{2,1,0:T(8,128)(2,1)}, bf16[8,128,768]{2,1,0:T(8,128)(2,1)}) custom-call(s32[9]{0:T(128)S(1)} %pad_add_fusion.at_ref, bf16[2048,256]{1,0:T(8,128)(2,1)S(1)} %copy-done.29, bf16[256,1536]{1,0:T(8,128)(2,1)S(1)} %copy-done.7), custom_call_target="tpu_custom_call" | custom-call | flops 1610612736 | bytes 8388608 | tf_op jit(solution)/shard_map/pallas_call | solution.py:296
  313.6 3.2 collective-permute-done.43
  318.2 6.8 %shard_map.224 = bf16[256,1536]{1,0:T(8,128)(2,1)S(1)} custom-call(s32[9]{0:T(128)S(1)} %pad_add_fusion.at_ref, bf16[8,128,512]{2,1,0:T(8,128)(2,1)S(1)} %pad_maximum_fusion.refs_0_, bf16[8,128,512]{2,1,0:T(8,128)(2,1)S(1)} %copy-done.2, bf16[8,128,512]{2,1,0:T(8,128)(2,1)S(1)} %pad_maximum_fusion.1.refs_2_, bf16[8,128,512]{2,1,0:T(8,128)(2,1)S(1)} %copy-done.5, ...), custom_call_target="tpu_custom_call" | custom-call | flops 1610612736 | bytes 8388608 | tf_op jit(solution)/shard_map/pallas_call | solution.py:296
  325.1 2.9 collective-permute-done.45
  329.2 11.1 %collective-permute-done.46 = bf16[2,2,2,96,128]{4,3,2,1,0:T(8,128)(2,1)S(1)} collective-permute-done((bf16[2,2,2,96,128]{4,3,2,1,0:T(8,128)(2,1)S(1)}, bf16[2,2,2,96,128]{4,3,2,1,0:T(8,128)(2,1)S(1)}, u32[]{:S(2)}, u32[]{:S(2)}) %collective-permute-start.46) | collective-permute-done | bytes 196640 | tf_op jit(solution)/shard_map/ppermute | solution.py:164
  343.8 18.2 %shard_map.225 = (bf16[2,96,1024]{2,1,0:T(8,128)(2,1)S(1)}, bf16[2,2,96,1024]{3,2,1,0:T(8,128)(2,1)S(1)}, bf16[2,2,96,1024]{3,2,1,0:T(8,128)(2,1)S(1)}) custom-call(s32[9]{0:T(128)S(1)} %pad_add_fusion.at_ref, bf16[2,96,1024]{2,1,0:T(8,128)(2,1)S(1)} %copy-done.77, bf16[2,96,1024]{2,1,0:T(8,128)(2,1)S(1)} %copy-done.56, bf16[2,96,1024]{2,1,0:T(8,128)(2,1)S(1)} %copy-done.58, ...), custom_call_target="tpu_custom_call" | custom-call | flops 4026531840 | bytes 12582912 | tf_op jit(solution)/shard_map/pallas_call | solution.py:296
  362.0 4.8 collective-permute-done.50
  367.1 2.1 collective-permute-done.52
  371.0 2.5 collective-permute-start.54
  376.5 2.4 collective-permute-start.53
  378.9 9.8 %collective-permute-done.56 = bf16[2,2,96,512]{3,2,1,0:T(8,128)(2,1)S(1)} collective-permute-done((bf16[2,2,96,512]{3,2,1,0:T(8,128)(2,1)S(1)}, bf16[2,2,96,512]{3,2,1,0:T(8,128)(2,1)S(1)}, u32[]{:S(2)}, u32[]{:S(2)}) %collective-permute-start.56) | collective-permute-done | bytes 393248 | tf_op jit(solution)/shard_map/ppermute | solution.py:164
  393.2 6.8 %shard_map.226 = bf16[96,1536]{1,0:T(8,128)(2,1)S(1)} custom-call(s32[9]{0:T(128)S(1)} %pad_add_fusion.at_ref, f32[2,96,1024]{2,1,0:T(8,128)S(1)} %copy-done.37, bf16[2048,1536]{1,0:T(8,128)(2,1)} %all-gather.11.cloned.1.call-done.rows_ref), custom_call_target="tpu_custom_call" | custom-call | flops 603979776 | bytes 8388608 | tf_op jit(solution)/shard_map/pallas_call | solution.py:296
  400.5 2.4 collective-permute-done.57
  403.0 6.2 %shard_map.227 = (bf16[8,128,512]{2,1,0:T(8,128)(2,1)S(1)}, bf16[8,128,512]{2,1,0:T(8,128)(2,1)}, bf16[8,128,512]{2,1,0:T(8,128)(2,1)S(1)}, bf16[8,128,512]{2,1,...) custom-call(s32[9]{0:T(128)S(1)} %pad_add_fusion.at_ref, bf16[1536,192]{1,0:T(8,128)(2,1)S(1)} %copy-done.18, ...), custom_call_target="tpu_custom_call" | custom-call | flops 1207959552 | bytes 8388608 | tf_op jit(solution)/shard_map/pallas_call | solution.py:296
  413.7 3.1 collective-permute-done.62
  427.2 8.1 %collective-permute-done.68 = bf16[256,1536]{1,0:T(8,128)(2,1)S(1)} collective-permute-done((bf16[256,1536]{1,0:T(8,128)(2,1)S(1)}, bf16[256,1536]{1,0:T(8,128)(2,1)S(1)}, u32[]{:S(2)}, u32[]{:S(2)}) %collective-permute-start.68) | collective-permute-done | bytes 786464 | tf_op jit(solution)/shard_map/ppermute | solution.py:164
  435.3 7.8 %shard_map.228 = (bf16[8,96,192]{2,1,0:T(8,128)(2,1)S(1)}, bf16[8,96,192]{2,1,0:T(8,128)(2,1)S(1)}) custom-call(s32[25]{0:T(128)S(1)} %copy-done.69, bf16[2048,1536]{1,0:T(8,128)(2,1)} %all-gather.5.cloned.1.call-done.rows_ref, f32[48,1024]{1,0:T(8,128)S(1)} %get-tuple-element.279.cos2_ref.cos_ref, f32[48,1024]{1,0:T(8,128)S(1)} %get-tuple-element.280.sin2_ref.sin_ref, ...), custom_call_target="tpu_custom_call" | custom-call | flops 1207959552 | bytes 8388608 | tf_op jit(solution)/shard_map/pallas_call | solution.py:296
  443.1 3.7 collective-permute-done.66
  447.6 2.8 collective-permute-done.67
  451.5 2.5 collective-permute-start.70
  455.8 11.5 %collective-permute-done.72.far_ref = bf16[8,96,512]{2,1,0:T(8,128)(2,1)S(1)} collective-permute-done((bf16[8,96,512]{2,1,0:T(8,128)(2,1)S(1)}, bf16[8,96,512]{2,1,0:T(8,128)(2,1)S(1)}, u32[]{:S(2)}, u32[]{:S(2)}) %collective-permute-start.72) | collective-permute-done | bytes 786464 | tf_op jit(solution)/shard_map/ppermute | solution.py:164
  467.3 3.4 collective-permute-done.71
  471.8 4.3 collective-permute-start.83
  476.1 3.1 shard_map.230
  481.8 2.1 collective-permute-start.77
  486.7 1.9 collective-permute-done.77
  490.5 3.9 collective-permute-done.78
  499.8 13.6 %collective-permute-done.81.far_ref = bf16[8,96,192]{2,1,0:T(8,128)(2,1)S(1)} collective-permute-done((bf16[8,96,192]{2,1,0:T(8,128)(2,1)S(1)}, bf16[8,96,192]{2,1,0:T(8,128)(2,1)S(1)}, u32[]{:S(2)}, u32[]{:S(2)}) %collective-permute-start.81) | collective-permute-done | bytes 294944 | tf_op jit(solution)/shard_map/ppermute | solution.py:164
  513.5 3.3 shard_map.229
  (486 shorter events, 112.2 us)
Async XLA Ops:
  7.2 62.3 %all-gather.5.cloned.1.call-start = ((), (), s32[]{:S(2)}) async-start(), calls=%async_computation | async-start | bytes 6684672 | tf_op jit(solution)/shard_map/all_gather | solution.py:216
  10.5 129.4 %all-gather.7.cloned.1.call-start = ((), (), s32[]{:S(2)}) async-start(), calls=%async_computation.1 | async-start | bytes 5013504 | tf_op jit(solution)/shard_map/all_gather | solution.py:216
  13.5 9.0 %collective-permute-start.1 = (bf16[2,2,96,192]{3,2,0,1:T(8,128)(2,1)S(1)}, bf16[2,2,96,192]{3,2,0,1:T(8,128)(2,1)S(1)}, u32[]{:S(2)}, u32[]{:S(2)}) collective-permute-start(bf16[2,2,96,192]{3,2,0,1:T(8,128)(2,1)S(1)} %get-tuple-element.611), channel_id=1, source_target_pairs={{0,2},{1,3},{2,0},{3,1},{4,6},{5,7},{6,4},{7,5},{8,10},{9,11},{10,... | collective-permute-start | bytes 442376 | tf_op jit(solution)/shard_map/ppermute | solution.py:164
  17.3 26.3 %collective-permute-start.3 = (bf16[96,1536]{1,0:T(8,128)(2,1)S(1)}, bf16[96,1536]{1,0:T(8,128)(2,1)}, u32[]{:S(2)}, u32[]{:S(2)}) collective-permute-start(bf16[96,1536]{1,0:T(8,128)(2,1)S(1)} %copy-done.96), channel_id=1, source_target_pairs={{0,8},{1,9},{2,10},{3,11},{4,12},{5,13},{6,14},{7,15},{24,16},{25,... | collective-permute-start | bytes 884744 | tf_op jit(solution)/shard_map/ppermute | solution.py:164
  22.6 20.9 %collective-permute-start.2 = (bf16[2,2,96,192]{3,2,1,0:T(8,128)(2,1)S(1)}, bf16[2,2,96,192]{3,2,1,0:T(8,128)(2,1)S(1)}, u32[]{:S(2)}, u32[]{:S(2)}) collective-permute-start(bf16[2,2,96,192]{3,2,1,0:T(8,128)(2,1)S(1)} %get-tuple-element.609), channel_id=1, source_target_pairs={{0,4},{1,5},{2,6},{3,7},{4,0},{5,1},{6,2},{7,3},{8,12},{9,13},{10,... | collective-permute-start | bytes 442376 | tf_op jit(solution)/shard_map/ppermute | solution.py:164
  24.4 19.4 %collective-permute-start.7 = (s32[1,2048]{1,0:T(1,128)S(1)}, s32[1,2048]{1,0:T(1,128)S(1)}, u32[]{:S(2)}, u32[]{:S(2)}) collective-permute-start(s32[1,2048]{1,0:T(1,128)S(1)} %copy-done.102), channel_id=1, source_target_pairs={{0,16},{1,17},{2,18},{3,19},{4,20},{5,21},{6,22},{7,23},{8,24},{9,... | collective-permute-start | bytes 24584 | tf_op jit(solution)/shard_map/ppermute | solution.py:164
  44.1 19.2 %collective-permute-start.4 = (bf16[8,96,192]{2,1,0:T(8,128)(2,1)S(1)}, bf16[8,96,192]{2,1,0:T(8,128)(2,1)S(1)}, u32[]{:S(2)}, u32[]{:S(2)}) collective-permute-start(bf16[8,96,192]{2,1,0:T(8,128)(2,1)S(1)} %bitcast.187), channel_id=1, source_target_pairs={{0,8},{1,9},{2,10},{3,11},{4,12},{5,13},{6,14},{7,15},{8,0},{9,1},... | collective-permute-start | bytes 884744 | tf_op jit(solution)/shard_map/ppermute | solution.py:164
  45.6 11.2 %collective-permute-start.6 = (bf16[2,2,96,512]{3,2,0,1:T(8,128)(2,1)S(1)}, bf16[2,2,96,512]{3,2,0,1:T(8,128)(2,1)S(1)}, u32[]{:S(2)}, u32[]{:S(2)}) collective-permute-start(bf16[2,2,96,512]{3,2,0,1:T(8,128)(2,1)S(1)} %get-tuple-element.570), channel_id=1, source_target_pairs={{0,2},{1,3},{2,0},{3,1},{4,6},{5,7},{6,4},{7,5},{8,10},{9,11},{10,... | collective-permute-start | bytes 1179656 | tf_op jit(solution)/shard_map/ppermute | solution.py:164
  69.6 173.9 %all-gather.9.cloned.1.call-start = ((), (), s32[]{:S(2)}) async-start(), calls=%async_computation.2 | async-start | bytes 6684672 | tf_op jit(solution)/shard_map/all_gather | solution.py:216
  69.7 13.1 %collective-permute-start.10 = (bf16[1,128,512]{2,1,0:T(8,128)(2,1)S(1)}, bf16[1,128,512]{2,1,0:T(8,128)(2,1)S(1)}, u32[]{:S(2)}, u32[]{:S(2)}) collective-permute-start(bf16[1,128,512]{2,1,0:T(8,128)(2,1)S(1)} %get-tuple-element.605), channel_id=1, source_target_pairs={{0,4},{1,5},{2,6},{3,7},{4,0},{5,1},{6,2},{7,3},{8,12},{9,13},{10,... | collective-permute-start | bytes 393224 | tf_op jit(solution)/shard_map/ppermute | solution.py:164
  72.5 10.3 %collective-permute-start.9 = (bf16[1,128,512]{2,1,0:T(8,128)(2,1)S(1)}, bf16[1,128,512]{2,1,0:T(8,128)(2,1)S(1)}, u32[]{:S(2)}, u32[]{:S(2)}) collective-permute-start(bf16[1,128,512]{2,1,0:T(8,128)(2,1)S(1)} %get-tuple-element.606), channel_id=1, source_target_pairs={{0,2},{1,3},{2,0},{3,1},{4,6},{5,7},{6,4},{7,5},{8,10},{9,11},{10,... | collective-permute-start | bytes 393224 | tf_op jit(solution)/shard_map/ppermute | solution.py:164
  74.3 8.5 %collective-permute-start.8 = (bf16[1,128,512]{2,1,0:T(8,128)(2,1)S(1)}, bf16[1,128,512]{2,1,0:T(8,128)(2,1)S(1)}, u32[]{:S(2)}, u32[]{:S(2)}) collective-permute-start(bf16[1,128,512]{2,1,0:T(8,128)(2,1)S(1)} %get-tuple-element.607), channel_id=1, source_target_pairs={{0,16},{1,17},{2,18},{3,19},{4,20},{5,21},{6,22},{7,23},{8,24},{9,... | collective-permute-start | bytes 393224 | tf_op jit(solution)/shard_map/ppermute | solution.py:164
  83.0 22.0 %collective-permute-start.13 = (bf16[2,128,512]{2,1,0:T(8,128)(2,1)S(1)}, bf16[2,128,512]{2,1,0:T(8,128)(2,1)S(1)}, u32[]{:S(2)}, u32[]{:S(2)}) collective-permute-start(bf16[2,128,512]{2,1,0:T(8,128)(2,1)S(1)} %pad_maximum_fusion.27), channel_id=1, source_target_pairs={{0,4},{1,5},{2,6},{3,7},{4,0},{5,1},{6,2},{7,3},{8,12},{9,13},{10,... | collective-permute-start | bytes 786440 | tf_op jit(solution)/shard_map/ppermute | solution.py:164
  83.5 21.7 %collective-permute-start.11 = (bf16[2,96,1024]{2,1,0:T(8,128)(2,1)S(1)}, bf16[2,96,1024]{2,1,0:T(8,128)(2,1)S(1)}, u32[]{:S(2)}, u32[]{:S(2)}) collective-permute-start(bf16[2,96,1024]{2,1,0:T(8,128)(2,1)S(1)} %get-tuple-element.289.a_ref), channel_id=1, source_target_pairs={{0,8},{1,9},{2,10},{3,11},{4,12},{5,13},{6,14},{7,15},{8,0},{9,1},... | collective-permute-start | bytes 1179656 | tf_op jit(solution)/shard_map/ppermute | solution.py:164
  86.1 19.0 %collective-permute-start.14 = (bf16[2,128,512]{2,1,0:T(8,128)(2,1)S(1)}, bf16[2,128,512]{2,1,0:T(8,128)(2,1)S(1)}, u32[]{:S(2)}, u32[]{:S(2)}) collective-permute-start(bf16[2,128,512]{2,1,0:T(8,128)(2,1)S(1)} %pad_maximum_fusion.28), channel_id=1, source_target_pairs={{0,16},{1,17},{2,18},{3,19},{4,20},{5,21},{6,22},{7,23},{8,24},{9,... | collective-permute-start | bytes 786440 | tf_op jit(solution)/shard_map/ppermute | solution.py:164
  106.4 20.0 %collective-permute-start.16 = (bf16[2,2,96,512]{3,2,1,0:T(8,128)(2,1)S(1)}, bf16[2,2,96,512]{3,2,1,0:T(8,128)(2,1)S(1)}, u32[]{:S(2)}, u32[]{:S(2)}) collective-permute-start(bf16[2,2,96,512]{3,2,1,0:T(8,128)(2,1)S(1)} %get-tuple-element.568), channel_id=1, source_target_pairs={{0,4},{1,5},{2,6},{3,7},{4,0},{5,1},{6,2},{7,3},{8,12},{9,13},{10,... | collective-permute-start | bytes 1179656 | tf_op jit(solution)/shard_map/ppermute | solution.py:164
  112.1 26.7 %collective-permute-start.17 = (bf16[4,128,512]{2,1,0:T(8,128)(2,1)S(1)}, bf16[4,128,512]{2,1,0:T(8,128)(2,1)S(1)}, u32[]{:S(2)}, u32[]{:S(2)}) collective-permute-start(bf16[4,128,512]{2,1,0:T(8,128)(2,1)S(1)} %pad_maximum_fusion.10), channel_id=1, source_target_pairs={{0,4},{1,5},{2,6},{3,7},{4,0},{5,1},{6,2},{7,3},{8,12},{9,13},{10,... | collective-permute-start | bytes 1572872 | tf_op jit(solution)/shard_map/ppermute | solution.py:164
  114.2 24.6 %collective-permute-start.18 = (bf16[4,128,512]{2,1,0:T(8,128)(2,1)S(1)}, bf16[4,128,512]{2,1,0:T(8,128)(2,1)S(1)}, u32[]{:S(2)}, u32[]{:S(2)}) collective-permute-start(bf16[4,128,512]{2,1,0:T(8,128)(2,1)S(1)} %pad_maximum_fusion.11), channel_id=1, source_target_pairs={{0,16},{1,17},{2,18},{3,19},{4,20},{5,21},{6,22},{7,23},{8,24},{9,... | collective-permute-start | bytes 1572872 | tf_op jit(solution)/shard_map/ppermute | solution.py:164
  114.2 25.5 %collective-permute-start.19 = (bf16[4,128,512]{2,1,0:T(8,128)(2,1)S(1)}, bf16[4,128,512]{2,1,0:T(8,128)(2,1)S(1)}, u32[]{:S(2)}, u32[]{:S(2)}) collective-permute-start(bf16[4,128,512]{2,1,0:T(8,128)(2,1)S(1)} %pad_maximum_fusion.12), channel_id=1, source_target_pairs={{0,2},{1,3},{2,0},{3,1},{4,6},{5,7},{6,4},{7,5},{8,10},{9,11},{10,... | collective-permute-start | bytes 1572872 | tf_op jit(solution)/shard_map/ppermute | solution.py:164
  139.8 14.9 %collective-permute-start.21 = (bf16[8,128,512]{2,1,0:T(8,128)(2,1)S(1)}, bf16[8,128,512]{2,1,0:T(8,128)(2,1)S(1)}, u32[]{:S(2)}, u32[]{:S(2)}) collective-permute-start(bf16[8,128,512]{2,1,0:T(8,128)(2,1)S(1)} %pad_maximum_fusion.refs_0_), channel_id=1, source_target_pairs={{0,1},{1,0},{2,3},{3,2},{4,5},{5,4},{6,7},{7,6},{8,9},{9,8},{10,11... | collective-permute-start | bytes 3145736 | tf_op jit(solution)/shard_map/ppermute | solution.py:164
  140.0 14.7 %collective-permute-start.22 = (bf16[8,128,512]{2,1,0:T(8,128)(2,1)S(1)}, bf16[8,128,512]{2,1,0:T(8,128)(2,1)S(1)}, u32[]{:S(2)}, u32[]{:S(2)}) collective-permute-start(bf16[8,128,512]{2,1,0:T(8,128)(2,1)S(1)} %pad_maximum_fusion.1.refs_2_), channel_id=1, source_target_pairs={{0,1},{1,0},{2,3},{3,2},{4,5},{5,4},{6,7},{7,6},{8,9},{9,8},{10,11... | collective-permute-start | bytes 3145736 | tf_op jit(solution)/shard_map/ppermute | solution.py:164
  140.4 14.3 %collective-permute-start.23 = (bf16[8,128,512]{2,1,0:T(8,128)(2,1)S(1)}, bf16[8,128,512]{2,1,0:T(8,128)(2,1)S(1)}, u32[]{:S(2)}, u32[]{:S(2)}) collective-permute-start(bf16[8,128,512]{2,1,0:T(8,128)(2,1)S(1)} %pad_maximum_fusion.2.refs_4_), channel_id=1, source_target_pairs={{0,1},{1,0},{2,3},{3,2},{4,5},{5,4},{6,7},{7,6},{8,9},{9,8},{10,11... | collective-permute-start | bytes 3145736 | tf_op jit(solution)/shard_map/ppermute | solution.py:164
  140.5 14.2 %collective-permute-start.24 = (bf16[256,1536]{1,0:T(8,128)(2,1)}, bf16[256,1536]{1,0:T(8,128)(2,1)S(1)}, u32[]{:S(2)}, u32[]{:S(2)}) collective-permute-start(bf16[256,1536]{1,0:T(8,128)(2,1)} %param.23), channel_id=1, source_target_pairs={{0,8},{2,10},{4,12},{6,14},{9,1},{11,3},{13,5},{15,7},{17,25},{19,... | collective-permute-start | bytes 2359304 | tf_op jit(solution)/shard_map/ppermute | solution.py:164
  155.3 16.5 %collective-permute-start.27 = (bf16[4,96,512]{2,1,0:T(8,128)(2,1)S(1)}, bf16[4,96,512]{2,1,0:T(8,128)(2,1)S(1)}, u32[]{:S(2)}, u32[]{:S(2)}) collective-permute-start(bf16[4,96,512]{2,1,0:T(8,128)(2,1)S(1)} %bitcast.193), channel_id=1, source_target_pairs={{0,8},{1,9},{2,10},{3,11},{4,12},{5,13},{6,14},{7,15},{8,0},{9,1},... | collective-permute-start | bytes 1179656 | tf_op jit(solution)/shard_map/ppermute | solution.py:164
  171.8 18.0 %collective-permute-start.28 = (bf16[2,2,2,96,128]{4,3,2,1,0:T(8,128)(2,1)S(1)}, bf16[2,2,2,96,128]{4,3,2,1,0:T(8,128)(2,1)S(1)}, u32[]{:S(2)}, u32[]{:S(2)}) collective-permute-start(bf16[2,2,2,96,128]{4,3,2,1,0:T(8,128)(2,1)S(1)} %get-tuple-element.600), channel_id=1, source_target_pairs={{0,4},{1,5},{2,6},{3,7},{4,0},{5,1},{6,2},{7,3},{8,12},{9,13},{10,... | collective-permute-start | bytes 589832 | tf_op jit(solution)/shard_map/ppermute | solution.py:164
  196.0 194.2 %all-gather.11.cloned.1.call-start = ((), (), s32[]{:S(2)}) async-start(), calls=%async_computation.3 | async-start | bytes 6684672 | tf_op jit(solution)/shard_map/all_gather | solution.py:216
  196.3 20.0 %collective-permute-start.29 = (bf16[4,96,512]{2,1,0:T(8,128)(2,1)}, bf16[4,96,512]{2,1,0:T(8,128)(2,1)S(1)}, u32[]{:S(2)}, u32[]{:S(2)}) collective-permute-start(bf16[4,96,512]{2,1,0:T(8,128)(2,1)} %bitcast.191), channel_id=1, source_target_pairs={{0,8},{1,9},{2,10},{3,11},{4,12},{5,13},{6,14},{7,15},{8,0},{9,1},... | collective-permute-start | bytes 1179656 | tf_op jit(solution)/shard_map/ppermute | solution.py:164
  262.7 14.1 %collective-permute-start.33 = (bf16[4,128,512]{2,1,0:T(8,128)(2,1)S(1)}, bf16[4,128,512]{2,1,0:T(8,128)(2,1)S(1)}, u32[]{:S(2)}, u32[]{:S(2)}) collective-permute-start(bf16[4,128,512]{2,1,0:T(8,128)(2,1)S(1)} %get-tuple-element.537), channel_id=1, source_target_pairs={{0,4},{1,5},{2,6},{3,7},{4,0},{5,1},{6,2},{7,3},{8,12},{9,13},{10,... | collective-permute-start | bytes 1572872 | tf_op jit(solution)/shard_map/ppermute | solution.py:164
  263.5 13.8 %collective-permute-start.34 = (bf16[4,128,512]{2,1,0:T(8,128)(2,1)S(1)}, bf16[4,128,512]{2,1,0:T(8,128)(2,1)S(1)}, u32[]{:S(2)}, u32[]{:S(2)}) collective-permute-start(bf16[4,128,512]{2,1,0:T(8,128)(2,1)S(1)} %get-tuple-element.535), channel_id=1, source_target_pairs={{0,16},{1,17},{2,18},{3,19},{4,20},{5,21},{6,22},{7,23},{8,24},{9,... | collective-permute-start | bytes 1572872 | tf_op jit(solution)/shard_map/ppermute | solution.py:164
  264.6 13.6 %collective-permute-start.35 = (bf16[4,128,512]{2,1,0:T(8,128)(2,1)S(1)}, bf16[4,128,512]{2,1,0:T(8,128)(2,1)S(1)}, u32[]{:S(2)}, u32[]{:S(2)}) collective-permute-start(bf16[4,128,512]{2,1,0:T(8,128)(2,1)S(1)} %get-tuple-element.533), channel_id=1, source_target_pairs={{0,2},{1,3},{2,0},{3,1},{4,6},{5,7},{6,4},{7,5},{8,10},{9,11},{10,... | collective-permute-start | bytes 1572872 | tf_op jit(solution)/shard_map/ppermute | solution.py:164
  306.1 10.8 %collective-permute-start.43 = (bf16[2,2,2,96,128]{4,3,0,2,1:T(8,128)(2,1)S(1)}, bf16[2,2,2,96,128]{4,3,0,2,1:T(8,128)(2,1)S(1)}, u32[]{:S(2)}, u32[]{:S(2)}) collective-permute-start(bf16[2,2,2,96,128]{4,3,0,2,1:T(8,128)(2,1)S(1)} %get-tuple-element.598), channel_id=1, source_target_pairs={{0,16},{1,17},{2,18},{3,19},{4,20},{5,21},{6,22},{7,23},{8,24},{9,... | collective-permute-start | bytes 589832 | tf_op jit(solution)/shard_map/ppermute | solution.py:164
  307.7 20.3 %collective-permute-start.45 = (bf16[4,96,512]{2,1,0:T(8,128)(2,1)S(1)}, bf16[4,96,512]{2,1,0:T(8,128)(2,1)S(1)}, u32[]{:S(2)}, u32[]{:S(2)}) collective-permute-start(bf16[4,96,512]{2,1,0:T(8,128)(2,1)S(1)} %slice.526), channel_id=1, source_target_pairs={{0,8},{1,9},{2,10},{3,11},{4,12},{5,13},{6,14},{7,15},{8,0},{9,1},... | collective-permute-start | bytes 1179656 | tf_op jit(solution)/shard_map/ppermute | solution.py:164
  316.9 8.1 %collective-permute-start.44 = (bf16[2,2,2,96,128]{4,3,1,0,2:T(8,128)(2,1)S(1)}, bf16[2,2,2,96,128]{4,3,1,0,2:T(8,128)(2,1)S(1)}, u32[]{:S(2)}, u32[]{:S(2)}) collective-permute-start(bf16[2,2,2,96,128]{4,3,1,0,2:T(8,128)(2,1)S(1)} %get-tuple-element.596), channel_id=1, source_target_pairs={{0,2},{1,3},{2,0},{3,1},{4,6},{5,7},{6,4},{7,5},{8,10},{9,11},{10,... | collective-permute-start | bytes 589832 | tf_op jit(solution)/shard_map/ppermute | solution.py:164
  328.0 12.3 %collective-permute-start.47 = (bf16[8,128,768]{2,1,0:T(8,128)(2,1)S(1)}, bf16[8,128,768]{2,1,0:T(8,128)(2,1)S(1)}, u32[]{:S(2)}, u32[]{:S(2)}) collective-permute-start(bf16[8,128,768]{2,1,0:T(8,128)(2,1)S(1)} %get-tuple-element.418), channel_id=1, source_target_pairs={{0,1},{1,0},{2,3},{3,2},{4,5},{5,4},{6,7},{7,6},{8,9},{9,8},{10,11... | collective-permute-start | bytes 4718600 | tf_op jit(solution)/shard_map/ppermute | solution.py:164
  328.0 12.3 %collective-permute-start.48 = (bf16[8,128,768]{2,1,0:T(8,128)(2,1)S(1)}, bf16[8,128,768]{2,1,0:T(8,128)(2,1)S(1)}, u32[]{:S(2)}, u32[]{:S(2)}) collective-permute-start(bf16[8,128,768]{2,1,0:T(8,128)(2,1)S(1)} %copy-done.107), channel_id=1, source_target_pairs={{0,1},{1,0},{2,3},{3,2},{4,5},{5,4},{6,7},{7,6},{8,9},{9,8},{10,11... | collective-permute-start | bytes 4718600 | tf_op jit(solution)/shard_map/ppermute | solution.py:164
  328.5 11.7 %collective-permute-start.46 = (bf16[2,2,2,96,128]{4,3,2,1,0:T(8,128)(2,1)S(1)}, bf16[2,2,2,96,128]{4,3,2,1,0:T(8,128)(2,1)S(1)}, u32[]{:S(2)}, u32[]{:S(2)}) collective-permute-start(bf16[2,2,2,96,128]{4,3,2,1,0:T(8,128)(2,1)S(1)} %get-tuple-element.594), channel_id=1, source_target_pairs={{0,4},{1,5},{2,6},{3,7},{4,0},{5,1},{6,2},{7,3},{8,12},{9,13},{10,... | collective-permute-start | bytes 589832 | tf_op jit(solution)/shard_map/ppermute | solution.py:164
  340.8 21.2 %collective-permute-start.49 = (bf16[4,128,768]{2,1,0:T(8,128)(2,1)S(1)}, bf16[4,128,768]{2,1,0:T(8,128)(2,1)S(1)}, u32[]{:S(2)}, u32[]{:S(2)}) collective-permute-start(bf16[4,128,768]{2,1,0:T(8,128)(2,1)S(1)} %get-tuple-element.525), channel_id=1, source_target_pairs={{0,2},{1,3},{2,0},{3,1},{4,6},{5,7},{6,4},{7,5},{8,10},{9,11},{10,... | collective-permute-start | bytes 2359304 | tf_op jit(solution)/shard_map/ppermute | solution.py:164
  342.5 24.4 %collective-permute-start.50 = (bf16[4,128,768]{2,1,0:T(8,128)(2,1)S(1)}, bf16[4,128,768]{2,1,0:T(8,128)(2,1)S(1)}, u32[]{:S(2)}, u32[]{:S(2)}) collective-permute-start(bf16[4,128,768]{2,1,0:T(8,128)(2,1)S(1)} %get-tuple-element.523), channel_id=1, source_target_pairs={{0,16},{1,17},{2,18},{3,19},{4,20},{5,21},{6,22},{7,23},{8,24},{9,... | collective-permute-start | bytes 2359304 | tf_op jit(solution)/shard_map/ppermute | solution.py:164
  342.6 19.4 %collective-permute-start.51 = (bf16[4,96,512]{2,1,0:T(8,128)(2,1)S(1)}, bf16[4,96,512]{2,1,0:T(8,128)(2,1)S(1)}, u32[]{:S(2)}, u32[]{:S(2)}) collective-permute-start(bf16[4,96,512]{2,1,0:T(8,128)(2,1)S(1)} %slice.537), channel_id=1, source_target_pairs={{0,8},{1,9},{2,10},{3,11},{4,12},{5,13},{6,14},{7,15},{8,0},{9,1},... | collective-permute-start | bytes 1179656 | tf_op jit(solution)/shard_map/ppermute | solution.py:164
  371.0 17.8 %collective-permute-start.54 = (bf16[2,128,768]{2,1,0:T(8,128)(2,1)S(1)}, bf16[2,128,768]{2,1,0:T(8,128)(2,1)S(1)}, u32[]{:S(2)}, u32[]{:S(2)}) collective-permute-start(bf16[2,128,768]{2,1,0:T(8,128)(2,1)S(1)} %get-tuple-element.541), channel_id=1, source_target_pairs={{0,16},{1,17},{2,18},{3,19},{4,20},{5,21},{6,22},{7,23},{8,24},{9,... | collective-permute-start | bytes 1179656 | tf_op jit(solution)/shard_map/ppermute | solution.py:164
  373.6 15.2 %collective-permute-start.56 = (bf16[2,2,96,512]{3,2,1,0:T(8,128)(2,1)S(1)}, bf16[2,2,96,512]{3,2,1,0:T(8,128)(2,1)S(1)}, u32[]{:S(2)}, u32[]{:S(2)}) collective-permute-start(bf16[2,2,96,512]{3,2,1,0:T(8,128)(2,1)S(1)} %bitcast.213), channel_id=1, source_target_pairs={{0,4},{1,5},{2,6},{3,7},{4,0},{5,1},{6,2},{7,3},{8,12},{9,13},{10,... | collective-permute-start | bytes 1179656 | tf_op jit(solution)/shard_map/ppermute | solution.py:164
  374.9 15.3 %collective-permute-start.55 = (bf16[2,128,768]{2,1,0:T(8,128)(2,1)S(1)}, bf16[2,128,768]{2,1,0:T(8,128)(2,1)}, u32[]{:S(2)}, u32[]{:S(2)}) collective-permute-start(bf16[2,128,768]{2,1,0:T(8,128)(2,1)S(1)} %get-tuple-element.539), channel_id=1, source_target_pairs={{0,2},{1,3},{2,0},{3,1},{4,6},{5,7},{6,4},{7,5},{8,10},{9,11},{10,... | collective-permute-start | bytes 1179656 | tf_op jit(solution)/shard_map/ppermute | solution.py:164
  376.5 12.3 %collective-permute-start.53 = (bf16[96,1024]{1,0:T(8,128)(2,1)S(1)}, bf16[96,1024]{1,0:T(8,128)(2,1)S(1)}, u32[]{:S(2)}, u32[]{:S(2)}) collective-permute-start(bf16[96,1024]{1,0:T(8,128)(2,1)S(1)} %get-tuple-element.443), channel_id=1, source_target_pairs={{0,8},{1,9},{2,10},{3,11},{4,12},{5,13},{6,14},{7,15},{8,0},{9,1},... | collective-permute-start | bytes 589832 | tf_op jit(solution)/shard_map/ppermute | solution.py:164
  390.3 10.1 %collective-permute-start.58 = (bf16[2,2,96,512]{3,2,0,1:T(8,128)(2,1)S(1)}, bf16[2,2,96,512]{3,2,0,1:T(8,128)(2,1)S(1)}, u32[]{:S(2)}, u32[]{:S(2)}) collective-permute-start(bf16[2,2,96,512]{3,2,0,1:T(8,128)(2,1)S(1)} %get-tuple-element.562), channel_id=1, source_target_pairs={{0,2},{1,3},{2,0},{3,1},{4,6},{5,7},{6,4},{7,5},{8,10},{9,11},{10,... | collective-permute-start | bytes 1179656 | tf_op jit(solution)/shard_map/ppermute | solution.py:164
  392.0 10.8 %collective-permute-start.57 = (bf16[96,1024]{1,0:T(8,128)(2,1)}, bf16[96,1024]{1,0:T(8,128)(2,1)S(1)}, u32[]{:S(2)}, u32[]{:S(2)}) collective-permute-start(bf16[96,1024]{1,0:T(8,128)(2,1)} %get-tuple-element.452), channel_id=1, source_target_pairs={{0,8},{1,9},{2,10},{3,11},{4,12},{5,13},{6,14},{7,15},{8,0},{9,1},... | collective-permute-start | bytes 589832 | tf_op jit(solution)/shard_map/ppermute | solution.py:164
  410.2 7.8 %collective-permute-start.60 = (bf16[8,128,512]{2,1,0:T(8,128)(2,1)}, bf16[8,128,512]{2,1,0:T(8,128)(2,1)}, u32[]{:S(2)}, u32[]{:S(2)}) collective-permute-start(bf16[8,128,512]{2,1,0:T(8,128)(2,1)} %get-tuple-element.463), channel_id=1, source_target_pairs={{0,1},{1,0},{2,3},{3,2},{4,5},{5,4},{6,7},{7,6},{8,9},{9,8},{10,11... | collective-permute-start | bytes 3145736 | tf_op jit(solution)/shard_map/ppermute | solution.py:164
  412.3 23.0 %collective-permute-start.68 = (bf16[256,1536]{1,0:T(8,128)(2,1)S(1)}, bf16[256,1536]{1,0:T(8,128)(2,1)S(1)}, u32[]{:S(2)}, u32[]{:S(2)}) collective-permute-start(bf16[256,1536]{1,0:T(8,128)(2,1)S(1)} %copy-done.9), channel_id=1, source_target_pairs={{1,9},{3,11},{5,13},{7,15},{8,0},{10,2},{12,4},{14,6},{16,24},{18,... | collective-permute-start | bytes 2359304 | tf_op jit(solution)/shard_map/ppermute | solution.py:164
  419.6 30.8 %collective-permute-start.63 = (bf16[4,128,512]{2,1,0:T(8,128)(2,1)S(1)}, bf16[4,128,512]{2,1,0:T(8,128)(2,1)S(1)}, u32[]{:S(2)}, u32[]{:S(2)}) collective-permute-start(bf16[4,128,512]{2,1,0:T(8,128)(2,1)S(1)} %get-tuple-element.531), channel_id=1, source_target_pairs={{0,4},{1,5},{2,6},{3,7},{4,0},{5,1},{6,2},{7,3},{8,12},{9,13},{10,... | collective-permute-start | bytes 1572872 | tf_op jit(solution)/shard_map/ppermute | solution.py:164
  421.4 29.0 %collective-permute-start.64 = (bf16[4,128,512]{2,1,0:T(8,128)(2,1)S(1)}, bf16[4,128,512]{2,1,0:T(8,128)(2,1)S(1)}, u32[]{:S(2)}, u32[]{:S(2)}) collective-permute-start(bf16[4,128,512]{2,1,0:T(8,128)(2,1)S(1)} %get-tuple-element.529), channel_id=1, source_target_pairs={{0,16},{1,17},{2,18},{3,19},{4,20},{5,21},{6,22},{7,23},{8,24},{9,... | collective-permute-start | bytes 1572872 | tf_op jit(solution)/shard_map/ppermute | solution.py:164
  423.6 26.7 %collective-permute-start.65 = (bf16[4,128,512]{2,1,0:T(8,128)(2,1)S(1)}, bf16[4,128,512]{2,1,0:T(8,128)(2,1)S(1)}, u32[]{:S(2)}, u32[]{:S(2)}) collective-permute-start(bf16[4,128,512]{2,1,0:T(8,128)(2,1)S(1)} %get-tuple-element.527), channel_id=1, source_target_pairs={{0,2},{1,3},{2,0},{3,1},{4,6},{5,7},{6,4},{7,5},{8,10},{9,11},{10,... | collective-permute-start | bytes 1572872 | tf_op jit(solution)/shard_map/ppermute | solution.py:164
  424.8 22.0 %collective-permute-start.66 = (bf16[1,128,768]{2,1,0:T(8,128)(2,1)S(1)}, bf16[1,128,768]{2,1,0:T(8,128)(2,1)S(1)}, u32[]{:S(2)}, u32[]{:S(2)}) collective-permute-start(bf16[1,128,768]{2,1,0:T(8,128)(2,1)S(1)} %get-tuple-element.557), channel_id=1, source_target_pairs={{0,4},{1,5},{2,6},{3,7},{4,0},{5,1},{6,2},{7,3},{8,12},{9,13},{10,... | collective-permute-start | bytes 589832 | tf_op jit(solution)/shard_map/ppermute | solution.py:164
  435.3 15.1 %collective-permute-start.67 = (bf16[1,128,768]{2,1,0:T(8,128)(2,1)S(1)}, bf16[1,128,768]{2,1,0:T(8,128)(2,1)S(1)}, u32[]{:S(2)}, u32[]{:S(2)}) collective-permute-start(bf16[1,128,768]{2,1,0:T(8,128)(2,1)S(1)} %get-tuple-element.555), channel_id=1, source_target_pairs={{0,4},{1,5},{2,6},{3,7},{4,0},{5,1},{6,2},{7,3},{8,12},{9,13},{10,... | collective-permute-start | bytes 589832 | tf_op jit(solution)/shard_map/ppermute | solution.py:164
  446.8 20.5 %collective-permute-start.72 = (bf16[8,96,512]{2,1,0:T(8,128)(2,1)S(1)}, bf16[8,96,512]{2,1,0:T(8,128)(2,1)S(1)}, u32[]{:S(2)}, u32[]{:S(2)}) collective-permute-start(bf16[8,96,512]{2,1,0:T(8,128)(2,1)S(1)} %bitcast.184), channel_id=1, source_target_pairs={{0,16},{1,17},{2,18},{3,19},{4,20},{5,21},{6,22},{7,23},{8,24},{9,... | collective-permute-start | bytes 2359304 | tf_op jit(solution)/shard_map/ppermute | solution.py:164
  450.7 16.6 %collective-permute-start.69 = (bf16[2,128,512]{2,1,0:T(8,128)(2,1)S(1)}, bf16[2,128,512]{2,1,0:T(8,128)(2,1)S(1)}, u32[]{:S(2)}, u32[]{:S(2)}) collective-permute-start(bf16[2,128,512]{2,1,0:T(8,128)(2,1)S(1)} %get-tuple-element.547), channel_id=1, source_target_pairs={{0,2},{1,3},{2,0},{3,1},{4,6},{5,7},{6,4},{7,5},{8,10},{9,11},{10,... | collective-permute-start | bytes 786440 | tf_op jit(solution)/shard_map/ppermute | solution.py:164
  450.9 29.0 %collective-permute-start.76 = (bf16[8,96,192]{2,1,0:T(8,128)(2,1)S(1)}, bf16[8,96,192]{2,1,0:T(8,128)(2,1)}, u32[]{:S(2)}, u32[]{:S(2)}) collective-permute-start(bf16[8,96,192]{2,1,0:T(8,128)(2,1)S(1)} %get-tuple-element.501), channel_id=1, source_target_pairs={{0,8},{1,9},{2,10},{3,11},{4,12},{5,13},{6,14},{7,15},{8,0},{9,1},... | collective-permute-start | bytes 884744 | tf_op jit(solution)/shard_map/ppermute | solution.py:164
  451.5 15.8 %collective-permute-start.70 = (bf16[2,128,512]{2,1,0:T(8,128)(2,1)S(1)}, bf16[2,128,512]{2,1,0:T(8,128)(2,1)S(1)}, u32[]{:S(2)}, u32[]{:S(2)}) collective-permute-start(bf16[2,128,512]{2,1,0:T(8,128)(2,1)S(1)} %get-tuple-element.545), channel_id=1, source_target_pairs={{0,4},{1,5},{2,6},{3,7},{4,0},{5,1},{6,2},{7,3},{8,12},{9,13},{10,... | collective-permute-start | bytes 786440 | tf_op jit(solution)/shard_map/ppermute | solution.py:164
  454.2 16.5 %collective-permute-start.71 = (bf16[2,128,512]{2,1,0:T(8,128)(2,1)S(1)}, bf16[2,128,512]{2,1,0:T(8,128)(2,1)S(1)}, u32[]{:S(2)}, u32[]{:S(2)}) collective-permute-start(bf16[2,128,512]{2,1,0:T(8,128)(2,1)S(1)} %get-tuple-element.543), channel_id=1, source_target_pairs={{0,16},{1,17},{2,18},{3,19},{4,20},{5,21},{6,22},{7,23},{8,24},{9,... | collective-permute-start | bytes 786440 | tf_op jit(solution)/shard_map/ppermute | solution.py:164
  470.8 9.1 %collective-permute-start.73 = (bf16[1,128,512]{2,1,0:T(8,128)(2,1)S(1)}, bf16[1,128,512]{2,1,0:T(8,128)(2,1)S(1)}, u32[]{:S(2)}, u32[]{:S(2)}) collective-permute-start(bf16[1,128,512]{2,1,0:T(8,128)(2,1)S(1)} %get-tuple-element.577), channel_id=1, source_target_pairs={{0,16},{1,17},{2,18},{3,19},{4,20},{5,21},{6,22},{7,23},{8,24},{9,... | collective-permute-start | bytes 393224 | tf_op jit(solution)/shard_map/ppermute | solution.py:164
  471.3 8.5 %collective-permute-start.74 = (bf16[1,128,512]{2,1,0:T(8,128)(2,1)S(1)}, bf16[1,128,512]{2,1,0:T(8,128)(2,1)S(1)}, u32[]{:S(2)}, u32[]{:S(2)}) collective-permute-start(bf16[1,128,512]{2,1,0:T(8,128)(2,1)S(1)} %get-tuple-element.575), channel_id=1, source_target_pairs={{0,2},{1,3},{2,0},{3,1},{4,6},{5,7},{6,4},{7,5},{8,10},{9,11},{10,... | collective-permute-start | bytes 393224 | tf_op jit(solution)/shard_map/ppermute | solution.py:164
  471.6 8.3 %collective-permute-start.75 = (bf16[1,128,512]{2,1,0:T(8,128)(2,1)S(1)}, bf16[1,128,512]{2,1,0:T(8,128)(2,1)S(1)}, u32[]{:S(2)}, u32[]{:S(2)}) collective-permute-start(bf16[1,128,512]{2,1,0:T(8,128)(2,1)S(1)} %get-tuple-element.573), channel_id=1, source_target_pairs={{0,4},{1,5},{2,6},{3,7},{4,0},{5,1},{6,2},{7,3},{8,12},{9,13},{10,... | collective-permute-start | bytes 393224 | tf_op jit(solution)/shard_map/ppermute | solution.py:164
  471.8 26.7 %collective-permute-start.83 = (bf16[256,1536]{1,0:T(8,128)(2,1)S(1)}, bf16[256,1536]{1,0:T(8,128)(2,1)}, u32[]{:S(2)}, u32[]{:S(2)}) collective-permute-start(bf16[256,1536]{1,0:T(8,128)(2,1)S(1)} %add_convert_fusion), channel_id=1, source_target_pairs={{0,16},{2,18},{4,20},{6,22},{9,25},{11,27},{13,29},{15,31},{17,1},... | collective-permute-start | bytes 2359304 | tf_op jit(solution)/shard_map/ppermute | solution.py:164
  483.8 13.1 %collective-permute-start.80 = (bf16[96,1536]{1,0:T(8,128)(2,1)S(1)}, bf16[96,1536]{1,0:T(8,128)(2,1)S(1)}, u32[]{:S(2)}, u32[]{:S(2)}) collective-permute-start(bf16[96,1536]{1,0:T(8,128)(2,1)S(1)} %shard_map.226), channel_id=1, source_target_pairs={{8,0},{9,1},{10,2},{11,3},{12,4},{13,5},{14,6},{15,7},{16,24},{17,... | collective-permute-start | bytes 884744 | tf_op jit(solution)/shard_map/ppermute | solution.py:164
  497.0 20.4 %collective-permute-start.82 = (bf16[96,1536]{1,0:T(8,128)(2,1)S(1)}, bf16[96,1536]{1,0:T(8,128)(2,1)S(1)}, u32[]{:S(2)}, u32[]{:S(2)}) collective-permute-start(bf16[96,1536]{1,0:T(8,128)(2,1)S(1)} %add_convert_fusion.25), channel_id=1, source_target_pairs={{0,16},{1,17},{2,18},{3,19},{4,20},{5,21},{6,22},{7,23},{24,8},{25... | collective-permute-start | bytes 884744 | tf_op jit(solution)/shard_map/ppermute | solution.py:164
  498.5 14.9 %collective-permute-start.81 = (bf16[8,96,192]{2,1,0:T(8,128)(2,1)S(1)}, bf16[8,96,192]{2,1,0:T(8,128)(2,1)S(1)}, u32[]{:S(2)}, u32[]{:S(2)}) collective-permute-start(bf16[8,96,192]{2,1,0:T(8,128)(2,1)S(1)} %bitcast.189), channel_id=1, source_target_pairs={{0,16},{1,17},{2,18},{3,19},{4,20},{5,21},{6,22},{7,23},{8,24},{9,... | collective-permute-start | bytes 884744 | tf_op jit(solution)/shard_map/ppermute | solution.py:164
  (135 other events, 1224.8 us)
Sparse Core Ops, SparseCore 0:
  10.6 58.9 all-gather.4
  71.7 53.3 all-gather.6
  196.2 47.2 all-gather.8
  303.5 58.2 all-gather.10

commit v3 on v2

--- a/solution.py
+++ b/solution.py
@@ -488,12 +488,8 @@
 
 
 def project(at, normed, w_heads, tables):
-    def body(at_ref, rows_ref, w_ref, cos_ref, sin_ref, cos2_ref, sin2_ref, q_ref, own_ref, wt_scr):
-        @pl.when(pl.program_id(0) == 0)
-        def _():
-            wt_scr[...] = w_ref[...].astype(wide).T.astype(low)
-
-        made = times_back(wt_scr[...], rows_ref[...])
+    def body(at_ref, rows_ref, w_ref, cos_ref, sin_ref, cos2_ref, sin2_ref, q_ref, own_ref):
+        made = jnp.dot(rows_ref[...], w_ref[...], preferred_element_type=wide).T
         q_ref[0] = turn(made[:96], cos_ref[...], sin_ref[...]).astype(low)
         own_ref[0] = turn(made[96:], cos2_ref[...], sin2_ref[...]).astype(low)
 
@@ -505,7 +501,7 @@
         [cube_spec(), whole_spec((1536, 192))] + table_specs(),
         [out_spec, out_spec],
         [shape, shape],
-        [pltpu.VMEM((192, 1536), low)],
+        [],
         2 * 2048 * 1536 * 192,
         8 * 1024 * 1024,
         (at, normed, w_heads, *tables),
@@ -799,15 +795,9 @@
 
 
 def project_back(at, w_heads, tables, grad_queries, grad_own):
-    def body(at_ref, w_ref, cos_ref, sin_ref, dq_ref, ds_ref, *rest):
-        outs, wt_scr = rest[:6], rest[6]
-
-        @pl.when(pl.program_id(0) == 0)
-        def _():
-            wt_scr[...] = w_ref[...].astype(wide).T.astype(low)
-
+    def body(at_ref, w_ref, cos_ref, sin_ref, dq_ref, ds_ref, *outs):
         both = align(at_ref[8], head_grads(dq_ref, ds_ref, cos_ref, sin_ref))
-        store_rows(outs, jnp.dot(both.T.astype(low), wt_scr[...], preferred_element_type=wide))
+        store_rows(outs, times_back(both.T.astype(low), w_ref[...]))
 
     return kernel_call(
         body,
@@ -815,7 +805,7 @@
         [whole_spec((1536, 192))] + head_grad_specs(),
         row_specs(THIRDS, lambda g, t: g),
         row_shapes(THIRDS),
-        [pltpu.VMEM((192, 1536), low)],
+        [],
         2 * 2048 * 1536 * 192,
         8 * 1024 * 1024,
         (at, w_heads, *tables[2:], grad_queries, grad_own),
@@ -824,13 +814,13 @@
 
 def hidden_back(at, grads, w_rows):
     def body(at_ref, *refs):
-        rows, (w_ref, out_ref) = refs[:6], refs[6:]
+        rows, (w_ref, out_ref) = refs[:4], refs[4:]
         out_ref[...] = align_rows(at_ref[8], times_back(load_rows(rows), w_ref[...]))
 
     return kernel_call(
         body,
         (8,),
-        row_specs(THIRDS, lambda g, t: g) + [whole_spec((256, 1536))],
+        row_specs(HALVES, lambda g, t: g) + [whole_spec((256, 1536))],
         pl.BlockSpec((256, 256), lambda g, t: (g, 0)),
         jax.ShapeDtypeStruct((2048, 256), wide),
         [],
@@ -842,12 +832,7 @@
 
 def feed_back(at, normed, w_both, grad_hidden):
     def body(at_ref, rows_ref, w_ref, dh_ref, *rest):
-        outs, (hidden_ref, both_ref, wt_scr) = rest[:6], rest[6:]
-
-        @pl.when(pl.program_id(0) == 0)
-        def _():
-            wt_scr[...] = w_ref[...].astype(wide).T.astype(low)
-
+        outs, (hidden_ref, both_ref) = rest[:6], rest[6:]
         both = jnp.dot(rows_ref[...], w_ref[...], preferred_element_type=wide)
         gate, up = both[:, :256], both[:, 256:]
         bend = jax.nn.sigmoid(gate)
@@ -857,8 +842,7 @@
         grad_gate = grad_hidden * up * (bend + smooth * (1.0 - bend))
         grad_both = jnp.concatenate([grad_gate, grad_hidden * smooth], axis=1).astype(low)
         both_ref[...] = grad_both
-        grad_both = align_rows(at_ref[8], grad_both.astype(wide)).astype(low)
-        store_rows(outs, jnp.dot(grad_both, wt_scr[...], preferred_element_type=wide))
+        store_rows(outs, align_rows(at_ref[8], times_back(grad_both, w_ref[...])))
 
     return kernel_call(
         body,
@@ -874,7 +858,7 @@
             jax.ShapeDtypeStruct((2048, 256), low),
             jax.ShapeDtypeStruct((2048, 512), low),
         ],
-        [pltpu.VMEM((512, 1536), low)],
+        [],
         4 * 2048 * 1536 * 512,
         18 * 1024 * 1024,
         (at, normed, w_both, grad_hidden),
@@ -902,7 +886,7 @@
 
 def down_weights(at, hidden, grads):
     def body(at_ref, *refs):
-        rows, (hidden_ref, gw_ref, gw_scr) = refs[:6], refs[6:]
+        rows, (hidden_ref, gw_ref, gw_scr) = refs[:4], refs[4:]
         g = pl.program_id(0)
 
         @pl.when(g == 0)
@@ -919,7 +903,7 @@
     return kernel_call(
         body,
         (8,),
-        row_specs(THIRDS, lambda g, t: g) + [pl.BlockSpec((256, 256), lambda g, t: (g, 0))],
+        row_specs(HALVES, lambda g, t: g) + [pl.BlockSpec((256, 256), lambda g, t: (g, 0))],
         whole_spec((256, 1536)),
         jax.ShapeDtypeStruct((256, 1536), low),
         [pltpu.VMEM((256, 1536), wide)],
@@ -1080,6 +1064,7 @@
     heads_far = swap(heads, BIT_ZH)
     both_blocks = trade_block(both_blocks.reshape(2, 2, 2, 96, 512), 0, BIT_C)
     both_blocks = trade_block(both_blocks, 1, BIT_Y)
+    both_blocks = trade_block(both_blocks, 2, BIT_ZL)
     w_out_head = jnp.where(out_owner, w_out, out_near)
     heads, heads_far, both_blocks, w_down_held, tables = sync(
         heads, heads_far, both_blocks, w_down, tables
@@ -1096,46 +1081,44 @@
     )
 
     out_full = cube_gather(w_out_head)
-    grads = gather_next(gather_start(rows_dy, THIRDS), THIRDS, 0)
+    grads = gather_next(gather_start(rows_dy, HALVES), HALVES, 0)
     queries, own_part = project(spots, normed, w_heads, tables)
     queries, own_part, grads, both_blocks = sync(queries, own_part, grads, both_blocks)
     far_part = swap(own_part, BIT_ZH)
-    grads = gather_next(grads, THIRDS, 1)
+    grads = gather_next(grads, HALVES, 1)
     far_part, grads, both_blocks = sync(far_part, grads, both_blocks)
     other_parts = swap(jnp.stack([own_part, far_part]), BIT_C)
-    both_blocks = trade_block(both_blocks, 2, BIT_ZL)
     other_parts, far_part, grads = sync(other_parts, far_part, grads)
     held = (own_part, far_part, other_parts, other_parts)
-    grads = gather_next(grads, THIRDS, 2)
-    down_near = swap(w_down_held, BIT_ZH, owns_down)
+    grads = gather_next(grads, HALVES, 2)
+    near_rows = [both_blocks[0].reshape(4, 96, 512), both_blocks[1].reshape(4, 96, 512)]
+    far_first = swap(near_rows[0], BIT_ZH)
     keep, send, attention, totals = attend_forward(
         spots, queries, held, query_blk, key_blk, score_scale
     )
-    keep, send, attention, totals, both_blocks, grads, out_full = sync(
-        keep, send, attention, totals, both_blocks, grads, out_full
-    )
-
-    near_rows = [both_blocks[0].reshape(4, 96, 512), both_blocks[1].reshape(4, 96, 512)]
+    keep, send, attention, totals, near_rows, out_full, w_down_held = sync(
+        keep, send, attention, totals, near_rows, out_full, w_down_held
+    )
+
     traded = jnp.stack([keep, swap(send, BIT_C)]).reshape(2, 2, 2, 2, 96, 128)
+    traded, far_first, w_down_held = sync(traded, far_first, w_down_held)
+    traded = trade_block(traded, 3, BIT_ZL)
+    traded, grads, w_down_held = sync(traded, grads, w_down_held)
+    down_near = swap(w_down_held, BIT_ZH, owns_down)
     grads = gather_last(grads)
-    traded, grads, down_near, near_rows = sync(traded, grads, down_near, near_rows)
-    far_first = swap(near_rows[0], BIT_ZH)
-    traded = trade_block(traded, 1, BIT_X)
-    traded, near_rows = sync(traded, near_rows)
-    traded = trade_block(traded, 2, BIT_Y)
-    traded, far_first, near_rows = sync(traded, far_first, near_rows)
+    traded = trade_block(traded, 2, BIT_X)
+    traded, grads = sync(traded, grads)
+    traded = trade_block(traded, 3, BIT_Y).reshape(16, 96, 128)
+    traded, residual, down_near, near_rows = sync(traded, residual, down_near, near_rows)
     far_second = swap(near_rows[1], BIT_ZH)
-    traded = trade_block(traded, 3, BIT_ZL).reshape(16, 96, 128)
-    traded, residual = sync(traded, residual)
-    lyxc = ((sixteen & 8) >> 1) | ((sixteen & 4) >> 1) | (sixteen & 1)
-    head_from = (x ^ ((sixteen & 2) >> 1)) * 8 + ((seq_at ^ lyxc) & 7)
+    yxlc = ((sixteen & 8) >> 2) | ((sixteen & 2) << 1) | (sixteen & 1)
+    head_from = (x ^ ((sixteen & 4) >> 2)) * 8 + ((seq_at ^ yxlc) & 7)
     middle, scale_second, rows_second = out_project(head_from, traded, out_full, residual)
 
     rows_second, middle, scale_second, grads = sync(rows_second, middle, scale_second, grads)
     normed_mlp = cube_gather(rows_second)
     w_rows = jnp.where(down_owner, w_down_held, down_near)
     grad_hidden = hidden_back(spots, grads, w_rows)
-    grad_hidden, far_second = sync(grad_hidden, far_second)
     w_both = assemble_rows(natural, *near_rows, far_first, far_second)
     normed_mlp, grad_hidden, w_both = sync(normed_mlp, grad_hidden, w_both)
     made = feed_back(spots, normed_mlp, w_both, grad_hidden)
@@ -1158,22 +1141,27 @@
         grad_middle, grad_low, keep, send, hidden, send_both
     )
     middle_rows = cube_gather(grad_low)
-    arrived_first = swap(send_both[:4], BIT_ZH)
+    arrived_second = swap(send_both[4:], BIT_ZH)
     traded = jnp.stack([keep, swap(send, BIT_C)]).reshape(2, 2, 2, 2, 96, 128)
     traded, hidden = sync(traded, hidden)
+    grad_down = down_weights(spots, hidden, grads)
+    traded = trade_block(traded, 1, BIT_X)
+    traded, grad_down, hidden, arrived_second, send_both = sync(
+        traded, grad_down, hidden, arrived_second, send_both
+    )
+    arrived_first = swap(send_both[:4], BIT_ZH)
     out_terms = feed_out(spots, hidden, w_rows)
-    traded = trade_block(traded, 1, BIT_X)
-    traded, out_terms, hidden = sync(traded, out_terms, hidden)
-    grad_down = down_weights(spots, hidden, grads)
     traded = trade_block(traded, 2, BIT_Y)
-    traded, grad_down, arrived_first, send_both, out_terms = sync(
-        traded, grad_down, arrived_first, send_both, out_terms
-    )
-    arrived_second = swap(send_both[4:], BIT_ZH)
+    traded, grad_down, out_terms = sync(traded, grad_down, out_terms)
     traded = trade_block(traded, 3, BIT_ZL).reshape(8, 2, 96, 128)
     out_sums = scatter_start(paired(out_terms))
-    traded, out_sums = sync(traded, out_sums)
+    both_send = sum_low(keep_both[4:], arrived_second)
+    traded, out_sums, arrived_first, both_send, grad_down = sync(
+        traded, out_sums, arrived_first, both_send, grad_down
+    )
     out_sums = scatter_next(out_sums, HALVES, 2)
+    down_arrived = swap(grad_down, BIT_ZH, lacks_down)
+    both_sent = swap(both_send, BIT_ZL)
     made = attend_backward(
         spots,
         queries,
@@ -1186,67 +1174,66 @@
         tables,
         score_scale,
     )
-    made, out_sums, arrived_second = sync(made, out_sums, arrived_second)
+    made, out_sums, down_arrived, both_sent = sync(made, out_sums, down_arrived, both_sent)
     grad_queries, mine, sent = made
-    both_sum = sum_low(keep_both, jnp.concatenate([arrived_first, arrived_second], axis=0))
+    both_sum = jnp.stack([sum_low(keep_both[:4], arrived_first), both_sent])
     arrived = swap(sent, BIT_C)
     arrived, both_sum, grad_down = sync(arrived, both_sum, grad_down)
     far_terms = sum_low(mine[1], arrived[1])
-    far_terms, out_sums, both_sum = sync([far_terms[0], far_terms[1]], out_sums, both_sum)
+    far_terms, out_sums, both_sum, attention, middle_rows = sync(
+        [far_terms[0], far_terms[1]], out_sums, both_sum, attention, middle_rows
+    )
     far_first = swap(far_terms[0], BIT_ZH)
     out_sums = scatter_next(out_sums, HALVES, 1)
-    both_sum = trade_block(both_sum.reshape(2, 2, 2, 96, 512), 0, BIT_ZL)
-    far_first, far_terms, out_sums, both_sum, middle_rows = sync(
-        far_first, far_terms, out_sums, both_sum, middle_rows
+    grad_out_head = out_weights(spots, attention, middle_rows)
+    far_first, far_terms, out_sums, both_sum, grad_out_head, grad_down = sync(
+        far_first, far_terms, out_sums, both_sum, grad_out_head, grad_down
     )
     far_second = swap(far_terms[1], BIT_ZH)
-    both_sum = trade_block(both_sum, 1, BIT_Y)
-    grad_out_head = out_weights(spots, attention, middle_rows)
-    far_second, both_sum, grad_out_head, out_sums = sync(
-        far_second, both_sum, grad_out_head, out_sums
-    )
+    both_sum = trade_block(both_sum.reshape(2, 2, 2, 96, 512), 1, BIT_Y)
+    down_sum = sum_low(grad_down, down_arrived)
+    down_far = swap(down_sum, BIT_X, owns_down)
+    far_second, both_sum, out_sums = sync(far_second, both_sum, out_sums)
+    out_sums = scatter_next(out_sums, HALVES, 0)
+    both_near = trade_block(both_sum, 2, BIT_C).reshape(8, 96, 512)
     grad_own = (
         mine[0].astype(wide)
         + arrived[0].astype(wide)
         + jnp.stack([far_first, far_second]).astype(wide)
     )
-    out_sums = scatter_next(out_sums, HALVES, 0)
-    down_arrived = swap(grad_down, BIT_ZH, lacks_down)
-    both_near = trade_block(both_sum, 2, BIT_C).reshape(8, 96, 512)
-    made = project_back(spots, w_heads, tables, grad_queries, grad_own)
-    sums = scatter_start(paired(made))
-    sums, grad_own, both_near = sync(sums, grad_own, both_near)
-    both_far = swap(both_near, BIT_X)
     keep_heads, send_heads = head_weights(
         spots_rows, normed, tables, grad_queries, grad_own
     )
+    keep_heads, send_heads, grad_own, both_near, down_far = sync(
+        keep_heads, send_heads, grad_own, both_near, down_far
+    )
+    both_far = swap(both_near, BIT_X)
+    heads_first = swap(send_heads, BIT_ZH)
+    made = project_back(spots, w_heads, tables, grad_queries, grad_own)
+    made, heads_first, both_far, out_sums = sync(made, heads_first, both_far, out_sums)
+    sums = scatter_start(paired(made))
+    heads_sum = sum_low(keep_heads, heads_first)
+    sums, heads_sum = sync(sums, heads_sum)
+    heads_sum = trade_block(heads_sum.reshape(2, 2, 2, 96, 192), 0, BIT_ZL)
     sums = scatter_next(sums, THIRDS, 2)
-    sums, keep_heads, send_heads, out_sums, down_arrived = sync(
-        sums, keep_heads, send_heads, out_sums, down_arrived
-    )
-    heads_first = swap(send_heads, BIT_ZH)
+    sums, heads_sum, grad_out_head = sync(sums, heads_sum, grad_out_head)
+    out_arrived = swap(grad_out_head, BIT_ZH, lacks_out)
     output = jnp.concatenate([part[0] for part in scatter_last(out_sums)], axis=1)
     output = (middle + output).astype(low)
-    down_sum = sum_low(grad_down, down_arrived)
+    heads_sum = trade_block(heads_sum, 1, BIT_Y)
     sums = scatter_next(sums, THIRDS, 1)
-    sums, output, down_sum, both_far = sync(sums, output, down_sum, both_far)
-    down_far = swap(down_sum, BIT_X, owns_down)
+    sums, output, heads_sum = sync(sums, output, heads_sum)
+    heads_near = trade_block(heads_sum, 2, BIT_C).reshape(8, 96, 192)
+    heads_far = swap(heads_near, BIT_X)
     sums = scatter_next(sums, THIRDS, 0)
-    sums, heads_first, grad_out_head = sync(sums, heads_first, grad_out_head)
-    out_arrived = swap(grad_out_head, BIT_ZH, lacks_out)
-    heads_sum = sum_low(keep_heads, heads_first)
-    heads_sum = trade_block(heads_sum.reshape(2, 2, 2, 96, 192), 0, BIT_ZL)
+    sums, heads_far, out_arrived = sync(sums, heads_far, out_arrived)
+    out_sum = sum_low(grad_out_head, out_arrived)
+    out_far = swap(out_sum, BIT_X, owns_out)
     scaled_first = jnp.concatenate([part[0] for part in scatter_last(sums)], axis=1)
     grad_inputs = grad_middle + scale_first * (
         scaled_first
         - normed_first * jnp.mean(scaled_first * normed_first, axis=-1, keepdims=True)
     )
-    heads_sum = trade_block(heads_sum, 1, BIT_Y)
-    heads_near = trade_block(heads_sum, 2, BIT_C).reshape(8, 96, 192)
-    heads_near, out_arrived = sync(heads_near, out_arrived)
-    heads_far = swap(heads_near, BIT_X)
-    out_sum = sum_low(grad_out_head, out_arrived)
-    out_far = swap(out_sum, BIT_X, owns_out)
 
     back = seq_at ^ cyl
     home = jnp.concatenate([x * 8 + (back & 7), (1 - x) * 8 + (back & 7)])

time: 527 us -> 500 us (0.949)
  waiting for transfers between devices: 238 us -> 201 us
  other arithmetic: 31.5 us -> 43.7 us
    ppermute x84 -> x80, waiting for transfers between devices: 207 us -> 166 us  [swap(): return lax.ppermute(value, AXES, pairs)]
    unnamed x222 -> x232, local copies, waits for them, and re-layouts: 11.7 us -> 14.2 us
    ppermute x84 -> x80, starting transfers between devices: 103 us -> 102 us  [swap(): return lax.ppermute(value, AXES, pairs)]
  transfers between devices with their start and end apart: 88 -> 84, of which waited for: 48 -> 47; matrix products, arithmetic and copies ran while one was open for 6% -> 7% of each run, Pallas kernels for 17% -> 19%
where the time goes in v3:
time: 500 us; the launch traced here: 498 us
  waiting for transfers between devices  201 us (40%)
  Pallas kernels  118 us (24%)
  starting transfers between devices  102 us (20%)
  other arithmetic  43.7 us (9%)
  local copies, waits for them, and re-layouts  17.8 us (4%)
  between operations  15.7 us (3%)
    ppermute x80, waiting for transfers between devices, swap(): return lax.ppermute(value, AXES, pairs)  166 us
    pallas_call x19, Pallas kernels, kernel_call(): pl.pallas_call(body, out_shape=out_shape, grid_spec=pltpu.PrefetchScalarG...  118 us
    ppermute x80, starting transfers between devices, swap(): return lax.ppermute(value, AXES, pairs)  102 us
    all_gather x4, waiting for transfers between devices, cube_gather(): lax.all_gather(rows, AXES, axis=0, tiled=True, axis_index_groups=cube_gro...  34.9 us
    unnamed x232, local copies, waits for them, and re-layouts  14.2 us
    convert_element_type x24, other arithmetic, scatter_next(): sent = (kept[half:].astype(wide) + arrived[half:].astype(wide)).astype(low)  12.8 us
  transfers between devices with their start and end apart: 84, of which 47 were waited for; matrix products, arithmetic and copies ran while one was open for 7% of the time, Pallas kernels for 19%

profile of v3, /device:TPU:0, one launch (start us, length us, event | category | flops | bytes accessed | tf_op | source)
XLA Modules:
  0.0 498.0 jit_solution(8330645952971410561)
XLA Ops:
  9.1 1.9 multiply_convert_fusion
  14.0 3.0 collective-permute-start.1
  16.9 5.2 %collective-permute-start.3 = (bf16[96,1536]{1,0:T(8,128)(2,1)S(1)}, bf16[96,1536]{1,0:T(8,128)(2,1)}, u32[]{:S(2)}, u32[]{:S(2)}) collective-permute-start(bf16[96,1536]{1,0:T(8,128)(2,1)S(1)} %copy-done.102), channel_id=1, source_target_pairs={{0,8},{1,9},{2,10},{3,11},{4,12},{5,13},{6,14},{7,15},{24,16},{25,... | collective-permute-start | bytes 884744 | tf_op jit(solution)/shard_map/ppermute | solution.py:164
  22.3 1.8 collective-permute-start.2
  25.1 18.1 %collective-permute-done.2 = bf16[2,2,96,192]{3,2,1,0:T(8,128)(2,1)S(1)} collective-permute-done((bf16[2,2,96,192]{3,2,1,0:T(8,128)(2,1)S(1)}, bf16[2,2,96,192]{3,2,1,0:T(8,128)(2,1)S(1)}, u32[]{:S(2)}, u32[]{:S(2)}) %collective-permute-start.2) | collective-permute-done | bytes 147488 | tf_op jit(solution)/shard_map/ppermute | solution.py:164
  45.5 2.5 collective-permute-done.8
  48.3 8.1 %collective-permute-done.6 = bf16[2,2,96,512]{3,2,0,1:T(8,128)(2,1)S(1)} collective-permute-done((bf16[2,2,96,512]{3,2,0,1:T(8,128)(2,1)S(1)}, bf16[2,2,96,512]{3,2,0,1:T(8,128)(2,1)S(1)}, u32[]{:S(2)}, u32[]{:S(2)}) %collective-permute-start.6) | collective-permute-done | bytes 393248 | tf_op jit(solution)/shard_map/ppermute | solution.py:164
  56.5 2.6 collective-permute-start.7
  59.8 17.3 %collective-permute-done.7 = bf16[2,2,96,512]{3,2,1,0:T(8,128)(2,1)S(1)} collective-permute-done((bf16[2,2,96,512]{3,2,1,0:T(8,128)(2,1)S(1)}, bf16[2,2,96,512]{3,2,1,0:T(8,128)(2,1)S(1)}, u32[]{:S(2)}, u32[]{:S(2)}) %collective-permute-start.7) | collective-permute-done | bytes 393248 | tf_op jit(solution)/shard_map/ppermute | solution.py:164
  78.8 2.5 collective-permute-start.10
  81.4 7.8 %shard_map.215 = (bf16[2,96,1024]{2,1,0:T(8,128)(2,1)S(1)}, bf16[2,96,1024]{2,1,0:T(8,128)(2,1)S(1)}) custom-call(s32[9]{0:T(128)S(1)} %pad_add_fusion.at_ref, bf16[2048,1536]{1,0:T(8,128)(2,1)} %all-gather.5.cloned.1.call-done.rows_ref, bf16[1536,192]{1,0:T(8,128)(2,1)S(1)} %shard_map.214.w_ref, f32[48,1024]{1,0:T(8,128)S(1)} %get-tuple-element.283.cos_ref.rest_2_, ...), custom_call_target="tpu_custom_call" | custom-call | flops 1207959552 | bytes 8388608 | tf_op jit(solution)/shard_map/pallas_call | solution.py:296
  89.4 2.2 collective-permute-done.9
  91.7 2.1 collective-permute-start.13
  93.8 2.9 collective-permute-start.11
  96.7 14.2 %collective-permute-done.12 = bf16[2,128,768]{2,1,0:T(8,128)(2,1)S(1)} collective-permute-done((bf16[2,128,768]{2,1,0:T(8,128)(2,1)S(1)}, bf16[2,128,768]{2,1,0:T(8,128)(2,1)S(1)}, u32[]{:S(2)}, u32[]{:S(2)}) %collective-permute-start.12) | collective-permute-done | bytes 393248 | tf_op jit(solution)/shard_map/ppermute | solution.py:164
  113.0 2.3 collective-permute-done.14.c_ref.d_ref
  115.3 2.1 collective-permute-start.18
  118.2 3.1 collective-permute-start.16
  122.3 11.3 %shard_map.216 = (bf16[8,96,128]{2,1,0:T(8,128)(2,1)S(1)}, bf16[8,96,128]{2,1,0:T(8,128)(2,1)S(1)}, f32[2,96,1024]{2,1,0:T(8,128)S(1)}, f32[2,1,1024]{2,1,0:T(1,128)S(1)}) custom-call(s32[9]{0:T(128)S(1)} %pad_add_fusion.at_ref, bf16[2,96,1024]{2,1,0:T(8,128)(2,1)S(1)} %get-tuple-element.289.q_ref, bf16[2,96,1024]{2,1,0:T(8,128)(2,1)S(1)} %get-tuple-element.290.a_ref, ...), custom_call_target="tpu_custom_call" | custom-call | flops 1610612736 | bytes 12582912 | tf_op jit(solution)/shard_map/pallas_call | solution.py:296
  136.0 2.8 collective-permute-done.16.refs_2_
  142.8 2.2 collective-permute-done.17
  146.8 5.0 %collective-permute-start.24 = (bf16[256,1536]{1,0:T(8,128)(2,1)S(1)}, bf16[256,1536]{1,0:T(8,128)(2,1)S(1)}, u32[]{:S(2)}, u32[]{:S(2)}) collective-permute-start(bf16[256,1536]{1,0:T(8,128)(2,1)S(1)} %copy-done.88), channel_id=1, source_target_pairs={{0,8},{2,10},{4,12},{6,14},{9,1},{11,3},{13,5},{15,7},{17,25},{19,... | collective-permute-start | bytes 2359304 | tf_op jit(solution)/shard_map/ppermute | solution.py:164
  155.1 4.9 collective-permute-done.23
  161.3 3.9 shard_map.217
  167.7 3.5 collective-permute-start.25
  172.5 7.6 %shard_map.218.dh_ref = f32[2048,256]{1,0:T(8,128)} custom-call(s32[9]{0:T(128)S(1)} %pad_add_fusion.at_ref, bf16[8,128,768]{2,1,0:T(8,128)(2,1)S(1)} %pad_maximum_fusion.refs_0_, bf16[8,128,768]{2,1,0:T(8,128)(2,1)S(1)} %copy-done.2, bf16[8,128,768]{2,1,0:T(8,128)(2,1)S(1)} %pad_maximum_fusion.1.refs_2_, bf16[8,128,768]{2,1,0:T(8,128)(2,1)} %copy-done.80, ...), custom_call_target="tpu_custom_call" | custom-call | flops 1610612736 | bytes 8388608 | tf_op jit(solution)/shard_map/pallas_call | solution.py:296
  182.7 34.9 %all-gather.9.cloned.1.call-done.rows_ref = bf16[2048,1536]{1,0:T(8,128)(2,1)} async-done(((bf16[128,1536]{1,0:T(8,128)(2,1)}), bf16[2048,1536]{1,0:T(8,128)(2,1)}) %all-gather.9.cloned.1.call-update) | async-done | bytes 6291472 | tf_op jit(solution)/shard_map/all_gather | solution.py:216
  217.6 12.4 %shard_map.220 = (bf16[8,128,512]{2,1,0:T(8,128)(2,1)S(1)}, bf16[8,128,512]{2,1,0:T(8,128)(2,1)S(1)}, bf16[8,128,512]{2,1,0:T(8,128)(2,1)S(1)}, bf16[8,128,512]{...) custom-call(s32[9]{0:T(128)S(1)} %pad_add_fusion.at_ref, ...), custom_call_target="tpu_custom_call" | custom-call | flops 6442450944 | bytes 18874368 | tf_op jit(solution)/shard_map/pallas_call | solution.py:296
  230.8 1.9 collective-permute-done.26
  232.7 3.0 collective-permute-done.27
  239.9 9.5 %shard_map.221 = (bf16[8,96,512]{2,1,0:T(8,128)(2,1)S(1)}, bf16[8,96,512]{2,1,0:T(8,128)(2,1)S(1)}) custom-call(s32[25]{0:T(128)S(1)} %pad_add_fusion.2.at_ref, bf16[2048,1536]{1,0:T(8,128)(2,1)} %all-gather.9.cloned.1.call-done.rows_ref, bf16[2048,512]{1,0:T(8,128)(2,1)S(1)} %copy-done.75), custom_call_target="tpu_custom_call" | custom-call | flops 3221225472 | bytes 14680064 | tf_op jit(solution)/shard_map/pallas_call | solution.py:296
  256.5 3.4 collective-permute-done.32
  269.3 4.5 shard_map.222
  278.1 3.5 collective-permute-start.40
  283.0 7.1 %shard_map.223 = bf16[256,1536]{1,0:T(8,128)(2,1)S(1)} custom-call(s32[9]{0:T(128)S(1)} %pad_add_fusion.at_ref, bf16[8,128,768]{2,1,0:T(8,128)(2,1)S(1)} %pad_maximum_fusion.refs_0_, bf16[8,128,768]{2,1,0:T(8,128)(2,1)S(1)} %copy-done.3, bf16[8,128,768]{2,1,0:T(8,128)(2,1)} %copy-done, bf16[8,128,768]{2,1,0:T(8,128)(2,1)} %copy-done.80, ...), custom_call_target="tpu_custom_call" | custom-call | flops 1610612736 | bytes 8388608 | tf_op jit(solution)/shard_map/pallas_call | solution.py:296
  290.1 3.7 collective-permute-done.39
  293.8 5.9 %collective-permute-done.40 = bf16[4,96,512]{2,1,0:T(8,128)(2,1)S(1)} collective-permute-done((bf16[4,96,512]{2,1,0:T(8,128)(2,1)S(1)}, bf16[4,96,512]{2,1,0:T(8,128)(2,1)S(1)}, u32[]{:S(2)}, u32[]{:S(2)}) %collective-permute-start.40) | collective-permute-done | bytes 393248 | tf_op jit(solution)/shard_map/ppermute | solution.py:164
  300.3 5.4 %shard_map.224 = (bf16[8,128,768]{2,1,0:T(8,128)(2,1)S(1)}, bf16[8,128,768]{2,1,0:T(8,128)(2,1)S(1)}, bf16[8,128,768]{2,1,0:T(8,128)(2,1)}, bf16[8,128,768]{2,1,0:T(8,128)(2,1)}) custom-call(s32[9]{0:T(128)S(1)} %pad_add_fusion.at_ref, bf16[2048,256]{1,0:T(8,128)(2,1)S(1)} %copy-done.27, bf16[256,1536]{1,0:T(8,128)(2,1)S(1)} %copy-done.5), custom_call_target="tpu_custom_call" | custom-call | flops 1610612736 | bytes 8388608 | tf_op jit(solution)/shard_map/pallas_call | solution.py:296
  308.1 3.2 collective-permute-start.42
  312.2 17.3 %collective-permute-done.42 = bf16[2,2,2,96,128]{4,3,2,1,0:T(8,128)(2,1)S(1)} collective-permute-done((bf16[2,2,2,96,128]{4,3,2,1,0:T(8,128)(2,1)S(1)}, bf16[2,2,2,96,128]{4,3,2,1,0:T(8,128)(2,1)S(1)}, u32[]{:S(2)}, u32[]{:S(2)}) %collective-permute-start.42) | collective-permute-done | bytes 196640 | tf_op jit(solution)/shard_map/ppermute | solution.py:164
  335.2 2.6 collective-permute-start.49
  337.9 18.0 %shard_map.225 = (bf16[2,96,1024]{2,1,0:T(8,128)(2,1)S(1)}, bf16[2,2,96,1024]{3,2,1,0:T(8,128)(2,1)S(1)}, bf16[2,2,96,1024]{3,2,1,0:T(8,128)(2,1)S(1)}) custom-call(s32[9]{0:T(128)S(1)} %pad_add_fusion.at_ref, bf16[2,96,1024]{2,1,0:T(8,128)(2,1)S(1)} %copy-done.73, bf16[2,96,1024]{2,1,0:T(8,128)(2,1)S(1)} %copy-done.53, bf16[2,96,1024]{2,1,0:T(8,128)(2,1)S(1)} %copy-done.55, ...), custom_call_target="tpu_custom_call" | custom-call | flops 4026531840 | bytes 12582912 | tf_op jit(solution)/shard_map/pallas_call | solution.py:296
  361.6 1.8 collective-permute-start.52
  364.1 3.2 collective-permute-start.51
  367.3 6.8 %shard_map.226 = bf16[96,1536]{1,0:T(8,128)(2,1)S(1)} custom-call(s32[9]{0:T(128)S(1)} %pad_add_fusion.at_ref, f32[2,96,1024]{2,1,0:T(8,128)S(1)} %copy-done.35, bf16[2048,1536]{1,0:T(8,128)(2,1)} %all-gather.11.cloned.1.call-done.rows_ref), custom_call_target="tpu_custom_call" | custom-call | flops 603979776 | bytes 8388608 | tf_op jit(solution)/shard_map/pallas_call | solution.py:296
  374.1 2.2 collective-permute-done.51
  378.6 2.3 collective-permute-start.57
  380.9 6.2 %collective-permute-done.55 = bf16[2,2,96,512]{3,2,0,1:T(8,128)(2,1)S(1)} collective-permute-done((bf16[2,2,96,512]{3,2,0,1:T(8,128)(2,1)S(1)}, bf16[2,2,96,512]{3,2,0,1:T(8,128)(2,1)S(1)}, u32[]{:S(2)}, u32[]{:S(2)}) %collective-permute-start.55) | collective-permute-done | bytes 393248 | tf_op jit(solution)/shard_map/ppermute | solution.py:164
  388.4 7.8 %shard_map.227 = (bf16[8,96,192]{2,1,0:T(8,128)(2,1)S(1)}, bf16[8,96,192]{2,1,0:T(8,128)(2,1)S(1)}) custom-call(s32[25]{0:T(128)S(1)} %copy-done.65, bf16[2048,1536]{1,0:T(8,128)(2,1)} %all-gather.5.cloned.1.call-done.rows_ref, f32[48,1024]{1,0:T(8,128)S(1)} %get-tuple-element.280.cos2_ref.cos_ref, f32[48,1024]{1,0:T(8,128)S(1)} %get-tuple-element.281.sin2_ref.sin_ref, ...), custom_call_target="tpu_custom_call" | custom-call | flops 1207959552 | bytes 8388608 | tf_op jit(solution)/shard_map/pallas_call | solution.py:296
  400.2 1.8 collective-permute-start.58
  402.1 2.1 collective-permute-start.61
  404.2 5.8 %shard_map.228 = (bf16[8,128,512]{2,1,0:T(8,128)(2,1)S(1)}, bf16[8,128,512]{2,1,0:T(8,128)(2,1)}, bf16[8,128,512]{2,1,0:T(8,128)(2,1)S(1)}, bf16[8,128,512]{2,1,...) custom-call(s32[9]{0:T(128)S(1)} %pad_add_fusion.at_ref, bf16[1536,192]{1,0:T(8,128)(2,1)S(1)} %copy-done.16, ...), custom_call_target="tpu_custom_call" | custom-call | flops 1207959552 | bytes 8388608 | tf_op jit(solution)/shard_map/pallas_call | solution.py:296
  412.0 4.5 collective-permute-done.61
  416.5 3.1 collective-permute-done.58
  434.1 2.0 collective-permute-start.68
  436.2 10.0 %collective-permute-done.68 = bf16[2,2,96,192]{3,2,1,0:T(8,128)(2,1)S(1)} collective-permute-done((bf16[2,2,96,192]{3,2,1,0:T(8,128)(2,1)S(1)}, bf16[2,2,96,192]{3,2,1,0:T(8,128)(2,1)S(1)}, u32[]{:S(2)}, u32[]{:S(2)}) %collective-permute-start.68) | collective-permute-done | bytes 147488 | tf_op jit(solution)/shard_map/ppermute | solution.py:164
  448.7 1.7 collective-permute-start.70
  453.7 4.5 collective-permute-done.72
  466.7 3.1 shard_map.230
  470.9 4.7 collective-permute-done.77.far_ref
  475.6 1.7 add_convert_fusion.26
  480.6 3.7 collective-permute-start.79
  484.3 3.3 shard_map.229
  489.7 1.8 select_convert_fusion.1
  (487 shorter events, 121.2 us)
Async XLA Ops:
  7.2 71.4 %all-gather.5.cloned.1.call-start = ((), (), s32[]{:S(2)}) async-start(), calls=%async_computation | async-start | bytes 6684672 | tf_op jit(solution)/shard_map/all_gather | solution.py:216
  11.0 123.6 %all-gather.7.cloned.1.call-start = ((), (), s32[]{:S(2)}) async-start(), calls=%async_computation.1 | async-start | bytes 5013504 | tf_op jit(solution)/shard_map/all_gather | solution.py:216
  14.0 8.2 %collective-permute-start.1 = (bf16[2,2,96,192]{3,2,0,1:T(8,128)(2,1)S(1)}, bf16[2,2,96,192]{3,2,0,1:T(8,128)(2,1)S(1)}, u32[]{:S(2)}, u32[]{:S(2)}) collective-permute-start(bf16[2,2,96,192]{3,2,0,1:T(8,128)(2,1)S(1)} %get-tuple-element.610), channel_id=1, source_target_pairs={{0,2},{1,3},{2,0},{3,1},{4,6},{5,7},{6,4},{7,5},{8,10},{9,11},{10,... | collective-permute-start | bytes 442376 | tf_op jit(solution)/shard_map/ppermute | solution.py:164
  16.9 26.3 %collective-permute-start.3 = (bf16[96,1536]{1,0:T(8,128)(2,1)S(1)}, bf16[96,1536]{1,0:T(8,128)(2,1)}, u32[]{:S(2)}, u32[]{:S(2)}) collective-permute-start(bf16[96,1536]{1,0:T(8,128)(2,1)S(1)} %copy-done.102), channel_id=1, source_target_pairs={{0,8},{1,9},{2,10},{3,11},{4,12},{5,13},{6,14},{7,15},{24,16},{25,... | collective-permute-start | bytes 884744 | tf_op jit(solution)/shard_map/ppermute | solution.py:164
  22.3 20.8 %collective-permute-start.2 = (bf16[2,2,96,192]{3,2,1,0:T(8,128)(2,1)S(1)}, bf16[2,2,96,192]{3,2,1,0:T(8,128)(2,1)S(1)}, u32[]{:S(2)}, u32[]{:S(2)}) collective-permute-start(bf16[2,2,96,192]{3,2,1,0:T(8,128)(2,1)S(1)} %get-tuple-element.608), channel_id=1, source_target_pairs={{0,4},{1,5},{2,6},{3,7},{4,0},{5,1},{6,2},{7,3},{8,12},{9,13},{10,... | collective-permute-start | bytes 442376 | tf_op jit(solution)/shard_map/ppermute | solution.py:164
  45.2 11.2 %collective-permute-start.6 = (bf16[2,2,96,512]{3,2,0,1:T(8,128)(2,1)S(1)}, bf16[2,2,96,512]{3,2,0,1:T(8,128)(2,1)S(1)}, u32[]{:S(2)}, u32[]{:S(2)}) collective-permute-start(bf16[2,2,96,512]{3,2,0,1:T(8,128)(2,1)S(1)} %get-tuple-element.570), channel_id=1, source_target_pairs={{0,2},{1,3},{2,0},{3,1},{4,6},{5,7},{6,4},{7,5},{8,10},{9,11},{10,... | collective-permute-start | bytes 1179656 | tf_op jit(solution)/shard_map/ppermute | solution.py:164
  48.3 29.7 %collective-permute-start.4 = (bf16[8,96,192]{2,1,0:T(8,128)(2,1)S(1)}, bf16[8,96,192]{2,1,0:T(8,128)(2,1)S(1)}, u32[]{:S(2)}, u32[]{:S(2)}) collective-permute-start(bf16[8,96,192]{2,1,0:T(8,128)(2,1)S(1)} %bitcast.180), channel_id=1, source_target_pairs={{0,8},{1,9},{2,10},{3,11},{4,12},{5,13},{6,14},{7,15},{8,0},{9,1},... | collective-permute-start | bytes 884744 | tf_op jit(solution)/shard_map/ppermute | solution.py:164
  56.5 20.6 %collective-permute-start.7 = (bf16[2,2,96,512]{3,2,1,0:T(8,128)(2,1)S(1)}, bf16[2,2,96,512]{3,2,1,0:T(8,128)(2,1)S(1)}, u32[]{:S(2)}, u32[]{:S(2)}) collective-permute-start(bf16[2,2,96,512]{3,2,1,0:T(8,128)(2,1)S(1)} %get-tuple-element.568), channel_id=1, source_target_pairs={{0,4},{1,5},{2,6},{3,7},{4,0},{5,1},{6,2},{7,3},{8,12},{9,13},{10,... | collective-permute-start | bytes 1179656 | tf_op jit(solution)/shard_map/ppermute | solution.py:164
  78.7 138.9 %all-gather.9.cloned.1.call-start = ((), (), s32[]{:S(2)}) async-start(), calls=%async_computation.2 | async-start | bytes 6684672 | tf_op jit(solution)/shard_map/all_gather | solution.py:216
  78.8 10.5 %collective-permute-start.10 = (bf16[1,128,768]{2,1,0:T(8,128)(2,1)S(1)}, bf16[1,128,768]{2,1,0:T(8,128)(2,1)S(1)}, u32[]{:S(2)}, u32[]{:S(2)}) collective-permute-start(bf16[1,128,768]{2,1,0:T(8,128)(2,1)S(1)} %get-tuple-element.605), channel_id=1, source_target_pairs={{0,4},{1,5},{2,6},{3,7},{4,0},{5,1},{6,2},{7,3},{8,12},{9,13},{10,... | collective-permute-start | bytes 589832 | tf_op jit(solution)/shard_map/ppermute | solution.py:164
  81.4 10.1 %collective-permute-start.9 = (bf16[1,128,768]{2,1,0:T(8,128)(2,1)S(1)}, bf16[1,128,768]{2,1,0:T(8,128)(2,1)S(1)}, u32[]{:S(2)}, u32[]{:S(2)}) collective-permute-start(bf16[1,128,768]{2,1,0:T(8,128)(2,1)S(1)} %get-tuple-element.606), channel_id=1, source_target_pairs={{0,4},{1,5},{2,6},{3,7},{4,0},{5,1},{6,2},{7,3},{8,12},{9,13},{10,... | collective-permute-start | bytes 589832 | tf_op jit(solution)/shard_map/ppermute | solution.py:164
  91.6 19.3 %collective-permute-start.12 = (bf16[2,128,768]{2,1,0:T(8,128)(2,1)S(1)}, bf16[2,128,768]{2,1,0:T(8,128)(2,1)S(1)}, u32[]{:S(2)}, u32[]{:S(2)}) collective-permute-start(bf16[2,128,768]{2,1,0:T(8,128)(2,1)S(1)} %pad_maximum_fusion.15), channel_id=1, source_target_pairs={{0,16},{1,17},{2,18},{3,19},{4,20},{5,21},{6,22},{7,23},{8,24},{9,... | collective-permute-start | bytes 1179656 | tf_op jit(solution)/shard_map/ppermute | solution.py:164
  91.7 20.2 %collective-permute-start.13 = (bf16[2,128,768]{2,1,0:T(8,128)(2,1)S(1)}, bf16[2,128,768]{2,1,0:T(8,128)(2,1)S(1)}, u32[]{:S(2)}, u32[]{:S(2)}) collective-permute-start(bf16[2,128,768]{2,1,0:T(8,128)(2,1)S(1)} %pad_maximum_fusion.16), channel_id=1, source_target_pairs={{0,2},{1,3},{2,0},{3,1},{4,6},{5,7},{6,4},{7,5},{8,10},{9,11},{10,... | collective-permute-start | bytes 1179656 | tf_op jit(solution)/shard_map/ppermute | solution.py:164
  93.8 19.0 %collective-permute-start.11 = (bf16[2,96,1024]{2,1,0:T(8,128)(2,1)S(1)}, bf16[2,96,1024]{2,1,0:T(8,128)(2,1)S(1)}, u32[]{:S(2)}, u32[]{:S(2)}) collective-permute-start(bf16[2,96,1024]{2,1,0:T(8,128)(2,1)S(1)} %get-tuple-element.290.a_ref), channel_id=1, source_target_pairs={{0,8},{1,9},{2,10},{3,11},{4,12},{5,13},{6,14},{7,15},{8,0},{9,1},... | collective-permute-start | bytes 1179656 | tf_op jit(solution)/shard_map/ppermute | solution.py:164
  115.3 24.5 %collective-permute-start.18 = (bf16[4,128,768]{2,1,0:T(8,128)(2,1)}, bf16[4,128,768]{2,1,0:T(8,128)(2,1)}, u32[]{:S(2)}, u32[]{:S(2)}) collective-permute-start(bf16[4,128,768]{2,1,0:T(8,128)(2,1)} %pad_maximum_fusion.3), channel_id=1, source_target_pairs={{0,2},{1,3},{2,0},{3,1},{4,6},{5,7},{6,4},{7,5},{8,10},{9,11},{10,... | collective-permute-start | bytes 2359304 | tf_op jit(solution)/shard_map/ppermute | solution.py:164
  118.2 20.7 %collective-permute-start.16 = (bf16[4,96,512]{2,1,0:T(8,128)(2,1)S(1)}, bf16[4,96,512]{2,1,0:T(8,128)(2,1)S(1)}, u32[]{:S(2)}, u32[]{:S(2)}) collective-permute-start(bf16[4,96,512]{2,1,0:T(8,128)(2,1)S(1)} %bitcast.186), channel_id=1, source_target_pairs={{0,8},{1,9},{2,10},{3,11},{4,12},{5,13},{6,14},{7,15},{8,0},{9,1},... | collective-permute-start | bytes 1179656 | tf_op jit(solution)/shard_map/ppermute | solution.py:164
  121.2 20.1 %collective-permute-start.19 = (bf16[4,128,768]{2,1,0:T(8,128)(2,1)}, bf16[4,128,768]{2,1,0:T(8,128)(2,1)}, u32[]{:S(2)}, u32[]{:S(2)}) collective-permute-start(bf16[4,128,768]{2,1,0:T(8,128)(2,1)} %pad_maximum_fusion.4), channel_id=1, source_target_pairs={{0,16},{1,17},{2,18},{3,19},{4,20},{5,21},{6,22},{7,23},{8,24},{9,... | collective-permute-start | bytes 2359304 | tf_op jit(solution)/shard_map/ppermute | solution.py:164
  145.1 7.6 %collective-permute-start.21 = (bf16[8,128,768]{2,1,0:T(8,128)(2,1)S(1)}, bf16[8,128,768]{2,1,0:T(8,128)(2,1)S(1)}, u32[]{:S(2)}, u32[]{:S(2)}) collective-permute-start(bf16[8,128,768]{2,1,0:T(8,128)(2,1)S(1)} %pad_maximum_fusion.refs_0_), channel_id=1, source_target_pairs={{0,1},{1,0},{2,3},{3,2},{4,5},{5,4},{6,7},{7,6},{8,9},{9,8},{10,11... | collective-permute-start | bytes 4718600 | tf_op jit(solution)/shard_map/ppermute | solution.py:164
  145.2 8.7 %collective-permute-start.22 = (bf16[8,128,768]{2,1,0:T(8,128)(2,1)S(1)}, bf16[8,128,768]{2,1,0:T(8,128)(2,1)S(1)}, u32[]{:S(2)}, u32[]{:S(2)}) collective-permute-start(bf16[8,128,768]{2,1,0:T(8,128)(2,1)S(1)} %pad_maximum_fusion.1.refs_2_), channel_id=1, source_target_pairs={{0,1},{1,0},{2,3},{3,2},{4,5},{5,4},{6,7},{7,6},{8,9},{9,8},{10,11... | collective-permute-start | bytes 4718600 | tf_op jit(solution)/shard_map/ppermute | solution.py:164
  145.7 7.0 %collective-permute-start.20 = (bf16[2,2,2,96,128]{4,3,1,0,2:T(8,128)(2,1)S(1)}, bf16[2,2,2,96,128]{4,3,1,0,2:T(8,128)(2,1)S(1)}, u32[]{:S(2)}, u32[]{:S(2)}) collective-permute-start(bf16[2,2,2,96,128]{4,3,1,0,2:T(8,128)(2,1)S(1)} %get-tuple-element.602), channel_id=1, source_target_pairs={{0,16},{1,17},{2,18},{3,19},{4,20},{5,21},{6,22},{7,23},{8,24},{9,... | collective-permute-start | bytes 589832 | tf_op jit(solution)/shard_map/ppermute | solution.py:164
  146.8 14.5 %collective-permute-start.24 = (bf16[256,1536]{1,0:T(8,128)(2,1)S(1)}, bf16[256,1536]{1,0:T(8,128)(2,1)S(1)}, u32[]{:S(2)}, u32[]{:S(2)}) collective-permute-start(bf16[256,1536]{1,0:T(8,128)(2,1)S(1)} %copy-done.88), channel_id=1, source_target_pairs={{0,8},{2,10},{4,12},{6,14},{9,1},{11,3},{13,5},{15,7},{17,25},{19,... | collective-permute-start | bytes 2359304 | tf_op jit(solution)/shard_map/ppermute | solution.py:164
  167.4 192.7 %all-gather.11.cloned.1.call-start = ((), (), s32[]{:S(2)}) async-start(), calls=%async_computation.3 | async-start | bytes 6684672 | tf_op jit(solution)/shard_map/all_gather | solution.py:216
  167.7 13.2 %collective-permute-start.25 = (bf16[4,96,512]{2,1,0:T(8,128)(2,1)}, bf16[4,96,512]{2,1,0:T(8,128)(2,1)S(1)}, u32[]{:S(2)}, u32[]{:S(2)}) collective-permute-start(bf16[4,96,512]{2,1,0:T(8,128)(2,1)} %bitcast.184), channel_id=1, source_target_pairs={{0,8},{1,9},{2,10},{3,11},{4,12},{5,13},{6,14},{7,15},{8,0},{9,1},... | collective-permute-start | bytes 1179656 | tf_op jit(solution)/shard_map/ppermute | solution.py:164
  236.2 14.1 %collective-permute-start.29 = (bf16[4,128,512]{2,1,0:T(8,128)(2,1)S(1)}, bf16[4,128,512]{2,1,0:T(8,128)(2,1)S(1)}, u32[]{:S(2)}, u32[]{:S(2)}) collective-permute-start(bf16[4,128,512]{2,1,0:T(8,128)(2,1)S(1)} %get-tuple-element.539), channel_id=1, source_target_pairs={{0,4},{1,5},{2,6},{3,7},{4,0},{5,1},{6,2},{7,3},{8,12},{9,13},{10,... | collective-permute-start | bytes 1572872 | tf_op jit(solution)/shard_map/ppermute | solution.py:164
  237.3 13.9 %collective-permute-start.30 = (bf16[4,128,512]{2,1,0:T(8,128)(2,1)S(1)}, bf16[4,128,512]{2,1,0:T(8,128)(2,1)S(1)}, u32[]{:S(2)}, u32[]{:S(2)}) collective-permute-start(bf16[4,128,512]{2,1,0:T(8,128)(2,1)S(1)} %get-tuple-element.537), channel_id=1, source_target_pairs={{0,16},{1,17},{2,18},{3,19},{4,20},{5,21},{6,22},{7,23},{8,24},{9,... | collective-permute-start | bytes 1572872 | tf_op jit(solution)/shard_map/ppermute | solution.py:164
  239.2 13.6 %collective-permute-start.31 = (bf16[4,128,512]{2,1,0:T(8,128)(2,1)S(1)}, bf16[4,128,512]{2,1,0:T(8,128)(2,1)S(1)}, u32[]{:S(2)}, u32[]{:S(2)}) collective-permute-start(bf16[4,128,512]{2,1,0:T(8,128)(2,1)S(1)} %get-tuple-element.535), channel_id=1, source_target_pairs={{0,2},{1,3},{2,0},{3,1},{4,6},{5,7},{6,4},{7,5},{8,10},{9,11},{10,... | collective-permute-start | bytes 1572872 | tf_op jit(solution)/shard_map/ppermute | solution.py:164
  252.9 7.1 %collective-permute-start.32 = (bf16[2,128,512]{2,1,0:T(8,128)(2,1)S(1)}, bf16[2,128,512]{2,1,0:T(8,128)(2,1)S(1)}, u32[]{:S(2)}, u32[]{:S(2)}) collective-permute-start(bf16[2,128,512]{2,1,0:T(8,128)(2,1)S(1)} %get-tuple-element.555), channel_id=1, source_target_pairs={{0,2},{1,3},{2,0},{3,1},{4,6},{5,7},{6,4},{7,5},{8,10},{9,11},{10,... | collective-permute-start | bytes 786440 | tf_op jit(solution)/shard_map/ppermute | solution.py:164
  253.7 6.8 %collective-permute-start.33 = (bf16[2,128,512]{2,1,0:T(8,128)(2,1)S(1)}, bf16[2,128,512]{2,1,0:T(8,128)(2,1)S(1)}, u32[]{:S(2)}, u32[]{:S(2)}) collective-permute-start(bf16[2,128,512]{2,1,0:T(8,128)(2,1)S(1)} %get-tuple-element.553), channel_id=1, source_target_pairs={{0,4},{1,5},{2,6},{3,7},{4,0},{5,1},{6,2},{7,3},{8,12},{9,13},{10,... | collective-permute-start | bytes 786440 | tf_op jit(solution)/shard_map/ppermute | solution.py:164
  278.1 21.6 %collective-permute-start.40 = (bf16[4,96,512]{2,1,0:T(8,128)(2,1)S(1)}, bf16[4,96,512]{2,1,0:T(8,128)(2,1)S(1)}, u32[]{:S(2)}, u32[]{:S(2)}) collective-permute-start(bf16[4,96,512]{2,1,0:T(8,128)(2,1)S(1)} %slice.516), channel_id=1, source_target_pairs={{0,8},{1,9},{2,10},{3,11},{4,12},{5,13},{6,14},{7,15},{8,0},{9,1},... | collective-permute-start | bytes 1179656 | tf_op jit(solution)/shard_map/ppermute | solution.py:164
  282.6 11.2 %collective-permute-start.39 = (bf16[2,2,2,96,128]{4,3,0,2,1:T(8,128)(2,1)S(1)}, bf16[2,2,2,96,128]{4,3,0,2,1:T(8,128)(2,1)S(1)}, u32[]{:S(2)}, u32[]{:S(2)}) collective-permute-start(bf16[2,2,2,96,128]{4,3,0,2,1:T(8,128)(2,1)S(1)} %get-tuple-element.598), channel_id=1, source_target_pairs={{0,16},{1,17},{2,18},{3,19},{4,20},{5,21},{6,22},{7,23},{8,24},{9,... | collective-permute-start | bytes 589832 | tf_op jit(solution)/shard_map/ppermute | solution.py:164
  299.7 6.6 %collective-permute-start.41 = (bf16[2,2,2,96,128]{4,3,1,0,2:T(8,128)(2,1)S(1)}, bf16[2,2,2,96,128]{4,3,1,0,2:T(8,128)(2,1)S(1)}, u32[]{:S(2)}, u32[]{:S(2)}) collective-permute-start(bf16[2,2,2,96,128]{4,3,1,0,2:T(8,128)(2,1)S(1)} %get-tuple-element.596), channel_id=1, source_target_pairs={{0,2},{1,3},{2,0},{3,1},{4,6},{5,7},{6,4},{7,5},{8,10},{9,11},{10,... | collective-permute-start | bytes 589832 | tf_op jit(solution)/shard_map/ppermute | solution.py:164
  306.4 23.2 %collective-permute-start.43 = (bf16[8,128,768]{2,1,0:T(8,128)(2,1)S(1)}, bf16[8,128,768]{2,1,0:T(8,128)(2,1)S(1)}, u32[]{:S(2)}, u32[]{:S(2)}) collective-permute-start(bf16[8,128,768]{2,1,0:T(8,128)(2,1)S(1)} %get-tuple-element.406), channel_id=1, source_target_pairs={{0,1},{1,0},{2,3},{3,2},{4,5},{5,4},{6,7},{7,6},{8,9},{9,8},{10,11... | collective-permute-start | bytes 4718600 | tf_op jit(solution)/shard_map/ppermute | solution.py:164
  306.4 23.1 %collective-permute-start.44 = (bf16[8,128,768]{2,1,0:T(8,128)(2,1)}, bf16[8,128,768]{2,1,0:T(8,128)(2,1)S(1)}, u32[]{:S(2)}, u32[]{:S(2)}) collective-permute-start(bf16[8,128,768]{2,1,0:T(8,128)(2,1)} %get-tuple-element.408), channel_id=1, source_target_pairs={{0,1},{1,0},{2,3},{3,2},{4,5},{5,4},{6,7},{7,6},{8,9},{9,8},{10,11... | collective-permute-start | bytes 4718600 | tf_op jit(solution)/shard_map/ppermute | solution.py:164
  307.0 22.6 %collective-permute-start.45 = (bf16[4,96,512]{2,1,0:T(8,128)(2,1)S(1)}, bf16[4,96,512]{2,1,0:T(8,128)(2,1)S(1)}, u32[]{:S(2)}, u32[]{:S(2)}) collective-permute-start(bf16[4,96,512]{2,1,0:T(8,128)(2,1)S(1)} %slice.521), channel_id=1, source_target_pairs={{0,8},{1,9},{2,10},{3,11},{4,12},{5,13},{6,14},{7,15},{8,0},{9,1},... | collective-permute-start | bytes 1179656 | tf_op jit(solution)/shard_map/ppermute | solution.py:164
  308.1 21.3 %collective-permute-start.42 = (bf16[2,2,2,96,128]{4,3,2,1,0:T(8,128)(2,1)S(1)}, bf16[2,2,2,96,128]{4,3,2,1,0:T(8,128)(2,1)S(1)}, u32[]{:S(2)}, u32[]{:S(2)}) collective-permute-start(bf16[2,2,2,96,128]{4,3,2,1,0:T(8,128)(2,1)S(1)} %get-tuple-element.594), channel_id=1, source_target_pairs={{0,4},{1,5},{2,6},{3,7},{4,0},{5,1},{6,2},{7,3},{8,12},{9,13},{10,... | collective-permute-start | bytes 589832 | tf_op jit(solution)/shard_map/ppermute | solution.py:164
  329.6 26.3 %collective-permute-start.48 = (bf16[256,1536]{1,0:T(8,128)(2,1)S(1)}, bf16[256,1536]{1,0:T(8,128)(2,1)S(1)}, u32[]{:S(2)}, u32[]{:S(2)}) collective-permute-start(bf16[256,1536]{1,0:T(8,128)(2,1)S(1)} %shard_map.223), channel_id=1, source_target_pairs={{1,9},{3,11},{5,13},{7,15},{8,0},{10,2},{12,4},{14,6},{16,24},{18,... | collective-permute-start | bytes 2359304 | tf_op jit(solution)/shard_map/ppermute | solution.py:164
  331.7 24.2 %collective-permute-start.46 = (bf16[4,128,768]{2,1,0:T(8,128)(2,1)S(1)}, bf16[4,128,768]{2,1,0:T(8,128)(2,1)S(1)}, u32[]{:S(2)}, u32[]{:S(2)}) collective-permute-start(bf16[4,128,768]{2,1,0:T(8,128)(2,1)S(1)} %get-tuple-element.527), channel_id=1, source_target_pairs={{0,2},{1,3},{2,0},{3,1},{4,6},{5,7},{6,4},{7,5},{8,10},{9,11},{10,... | collective-permute-start | bytes 2359304 | tf_op jit(solution)/shard_map/ppermute | solution.py:164
  334.1 21.9 %collective-permute-start.47 = (bf16[4,128,768]{2,1,0:T(8,128)(2,1)S(1)}, bf16[4,128,768]{2,1,0:T(8,128)(2,1)S(1)}, u32[]{:S(2)}, u32[]{:S(2)}) collective-permute-start(bf16[4,128,768]{2,1,0:T(8,128)(2,1)S(1)} %get-tuple-element.525), channel_id=1, source_target_pairs={{0,16},{1,17},{2,18},{3,19},{4,20},{5,21},{6,22},{7,23},{8,24},{9,... | collective-permute-start | bytes 2359304 | tf_op jit(solution)/shard_map/ppermute | solution.py:164
  335.2 20.7 %collective-permute-start.49 = (bf16[4,96,512]{2,1,0:T(8,128)(2,1)}, bf16[4,96,512]{2,1,0:T(8,128)(2,1)S(1)}, u32[]{:S(2)}, u32[]{:S(2)}) collective-permute-start(bf16[4,96,512]{2,1,0:T(8,128)(2,1)} %add_convert_fusion.25), channel_id=1, source_target_pairs={{0,4},{1,5},{2,6},{3,7},{4,0},{5,1},{6,2},{7,3},{8,12},{9,13},{10,... | collective-permute-start | bytes 1179656 | tf_op jit(solution)/shard_map/ppermute | solution.py:164
  361.6 14.7 %collective-permute-start.52 = (bf16[2,128,768]{2,1,0:T(8,128)(2,1)S(1)}, bf16[2,128,768]{2,1,0:T(8,128)(2,1)S(1)}, u32[]{:S(2)}, u32[]{:S(2)}) collective-permute-start(bf16[2,128,768]{2,1,0:T(8,128)(2,1)S(1)} %get-tuple-element.543), channel_id=1, source_target_pairs={{0,16},{1,17},{2,18},{3,19},{4,20},{5,21},{6,22},{7,23},{8,24},{9,... | collective-permute-start | bytes 1179656 | tf_op jit(solution)/shard_map/ppermute | solution.py:164
  363.6 12.7 %collective-permute-start.53 = (bf16[2,128,768]{2,1,0:T(8,128)(2,1)S(1)}, bf16[2,128,768]{2,1,0:T(8,128)(2,1)S(1)}, u32[]{:S(2)}, u32[]{:S(2)}) collective-permute-start(bf16[2,128,768]{2,1,0:T(8,128)(2,1)S(1)} %get-tuple-element.541), channel_id=1, source_target_pairs={{0,2},{1,3},{2,0},{3,1},{4,6},{5,7},{6,4},{7,5},{8,10},{9,11},{10,... | collective-permute-start | bytes 1179656 | tf_op jit(solution)/shard_map/ppermute | solution.py:164
  364.1 12.3 %collective-permute-start.51 = (bf16[96,1024]{1,0:T(8,128)(2,1)}, bf16[96,1024]{1,0:T(8,128)(2,1)S(1)}, u32[]{:S(2)}, u32[]{:S(2)}) collective-permute-start(bf16[96,1024]{1,0:T(8,128)(2,1)} %get-tuple-element.435), channel_id=1, source_target_pairs={{0,8},{1,9},{2,10},{3,11},{4,12},{5,13},{6,14},{7,15},{8,0},{9,1},... | collective-permute-start | bytes 589832 | tf_op jit(solution)/shard_map/ppermute | solution.py:164
  376.3 10.8 %collective-permute-start.54 = (bf16[96,1024]{1,0:T(8,128)(2,1)S(1)}, bf16[96,1024]{1,0:T(8,128)(2,1)S(1)}, u32[]{:S(2)}, u32[]{:S(2)}) collective-permute-start(bf16[96,1024]{1,0:T(8,128)(2,1)S(1)} %copy-done.105), channel_id=1, source_target_pairs={{0,8},{1,9},{2,10},{3,11},{4,12},{5,13},{6,14},{7,15},{8,0},{9,1},... | collective-permute-start | bytes 589832 | tf_op jit(solution)/shard_map/ppermute | solution.py:164
  377.3 9.8 %collective-permute-start.55 = (bf16[2,2,96,512]{3,2,0,1:T(8,128)(2,1)S(1)}, bf16[2,2,96,512]{3,2,0,1:T(8,128)(2,1)S(1)}, u32[]{:S(2)}, u32[]{:S(2)}) collective-permute-start(bf16[2,2,96,512]{3,2,0,1:T(8,128)(2,1)S(1)} %bitcast.204), channel_id=1, source_target_pairs={{0,2},{1,3},{2,0},{3,1},{4,6},{5,7},{6,4},{7,5},{8,10},{9,11},{10,... | collective-permute-start | bytes 1179656 | tf_op jit(solution)/shard_map/ppermute | solution.py:164
  378.6 18.5 %collective-permute-start.57 = (bf16[256,1536]{1,0:T(8,128)(2,1)S(1)}, bf16[256,1536]{1,0:T(8,128)(2,1)S(1)}, u32[]{:S(2)}, u32[]{:S(2)}) collective-permute-start(bf16[256,1536]{1,0:T(8,128)(2,1)S(1)} %add_convert_fusion), channel_id=1, source_target_pairs={{0,16},{2,18},{4,20},{6,22},{9,25},{11,27},{13,29},{15,31},{17,1},... | collective-permute-start | bytes 2359304 | tf_op jit(solution)/shard_map/ppermute | solution.py:164
  387.2 9.7 %collective-permute-start.56 = (bf16[2,2,96,512]{3,2,1,0:T(8,128)(2,1)S(1)}, bf16[2,2,96,512]{3,2,1,0:T(8,128)(2,1)S(1)}, u32[]{:S(2)}, u32[]{:S(2)}) collective-permute-start(bf16[2,2,96,512]{3,2,1,0:T(8,128)(2,1)S(1)} %get-tuple-element.562), channel_id=1, source_target_pairs={{0,1},{1,0},{2,3},{3,2},{4,5},{5,4},{6,7},{7,6},{8,9},{9,8},{10,11... | collective-permute-start | bytes 1179656 | tf_op jit(solution)/shard_map/ppermute | solution.py:164
  397.1 22.6 %collective-permute-start.59 = (bf16[8,96,512]{2,1,0:T(8,128)(2,1)S(1)}, bf16[8,96,512]{2,1,0:T(8,128)(2,1)S(1)}, u32[]{:S(2)}, u32[]{:S(2)}) collective-permute-start(bf16[8,96,512]{2,1,0:T(8,128)(2,1)S(1)} %bitcast.177), channel_id=1, source_target_pairs={{0,16},{1,17},{2,18},{3,19},{4,20},{5,21},{6,22},{7,23},{8,24},{9,... | collective-permute-start | bytes 2359304 | tf_op jit(solution)/shard_map/ppermute | solution.py:164
  399.4 12.6 %collective-permute-start.60 = (bf16[1,128,768]{2,1,0:T(8,128)(2,1)S(1)}, bf16[1,128,768]{2,1,0:T(8,128)(2,1)S(1)}, u32[]{:S(2)}, u32[]{:S(2)}) collective-permute-start(bf16[1,128,768]{2,1,0:T(8,128)(2,1)S(1)} %get-tuple-element.559), channel_id=1, source_target_pairs={{0,4},{1,5},{2,6},{3,7},{4,0},{5,1},{6,2},{7,3},{8,12},{9,13},{10,... | collective-permute-start | bytes 589832 | tf_op jit(solution)/shard_map/ppermute | solution.py:164
  400.2 19.5 %collective-permute-start.58 = (bf16[8,96,192]{2,1,0:T(8,128)(2,1)S(1)}, bf16[8,96,192]{2,1,0:T(8,128)(2,1)S(1)}, u32[]{:S(2)}, u32[]{:S(2)}) collective-permute-start(bf16[8,96,192]{2,1,0:T(8,128)(2,1)S(1)} %get-tuple-element.465), channel_id=1, source_target_pairs={{0,8},{1,9},{2,10},{3,11},{4,12},{5,13},{6,14},{7,15},{8,0},{9,1},... | collective-permute-start | bytes 884744 | tf_op jit(solution)/shard_map/ppermute | solution.py:164
  402.1 14.4 %collective-permute-start.61 = (bf16[1,128,768]{2,1,0:T(8,128)(2,1)S(1)}, bf16[1,128,768]{2,1,0:T(8,128)(2,1)S(1)}, u32[]{:S(2)}, u32[]{:S(2)}) collective-permute-start(bf16[1,128,768]{2,1,0:T(8,128)(2,1)S(1)} %get-tuple-element.557), channel_id=1, source_target_pairs={{0,4},{1,5},{2,6},{3,7},{4,0},{5,1},{6,2},{7,3},{8,12},{9,13},{10,... | collective-permute-start | bytes 589832 | tf_op jit(solution)/shard_map/ppermute | solution.py:164
  427.9 18.3 %collective-permute-start.65 = (bf16[4,128,512]{2,1,0:T(8,128)(2,1)S(1)}, bf16[4,128,512]{2,1,0:T(8,128)(2,1)S(1)}, u32[]{:S(2)}, u32[]{:S(2)}) collective-permute-start(bf16[4,128,512]{2,1,0:T(8,128)(2,1)S(1)} %get-tuple-element.533), channel_id=1, source_target_pairs={{0,4},{1,5},{2,6},{3,7},{4,0},{5,1},{6,2},{7,3},{8,12},{9,13},{10,... | collective-permute-start | bytes 1572872 | tf_op jit(solution)/shard_map/ppermute | solution.py:164
  429.9 16.3 %collective-permute-start.66 = (bf16[4,128,512]{2,1,0:T(8,128)(2,1)S(1)}, bf16[4,128,512]{2,1,0:T(8,128)(2,1)S(1)}, u32[]{:S(2)}, u32[]{:S(2)}) collective-permute-start(bf16[4,128,512]{2,1,0:T(8,128)(2,1)S(1)} %get-tuple-element.531), channel_id=1, source_target_pairs={{0,16},{1,17},{2,18},{3,19},{4,20},{5,21},{6,22},{7,23},{8,24},{9,... | collective-permute-start | bytes 1572872 | tf_op jit(solution)/shard_map/ppermute | solution.py:164
  432.4 13.8 %collective-permute-start.67 = (bf16[4,128,512]{2,1,0:T(8,128)(2,1)S(1)}, bf16[4,128,512]{2,1,0:T(8,128)(2,1)S(1)}, u32[]{:S(2)}, u32[]{:S(2)}) collective-permute-start(bf16[4,128,512]{2,1,0:T(8,128)(2,1)S(1)} %get-tuple-element.529), channel_id=1, source_target_pairs={{0,2},{1,3},{2,0},{3,1},{4,6},{5,7},{6,4},{7,5},{8,10},{9,11},{10,... | collective-permute-start | bytes 1572872 | tf_op jit(solution)/shard_map/ppermute | solution.py:164
  434.1 12.0 %collective-permute-start.68 = (bf16[2,2,96,192]{3,2,1,0:T(8,128)(2,1)S(1)}, bf16[2,2,96,192]{3,2,1,0:T(8,128)(2,1)S(1)}, u32[]{:S(2)}, u32[]{:S(2)}) collective-permute-start(bf16[2,2,96,192]{3,2,1,0:T(8,128)(2,1)S(1)} %bitcast.224), channel_id=1, source_target_pairs={{0,4},{1,5},{2,6},{3,7},{4,0},{5,1},{6,2},{7,3},{8,12},{9,13},{10,... | collective-permute-start | bytes 442376 | tf_op jit(solution)/shard_map/ppermute | solution.py:164
  446.4 11.9 %collective-permute-start.69 = (bf16[2,128,512]{2,1,0:T(8,128)(2,1)S(1)}, bf16[2,128,512]{2,1,0:T(8,128)(2,1)S(1)}, u32[]{:S(2)}, u32[]{:S(2)}) collective-permute-start(bf16[2,128,512]{2,1,0:T(8,128)(2,1)S(1)} %get-tuple-element.549), channel_id=1, source_target_pairs={{0,2},{1,3},{2,0},{3,1},{4,6},{5,7},{6,4},{7,5},{8,10},{9,11},{10,... | collective-permute-start | bytes 786440 | tf_op jit(solution)/shard_map/ppermute | solution.py:164
  448.0 10.2 %collective-permute-start.72 = (bf16[2,2,96,192]{3,2,0,1:T(8,128)(2,1)S(1)}, bf16[2,2,96,192]{3,2,0,1:T(8,128)(2,1)S(1)}, u32[]{:S(2)}, u32[]{:S(2)}) collective-permute-start(bf16[2,2,96,192]{3,2,0,1:T(8,128)(2,1)S(1)} %get-tuple-element.588), channel_id=1, source_target_pairs={{0,2},{1,3},{2,0},{3,1},{4,6},{5,7},{6,4},{7,5},{8,10},{9,11},{10,... | collective-permute-start | bytes 442376 | tf_op jit(solution)/shard_map/ppermute | solution.py:164
  448.7 9.5 %collective-permute-start.70 = (bf16[2,128,512]{2,1,0:T(8,128)(2,1)S(1)}, bf16[2,128,512]{2,1,0:T(8,128)(2,1)S(1)}, u32[]{:S(2)}, u32[]{:S(2)}) collective-permute-start(bf16[2,128,512]{2,1,0:T(8,128)(2,1)S(1)} %get-tuple-element.547), channel_id=1, source_target_pairs={{0,4},{1,5},{2,6},{3,7},{4,0},{5,1},{6,2},{7,3},{8,12},{9,13},{10,... | collective-permute-start | bytes 786440 | tf_op jit(solution)/shard_map/ppermute | solution.py:164
  450.5 7.7 %collective-permute-start.71 = (bf16[2,128,512]{2,1,0:T(8,128)(2,1)S(1)}, bf16[2,128,512]{2,1,0:T(8,128)(2,1)S(1)}, u32[]{:S(2)}, u32[]{:S(2)}) collective-permute-start(bf16[2,128,512]{2,1,0:T(8,128)(2,1)S(1)} %get-tuple-element.545), channel_id=1, source_target_pairs={{0,16},{1,17},{2,18},{3,19},{4,20},{5,21},{6,22},{7,23},{8,24},{9,... | collective-permute-start | bytes 786440 | tf_op jit(solution)/shard_map/ppermute | solution.py:164
  452.2 18.2 %collective-permute-start.78 = (bf16[96,1536]{1,0:T(8,128)(2,1)S(1)}, bf16[96,1536]{1,0:T(8,128)(2,1)}, u32[]{:S(2)}, u32[]{:S(2)}) collective-permute-start(bf16[96,1536]{1,0:T(8,128)(2,1)S(1)} %shard_map.226), channel_id=1, source_target_pairs={{8,0},{9,1},{10,2},{11,3},{12,4},{13,5},{14,6},{15,7},{16,24},{17,... | collective-permute-start | bytes 884744 | tf_op jit(solution)/shard_map/ppermute | solution.py:164
  459.0 11.4 %collective-permute-start.73 = (bf16[1,128,512]{2,1,0:T(8,128)(2,1)}, bf16[1,128,512]{2,1,0:T(8,128)(2,1)}, u32[]{:S(2)}, u32[]{:S(2)}) collective-permute-start(bf16[1,128,512]{2,1,0:T(8,128)(2,1)} %get-tuple-element.577), channel_id=1, source_target_pairs={{0,16},{1,17},{2,18},{3,19},{4,20},{5,21},{6,22},{7,23},{8,24},{9,... | collective-permute-start | bytes 393224 | tf_op jit(solution)/shard_map/ppermute | solution.py:164
  461.1 9.3 %collective-permute-start.74 = (bf16[1,128,512]{2,1,0:T(8,128)(2,1)}, bf16[1,128,512]{2,1,0:T(8,128)(2,1)}, u32[]{:S(2)}, u32[]{:S(2)}) collective-permute-start(bf16[1,128,512]{2,1,0:T(8,128)(2,1)} %get-tuple-element.575), channel_id=1, source_target_pairs={{0,2},{1,3},{2,0},{3,1},{4,6},{5,7},{6,4},{7,5},{8,10},{9,11},{10,... | collective-permute-start | bytes 393224 | tf_op jit(solution)/shard_map/ppermute | solution.py:164
  463.5 7.4 %collective-permute-start.75 = (bf16[1,128,512]{2,1,0:T(8,128)(2,1)}, bf16[1,128,512]{2,1,0:T(8,128)(2,1)}, u32[]{:S(2)}, u32[]{:S(2)}) collective-permute-start(bf16[1,128,512]{2,1,0:T(8,128)(2,1)} %get-tuple-element.573), channel_id=1, source_target_pairs={{0,4},{1,5},{2,6},{3,7},{4,0},{5,1},{6,2},{7,3},{8,12},{9,13},{10,... | collective-permute-start | bytes 393224 | tf_op jit(solution)/shard_map/ppermute | solution.py:164
  464.3 11.2 %collective-permute-start.77 = (bf16[8,96,192]{2,1,0:T(8,128)(2,1)S(1)}, bf16[8,96,192]{2,1,0:T(8,128)(2,1)S(1)}, u32[]{:S(2)}, u32[]{:S(2)}) collective-permute-start(bf16[8,96,192]{2,1,0:T(8,128)(2,1)S(1)} %bitcast.182), channel_id=1, source_target_pairs={{0,16},{1,17},{2,18},{3,19},{4,20},{5,21},{6,22},{7,23},{8,24},{9,... | collective-permute-start | bytes 884744 | tf_op jit(solution)/shard_map/ppermute | solution.py:164
  480.6 9.1 %collective-permute-start.79 = (bf16[96,1536]{1,0:T(8,128)(2,1)}, bf16[96,1536]{1,0:T(8,128)(2,1)}, u32[]{:S(2)}, u32[]{:S(2)}) collective-permute-start(bf16[96,1536]{1,0:T(8,128)(2,1)} %add_convert_fusion.26), channel_id=1, source_target_pairs={{0,16},{1,17},{2,18},{3,19},{4,20},{5,21},{6,22},{7,23},{24,8},{25... | collective-permute-start | bytes 884744 | tf_op jit(solution)/shard_map/ppermute | solution.py:164
  (135 other events, 1041.6 us)
Sparse Core Ops, SparseCore 0:
  11.1 64.6 all-gather.4
  78.8 48.8 all-gather.6
  167.6 49.9 all-gather.8
  276.9 59.8 all-gather.10

commit v4 on v3

--- a/solution.py
+++ b/solution.py
@@ -1204,8 +1204,9 @@
     keep_heads, send_heads = head_weights(
         spots_rows, normed, tables, grad_queries, grad_own
     )
-    keep_heads, send_heads, grad_own, both_near, down_far = sync(
-        keep_heads, send_heads, grad_own, both_near, down_far
+    out_arrived = swap(grad_out_head, BIT_ZH, lacks_out)
+    keep_heads, send_heads, grad_own, both_near, down_far, out_arrived = sync(
+        keep_heads, send_heads, grad_own, both_near, down_far, out_arrived
     )
     both_far = swap(both_near, BIT_X)
     heads_first = swap(send_heads, BIT_ZH)
@@ -1216,19 +1217,18 @@
     sums, heads_sum = sync(sums, heads_sum)
     heads_sum = trade_block(heads_sum.reshape(2, 2, 2, 96, 192), 0, BIT_ZL)
     sums = scatter_next(sums, THIRDS, 2)
-    sums, heads_sum, grad_out_head = sync(sums, heads_sum, grad_out_head)
-    out_arrived = swap(grad_out_head, BIT_ZH, lacks_out)
+    sums, heads_sum = sync(sums, heads_sum)
+    out_sum = sum_low(grad_out_head, out_arrived)
+    out_far = swap(out_sum, BIT_X, owns_out)
     output = jnp.concatenate([part[0] for part in scatter_last(out_sums)], axis=1)
     output = (middle + output).astype(low)
     heads_sum = trade_block(heads_sum, 1, BIT_Y)
     sums = scatter_next(sums, THIRDS, 1)
-    sums, output, heads_sum = sync(sums, output, heads_sum)
+    sums, output, heads_sum, out_far = sync(sums, output, heads_sum, out_far)
     heads_near = trade_block(heads_sum, 2, BIT_C).reshape(8, 96, 192)
     heads_far = swap(heads_near, BIT_X)
     sums = scatter_next(sums, THIRDS, 0)
-    sums, heads_far, out_arrived = sync(sums, heads_far, out_arrived)
-    out_sum = sum_low(grad_out_head, out_arrived)
-    out_far = swap(out_sum, BIT_X, owns_out)
+    sums, heads_far = sync(sums, heads_far)
     scaled_first = jnp.concatenate([part[0] for part in scatter_last(sums)], axis=1)
     grad_inputs = grad_middle + scale_first * (
         scaled_first

time: 500 us -> 495 us (0.990)
  waiting for transfers between devices: 201 us -> 216 us
  other arithmetic: 43.7 us -> 32.7 us
    ppermute x80, waiting for transfers between devices: 166 us -> 181 us  [swap(): return lax.ppermute(value, AXES, pairs)]
    ppermute x80, starting transfers between devices: 102 us -> 96.8 us  [swap(): return lax.ppermute(value, AXES, pairs)]
    unnamed x232 -> x202, local copies, waits for them, and re-layouts: 14.2 us -> 11.6 us
  transfers between devices with their start and end apart: 84 -> 84, of which waited for: 47 -> 47; matrix products, arithmetic and copies ran while one was open for 7% -> 6% of each run, Pallas kernels for 19% -> 19%
where the time goes in v4:
time: 495 us; the launch traced here: 494 us
  waiting for transfers between devices  216 us (44%)
  Pallas kernels  117 us (24%)
  starting transfers between devices  97.1 us (20%)
  other arithmetic  32.7 us (7%)
  between operations  15.6 us (3%)
  local copies, waits for them, and re-layouts  15.1 us (3%)
    ppermute x80, waiting for transfers between devices, swap(): return lax.ppermute(value, AXES, pairs)  181 us
    pallas_call x19, Pallas kernels, kernel_call(): pl.pallas_call(body, out_shape=out_shape, grid_spec=pltpu.PrefetchScalarG...  117 us
    ppermute x80, starting transfers between devices, swap(): return lax.ppermute(value, AXES, pairs)  96.8 us
    all_gather x4, waiting for transfers between devices, cube_gather(): lax.all_gather(rows, AXES, axis=0, tiled=True, axis_index_groups=cube_gro...  34.9 us
    unnamed x202, local copies, waits for them, and re-layouts  11.6 us
    convert_element_type x24, other arithmetic, scatter_next(): sent = (kept[half:].astype(wide) + arrived[half:].astype(wide)).astype(low)  11.4 us
  transfers between devices with their start and end apart: 84, of which 47 were waited for; matrix products, arithmetic and copies ran while one was open for 6% of the time, Pallas kernels for 19%

profile of v4, /device:TPU:0, one launch (start us, length us, event | category | flops | bytes accessed | tf_op | source)
XLA Modules:
  0.0 493.7 jit_solution(1054334576792215966)
XLA Ops:
  9.1 1.9 multiply_convert_fusion
  14.0 3.0 collective-permute-start.1
  16.9 5.2 %collective-permute-start.3 = (bf16[96,1536]{1,0:T(8,128)(2,1)S(1)}, bf16[96,1536]{1,0:T(8,128)(2,1)}, u32[]{:S(2)}, u32[]{:S(2)}) collective-permute-start(bf16[96,1536]{1,0:T(8,128)(2,1)S(1)} %copy-done.91), channel_id=1, source_target_pairs={{0,8},{1,9},{2,10},{3,11},{4,12},{5,13},{6,14},{7,15},{24,16},{25,... | collective-permute-start | bytes 884744 | tf_op jit(solution)/shard_map/ppermute | solution.py:164
  22.3 1.8 collective-permute-start.2
  25.1 18.1 %collective-permute-done.2 = bf16[2,2,96,192]{3,2,1,0:T(8,128)(2,1)S(1)} collective-permute-done((bf16[2,2,96,192]{3,2,1,0:T(8,128)(2,1)S(1)}, bf16[2,2,96,192]{3,2,1,0:T(8,128)(2,1)S(1)}, u32[]{:S(2)}, u32[]{:S(2)}) %collective-permute-start.2) | collective-permute-done | bytes 147488 | tf_op jit(solution)/shard_map/ppermute | solution.py:164
  45.5 2.5 collective-permute-done.8
  48.3 8.1 %collective-permute-done.6 = bf16[2,2,96,512]{3,2,0,1:T(8,128)(2,1)S(1)} collective-permute-done((bf16[2,2,96,512]{3,2,0,1:T(8,128)(2,1)S(1)}, bf16[2,2,96,512]{3,2,0,1:T(8,128)(2,1)S(1)}, u32[]{:S(2)}, u32[]{:S(2)}) %collective-permute-start.6) | collective-permute-done | bytes 393248 | tf_op jit(solution)/shard_map/ppermute | solution.py:164
  56.5 2.6 collective-permute-start.7
  59.8 17.3 %collective-permute-done.7 = bf16[2,2,96,512]{3,2,1,0:T(8,128)(2,1)S(1)} collective-permute-done((bf16[2,2,96,512]{3,2,1,0:T(8,128)(2,1)S(1)}, bf16[2,2,96,512]{3,2,1,0:T(8,128)(2,1)S(1)}, u32[]{:S(2)}, u32[]{:S(2)}) %collective-permute-start.7) | collective-permute-done | bytes 393248 | tf_op jit(solution)/shard_map/ppermute | solution.py:164
  78.8 2.5 collective-permute-start.10
  81.4 7.8 %shard_map.215 = (bf16[2,96,1024]{2,1,0:T(8,128)(2,1)S(1)}, bf16[2,96,1024]{2,1,0:T(8,128)(2,1)S(1)}) custom-call(s32[9]{0:T(128)S(1)} %pad_add_fusion.at_ref, bf16[2048,1536]{1,0:T(8,128)(2,1)} %all-gather.5.cloned.1.call-done.rows_ref, bf16[1536,192]{1,0:T(8,128)(2,1)S(1)} %shard_map.214.w_ref, f32[48,1024]{1,0:T(8,128)S(1)} %get-tuple-element.283.cos_ref.rest_2_, ...), custom_call_target="tpu_custom_call" | custom-call | flops 1207959552 | bytes 8388608 | tf_op jit(solution)/shard_map/pallas_call | solution.py:296
  89.4 2.2 collective-permute-done.9
  91.7 2.1 collective-permute-start.13
  93.8 2.9 collective-permute-start.11
  96.7 14.2 %collective-permute-done.12 = bf16[2,128,768]{2,1,0:T(8,128)(2,1)S(1)} collective-permute-done((bf16[2,128,768]{2,1,0:T(8,128)(2,1)S(1)}, bf16[2,128,768]{2,1,0:T(8,128)(2,1)S(1)}, u32[]{:S(2)}, u32[]{:S(2)}) %collective-permute-start.12) | collective-permute-done | bytes 393248 | tf_op jit(solution)/shard_map/ppermute | solution.py:164
  113.0 2.3 collective-permute-done.14.c_ref.d_ref
  115.3 2.1 collective-permute-start.18
  118.2 3.1 collective-permute-start.16
  122.3 11.3 %shard_map.216 = (bf16[8,96,128]{2,1,0:T(8,128)(2,1)S(1)}, bf16[8,96,128]{2,1,0:T(8,128)(2,1)S(1)}, f32[2,96,1024]{2,1,0:T(8,128)S(1)}, f32[2,1,1024]{2,1,0:T(1,128)S(1)}) custom-call(s32[9]{0:T(128)S(1)} %pad_add_fusion.at_ref, bf16[2,96,1024]{2,1,0:T(8,128)(2,1)S(1)} %get-tuple-element.289.q_ref, bf16[2,96,1024]{2,1,0:T(8,128)(2,1)S(1)} %get-tuple-element.290.a_ref, ...), custom_call_target="tpu_custom_call" | custom-call | flops 1610612736 | bytes 12582912 | tf_op jit(solution)/shard_map/pallas_call | solution.py:296
  136.1 2.8 collective-permute-done.16.refs_2_
  142.8 2.2 collective-permute-done.17
  146.8 5.0 %collective-permute-start.24 = (bf16[256,1536]{1,0:T(8,128)(2,1)S(1)}, bf16[256,1536]{1,0:T(8,128)(2,1)S(1)}, u32[]{:S(2)}, u32[]{:S(2)}) collective-permute-start(bf16[256,1536]{1,0:T(8,128)(2,1)S(1)} %copy-done.82), channel_id=1, source_target_pairs={{0,8},{2,10},{4,12},{6,14},{9,1},{11,3},{13,5},{15,7},{17,25},{19,... | collective-permute-start | bytes 2359304 | tf_op jit(solution)/shard_map/ppermute | solution.py:164
  155.1 4.9 collective-permute-done.23
  161.3 3.9 shard_map.217
  167.8 3.5 collective-permute-start.25
  172.5 7.7 %shard_map.218.dh_ref = f32[2048,256]{1,0:T(8,128)} custom-call(s32[9]{0:T(128)S(1)} %pad_add_fusion.at_ref, bf16[8,128,768]{2,1,0:T(8,128)(2,1)S(1)} %pad_maximum_fusion.refs_0_, bf16[8,128,768]{2,1,0:T(8,128)(2,1)S(1)} %copy-done.2, bf16[8,128,768]{2,1,0:T(8,128)(2,1)S(1)} %pad_maximum_fusion.1.refs_2_, bf16[8,128,768]{2,1,0:T(8,128)(2,1)} %copy-done.75, ...), custom_call_target="tpu_custom_call" | custom-call | flops 1610612736 | bytes 8388608 | tf_op jit(solution)/shard_map/pallas_call | solution.py:296
  182.8 34.9 %all-gather.9.cloned.1.call-done.rows_ref = bf16[2048,1536]{1,0:T(8,128)(2,1)} async-done(((bf16[128,1536]{1,0:T(8,128)(2,1)}), bf16[2048,1536]{1,0:T(8,128)(2,1)}) %all-gather.9.cloned.1.call-update) | async-done | bytes 6291472 | tf_op jit(solution)/shard_map/all_gather | solution.py:216
  217.7 12.4 %shard_map.220 = (bf16[8,128,512]{2,1,0:T(8,128)(2,1)S(1)}, bf16[8,128,512]{2,1,0:T(8,128)(2,1)S(1)}, bf16[8,128,512]{2,1,0:T(8,128)(2,1)S(1)}, bf16[8,128,512]{...) custom-call(s32[9]{0:T(128)S(1)} %pad_add_fusion.at_ref, ...), custom_call_target="tpu_custom_call" | custom-call | flops 6442450944 | bytes 18874368 | tf_op jit(solution)/shard_map/pallas_call | solution.py:296
  230.9 1.9 collective-permute-done.26
  232.8 3.0 collective-permute-done.27
  239.9 9.5 %shard_map.221 = (bf16[8,96,512]{2,1,0:T(8,128)(2,1)S(1)}, bf16[8,96,512]{2,1,0:T(8,128)(2,1)S(1)}) custom-call(s32[25]{0:T(128)S(1)} %pad_add_fusion.2.at_ref, bf16[2048,1536]{1,0:T(8,128)(2,1)} %all-gather.9.cloned.1.call-done.rows_ref, bf16[2048,512]{1,0:T(8,128)(2,1)S(1)} %copy-done.70), custom_call_target="tpu_custom_call" | custom-call | flops 3221225472 | bytes 14680064 | tf_op jit(solution)/shard_map/pallas_call | solution.py:296
  256.6 3.4 collective-permute-done.32
  269.3 4.5 shard_map.222
  278.1 3.4 collective-permute-start.40
  283.0 7.1 %shard_map.223 = bf16[256,1536]{1,0:T(8,128)(2,1)S(1)} custom-call(s32[9]{0:T(128)S(1)} %pad_add_fusion.at_ref, bf16[8,128,768]{2,1,0:T(8,128)(2,1)S(1)} %pad_maximum_fusion.refs_0_, bf16[8,128,768]{2,1,0:T(8,128)(2,1)S(1)} %copy-done.3, bf16[8,128,768]{2,1,0:T(8,128)(2,1)} %copy-done, bf16[8,128,768]{2,1,0:T(8,128)(2,1)} %copy-done.75, ...), custom_call_target="tpu_custom_call" | custom-call | flops 1610612736 | bytes 8388608 | tf_op jit(solution)/shard_map/pallas_call | solution.py:296
  290.1 3.7 collective-permute-done.39
  293.8 5.9 %collective-permute-done.40 = bf16[4,96,512]{2,1,0:T(8,128)(2,1)S(1)} collective-permute-done((bf16[4,96,512]{2,1,0:T(8,128)(2,1)S(1)}, bf16[4,96,512]{2,1,0:T(8,128)(2,1)S(1)}, u32[]{:S(2)}, u32[]{:S(2)}) %collective-permute-start.40) | collective-permute-done | bytes 393248 | tf_op jit(solution)/shard_map/ppermute | solution.py:164
  300.4 5.4 %shard_map.224 = (bf16[8,128,768]{2,1,0:T(8,128)(2,1)S(1)}, bf16[8,128,768]{2,1,0:T(8,128)(2,1)S(1)}, bf16[8,128,768]{2,1,0:T(8,128)(2,1)}, bf16[8,128,768]{2,1,0:T(8,128)(2,1)}) custom-call(s32[9]{0:T(128)S(1)} %pad_add_fusion.at_ref, bf16[2048,256]{1,0:T(8,128)(2,1)S(1)} %copy-done.25, bf16[256,1536]{1,0:T(8,128)(2,1)S(1)} %copy-done.5), custom_call_target="tpu_custom_call" | custom-call | flops 1610612736 | bytes 8388608 | tf_op jit(solution)/shard_map/pallas_call | solution.py:296
  308.1 3.2 collective-permute-start.42
  311.5 18.0 %collective-permute-done.42 = bf16[2,2,2,96,128]{4,3,2,1,0:T(8,128)(2,1)S(1)} collective-permute-done((bf16[2,2,2,96,128]{4,3,2,1,0:T(8,128)(2,1)S(1)}, bf16[2,2,2,96,128]{4,3,2,1,0:T(8,128)(2,1)S(1)}, u32[]{:S(2)}, u32[]{:S(2)}) %collective-permute-start.42) | collective-permute-done | bytes 196640 | tf_op jit(solution)/shard_map/ppermute | solution.py:164
  336.1 2.6 collective-permute-start.49
  338.8 18.0 %shard_map.225 = (bf16[2,96,1024]{2,1,0:T(8,128)(2,1)S(1)}, bf16[2,2,96,1024]{3,2,1,0:T(8,128)(2,1)S(1)}, bf16[2,2,96,1024]{3,2,1,0:T(8,128)(2,1)S(1)}) custom-call(s32[9]{0:T(128)S(1)} %pad_add_fusion.at_ref, bf16[2,96,1024]{2,1,0:T(8,128)(2,1)S(1)} %copy-done.68, bf16[2,96,1024]{2,1,0:T(8,128)(2,1)S(1)} %copy-done.49, bf16[2,96,1024]{2,1,0:T(8,128)(2,1)S(1)} %copy-done.51, ...), custom_call_target="tpu_custom_call" | custom-call | flops 4026531840 | bytes 12582912 | tf_op jit(solution)/shard_map/pallas_call | solution.py:296
  357.6 1.7 collective-permute-done.50
  361.1 2.5 add_convert_fusion.21
  363.6 1.7 collective-permute-start.52
  366.8 3.2 collective-permute-start.51
  370.1 6.8 %shard_map.226 = bf16[96,1536]{1,0:T(8,128)(2,1)S(1)} custom-call(s32[9]{0:T(128)S(1)} %pad_add_fusion.at_ref, f32[2,96,1024]{2,1,0:T(8,128)S(1)} %copy-done.33, bf16[2048,1536]{1,0:T(8,128)(2,1)} %all-gather.11.cloned.1.call-done.rows_ref), custom_call_target="tpu_custom_call" | custom-call | flops 603979776 | bytes 8388608 | tf_op jit(solution)/shard_map/pallas_call | solution.py:296
  377.0 1.8 collective-permute-done.51
  382.7 5.1 %collective-permute-start.57 = (bf16[256,1536]{1,0:T(8,128)(2,1)S(1)}, bf16[256,1536]{1,0:T(8,128)(2,1)S(1)}, u32[]{:S(2)}, u32[]{:S(2)}) collective-permute-start(bf16[256,1536]{1,0:T(8,128)(2,1)S(1)} %add_convert_fusion), channel_id=1, source_target_pairs={{0,16},{2,18},{4,20},{6,22},{9,25},{11,27},{13,29},{15,31},{17,1},... | collective-permute-start | bytes 2359304 | tf_op jit(solution)/shard_map/ppermute | solution.py:164
  387.8 3.4 collective-permute-done.55
  391.3 5.6 %collective-permute-done.54 = bf16[96,1024]{1,0:T(8,128)(2,1)S(1)} collective-permute-done((bf16[96,1024]{1,0:T(8,128)(2,1)}, bf16[96,1024]{1,0:T(8,128)(2,1)S(1)}, u32[]{:S(2)}, u32[]{:S(2)}) %collective-permute-start.54) | collective-permute-done | bytes 196640 | tf_op jit(solution)/shard_map/ppermute | solution.py:164
  398.5 7.8 %shard_map.227 = (bf16[8,96,192]{2,1,0:T(8,128)(2,1)S(1)}, bf16[8,96,192]{2,1,0:T(8,128)(2,1)S(1)}) custom-call(s32[25]{0:T(128)S(1)} %copy-done.60, bf16[2048,1536]{1,0:T(8,128)(2,1)} %all-gather.5.cloned.1.call-done.rows_ref, f32[48,1024]{1,0:T(8,128)S(1)} %get-tuple-element.280.cos2_ref.cos_ref, f32[48,1024]{1,0:T(8,128)S(1)} %get-tuple-element.281.sin2_ref.sin_ref, ...), custom_call_target="tpu_custom_call" | custom-call | flops 1207959552 | bytes 8388608 | tf_op jit(solution)/shard_map/pallas_call | solution.py:296
  408.4 2.1 collective-permute-start.62
  410.9 3.5 collective-permute-start.74
  414.4 5.6 %shard_map.228 = (bf16[8,128,512]{2,1,0:T(8,128)(2,1)S(1)}, bf16[8,128,512]{2,1,0:T(8,128)(2,1)S(1)}, bf16[8,128,512]{2,1,0:T(8,128)(2,1)S(1)}, bf16[8,128,512]{...) custom-call(s32[9]{0:T(128)S(1)} %pad_add_fusion.at_ref, ...), custom_call_target="tpu_custom_call" | custom-call | flops 1207959552 | bytes 8388608 | tf_op jit(solution)/shard_map/pallas_call | solution.py:296
  420.0 10.7 %collective-permute-done.59 = bf16[8,96,192]{2,1,0:T(8,128)(2,1)S(1)} collective-permute-done((bf16[8,96,192]{2,1,0:T(8,128)(2,1)S(1)}, bf16[8,96,192]{2,1,0:T(8,128)(2,1)S(1)}, u32[]{:S(2)}, u32[]{:S(2)}) %collective-permute-start.59) | collective-permute-done | bytes 294944 | tf_op jit(solution)/shard_map/ppermute | solution.py:164
  432.7 2.2 collective-permute-done.63
  439.0 2.1 collective-permute-start.69
  441.1 14.1 %collective-permute-done.69 = bf16[2,2,96,192]{3,2,1,0:T(8,128)(2,1)S(1)} collective-permute-done((bf16[2,2,96,192]{3,2,1,0:T(8,128)(2,1)S(1)}, bf16[2,2,96,192]{3,2,1,0:T(8,128)(2,1)S(1)}, u32[]{:S(2)}, u32[]{:S(2)}) %collective-permute-start.69) | collective-permute-done | bytes 147488 | tf_op jit(solution)/shard_map/ppermute | solution.py:164
  455.8 1.8 collective-permute-start.73
  460.2 3.1 shard_map.230
  463.9 3.4 collective-permute-done.73
  475.0 6.7 %collective-permute-done.79.far_ref = bf16[8,96,192]{2,1,0:T(8,128)(2,1)S(1)} collective-permute-done((bf16[8,96,192]{2,1,0:T(8,128)(2,1)S(1)}, bf16[8,96,192]{2,1,0:T(8,128)(2,1)S(1)}, u32[]{:S(2)}, u32[]{:S(2)}) %collective-permute-start.79) | collective-permute-done | bytes 294944 | tf_op jit(solution)/shard_map/ppermute | solution.py:164
  482.2 3.3 shard_map.229
  (457 shorter events, 102.0 us)
Async XLA Ops:
  7.2 71.4 %all-gather.5.cloned.1.call-start = ((), (), s32[]{:S(2)}) async-start(), calls=%async_computation | async-start | bytes 6684672 | tf_op jit(solution)/shard_map/all_gather | solution.py:216
  11.0 123.6 %all-gather.7.cloned.1.call-start = ((), (), s32[]{:S(2)}) async-start(), calls=%async_computation.1 | async-start | bytes 5013504 | tf_op jit(solution)/shard_map/all_gather | solution.py:216
  14.0 8.2 %collective-permute-start.1 = (bf16[2,2,96,192]{3,2,0,1:T(8,128)(2,1)S(1)}, bf16[2,2,96,192]{3,2,0,1:T(8,128)(2,1)S(1)}, u32[]{:S(2)}, u32[]{:S(2)}) collective-permute-start(bf16[2,2,96,192]{3,2,0,1:T(8,128)(2,1)S(1)} %get-tuple-element.610), channel_id=1, source_target_pairs={{0,2},{1,3},{2,0},{3,1},{4,6},{5,7},{6,4},{7,5},{8,10},{9,11},{10,... | collective-permute-start | bytes 442376 | tf_op jit(solution)/shard_map/ppermute | solution.py:164
  16.9 26.3 %collective-permute-start.3 = (bf16[96,1536]{1,0:T(8,128)(2,1)S(1)}, bf16[96,1536]{1,0:T(8,128)(2,1)}, u32[]{:S(2)}, u32[]{:S(2)}) collective-permute-start(bf16[96,1536]{1,0:T(8,128)(2,1)S(1)} %copy-done.91), channel_id=1, source_target_pairs={{0,8},{1,9},{2,10},{3,11},{4,12},{5,13},{6,14},{7,15},{24,16},{25,... | collective-permute-start | bytes 884744 | tf_op jit(solution)/shard_map/ppermute | solution.py:164
  22.3 20.8 %collective-permute-start.2 = (bf16[2,2,96,192]{3,2,1,0:T(8,128)(2,1)S(1)}, bf16[2,2,96,192]{3,2,1,0:T(8,128)(2,1)S(1)}, u32[]{:S(2)}, u32[]{:S(2)}) collective-permute-start(bf16[2,2,96,192]{3,2,1,0:T(8,128)(2,1)S(1)} %get-tuple-element.608), channel_id=1, source_target_pairs={{0,4},{1,5},{2,6},{3,7},{4,0},{5,1},{6,2},{7,3},{8,12},{9,13},{10,... | collective-permute-start | bytes 442376 | tf_op jit(solution)/shard_map/ppermute | solution.py:164
  45.2 11.2 %collective-permute-start.6 = (bf16[2,2,96,512]{3,2,0,1:T(8,128)(2,1)S(1)}, bf16[2,2,96,512]{3,2,0,1:T(8,128)(2,1)S(1)}, u32[]{:S(2)}, u32[]{:S(2)}) collective-permute-start(bf16[2,2,96,512]{3,2,0,1:T(8,128)(2,1)S(1)} %get-tuple-element.570), channel_id=1, source_target_pairs={{0,2},{1,3},{2,0},{3,1},{4,6},{5,7},{6,4},{7,5},{8,10},{9,11},{10,... | collective-permute-start | bytes 1179656 | tf_op jit(solution)/shard_map/ppermute | solution.py:164
  48.3 29.7 %collective-permute-start.4 = (bf16[8,96,192]{2,1,0:T(8,128)(2,1)S(1)}, bf16[8,96,192]{2,1,0:T(8,128)(2,1)S(1)}, u32[]{:S(2)}, u32[]{:S(2)}) collective-permute-start(bf16[8,96,192]{2,1,0:T(8,128)(2,1)S(1)} %bitcast.180), channel_id=1, source_target_pairs={{0,8},{1,9},{2,10},{3,11},{4,12},{5,13},{6,14},{7,15},{8,0},{9,1},... | collective-permute-start | bytes 884744 | tf_op jit(solution)/shard_map/ppermute | solution.py:164
  56.5 20.6 %collective-permute-start.7 = (bf16[2,2,96,512]{3,2,1,0:T(8,128)(2,1)S(1)}, bf16[2,2,96,512]{3,2,1,0:T(8,128)(2,1)S(1)}, u32[]{:S(2)}, u32[]{:S(2)}) collective-permute-start(bf16[2,2,96,512]{3,2,1,0:T(8,128)(2,1)S(1)} %get-tuple-element.568), channel_id=1, source_target_pairs={{0,4},{1,5},{2,6},{3,7},{4,0},{5,1},{6,2},{7,3},{8,12},{9,13},{10,... | collective-permute-start | bytes 1179656 | tf_op jit(solution)/shard_map/ppermute | solution.py:164
  78.7 139.0 %all-gather.9.cloned.1.call-start = ((), (), s32[]{:S(2)}) async-start(), calls=%async_computation.2 | async-start | bytes 6684672 | tf_op jit(solution)/shard_map/all_gather | solution.py:216
  78.8 10.5 %collective-permute-start.10 = (bf16[1,128,768]{2,1,0:T(8,128)(2,1)S(1)}, bf16[1,128,768]{2,1,0:T(8,128)(2,1)S(1)}, u32[]{:S(2)}, u32[]{:S(2)}) collective-permute-start(bf16[1,128,768]{2,1,0:T(8,128)(2,1)S(1)} %get-tuple-element.605), channel_id=1, source_target_pairs={{0,4},{1,5},{2,6},{3,7},{4,0},{5,1},{6,2},{7,3},{8,12},{9,13},{10,... | collective-permute-start | bytes 589832 | tf_op jit(solution)/shard_map/ppermute | solution.py:164
  81.4 10.1 %collective-permute-start.9 = (bf16[1,128,768]{2,1,0:T(8,128)(2,1)S(1)}, bf16[1,128,768]{2,1,0:T(8,128)(2,1)S(1)}, u32[]{:S(2)}, u32[]{:S(2)}) collective-permute-start(bf16[1,128,768]{2,1,0:T(8,128)(2,1)S(1)} %get-tuple-element.606), channel_id=1, source_target_pairs={{0,4},{1,5},{2,6},{3,7},{4,0},{5,1},{6,2},{7,3},{8,12},{9,13},{10,... | collective-permute-start | bytes 589832 | tf_op jit(solution)/shard_map/ppermute | solution.py:164
  91.6 19.3 %collective-permute-start.12 = (bf16[2,128,768]{2,1,0:T(8,128)(2,1)S(1)}, bf16[2,128,768]{2,1,0:T(8,128)(2,1)S(1)}, u32[]{:S(2)}, u32[]{:S(2)}) collective-permute-start(bf16[2,128,768]{2,1,0:T(8,128)(2,1)S(1)} %pad_maximum_fusion.15), channel_id=1, source_target_pairs={{0,16},{1,17},{2,18},{3,19},{4,20},{5,21},{6,22},{7,23},{8,24},{9,... | collective-permute-start | bytes 1179656 | tf_op jit(solution)/shard_map/ppermute | solution.py:164
  91.7 20.2 %collective-permute-start.13 = (bf16[2,128,768]{2,1,0:T(8,128)(2,1)S(1)}, bf16[2,128,768]{2,1,0:T(8,128)(2,1)S(1)}, u32[]{:S(2)}, u32[]{:S(2)}) collective-permute-start(bf16[2,128,768]{2,1,0:T(8,128)(2,1)S(1)} %pad_maximum_fusion.16), channel_id=1, source_target_pairs={{0,2},{1,3},{2,0},{3,1},{4,6},{5,7},{6,4},{7,5},{8,10},{9,11},{10,... | collective-permute-start | bytes 1179656 | tf_op jit(solution)/shard_map/ppermute | solution.py:164
  93.8 19.0 %collective-permute-start.11 = (bf16[2,96,1024]{2,1,0:T(8,128)(2,1)S(1)}, bf16[2,96,1024]{2,1,0:T(8,128)(2,1)S(1)}, u32[]{:S(2)}, u32[]{:S(2)}) collective-permute-start(bf16[2,96,1024]{2,1,0:T(8,128)(2,1)S(1)} %get-tuple-element.290.a_ref), channel_id=1, source_target_pairs={{0,8},{1,9},{2,10},{3,11},{4,12},{5,13},{6,14},{7,15},{8,0},{9,1},... | collective-permute-start | bytes 1179656 | tf_op jit(solution)/shard_map/ppermute | solution.py:164
  115.3 24.5 %collective-permute-start.18 = (bf16[4,128,768]{2,1,0:T(8,128)(2,1)}, bf16[4,128,768]{2,1,0:T(8,128)(2,1)}, u32[]{:S(2)}, u32[]{:S(2)}) collective-permute-start(bf16[4,128,768]{2,1,0:T(8,128)(2,1)} %pad_maximum_fusion.3), channel_id=1, source_target_pairs={{0,2},{1,3},{2,0},{3,1},{4,6},{5,7},{6,4},{7,5},{8,10},{9,11},{10,... | collective-permute-start | bytes 2359304 | tf_op jit(solution)/shard_map/ppermute | solution.py:164
  118.2 20.7 %collective-permute-start.16 = (bf16[4,96,512]{2,1,0:T(8,128)(2,1)S(1)}, bf16[4,96,512]{2,1,0:T(8,128)(2,1)S(1)}, u32[]{:S(2)}, u32[]{:S(2)}) collective-permute-start(bf16[4,96,512]{2,1,0:T(8,128)(2,1)S(1)} %bitcast.186), channel_id=1, source_target_pairs={{0,8},{1,9},{2,10},{3,11},{4,12},{5,13},{6,14},{7,15},{8,0},{9,1},... | collective-permute-start | bytes 1179656 | tf_op jit(solution)/shard_map/ppermute | solution.py:164
  121.2 20.1 %collective-permute-start.19 = (bf16[4,128,768]{2,1,0:T(8,128)(2,1)}, bf16[4,128,768]{2,1,0:T(8,128)(2,1)}, u32[]{:S(2)}, u32[]{:S(2)}) collective-permute-start(bf16[4,128,768]{2,1,0:T(8,128)(2,1)} %pad_maximum_fusion.4), channel_id=1, source_target_pairs={{0,16},{1,17},{2,18},{3,19},{4,20},{5,21},{6,22},{7,23},{8,24},{9,... | collective-permute-start | bytes 2359304 | tf_op jit(solution)/shard_map/ppermute | solution.py:164
  138.9 6.2 %collective-permute-start.17 = (bf16[2,2,2,96,128]{4,3,0,2,1:T(8,128)(2,1)S(1)}, bf16[2,2,2,96,128]{4,3,0,2,1:T(8,128)(2,1)S(1)}, u32[]{:S(2)}, u32[]{:S(2)}) collective-permute-start(bf16[2,2,2,96,128]{4,3,0,2,1:T(8,128)(2,1)S(1)} %get-tuple-element.604), channel_id=1, source_target_pairs={{0,4},{1,5},{2,6},{3,7},{4,0},{5,1},{6,2},{7,3},{8,12},{9,13},{10,... | collective-permute-start | bytes 589832 | tf_op jit(solution)/shard_map/ppermute | solution.py:164
  145.1 7.6 %collective-permute-start.21 = (bf16[8,128,768]{2,1,0:T(8,128)(2,1)S(1)}, bf16[8,128,768]{2,1,0:T(8,128)(2,1)S(1)}, u32[]{:S(2)}, u32[]{:S(2)}) collective-permute-start(bf16[8,128,768]{2,1,0:T(8,128)(2,1)S(1)} %pad_maximum_fusion.refs_0_), channel_id=1, source_target_pairs={{0,1},{1,0},{2,3},{3,2},{4,5},{5,4},{6,7},{7,6},{8,9},{9,8},{10,11... | collective-permute-start | bytes 4718600 | tf_op jit(solution)/shard_map/ppermute | solution.py:164
  145.2 8.7 %collective-permute-start.22 = (bf16[8,128,768]{2,1,0:T(8,128)(2,1)S(1)}, bf16[8,128,768]{2,1,0:T(8,128)(2,1)S(1)}, u32[]{:S(2)}, u32[]{:S(2)}) collective-permute-start(bf16[8,128,768]{2,1,0:T(8,128)(2,1)S(1)} %pad_maximum_fusion.1.refs_2_), channel_id=1, source_target_pairs={{0,1},{1,0},{2,3},{3,2},{4,5},{5,4},{6,7},{7,6},{8,9},{9,8},{10,11... | collective-permute-start | bytes 4718600 | tf_op jit(solution)/shard_map/ppermute | solution.py:164
  145.7 7.0 %collective-permute-start.20 = (bf16[2,2,2,96,128]{4,3,1,0,2:T(8,128)(2,1)S(1)}, bf16[2,2,2,96,128]{4,3,1,0,2:T(8,128)(2,1)S(1)}, u32[]{:S(2)}, u32[]{:S(2)}) collective-permute-start(bf16[2,2,2,96,128]{4,3,1,0,2:T(8,128)(2,1)S(1)} %get-tuple-element.602), channel_id=1, source_target_pairs={{0,16},{1,17},{2,18},{3,19},{4,20},{5,21},{6,22},{7,23},{8,24},{9,... | collective-permute-start | bytes 589832 | tf_op jit(solution)/shard_map/ppermute | solution.py:164
  146.8 14.5 %collective-permute-start.24 = (bf16[256,1536]{1,0:T(8,128)(2,1)S(1)}, bf16[256,1536]{1,0:T(8,128)(2,1)S(1)}, u32[]{:S(2)}, u32[]{:S(2)}) collective-permute-start(bf16[256,1536]{1,0:T(8,128)(2,1)S(1)} %copy-done.82), channel_id=1, source_target_pairs={{0,8},{2,10},{4,12},{6,14},{9,1},{11,3},{13,5},{15,7},{17,25},{19,... | collective-permute-start | bytes 2359304 | tf_op jit(solution)/shard_map/ppermute | solution.py:164
  153.9 6.1 %collective-permute-start.23 = (bf16[2,2,2,96,128]{4,3,2,1,0:T(8,128)(2,1)S(1)}, bf16[2,2,2,96,128]{4,3,2,1,0:T(8,128)(2,1)S(1)}, u32[]{:S(2)}, u32[]{:S(2)}) collective-permute-start(bf16[2,2,2,96,128]{4,3,2,1,0:T(8,128)(2,1)S(1)} %get-tuple-element.600), channel_id=1, source_target_pairs={{0,2},{1,3},{2,0},{3,1},{4,6},{5,7},{6,4},{7,5},{8,10},{9,11},{10,... | collective-permute-start | bytes 589832 | tf_op jit(solution)/shard_map/ppermute | solution.py:164
  167.5 193.6 %all-gather.11.cloned.1.call-start = ((), (), s32[]{:S(2)}) async-start(), calls=%async_computation.3 | async-start | bytes 6684672 | tf_op jit(solution)/shard_map/all_gather | solution.py:216
  167.8 13.2 %collective-permute-start.25 = (bf16[4,96,512]{2,1,0:T(8,128)(2,1)}, bf16[4,96,512]{2,1,0:T(8,128)(2,1)S(1)}, u32[]{:S(2)}, u32[]{:S(2)}) collective-permute-start(bf16[4,96,512]{2,1,0:T(8,128)(2,1)} %bitcast.184), channel_id=1, source_target_pairs={{0,8},{1,9},{2,10},{3,11},{4,12},{5,13},{6,14},{7,15},{8,0},{9,1},... | collective-permute-start | bytes 1179656 | tf_op jit(solution)/shard_map/ppermute | solution.py:164
  236.3 14.1 %collective-permute-start.29 = (bf16[4,128,512]{2,1,0:T(8,128)(2,1)S(1)}, bf16[4,128,512]{2,1,0:T(8,128)(2,1)S(1)}, u32[]{:S(2)}, u32[]{:S(2)}) collective-permute-start(bf16[4,128,512]{2,1,0:T(8,128)(2,1)S(1)} %get-tuple-element.539), channel_id=1, source_target_pairs={{0,4},{1,5},{2,6},{3,7},{4,0},{5,1},{6,2},{7,3},{8,12},{9,13},{10,... | collective-permute-start | bytes 1572872 | tf_op jit(solution)/shard_map/ppermute | solution.py:164
  237.3 13.9 %collective-permute-start.30 = (bf16[4,128,512]{2,1,0:T(8,128)(2,1)S(1)}, bf16[4,128,512]{2,1,0:T(8,128)(2,1)S(1)}, u32[]{:S(2)}, u32[]{:S(2)}) collective-permute-start(bf16[4,128,512]{2,1,0:T(8,128)(2,1)S(1)} %get-tuple-element.537), channel_id=1, source_target_pairs={{0,16},{1,17},{2,18},{3,19},{4,20},{5,21},{6,22},{7,23},{8,24},{9,... | collective-permute-start | bytes 1572872 | tf_op jit(solution)/shard_map/ppermute | solution.py:164
  239.2 13.6 %collective-permute-start.31 = (bf16[4,128,512]{2,1,0:T(8,128)(2,1)S(1)}, bf16[4,128,512]{2,1,0:T(8,128)(2,1)S(1)}, u32[]{:S(2)}, u32[]{:S(2)}) collective-permute-start(bf16[4,128,512]{2,1,0:T(8,128)(2,1)S(1)} %get-tuple-element.535), channel_id=1, source_target_pairs={{0,2},{1,3},{2,0},{3,1},{4,6},{5,7},{6,4},{7,5},{8,10},{9,11},{10,... | collective-permute-start | bytes 1572872 | tf_op jit(solution)/shard_map/ppermute | solution.py:164
  252.9 7.1 %collective-permute-start.32 = (bf16[2,128,512]{2,1,0:T(8,128)(2,1)S(1)}, bf16[2,128,512]{2,1,0:T(8,128)(2,1)S(1)}, u32[]{:S(2)}, u32[]{:S(2)}) collective-permute-start(bf16[2,128,512]{2,1,0:T(8,128)(2,1)S(1)} %get-tuple-element.555), channel_id=1, source_target_pairs={{0,2},{1,3},{2,0},{3,1},{4,6},{5,7},{6,4},{7,5},{8,10},{9,11},{10,... | collective-permute-start | bytes 786440 | tf_op jit(solution)/shard_map/ppermute | solution.py:164
  253.7 6.8 %collective-permute-start.33 = (bf16[2,128,512]{2,1,0:T(8,128)(2,1)S(1)}, bf16[2,128,512]{2,1,0:T(8,128)(2,1)S(1)}, u32[]{:S(2)}, u32[]{:S(2)}) collective-permute-start(bf16[2,128,512]{2,1,0:T(8,128)(2,1)S(1)} %get-tuple-element.553), channel_id=1, source_target_pairs={{0,4},{1,5},{2,6},{3,7},{4,0},{5,1},{6,2},{7,3},{8,12},{9,13},{10,... | collective-permute-start | bytes 786440 | tf_op jit(solution)/shard_map/ppermute | solution.py:164
  255.0 6.5 %collective-permute-start.34 = (bf16[2,128,512]{2,1,0:T(8,128)(2,1)S(1)}, bf16[2,128,512]{2,1,0:T(8,128)(2,1)S(1)}, u32[]{:S(2)}, u32[]{:S(2)}) collective-permute-start(bf16[2,128,512]{2,1,0:T(8,128)(2,1)S(1)} %get-tuple-element.551), channel_id=1, source_target_pairs={{0,16},{1,17},{2,18},{3,19},{4,20},{5,21},{6,22},{7,23},{8,24},{9,... | collective-permute-start | bytes 786440 | tf_op jit(solution)/shard_map/ppermute | solution.py:164
  278.1 21.5 %collective-permute-start.40 = (bf16[4,96,512]{2,1,0:T(8,128)(2,1)S(1)}, bf16[4,96,512]{2,1,0:T(8,128)(2,1)S(1)}, u32[]{:S(2)}, u32[]{:S(2)}) collective-permute-start(bf16[4,96,512]{2,1,0:T(8,128)(2,1)S(1)} %slice.516), channel_id=1, source_target_pairs={{0,8},{1,9},{2,10},{3,11},{4,12},{5,13},{6,14},{7,15},{8,0},{9,1},... | collective-permute-start | bytes 1179656 | tf_op jit(solution)/shard_map/ppermute | solution.py:164
  282.6 11.2 %collective-permute-start.39 = (bf16[2,2,2,96,128]{4,3,0,2,1:T(8,128)(2,1)S(1)}, bf16[2,2,2,96,128]{4,3,0,2,1:T(8,128)(2,1)S(1)}, u32[]{:S(2)}, u32[]{:S(2)}) collective-permute-start(bf16[2,2,2,96,128]{4,3,0,2,1:T(8,128)(2,1)S(1)} %get-tuple-element.598), channel_id=1, source_target_pairs={{0,16},{1,17},{2,18},{3,19},{4,20},{5,21},{6,22},{7,23},{8,24},{9,... | collective-permute-start | bytes 589832 | tf_op jit(solution)/shard_map/ppermute | solution.py:164
  299.7 6.6 %collective-permute-start.41 = (bf16[2,2,2,96,128]{4,3,1,0,2:T(8,128)(2,1)S(1)}, bf16[2,2,2,96,128]{4,3,1,0,2:T(8,128)(2,1)S(1)}, u32[]{:S(2)}, u32[]{:S(2)}) collective-permute-start(bf16[2,2,2,96,128]{4,3,1,0,2:T(8,128)(2,1)S(1)} %get-tuple-element.596), channel_id=1, source_target_pairs={{0,2},{1,3},{2,0},{3,1},{4,6},{5,7},{6,4},{7,5},{8,10},{9,11},{10,... | collective-permute-start | bytes 589832 | tf_op jit(solution)/shard_map/ppermute | solution.py:164
  306.4 23.2 %collective-permute-start.43 = (bf16[8,128,768]{2,1,0:T(8,128)(2,1)S(1)}, bf16[8,128,768]{2,1,0:T(8,128)(2,1)S(1)}, u32[]{:S(2)}, u32[]{:S(2)}) collective-permute-start(bf16[8,128,768]{2,1,0:T(8,128)(2,1)S(1)} %get-tuple-element.406), channel_id=1, source_target_pairs={{0,1},{1,0},{2,3},{3,2},{4,5},{5,4},{6,7},{7,6},{8,9},{9,8},{10,11... | collective-permute-start | bytes 4718600 | tf_op jit(solution)/shard_map/ppermute | solution.py:164
  306.4 23.1 %collective-permute-start.44 = (bf16[8,128,768]{2,1,0:T(8,128)(2,1)}, bf16[8,128,768]{2,1,0:T(8,128)(2,1)S(1)}, u32[]{:S(2)}, u32[]{:S(2)}) collective-permute-start(bf16[8,128,768]{2,1,0:T(8,128)(2,1)} %get-tuple-element.408), channel_id=1, source_target_pairs={{0,1},{1,0},{2,3},{3,2},{4,5},{5,4},{6,7},{7,6},{8,9},{9,8},{10,11... | collective-permute-start | bytes 4718600 | tf_op jit(solution)/shard_map/ppermute | solution.py:164
  307.0 22.6 %collective-permute-start.45 = (bf16[4,96,512]{2,1,0:T(8,128)(2,1)S(1)}, bf16[4,96,512]{2,1,0:T(8,128)(2,1)S(1)}, u32[]{:S(2)}, u32[]{:S(2)}) collective-permute-start(bf16[4,96,512]{2,1,0:T(8,128)(2,1)S(1)} %slice.521), channel_id=1, source_target_pairs={{0,8},{1,9},{2,10},{3,11},{4,12},{5,13},{6,14},{7,15},{8,0},{9,1},... | collective-permute-start | bytes 1179656 | tf_op jit(solution)/shard_map/ppermute | solution.py:164
  308.1 21.4 %collective-permute-start.42 = (bf16[2,2,2,96,128]{4,3,2,1,0:T(8,128)(2,1)S(1)}, bf16[2,2,2,96,128]{4,3,2,1,0:T(8,128)(2,1)S(1)}, u32[]{:S(2)}, u32[]{:S(2)}) collective-permute-start(bf16[2,2,2,96,128]{4,3,2,1,0:T(8,128)(2,1)S(1)} %get-tuple-element.594), channel_id=1, source_target_pairs={{0,4},{1,5},{2,6},{3,7},{4,0},{5,1},{6,2},{7,3},{8,12},{9,13},{10,... | collective-permute-start | bytes 589832 | tf_op jit(solution)/shard_map/ppermute | solution.py:164
  329.6 27.2 %collective-permute-start.48 = (bf16[256,1536]{1,0:T(8,128)(2,1)S(1)}, bf16[256,1536]{1,0:T(8,128)(2,1)S(1)}, u32[]{:S(2)}, u32[]{:S(2)}) collective-permute-start(bf16[256,1536]{1,0:T(8,128)(2,1)S(1)} %shard_map.223), channel_id=1, source_target_pairs={{1,9},{3,11},{5,13},{7,15},{8,0},{10,2},{12,4},{14,6},{16,24},{18,... | collective-permute-start | bytes 2359304 | tf_op jit(solution)/shard_map/ppermute | solution.py:164
  332.6 24.2 %collective-permute-start.46 = (bf16[4,128,768]{2,1,0:T(8,128)(2,1)S(1)}, bf16[4,128,768]{2,1,0:T(8,128)(2,1)S(1)}, u32[]{:S(2)}, u32[]{:S(2)}) collective-permute-start(bf16[4,128,768]{2,1,0:T(8,128)(2,1)S(1)} %get-tuple-element.527), channel_id=1, source_target_pairs={{0,2},{1,3},{2,0},{3,1},{4,6},{5,7},{6,4},{7,5},{8,10},{9,11},{10,... | collective-permute-start | bytes 2359304 | tf_op jit(solution)/shard_map/ppermute | solution.py:164
  334.9 21.9 %collective-permute-start.47 = (bf16[4,128,768]{2,1,0:T(8,128)(2,1)S(1)}, bf16[4,128,768]{2,1,0:T(8,128)(2,1)S(1)}, u32[]{:S(2)}, u32[]{:S(2)}) collective-permute-start(bf16[4,128,768]{2,1,0:T(8,128)(2,1)S(1)} %get-tuple-element.525), channel_id=1, source_target_pairs={{0,16},{1,17},{2,18},{3,19},{4,20},{5,21},{6,22},{7,23},{8,24},{9,... | collective-permute-start | bytes 2359304 | tf_op jit(solution)/shard_map/ppermute | solution.py:164
  336.1 20.7 %collective-permute-start.49 = (bf16[4,96,512]{2,1,0:T(8,128)(2,1)S(1)}, bf16[4,96,512]{2,1,0:T(8,128)(2,1)S(1)}, u32[]{:S(2)}, u32[]{:S(2)}) collective-permute-start(bf16[4,96,512]{2,1,0:T(8,128)(2,1)S(1)} %add_convert_fusion.25), channel_id=1, source_target_pairs={{0,4},{1,5},{2,6},{3,7},{4,0},{5,1},{6,2},{7,3},{8,12},{9,13},{10,... | collective-permute-start | bytes 1179656 | tf_op jit(solution)/shard_map/ppermute | solution.py:164
  363.6 15.2 %collective-permute-start.52 = (bf16[2,128,768]{2,1,0:T(8,128)(2,1)}, bf16[2,128,768]{2,1,0:T(8,128)(2,1)}, u32[]{:S(2)}, u32[]{:S(2)}) collective-permute-start(bf16[2,128,768]{2,1,0:T(8,128)(2,1)} %get-tuple-element.543), channel_id=1, source_target_pairs={{0,16},{1,17},{2,18},{3,19},{4,20},{5,21},{6,22},{7,23},{8,24},{9,... | collective-permute-start | bytes 1179656 | tf_op jit(solution)/shard_map/ppermute | solution.py:164
  366.5 12.3 %collective-permute-start.53 = (bf16[2,128,768]{2,1,0:T(8,128)(2,1)}, bf16[2,128,768]{2,1,0:T(8,128)(2,1)}, u32[]{:S(2)}, u32[]{:S(2)}) collective-permute-start(bf16[2,128,768]{2,1,0:T(8,128)(2,1)} %get-tuple-element.541), channel_id=1, source_target_pairs={{0,2},{1,3},{2,0},{3,1},{4,6},{5,7},{6,4},{7,5},{8,10},{9,11},{10,... | collective-permute-start | bytes 1179656 | tf_op jit(solution)/shard_map/ppermute | solution.py:164
  366.8 12.0 %collective-permute-start.51 = (bf16[96,1024]{1,0:T(8,128)(2,1)S(1)}, bf16[96,1024]{1,0:T(8,128)(2,1)S(1)}, u32[]{:S(2)}, u32[]{:S(2)}) collective-permute-start(bf16[96,1024]{1,0:T(8,128)(2,1)S(1)} %get-tuple-element.435), channel_id=1, source_target_pairs={{0,8},{1,9},{2,10},{3,11},{4,12},{5,13},{6,14},{7,15},{8,0},{9,1},... | collective-permute-start | bytes 589832 | tf_op jit(solution)/shard_map/ppermute | solution.py:164
  378.8 18.1 %collective-permute-start.54 = (bf16[96,1024]{1,0:T(8,128)(2,1)}, bf16[96,1024]{1,0:T(8,128)(2,1)S(1)}, u32[]{:S(2)}, u32[]{:S(2)}) collective-permute-start(bf16[96,1024]{1,0:T(8,128)(2,1)} %get-tuple-element.446), channel_id=1, source_target_pairs={{0,8},{1,9},{2,10},{3,11},{4,12},{5,13},{6,14},{7,15},{8,0},{9,1},... | collective-permute-start | bytes 589832 | tf_op jit(solution)/shard_map/ppermute | solution.py:164
  380.1 26.3 %collective-permute-start.58 = (bf16[96,1536]{1,0:T(8,128)(2,1)S(1)}, bf16[96,1536]{1,0:T(8,128)(2,1)S(1)}, u32[]{:S(2)}, u32[]{:S(2)}) collective-permute-start(bf16[96,1536]{1,0:T(8,128)(2,1)S(1)} %shard_map.226), channel_id=1, source_target_pairs={{8,0},{9,1},{10,2},{11,3},{12,4},{13,5},{14,6},{15,7},{16,24},{17,... | collective-permute-start | bytes 884744 | tf_op jit(solution)/shard_map/ppermute | solution.py:164
  381.4 9.8 %collective-permute-start.55 = (bf16[2,2,96,512]{3,2,0,1:T(8,128)(2,1)S(1)}, bf16[2,2,96,512]{3,2,0,1:T(8,128)(2,1)S(1)}, u32[]{:S(2)}, u32[]{:S(2)}) collective-permute-start(bf16[2,2,96,512]{3,2,0,1:T(8,128)(2,1)S(1)} %bitcast.204), channel_id=1, source_target_pairs={{0,2},{1,3},{2,0},{3,1},{4,6},{5,7},{6,4},{7,5},{8,10},{9,11},{10,... | collective-permute-start | bytes 1179656 | tf_op jit(solution)/shard_map/ppermute | solution.py:164
  382.7 23.6 %collective-permute-start.57 = (bf16[256,1536]{1,0:T(8,128)(2,1)S(1)}, bf16[256,1536]{1,0:T(8,128)(2,1)S(1)}, u32[]{:S(2)}, u32[]{:S(2)}) collective-permute-start(bf16[256,1536]{1,0:T(8,128)(2,1)S(1)} %add_convert_fusion), channel_id=1, source_target_pairs={{0,16},{2,18},{4,20},{6,22},{9,25},{11,27},{13,29},{15,31},{17,1},... | collective-permute-start | bytes 2359304 | tf_op jit(solution)/shard_map/ppermute | solution.py:164
  397.0 9.3 %collective-permute-start.56 = (bf16[2,2,96,512]{3,2,1,0:T(8,128)(2,1)S(1)}, bf16[2,2,96,512]{3,2,1,0:T(8,128)(2,1)S(1)}, u32[]{:S(2)}, u32[]{:S(2)}) collective-permute-start(bf16[2,2,96,512]{3,2,1,0:T(8,128)(2,1)S(1)} %get-tuple-element.562), channel_id=1, source_target_pairs={{0,1},{1,0},{2,3},{3,2},{4,5},{5,4},{6,7},{7,6},{8,9},{9,8},{10,11... | collective-permute-start | bytes 1179656 | tf_op jit(solution)/shard_map/ppermute | solution.py:164
  398.2 21.8 %collective-permute-start.61 = (bf16[1,128,768]{2,1,0:T(8,128)(2,1)S(1)}, bf16[1,128,768]{2,1,0:T(8,128)(2,1)S(1)}, u32[]{:S(2)}, u32[]{:S(2)}) collective-permute-start(bf16[1,128,768]{2,1,0:T(8,128)(2,1)S(1)} %get-tuple-element.559), channel_id=1, source_target_pairs={{0,4},{1,5},{2,6},{3,7},{4,0},{5,1},{6,2},{7,3},{8,12},{9,13},{10,... | collective-permute-start | bytes 589832 | tf_op jit(solution)/shard_map/ppermute | solution.py:164
  406.4 24.4 %collective-permute-start.60 = (bf16[8,96,512]{2,1,0:T(8,128)(2,1)S(1)}, bf16[8,96,512]{2,1,0:T(8,128)(2,1)S(1)}, u32[]{:S(2)}, u32[]{:S(2)}) collective-permute-start(bf16[8,96,512]{2,1,0:T(8,128)(2,1)S(1)} %bitcast.177), channel_id=1, source_target_pairs={{0,16},{1,17},{2,18},{3,19},{4,20},{5,21},{6,22},{7,23},{8,24},{9,... | collective-permute-start | bytes 2359304 | tf_op jit(solution)/shard_map/ppermute | solution.py:164
  408.4 11.7 %collective-permute-start.62 = (bf16[1,128,768]{2,1,0:T(8,128)(2,1)S(1)}, bf16[1,128,768]{2,1,0:T(8,128)(2,1)S(1)}, u32[]{:S(2)}, u32[]{:S(2)}) collective-permute-start(bf16[1,128,768]{2,1,0:T(8,128)(2,1)S(1)} %get-tuple-element.557), channel_id=1, source_target_pairs={{0,4},{1,5},{2,6},{3,7},{4,0},{5,1},{6,2},{7,3},{8,12},{9,13},{10,... | collective-permute-start | bytes 589832 | tf_op jit(solution)/shard_map/ppermute | solution.py:164
  410.4 20.3 %collective-permute-start.59 = (bf16[8,96,192]{2,1,0:T(8,128)(2,1)S(1)}, bf16[8,96,192]{2,1,0:T(8,128)(2,1)S(1)}, u32[]{:S(2)}, u32[]{:S(2)}) collective-permute-start(bf16[8,96,192]{2,1,0:T(8,128)(2,1)S(1)} %get-tuple-element.466), channel_id=1, source_target_pairs={{0,8},{1,9},{2,10},{3,11},{4,12},{5,13},{6,14},{7,15},{8,0},{9,1},... | collective-permute-start | bytes 884744 | tf_op jit(solution)/shard_map/ppermute | solution.py:164
  410.9 56.4 %collective-permute-start.74 = (bf16[96,1536]{1,0:T(8,128)(2,1)S(1)}, bf16[96,1536]{1,0:T(8,128)(2,1)}, u32[]{:S(2)}, u32[]{:S(2)}) collective-permute-start(bf16[96,1536]{1,0:T(8,128)(2,1)S(1)} %add_convert_fusion.26), channel_id=1, source_target_pairs={{0,16},{1,17},{2,18},{3,19},{4,20},{5,21},{6,22},{7,23},{24,8},{25... | collective-permute-start | bytes 884744 | tf_op jit(solution)/shard_map/ppermute | solution.py:164
  436.9 18.3 %collective-permute-start.66 = (bf16[4,128,512]{2,1,0:T(8,128)(2,1)S(1)}, bf16[4,128,512]{2,1,0:T(8,128)(2,1)S(1)}, u32[]{:S(2)}, u32[]{:S(2)}) collective-permute-start(bf16[4,128,512]{2,1,0:T(8,128)(2,1)S(1)} %get-tuple-element.533), channel_id=1, source_target_pairs={{0,4},{1,5},{2,6},{3,7},{4,0},{5,1},{6,2},{7,3},{8,12},{9,13},{10,... | collective-permute-start | bytes 1572872 | tf_op jit(solution)/shard_map/ppermute | solution.py:164
  437.3 17.9 %collective-permute-start.67 = (bf16[4,128,512]{2,1,0:T(8,128)(2,1)S(1)}, bf16[4,128,512]{2,1,0:T(8,128)(2,1)S(1)}, u32[]{:S(2)}, u32[]{:S(2)}) collective-permute-start(bf16[4,128,512]{2,1,0:T(8,128)(2,1)S(1)} %get-tuple-element.531), channel_id=1, source_target_pairs={{0,16},{1,17},{2,18},{3,19},{4,20},{5,21},{6,22},{7,23},{8,24},{9,... | collective-permute-start | bytes 1572872 | tf_op jit(solution)/shard_map/ppermute | solution.py:164
  438.7 16.6 %collective-permute-start.68 = (bf16[4,128,512]{2,1,0:T(8,128)(2,1)S(1)}, bf16[4,128,512]{2,1,0:T(8,128)(2,1)S(1)}, u32[]{:S(2)}, u32[]{:S(2)}) collective-permute-start(bf16[4,128,512]{2,1,0:T(8,128)(2,1)S(1)} %get-tuple-element.529), channel_id=1, source_target_pairs={{0,2},{1,3},{2,0},{3,1},{4,6},{5,7},{6,4},{7,5},{8,10},{9,11},{10,... | collective-permute-start | bytes 1572872 | tf_op jit(solution)/shard_map/ppermute | solution.py:164
  439.0 16.2 %collective-permute-start.69 = (bf16[2,2,96,192]{3,2,1,0:T(8,128)(2,1)S(1)}, bf16[2,2,96,192]{3,2,1,0:T(8,128)(2,1)S(1)}, u32[]{:S(2)}, u32[]{:S(2)}) collective-permute-start(bf16[2,2,96,192]{3,2,1,0:T(8,128)(2,1)S(1)} %bitcast.224), channel_id=1, source_target_pairs={{0,4},{1,5},{2,6},{3,7},{4,0},{5,1},{6,2},{7,3},{8,12},{9,13},{10,... | collective-permute-start | bytes 442376 | tf_op jit(solution)/shard_map/ppermute | solution.py:164
  455.4 11.9 %collective-permute-start.70 = (bf16[2,128,512]{2,1,0:T(8,128)(2,1)S(1)}, bf16[2,128,512]{2,1,0:T(8,128)(2,1)S(1)}, u32[]{:S(2)}, u32[]{:S(2)}) collective-permute-start(bf16[2,128,512]{2,1,0:T(8,128)(2,1)S(1)} %get-tuple-element.549), channel_id=1, source_target_pairs={{0,2},{1,3},{2,0},{3,1},{4,6},{5,7},{6,4},{7,5},{8,10},{9,11},{10,... | collective-permute-start | bytes 786440 | tf_op jit(solution)/shard_map/ppermute | solution.py:164
  455.8 11.4 %collective-permute-start.73 = (bf16[2,2,96,192]{3,2,0,1:T(8,128)(2,1)S(1)}, bf16[2,2,96,192]{3,2,0,1:T(8,128)(2,1)S(1)}, u32[]{:S(2)}, u32[]{:S(2)}) collective-permute-start(bf16[2,2,96,192]{3,2,0,1:T(8,128)(2,1)S(1)} %get-tuple-element.588), channel_id=1, source_target_pairs={{0,2},{1,3},{2,0},{3,1},{4,6},{5,7},{6,4},{7,5},{8,10},{9,11},{10,... | collective-permute-start | bytes 442376 | tf_op jit(solution)/shard_map/ppermute | solution.py:164
  457.8 9.5 %collective-permute-start.71 = (bf16[2,128,512]{2,1,0:T(8,128)(2,1)S(1)}, bf16[2,128,512]{2,1,0:T(8,128)(2,1)S(1)}, u32[]{:S(2)}, u32[]{:S(2)}) collective-permute-start(bf16[2,128,512]{2,1,0:T(8,128)(2,1)S(1)} %get-tuple-element.547), channel_id=1, source_target_pairs={{0,4},{1,5},{2,6},{3,7},{4,0},{5,1},{6,2},{7,3},{8,12},{9,13},{10,... | collective-permute-start | bytes 786440 | tf_op jit(solution)/shard_map/ppermute | solution.py:164
  458.3 9.0 %collective-permute-start.72 = (bf16[2,128,512]{2,1,0:T(8,128)(2,1)S(1)}, bf16[2,128,512]{2,1,0:T(8,128)(2,1)S(1)}, u32[]{:S(2)}, u32[]{:S(2)}) collective-permute-start(bf16[2,128,512]{2,1,0:T(8,128)(2,1)S(1)} %get-tuple-element.545), channel_id=1, source_target_pairs={{0,16},{1,17},{2,18},{3,19},{4,20},{5,21},{6,22},{7,23},{8,24},{9,... | collective-permute-start | bytes 786440 | tf_op jit(solution)/shard_map/ppermute | solution.py:164
  470.5 11.2 %collective-permute-start.79 = (bf16[8,96,192]{2,1,0:T(8,128)(2,1)S(1)}, bf16[8,96,192]{2,1,0:T(8,128)(2,1)S(1)}, u32[]{:S(2)}, u32[]{:S(2)}) collective-permute-start(bf16[8,96,192]{2,1,0:T(8,128)(2,1)S(1)} %bitcast.182), channel_id=1, source_target_pairs={{0,16},{1,17},{2,18},{3,19},{4,20},{5,21},{6,22},{7,23},{8,24},{9,... | collective-permute-start | bytes 884744 | tf_op jit(solution)/shard_map/ppermute | solution.py:164
  (120 other events, 893.0 us)
Sparse Core Ops, SparseCore 0:
  11.1 64.6 all-gather.4
  78.8 48.8 all-gather.6
  167.6 49.9 all-gather.8
  277.0 59.7 all-gather.10

commit v5 on v4

--- a/solution.py
+++ b/solution.py
@@ -1181,33 +1181,27 @@
     arrived, both_sum, grad_down = sync(arrived, both_sum, grad_down)
     far_terms = sum_low(mine[1], arrived[1])
     far_terms, out_sums, both_sum, attention, middle_rows = sync(
-        [far_terms[0], far_terms[1]], out_sums, both_sum, attention, middle_rows
-    )
-    far_first = swap(far_terms[0], BIT_ZH)
+        far_terms, out_sums, both_sum, attention, middle_rows
+    )
+    far_sum = swap(far_terms, BIT_ZH)
     out_sums = scatter_next(out_sums, HALVES, 1)
     grad_out_head = out_weights(spots, attention, middle_rows)
-    far_first, far_terms, out_sums, both_sum, grad_out_head, grad_down = sync(
-        far_first, far_terms, out_sums, both_sum, grad_out_head, grad_down
-    )
-    far_second = swap(far_terms[1], BIT_ZH)
+    far_sum, out_sums, both_sum, grad_out_head = sync(
+        far_sum, out_sums, both_sum, grad_out_head
+    )
     both_sum = trade_block(both_sum.reshape(2, 2, 2, 96, 512), 1, BIT_Y)
     down_sum = sum_low(grad_down, down_arrived)
     down_far = swap(down_sum, BIT_X, owns_down)
-    far_second, both_sum, out_sums = sync(far_second, both_sum, out_sums)
     out_sums = scatter_next(out_sums, HALVES, 0)
-    both_near = trade_block(both_sum, 2, BIT_C).reshape(8, 96, 512)
-    grad_own = (
-        mine[0].astype(wide)
-        + arrived[0].astype(wide)
-        + jnp.stack([far_first, far_second]).astype(wide)
-    )
+    grad_own = mine[0].astype(wide) + arrived[0].astype(wide) + far_sum.astype(wide)
     keep_heads, send_heads = head_weights(
         spots_rows, normed, tables, grad_queries, grad_own
     )
     out_arrived = swap(grad_out_head, BIT_ZH, lacks_out)
-    keep_heads, send_heads, grad_own, both_near, down_far, out_arrived = sync(
-        keep_heads, send_heads, grad_own, both_near, down_far, out_arrived
-    )
+    keep_heads, send_heads, grad_own, both_sum, down_far, out_arrived = sync(
+        keep_heads, send_heads, grad_own, both_sum, down_far, out_arrived
+    )
+    both_near = trade_block(both_sum, 2, BIT_C).reshape(8, 96, 512)
     both_far = swap(both_near, BIT_X)
     heads_first = swap(send_heads, BIT_ZH)
     made = project_back(spots, w_heads, tables, grad_queries, grad_own)

time: 495 us -> 492 us (level)
  waiting for transfers between devices: 216 us -> 211 us
    ppermute x80 -> x79, waiting for transfers between devices: 181 us -> 176 us  [swap(): return lax.ppermute(value, AXES, pairs)]
    ppermute x80 -> x79, starting transfers between devices: 96.8 us -> 95 us  [swap(): return lax.ppermute(value, AXES, pairs)]
  transfers between devices with their start and end apart: 84 -> 83, of which waited for: 47 -> 47; matrix products, arithmetic and copies ran while one was open for 6% -> 7% of each run, Pallas kernels for 19% -> 19%
where the time goes in v5:
time: 492 us; the launch traced here: 490 us
  waiting for transfers between devices  211 us (43%)
  Pallas kernels  118 us (24%)
  starting transfers between devices  95.4 us (19%)
  other arithmetic  35.8 us (7%)
  between operations  15.6 us (3%)
  local copies, waits for them, and re-layouts  14 us (3%)
    ppermute x79, waiting for transfers between devices, swap(): return lax.ppermute(value, AXES, pairs)  176 us
    pallas_call x19, Pallas kernels, kernel_call(): pl.pallas_call(body, out_shape=out_shape, grid_spec=pltpu.PrefetchScalarG...  118 us
    ppermute x79, starting transfers between devices, swap(): return lax.ppermute(value, AXES, pairs)  95 us
    all_gather x4, waiting for transfers between devices, cube_gather(): lax.all_gather(rows, AXES, axis=0, tiled=True, axis_index_groups=cube_gro...  34.9 us
    unnamed x202, local copies, waits for them, and re-layouts  11.2 us
  transfers between devices with their start and end apart: 83, of which 47 were waited for; matrix products, arithmetic and copies ran while one was open for 7% of the time, Pallas kernels for 19%

profile of v5, /device:TPU:0, one launch (start us, length us, event | category | flops | bytes accessed | tf_op | source)
XLA Modules:
  0.0 490.1 jit_solution(2260479989920026927)
XLA Ops:
  8.6 1.9 multiply_convert_fusion
  13.5 3.0 collective-permute-start.1
  16.5 5.2 %collective-permute-start.3 = (bf16[96,1536]{1,0:T(8,128)(2,1)S(1)}, bf16[96,1536]{1,0:T(8,128)(2,1)}, u32[]{:S(2)}, u32[]{:S(2)}) collective-permute-start(bf16[96,1536]{1,0:T(8,128)(2,1)S(1)} %copy-done.91), channel_id=1, source_target_pairs={{0,8},{1,9},{2,10},{3,11},{4,12},{5,13},{6,14},{7,15},{24,16},{25,... | collective-permute-start | bytes 884744 | tf_op jit(solution)/shard_map/ppermute | solution.py:164
  21.8 1.9 collective-permute-start.2
  24.6 18.0 %collective-permute-done.2 = bf16[2,2,96,192]{3,2,1,0:T(8,128)(2,1)S(1)} collective-permute-done((bf16[2,2,96,192]{3,2,1,0:T(8,128)(2,1)S(1)}, bf16[2,2,96,192]{3,2,1,0:T(8,128)(2,1)S(1)}, u32[]{:S(2)}, u32[]{:S(2)}) %collective-permute-start.2) | collective-permute-done | bytes 147488 | tf_op jit(solution)/shard_map/ppermute | solution.py:164
  45.1 2.5 collective-permute-done.8
  47.8 8.1 %collective-permute-done.6 = bf16[2,2,96,512]{3,2,0,1:T(8,128)(2,1)S(1)} collective-permute-done((bf16[2,2,96,512]{3,2,0,1:T(8,128)(2,1)S(1)}, bf16[2,2,96,512]{3,2,0,1:T(8,128)(2,1)S(1)}, u32[]{:S(2)}, u32[]{:S(2)}) %collective-permute-start.6) | collective-permute-done | bytes 393248 | tf_op jit(solution)/shard_map/ppermute | solution.py:164
  56.0 2.6 collective-permute-start.7
  59.3 17.3 %collective-permute-done.7 = bf16[2,2,96,512]{3,2,1,0:T(8,128)(2,1)S(1)} collective-permute-done((bf16[2,2,96,512]{3,2,1,0:T(8,128)(2,1)S(1)}, bf16[2,2,96,512]{3,2,1,0:T(8,128)(2,1)S(1)}, u32[]{:S(2)}, u32[]{:S(2)}) %collective-permute-start.7) | collective-permute-done | bytes 393248 | tf_op jit(solution)/shard_map/ppermute | solution.py:164
  78.3 2.5 collective-permute-start.10
  80.9 7.8 %shard_map.215 = (bf16[2,96,1024]{2,1,0:T(8,128)(2,1)S(1)}, bf16[2,96,1024]{2,1,0:T(8,128)(2,1)S(1)}) custom-call(s32[9]{0:T(128)S(1)} %pad_add_fusion.at_ref, bf16[2048,1536]{1,0:T(8,128)(2,1)} %all-gather.5.cloned.1.call-done.rows_ref, bf16[1536,192]{1,0:T(8,128)(2,1)S(1)} %shard_map.214.w_ref, f32[48,1024]{1,0:T(8,128)S(1)} %get-tuple-element.274.cos_ref.rest_2_, ...), custom_call_target="tpu_custom_call" | custom-call | flops 1207959552 | bytes 8388608 | tf_op jit(solution)/shard_map/pallas_call | solution.py:296
  88.9 2.2 collective-permute-done.9
  91.2 2.1 collective-permute-start.13
  93.3 2.9 collective-permute-start.11
  96.2 14.2 %collective-permute-done.12 = bf16[2,128,768]{2,1,0:T(8,128)(2,1)S(1)} collective-permute-done((bf16[2,128,768]{2,1,0:T(8,128)(2,1)S(1)}, bf16[2,128,768]{2,1,0:T(8,128)(2,1)S(1)}, u32[]{:S(2)}, u32[]{:S(2)}) %collective-permute-start.12) | collective-permute-done | bytes 393248 | tf_op jit(solution)/shard_map/ppermute | solution.py:164
  112.5 2.3 collective-permute-done.14.c_ref.d_ref
  114.8 2.1 collective-permute-start.18
  117.7 3.1 collective-permute-start.16
  121.8 11.3 %shard_map.216 = (bf16[8,96,128]{2,1,0:T(8,128)(2,1)S(1)}, bf16[8,96,128]{2,1,0:T(8,128)(2,1)S(1)}, f32[2,96,1024]{2,1,0:T(8,128)S(1)}, f32[2,1,1024]{2,1,0:T(1,128)S(1)}) custom-call(s32[9]{0:T(128)S(1)} %pad_add_fusion.at_ref, bf16[2,96,1024]{2,1,0:T(8,128)(2,1)S(1)} %get-tuple-element.280.q_ref, bf16[2,96,1024]{2,1,0:T(8,128)(2,1)S(1)} %get-tuple-element.281.a_ref, ...), custom_call_target="tpu_custom_call" | custom-call | flops 1610612736 | bytes 12582912 | tf_op jit(solution)/shard_map/pallas_call | solution.py:296
  135.6 2.8 collective-permute-done.16.refs_2_
  142.3 2.2 collective-permute-done.17
  146.3 5.0 %collective-permute-start.24 = (bf16[256,1536]{1,0:T(8,128)(2,1)S(1)}, bf16[256,1536]{1,0:T(8,128)(2,1)S(1)}, u32[]{:S(2)}, u32[]{:S(2)}) collective-permute-start(bf16[256,1536]{1,0:T(8,128)(2,1)S(1)} %copy-done.82), channel_id=1, source_target_pairs={{0,8},{2,10},{4,12},{6,14},{9,1},{11,3},{13,5},{15,7},{17,25},{19,... | collective-permute-start | bytes 2359304 | tf_op jit(solution)/shard_map/ppermute | solution.py:164
  154.6 4.9 %collective-permute-done.23 = bf16[2,2,2,96,128]{4,3,2,1,0:T(8,128)(2,1)S(1)} collective-permute-done((bf16[2,2,2,96,128]{4,3,2,1,0:T(8,128)(2,1)S(1)}, bf16[2,2,2,96,128]{4,3,2,1,0:T(8,128)(2,1)S(1)}, u32[]{:S(2)}, u32[]{:S(2)}) %collective-permute-start.23) | collective-permute-done | bytes 196640 | tf_op jit(solution)/shard_map/ppermute | solution.py:164
  160.8 3.9 shard_map.217
  167.3 3.5 collective-permute-start.25
  172.0 7.7 %shard_map.218.dh_ref = f32[2048,256]{1,0:T(8,128)} custom-call(s32[9]{0:T(128)S(1)} %pad_add_fusion.at_ref, bf16[8,128,768]{2,1,0:T(8,128)(2,1)S(1)} %pad_maximum_fusion.refs_0_, bf16[8,128,768]{2,1,0:T(8,128)(2,1)S(1)} %copy-done.2, bf16[8,128,768]{2,1,0:T(8,128)(2,1)S(1)} %pad_maximum_fusion.1.refs_2_, bf16[8,128,768]{2,1,0:T(8,128)(2,1)} %copy-done.75, ...), custom_call_target="tpu_custom_call" | custom-call | flops 1610612736 | bytes 8388608 | tf_op jit(solution)/shard_map/pallas_call | solution.py:296
  182.3 34.9 %all-gather.9.cloned.1.call-done.rows_ref = bf16[2048,1536]{1,0:T(8,128)(2,1)} async-done(((bf16[128,1536]{1,0:T(8,128)(2,1)}), bf16[2048,1536]{1,0:T(8,128)(2,1)}) %all-gather.9.cloned.1.call-update) | async-done | bytes 6291472 | tf_op jit(solution)/shard_map/all_gather | solution.py:216
  217.2 12.4 %shard_map.220 = (bf16[8,128,512]{2,1,0:T(8,128)(2,1)S(1)}, bf16[8,128,512]{2,1,0:T(8,128)(2,1)S(1)}, bf16[8,128,512]{2,1,0:T(8,128)(2,1)S(1)}, bf16[8,128,512]{...) custom-call(s32[9]{0:T(128)S(1)} %pad_add_fusion.at_ref, ...), custom_call_target="tpu_custom_call" | custom-call | flops 6442450944 | bytes 18874368 | tf_op jit(solution)/shard_map/pallas_call | solution.py:296
  230.4 1.9 collective-permute-done.26
  232.3 3.0 collective-permute-done.27
  239.4 9.5 %shard_map.221 = (bf16[8,96,512]{2,1,0:T(8,128)(2,1)S(1)}, bf16[8,96,512]{2,1,0:T(8,128)(2,1)S(1)}) custom-call(s32[25]{0:T(128)S(1)} %pad_add_fusion.2.at_ref, bf16[2048,1536]{1,0:T(8,128)(2,1)} %all-gather.9.cloned.1.call-done.rows_ref, bf16[2048,512]{1,0:T(8,128)(2,1)S(1)} %copy-done.70), custom_call_target="tpu_custom_call" | custom-call | flops 3221225472 | bytes 14680064 | tf_op jit(solution)/shard_map/pallas_call | solution.py:296
  256.1 3.4 collective-permute-done.32
  268.8 4.5 shard_map.222
  277.7 3.4 collective-permute-start.40
  282.5 7.1 %shard_map.223 = bf16[256,1536]{1,0:T(8,128)(2,1)S(1)} custom-call(s32[9]{0:T(128)S(1)} %pad_add_fusion.at_ref, bf16[8,128,768]{2,1,0:T(8,128)(2,1)S(1)} %pad_maximum_fusion.refs_0_, bf16[8,128,768]{2,1,0:T(8,128)(2,1)S(1)} %copy-done.3, bf16[8,128,768]{2,1,0:T(8,128)(2,1)} %copy-done, bf16[8,128,768]{2,1,0:T(8,128)(2,1)} %copy-done.75, ...), custom_call_target="tpu_custom_call" | custom-call | flops 1610612736 | bytes 8388608 | tf_op jit(solution)/shard_map/pallas_call | solution.py:296
  289.6 3.7 collective-permute-done.39
  293.3 5.9 %collective-permute-done.40 = bf16[4,96,512]{2,1,0:T(8,128)(2,1)S(1)} collective-permute-done((bf16[4,96,512]{2,1,0:T(8,128)(2,1)S(1)}, bf16[4,96,512]{2,1,0:T(8,128)(2,1)S(1)}, u32[]{:S(2)}, u32[]{:S(2)}) %collective-permute-start.40) | collective-permute-done | bytes 393248 | tf_op jit(solution)/shard_map/ppermute | solution.py:164
  299.8 5.4 %shard_map.224 = (bf16[8,128,768]{2,1,0:T(8,128)(2,1)S(1)}, bf16[8,128,768]{2,1,0:T(8,128)(2,1)S(1)}, bf16[8,128,768]{2,1,0:T(8,128)(2,1)}, bf16[8,128,768]{2,1,0:T(8,128)(2,1)}) custom-call(s32[9]{0:T(128)S(1)} %pad_add_fusion.at_ref, bf16[2048,256]{1,0:T(8,128)(2,1)S(1)} %copy-done.25, bf16[256,1536]{1,0:T(8,128)(2,1)S(1)} %copy-done.5), custom_call_target="tpu_custom_call" | custom-call | flops 1610612736 | bytes 8388608 | tf_op jit(solution)/shard_map/pallas_call | solution.py:296
  307.6 3.2 collective-permute-start.42
  310.9 18.0 %collective-permute-done.42 = bf16[2,2,2,96,128]{4,3,2,1,0:T(8,128)(2,1)S(1)} collective-permute-done((bf16[2,2,2,96,128]{4,3,2,1,0:T(8,128)(2,1)S(1)}, bf16[2,2,2,96,128]{4,3,2,1,0:T(8,128)(2,1)S(1)}, u32[]{:S(2)}, u32[]{:S(2)}) %collective-permute-start.42) | collective-permute-done | bytes 196640 | tf_op jit(solution)/shard_map/ppermute | solution.py:164
  335.6 2.5 collective-permute-start.49
  338.2 18.8 %shard_map.225 = (bf16[2,96,1024]{2,1,0:T(8,128)(2,1)S(1)}, bf16[2,2,96,1024]{3,2,1,0:T(8,128)(2,1)S(1)}, bf16[2,2,96,1024]{3,2,1,0:T(8,128)(2,1)}) custom-call(s32[9]{0:T(128)S(1)} %pad_add_fusion.at_ref, bf16[2,96,1024]{2,1,0:T(8,128)(2,1)S(1)} %copy-done.68, bf16[2,96,1024]{2,1,0:T(8,128)(2,1)S(1)} %copy-done.49, bf16[2,96,1024]{2,1,0:T(8,128)(2,1)S(1)} %copy-done.51, ...), custom_call_target="tpu_custom_call" | custom-call | flops 4026531840 | bytes 12582912 | tf_op jit(solution)/shard_map/pallas_call | solution.py:296
  360.5 2.0 pad_maximum_fusion.6
  362.6 1.9 fusion.2
  364.4 1.8 collective-permute-start.51
  367.6 2.1 collective-permute-start.52
  371.1 2.1 collective-permute-start.55
  373.2 6.8 %shard_map.226 = bf16[96,1536]{1,0:T(8,128)(2,1)S(1)} custom-call(s32[9]{0:T(128)S(1)} %pad_add_fusion.at_ref, f32[2,96,1024]{2,1,0:T(8,128)S(1)} %copy-done.33, bf16[2048,1536]{1,0:T(8,128)(2,1)} %all-gather.11.cloned.1.call-done.rows_ref), custom_call_target="tpu_custom_call" | custom-call | flops 603979776 | bytes 8388608 | tf_op jit(solution)/shard_map/pallas_call | solution.py:296
  380.1 4.9 %collective-permute-done.51 = bf16[2,96,1024]{2,1,0:T(8,128)(2,1)S(1)} collective-permute-done((bf16[2,96,1024]{2,1,0:T(8,128)(2,1)}, bf16[2,96,1024]{2,1,0:T(8,128)(2,1)S(1)}, u32[]{:S(2)}, u32[]{:S(2)}) %collective-permute-start.51) | collective-permute-done | bytes 393248 | tf_op jit(solution)/shard_map/ppermute | solution.py:164
  389.2 7.8 %shard_map.227 = (bf16[8,96,192]{2,1,0:T(8,128)(2,1)S(1)}, bf16[8,96,192]{2,1,0:T(8,128)(2,1)S(1)}) custom-call(s32[25]{0:T(128)S(1)} %copy-done.60, bf16[2048,1536]{1,0:T(8,128)(2,1)} %all-gather.5.cloned.1.call-done.rows_ref, f32[48,1024]{1,0:T(8,128)S(1)} %get-tuple-element.271.cos2_ref.cos_ref, f32[48,1024]{1,0:T(8,128)S(1)} %get-tuple-element.272.sin2_ref.sin_ref, ...), custom_call_target="tpu_custom_call" | custom-call | flops 1207959552 | bytes 8388608 | tf_op jit(solution)/shard_map/pallas_call | solution.py:296
  397.1 5.0 %collective-permute-done.56 = bf16[96,1536]{1,0:T(8,128)(2,1)S(1)} collective-permute-done((bf16[96,1536]{1,0:T(8,128)(2,1)S(1)}, bf16[96,1536]{1,0:T(8,128)(2,1)S(1)}, u32[]{:S(2)}, u32[]{:S(2)}) %collective-permute-start.56) | collective-permute-done | bytes 294944 | tf_op jit(solution)/shard_map/ppermute | solution.py:164
  405.3 3.4 collective-permute-start.57
  408.8 2.2 collective-permute-start.73
  411.0 5.7 %shard_map.228 = (bf16[8,128,512]{2,1,0:T(8,128)(2,1)S(1)}, bf16[8,128,512]{2,1,0:T(8,128)(2,1)S(1)}, bf16[8,128,512]{2,1,0:T(8,128)(2,1)S(1)}, bf16[8,128,512]{...) custom-call(s32[9]{0:T(128)S(1)} %pad_add_fusion.at_ref, ...), custom_call_target="tpu_custom_call" | custom-call | flops 1207959552 | bytes 8388608 | tf_op jit(solution)/shard_map/pallas_call | solution.py:296
  416.7 1.9 collective-permute-done.61
  418.5 7.5 %collective-permute-done.57 = bf16[8,96,192]{2,1,0:T(8,128)(2,1)S(1)} collective-permute-done((bf16[8,96,192]{2,1,0:T(8,128)(2,1)S(1)}, bf16[8,96,192]{2,1,0:T(8,128)(2,1)S(1)}, u32[]{:S(2)}, u32[]{:S(2)}) %collective-permute-start.57) | collective-permute-done | bytes 294944 | tf_op jit(solution)/shard_map/ppermute | solution.py:164
  427.9 2.2 collective-permute-done.62
  435.3 2.1 collective-permute-start.68
  437.5 13.0 %collective-permute-done.68 = bf16[2,2,96,192]{3,2,1,0:T(8,128)(2,1)S(1)} collective-permute-done((bf16[2,2,96,192]{3,2,1,0:T(8,128)(2,1)S(1)}, bf16[2,2,96,192]{3,2,1,0:T(8,128)(2,1)S(1)}, u32[]{:S(2)}, u32[]{:S(2)}) %collective-permute-start.68) | collective-permute-done | bytes 147488 | tf_op jit(solution)/shard_map/ppermute | solution.py:164
  456.7 3.1 shard_map.230
  460.5 2.0 collective-permute-done.72
  468.9 2.5 collective-permute-done.76
  471.3 6.7 %collective-permute-done.78.far_ref = bf16[8,96,192]{2,1,0:T(8,128)(2,1)S(1)} collective-permute-done((bf16[8,96,192]{2,1,0:T(8,128)(2,1)S(1)}, bf16[8,96,192]{2,1,0:T(8,128)(2,1)S(1)}, u32[]{:S(2)}, u32[]{:S(2)}) %collective-permute-start.78) | collective-permute-done | bytes 294944 | tf_op jit(solution)/shard_map/ppermute | solution.py:164
  478.5 3.3 shard_map.229
  (454 shorter events, 106.0 us)
Async XLA Ops:
  7.2 70.9 %all-gather.5.cloned.1.call-start = ((), (), s32[]{:S(2)}) async-start(), calls=%async_computation | async-start | bytes 6684672 | tf_op jit(solution)/shard_map/all_gather | solution.py:216
  10.5 123.6 %all-gather.7.cloned.1.call-start = ((), (), s32[]{:S(2)}) async-start(), calls=%async_computation.1 | async-start | bytes 5013504 | tf_op jit(solution)/shard_map/all_gather | solution.py:216
  13.5 8.2 %collective-permute-start.1 = (bf16[2,2,96,192]{3,2,0,1:T(8,128)(2,1)S(1)}, bf16[2,2,96,192]{3,2,0,1:T(8,128)(2,1)S(1)}, u32[]{:S(2)}, u32[]{:S(2)}) collective-permute-start(bf16[2,2,96,192]{3,2,0,1:T(8,128)(2,1)S(1)} %get-tuple-element.590), channel_id=1, source_target_pairs={{0,2},{1,3},{2,0},{3,1},{4,6},{5,7},{6,4},{7,5},{8,10},{9,11},{10,... | collective-permute-start | bytes 442376 | tf_op jit(solution)/shard_map/ppermute | solution.py:164
  16.5 26.3 %collective-permute-start.3 = (bf16[96,1536]{1,0:T(8,128)(2,1)S(1)}, bf16[96,1536]{1,0:T(8,128)(2,1)}, u32[]{:S(2)}, u32[]{:S(2)}) collective-permute-start(bf16[96,1536]{1,0:T(8,128)(2,1)S(1)} %copy-done.91), channel_id=1, source_target_pairs={{0,8},{1,9},{2,10},{3,11},{4,12},{5,13},{6,14},{7,15},{24,16},{25,... | collective-permute-start | bytes 884744 | tf_op jit(solution)/shard_map/ppermute | solution.py:164
  21.8 20.8 %collective-permute-start.2 = (bf16[2,2,96,192]{3,2,1,0:T(8,128)(2,1)S(1)}, bf16[2,2,96,192]{3,2,1,0:T(8,128)(2,1)S(1)}, u32[]{:S(2)}, u32[]{:S(2)}) collective-permute-start(bf16[2,2,96,192]{3,2,1,0:T(8,128)(2,1)S(1)} %get-tuple-element.588), channel_id=1, source_target_pairs={{0,4},{1,5},{2,6},{3,7},{4,0},{5,1},{6,2},{7,3},{8,12},{9,13},{10,... | collective-permute-start | bytes 442376 | tf_op jit(solution)/shard_map/ppermute | solution.py:164
  44.7 11.2 %collective-permute-start.6 = (bf16[2,2,96,512]{3,2,0,1:T(8,128)(2,1)S(1)}, bf16[2,2,96,512]{3,2,0,1:T(8,128)(2,1)S(1)}, u32[]{:S(2)}, u32[]{:S(2)}) collective-permute-start(bf16[2,2,96,512]{3,2,0,1:T(8,128)(2,1)S(1)} %get-tuple-element.552), channel_id=1, source_target_pairs={{0,2},{1,3},{2,0},{3,1},{4,6},{5,7},{6,4},{7,5},{8,10},{9,11},{10,... | collective-permute-start | bytes 1179656 | tf_op jit(solution)/shard_map/ppermute | solution.py:164
  47.8 29.7 %collective-permute-start.4 = (bf16[8,96,192]{2,1,0:T(8,128)(2,1)S(1)}, bf16[8,96,192]{2,1,0:T(8,128)(2,1)S(1)}, u32[]{:S(2)}, u32[]{:S(2)}) collective-permute-start(bf16[8,96,192]{2,1,0:T(8,128)(2,1)S(1)} %bitcast.176), channel_id=1, source_target_pairs={{0,8},{1,9},{2,10},{3,11},{4,12},{5,13},{6,14},{7,15},{8,0},{9,1},... | collective-permute-start | bytes 884744 | tf_op jit(solution)/shard_map/ppermute | solution.py:164
  56.0 20.6 %collective-permute-start.7 = (bf16[2,2,96,512]{3,2,1,0:T(8,128)(2,1)S(1)}, bf16[2,2,96,512]{3,2,1,0:T(8,128)(2,1)S(1)}, u32[]{:S(2)}, u32[]{:S(2)}) collective-permute-start(bf16[2,2,96,512]{3,2,1,0:T(8,128)(2,1)S(1)} %get-tuple-element.550), channel_id=1, source_target_pairs={{0,4},{1,5},{2,6},{3,7},{4,0},{5,1},{6,2},{7,3},{8,12},{9,13},{10,... | collective-permute-start | bytes 1179656 | tf_op jit(solution)/shard_map/ppermute | solution.py:164
  78.2 139.0 %all-gather.9.cloned.1.call-start = ((), (), s32[]{:S(2)}) async-start(), calls=%async_computation.2 | async-start | bytes 6684672 | tf_op jit(solution)/shard_map/all_gather | solution.py:216
  78.3 10.5 %collective-permute-start.10 = (bf16[1,128,768]{2,1,0:T(8,128)(2,1)S(1)}, bf16[1,128,768]{2,1,0:T(8,128)(2,1)S(1)}, u32[]{:S(2)}, u32[]{:S(2)}) collective-permute-start(bf16[1,128,768]{2,1,0:T(8,128)(2,1)S(1)} %get-tuple-element.585), channel_id=1, source_target_pairs={{0,4},{1,5},{2,6},{3,7},{4,0},{5,1},{6,2},{7,3},{8,12},{9,13},{10,... | collective-permute-start | bytes 589832 | tf_op jit(solution)/shard_map/ppermute | solution.py:164
  80.9 10.1 %collective-permute-start.9 = (bf16[1,128,768]{2,1,0:T(8,128)(2,1)S(1)}, bf16[1,128,768]{2,1,0:T(8,128)(2,1)S(1)}, u32[]{:S(2)}, u32[]{:S(2)}) collective-permute-start(bf16[1,128,768]{2,1,0:T(8,128)(2,1)S(1)} %get-tuple-element.586), channel_id=1, source_target_pairs={{0,4},{1,5},{2,6},{3,7},{4,0},{5,1},{6,2},{7,3},{8,12},{9,13},{10,... | collective-permute-start | bytes 589832 | tf_op jit(solution)/shard_map/ppermute | solution.py:164
  91.1 19.3 %collective-permute-start.12 = (bf16[2,128,768]{2,1,0:T(8,128)(2,1)S(1)}, bf16[2,128,768]{2,1,0:T(8,128)(2,1)S(1)}, u32[]{:S(2)}, u32[]{:S(2)}) collective-permute-start(bf16[2,128,768]{2,1,0:T(8,128)(2,1)S(1)} %pad_maximum_fusion.15), channel_id=1, source_target_pairs={{0,16},{1,17},{2,18},{3,19},{4,20},{5,21},{6,22},{7,23},{8,24},{9,... | collective-permute-start | bytes 1179656 | tf_op jit(solution)/shard_map/ppermute | solution.py:164
  91.2 20.2 %collective-permute-start.13 = (bf16[2,128,768]{2,1,0:T(8,128)(2,1)S(1)}, bf16[2,128,768]{2,1,0:T(8,128)(2,1)S(1)}, u32[]{:S(2)}, u32[]{:S(2)}) collective-permute-start(bf16[2,128,768]{2,1,0:T(8,128)(2,1)S(1)} %pad_maximum_fusion.16), channel_id=1, source_target_pairs={{0,2},{1,3},{2,0},{3,1},{4,6},{5,7},{6,4},{7,5},{8,10},{9,11},{10,... | collective-permute-start | bytes 1179656 | tf_op jit(solution)/shard_map/ppermute | solution.py:164
  93.3 19.0 %collective-permute-start.11 = (bf16[2,96,1024]{2,1,0:T(8,128)(2,1)S(1)}, bf16[2,96,1024]{2,1,0:T(8,128)(2,1)S(1)}, u32[]{:S(2)}, u32[]{:S(2)}) collective-permute-start(bf16[2,96,1024]{2,1,0:T(8,128)(2,1)S(1)} %get-tuple-element.281.a_ref), channel_id=1, source_target_pairs={{0,8},{1,9},{2,10},{3,11},{4,12},{5,13},{6,14},{7,15},{8,0},{9,1},... | collective-permute-start | bytes 1179656 | tf_op jit(solution)/shard_map/ppermute | solution.py:164
  114.8 24.5 %collective-permute-start.18 = (bf16[4,128,768]{2,1,0:T(8,128)(2,1)}, bf16[4,128,768]{2,1,0:T(8,128)(2,1)}, u32[]{:S(2)}, u32[]{:S(2)}) collective-permute-start(bf16[4,128,768]{2,1,0:T(8,128)(2,1)} %pad_maximum_fusion.3), channel_id=1, source_target_pairs={{0,2},{1,3},{2,0},{3,1},{4,6},{5,7},{6,4},{7,5},{8,10},{9,11},{10,... | collective-permute-start | bytes 2359304 | tf_op jit(solution)/shard_map/ppermute | solution.py:164
  117.7 20.7 %collective-permute-start.16 = (bf16[4,96,512]{2,1,0:T(8,128)(2,1)S(1)}, bf16[4,96,512]{2,1,0:T(8,128)(2,1)S(1)}, u32[]{:S(2)}, u32[]{:S(2)}) collective-permute-start(bf16[4,96,512]{2,1,0:T(8,128)(2,1)S(1)} %bitcast.182), channel_id=1, source_target_pairs={{0,8},{1,9},{2,10},{3,11},{4,12},{5,13},{6,14},{7,15},{8,0},{9,1},... | collective-permute-start | bytes 1179656 | tf_op jit(solution)/shard_map/ppermute | solution.py:164
  120.7 20.1 %collective-permute-start.19 = (bf16[4,128,768]{2,1,0:T(8,128)(2,1)}, bf16[4,128,768]{2,1,0:T(8,128)(2,1)}, u32[]{:S(2)}, u32[]{:S(2)}) collective-permute-start(bf16[4,128,768]{2,1,0:T(8,128)(2,1)} %pad_maximum_fusion.4), channel_id=1, source_target_pairs={{0,16},{1,17},{2,18},{3,19},{4,20},{5,21},{6,22},{7,23},{8,24},{9,... | collective-permute-start | bytes 2359304 | tf_op jit(solution)/shard_map/ppermute | solution.py:164
  138.4 6.2 %collective-permute-start.17 = (bf16[2,2,2,96,128]{4,3,0,2,1:T(8,128)(2,1)S(1)}, bf16[2,2,2,96,128]{4,3,0,2,1:T(8,128)(2,1)S(1)}, u32[]{:S(2)}, u32[]{:S(2)}) collective-permute-start(bf16[2,2,2,96,128]{4,3,0,2,1:T(8,128)(2,1)S(1)} %get-tuple-element.584), channel_id=1, source_target_pairs={{0,4},{1,5},{2,6},{3,7},{4,0},{5,1},{6,2},{7,3},{8,12},{9,13},{10,... | collective-permute-start | bytes 589832 | tf_op jit(solution)/shard_map/ppermute | solution.py:164
  144.6 7.6 %collective-permute-start.21 = (bf16[8,128,768]{2,1,0:T(8,128)(2,1)S(1)}, bf16[8,128,768]{2,1,0:T(8,128)(2,1)S(1)}, u32[]{:S(2)}, u32[]{:S(2)}) collective-permute-start(bf16[8,128,768]{2,1,0:T(8,128)(2,1)S(1)} %pad_maximum_fusion.refs_0_), channel_id=1, source_target_pairs={{0,1},{1,0},{2,3},{3,2},{4,5},{5,4},{6,7},{7,6},{8,9},{9,8},{10,11... | collective-permute-start | bytes 4718600 | tf_op jit(solution)/shard_map/ppermute | solution.py:164
  144.7 8.7 %collective-permute-start.22 = (bf16[8,128,768]{2,1,0:T(8,128)(2,1)S(1)}, bf16[8,128,768]{2,1,0:T(8,128)(2,1)S(1)}, u32[]{:S(2)}, u32[]{:S(2)}) collective-permute-start(bf16[8,128,768]{2,1,0:T(8,128)(2,1)S(1)} %pad_maximum_fusion.1.refs_2_), channel_id=1, source_target_pairs={{0,1},{1,0},{2,3},{3,2},{4,5},{5,4},{6,7},{7,6},{8,9},{9,8},{10,11... | collective-permute-start | bytes 4718600 | tf_op jit(solution)/shard_map/ppermute | solution.py:164
  145.2 7.0 %collective-permute-start.20 = (bf16[2,2,2,96,128]{4,3,1,0,2:T(8,128)(2,1)S(1)}, bf16[2,2,2,96,128]{4,3,1,0,2:T(8,128)(2,1)S(1)}, u32[]{:S(2)}, u32[]{:S(2)}) collective-permute-start(bf16[2,2,2,96,128]{4,3,1,0,2:T(8,128)(2,1)S(1)} %get-tuple-element.582), channel_id=1, source_target_pairs={{0,16},{1,17},{2,18},{3,19},{4,20},{5,21},{6,22},{7,23},{8,24},{9,... | collective-permute-start | bytes 589832 | tf_op jit(solution)/shard_map/ppermute | solution.py:164
  146.3 14.5 %collective-permute-start.24 = (bf16[256,1536]{1,0:T(8,128)(2,1)S(1)}, bf16[256,1536]{1,0:T(8,128)(2,1)S(1)}, u32[]{:S(2)}, u32[]{:S(2)}) collective-permute-start(bf16[256,1536]{1,0:T(8,128)(2,1)S(1)} %copy-done.82), channel_id=1, source_target_pairs={{0,8},{2,10},{4,12},{6,14},{9,1},{11,3},{13,5},{15,7},{17,25},{19,... | collective-permute-start | bytes 2359304 | tf_op jit(solution)/shard_map/ppermute | solution.py:164
  153.4 6.1 %collective-permute-start.23 = (bf16[2,2,2,96,128]{4,3,2,1,0:T(8,128)(2,1)S(1)}, bf16[2,2,2,96,128]{4,3,2,1,0:T(8,128)(2,1)S(1)}, u32[]{:S(2)}, u32[]{:S(2)}) collective-permute-start(bf16[2,2,2,96,128]{4,3,2,1,0:T(8,128)(2,1)S(1)} %get-tuple-element.580), channel_id=1, source_target_pairs={{0,2},{1,3},{2,0},{3,1},{4,6},{5,7},{6,4},{7,5},{8,10},{9,11},{10,... | collective-permute-start | bytes 589832 | tf_op jit(solution)/shard_map/ppermute | solution.py:164
  167.0 197.4 %all-gather.11.cloned.1.call-start = ((), (), s32[]{:S(2)}) async-start(), calls=%async_computation.3 | async-start | bytes 6684672 | tf_op jit(solution)/shard_map/all_gather | solution.py:216
  167.3 13.2 %collective-permute-start.25 = (bf16[4,96,512]{2,1,0:T(8,128)(2,1)}, bf16[4,96,512]{2,1,0:T(8,128)(2,1)S(1)}, u32[]{:S(2)}, u32[]{:S(2)}) collective-permute-start(bf16[4,96,512]{2,1,0:T(8,128)(2,1)} %bitcast.180), channel_id=1, source_target_pairs={{0,8},{1,9},{2,10},{3,11},{4,12},{5,13},{6,14},{7,15},{8,0},{9,1},... | collective-permute-start | bytes 1179656 | tf_op jit(solution)/shard_map/ppermute | solution.py:164
  229.8 5.4 %collective-permute-start.27 = (bf16[8,128,512]{2,1,0:T(8,128)(2,1)S(1)}, bf16[8,128,512]{2,1,0:T(8,128)(2,1)S(1)}, u32[]{:S(2)}, u32[]{:S(2)}) collective-permute-start(bf16[8,128,512]{2,1,0:T(8,128)(2,1)S(1)} %get-tuple-element.340), channel_id=1, source_target_pairs={{0,1},{1,0},{2,3},{3,2},{4,5},{5,4},{6,7},{7,6},{8,9},{9,8},{10,11... | collective-permute-start | bytes 3145736 | tf_op jit(solution)/shard_map/ppermute | solution.py:164
  235.8 14.1 %collective-permute-start.29 = (bf16[4,128,512]{2,1,0:T(8,128)(2,1)S(1)}, bf16[4,128,512]{2,1,0:T(8,128)(2,1)S(1)}, u32[]{:S(2)}, u32[]{:S(2)}) collective-permute-start(bf16[4,128,512]{2,1,0:T(8,128)(2,1)S(1)} %get-tuple-element.521), channel_id=1, source_target_pairs={{0,4},{1,5},{2,6},{3,7},{4,0},{5,1},{6,2},{7,3},{8,12},{9,13},{10,... | collective-permute-start | bytes 1572872 | tf_op jit(solution)/shard_map/ppermute | solution.py:164
  236.8 13.9 %collective-permute-start.30 = (bf16[4,128,512]{2,1,0:T(8,128)(2,1)S(1)}, bf16[4,128,512]{2,1,0:T(8,128)(2,1)S(1)}, u32[]{:S(2)}, u32[]{:S(2)}) collective-permute-start(bf16[4,128,512]{2,1,0:T(8,128)(2,1)S(1)} %get-tuple-element.519), channel_id=1, source_target_pairs={{0,16},{1,17},{2,18},{3,19},{4,20},{5,21},{6,22},{7,23},{8,24},{9,... | collective-permute-start | bytes 1572872 | tf_op jit(solution)/shard_map/ppermute | solution.py:164
  238.7 13.6 %collective-permute-start.31 = (bf16[4,128,512]{2,1,0:T(8,128)(2,1)S(1)}, bf16[4,128,512]{2,1,0:T(8,128)(2,1)S(1)}, u32[]{:S(2)}, u32[]{:S(2)}) collective-permute-start(bf16[4,128,512]{2,1,0:T(8,128)(2,1)S(1)} %get-tuple-element.517), channel_id=1, source_target_pairs={{0,2},{1,3},{2,0},{3,1},{4,6},{5,7},{6,4},{7,5},{8,10},{9,11},{10,... | collective-permute-start | bytes 1572872 | tf_op jit(solution)/shard_map/ppermute | solution.py:164
  252.4 7.1 %collective-permute-start.32 = (bf16[2,128,512]{2,1,0:T(8,128)(2,1)S(1)}, bf16[2,128,512]{2,1,0:T(8,128)(2,1)S(1)}, u32[]{:S(2)}, u32[]{:S(2)}) collective-permute-start(bf16[2,128,512]{2,1,0:T(8,128)(2,1)S(1)} %get-tuple-element.537), channel_id=1, source_target_pairs={{0,2},{1,3},{2,0},{3,1},{4,6},{5,7},{6,4},{7,5},{8,10},{9,11},{10,... | collective-permute-start | bytes 786440 | tf_op jit(solution)/shard_map/ppermute | solution.py:164
  253.2 6.8 %collective-permute-start.33 = (bf16[2,128,512]{2,1,0:T(8,128)(2,1)S(1)}, bf16[2,128,512]{2,1,0:T(8,128)(2,1)S(1)}, u32[]{:S(2)}, u32[]{:S(2)}) collective-permute-start(bf16[2,128,512]{2,1,0:T(8,128)(2,1)S(1)} %get-tuple-element.535), channel_id=1, source_target_pairs={{0,4},{1,5},{2,6},{3,7},{4,0},{5,1},{6,2},{7,3},{8,12},{9,13},{10,... | collective-permute-start | bytes 786440 | tf_op jit(solution)/shard_map/ppermute | solution.py:164
  254.5 6.5 %collective-permute-start.34 = (bf16[2,128,512]{2,1,0:T(8,128)(2,1)S(1)}, bf16[2,128,512]{2,1,0:T(8,128)(2,1)S(1)}, u32[]{:S(2)}, u32[]{:S(2)}) collective-permute-start(bf16[2,128,512]{2,1,0:T(8,128)(2,1)S(1)} %get-tuple-element.533), channel_id=1, source_target_pairs={{0,16},{1,17},{2,18},{3,19},{4,20},{5,21},{6,22},{7,23},{8,24},{9,... | collective-permute-start | bytes 786440 | tf_op jit(solution)/shard_map/ppermute | solution.py:164
  277.7 21.5 %collective-permute-start.40 = (bf16[4,96,512]{2,1,0:T(8,128)(2,1)S(1)}, bf16[4,96,512]{2,1,0:T(8,128)(2,1)S(1)}, u32[]{:S(2)}, u32[]{:S(2)}) collective-permute-start(bf16[4,96,512]{2,1,0:T(8,128)(2,1)S(1)} %slice.508), channel_id=1, source_target_pairs={{0,8},{1,9},{2,10},{3,11},{4,12},{5,13},{6,14},{7,15},{8,0},{9,1},... | collective-permute-start | bytes 1179656 | tf_op jit(solution)/shard_map/ppermute | solution.py:164
  282.1 11.2 %collective-permute-start.39 = (bf16[2,2,2,96,128]{4,3,0,2,1:T(8,128)(2,1)S(1)}, bf16[2,2,2,96,128]{4,3,0,2,1:T(8,128)(2,1)S(1)}, u32[]{:S(2)}, u32[]{:S(2)}) collective-permute-start(bf16[2,2,2,96,128]{4,3,0,2,1:T(8,128)(2,1)S(1)} %get-tuple-element.578), channel_id=1, source_target_pairs={{0,16},{1,17},{2,18},{3,19},{4,20},{5,21},{6,22},{7,23},{8,24},{9,... | collective-permute-start | bytes 589832 | tf_op jit(solution)/shard_map/ppermute | solution.py:164
  299.2 6.6 %collective-permute-start.41 = (bf16[2,2,2,96,128]{4,3,1,0,2:T(8,128)(2,1)S(1)}, bf16[2,2,2,96,128]{4,3,1,0,2:T(8,128)(2,1)S(1)}, u32[]{:S(2)}, u32[]{:S(2)}) collective-permute-start(bf16[2,2,2,96,128]{4,3,1,0,2:T(8,128)(2,1)S(1)} %get-tuple-element.576), channel_id=1, source_target_pairs={{0,2},{1,3},{2,0},{3,1},{4,6},{5,7},{6,4},{7,5},{8,10},{9,11},{10,... | collective-permute-start | bytes 589832 | tf_op jit(solution)/shard_map/ppermute | solution.py:164
  305.8 23.2 %collective-permute-start.43 = (bf16[8,128,768]{2,1,0:T(8,128)(2,1)S(1)}, bf16[8,128,768]{2,1,0:T(8,128)(2,1)S(1)}, u32[]{:S(2)}, u32[]{:S(2)}) collective-permute-start(bf16[8,128,768]{2,1,0:T(8,128)(2,1)S(1)} %get-tuple-element.397), channel_id=1, source_target_pairs={{0,1},{1,0},{2,3},{3,2},{4,5},{5,4},{6,7},{7,6},{8,9},{9,8},{10,11... | collective-permute-start | bytes 4718600 | tf_op jit(solution)/shard_map/ppermute | solution.py:164
  305.9 23.1 %collective-permute-start.44 = (bf16[8,128,768]{2,1,0:T(8,128)(2,1)}, bf16[8,128,768]{2,1,0:T(8,128)(2,1)S(1)}, u32[]{:S(2)}, u32[]{:S(2)}) collective-permute-start(bf16[8,128,768]{2,1,0:T(8,128)(2,1)} %get-tuple-element.399), channel_id=1, source_target_pairs={{0,1},{1,0},{2,3},{3,2},{4,5},{5,4},{6,7},{7,6},{8,9},{9,8},{10,11... | collective-permute-start | bytes 4718600 | tf_op jit(solution)/shard_map/ppermute | solution.py:164
  306.4 22.6 %collective-permute-start.45 = (bf16[4,96,512]{2,1,0:T(8,128)(2,1)S(1)}, bf16[4,96,512]{2,1,0:T(8,128)(2,1)S(1)}, u32[]{:S(2)}, u32[]{:S(2)}) collective-permute-start(bf16[4,96,512]{2,1,0:T(8,128)(2,1)S(1)} %slice.513), channel_id=1, source_target_pairs={{0,8},{1,9},{2,10},{3,11},{4,12},{5,13},{6,14},{7,15},{8,0},{9,1},... | collective-permute-start | bytes 1179656 | tf_op jit(solution)/shard_map/ppermute | solution.py:164
  307.6 21.3 %collective-permute-start.42 = (bf16[2,2,2,96,128]{4,3,2,1,0:T(8,128)(2,1)S(1)}, bf16[2,2,2,96,128]{4,3,2,1,0:T(8,128)(2,1)S(1)}, u32[]{:S(2)}, u32[]{:S(2)}) collective-permute-start(bf16[2,2,2,96,128]{4,3,2,1,0:T(8,128)(2,1)S(1)} %get-tuple-element.574), channel_id=1, source_target_pairs={{0,4},{1,5},{2,6},{3,7},{4,0},{5,1},{6,2},{7,3},{8,12},{9,13},{10,... | collective-permute-start | bytes 589832 | tf_op jit(solution)/shard_map/ppermute | solution.py:164
  329.1 27.9 %collective-permute-start.48 = (bf16[256,1536]{1,0:T(8,128)(2,1)S(1)}, bf16[256,1536]{1,0:T(8,128)(2,1)S(1)}, u32[]{:S(2)}, u32[]{:S(2)}) collective-permute-start(bf16[256,1536]{1,0:T(8,128)(2,1)S(1)} %shard_map.223), channel_id=1, source_target_pairs={{1,9},{3,11},{5,13},{7,15},{8,0},{10,2},{12,4},{14,6},{16,24},{18,... | collective-permute-start | bytes 2359304 | tf_op jit(solution)/shard_map/ppermute | solution.py:164
  332.1 24.9 %collective-permute-start.46 = (bf16[4,128,768]{2,1,0:T(8,128)(2,1)S(1)}, bf16[4,128,768]{2,1,0:T(8,128)(2,1)S(1)}, u32[]{:S(2)}, u32[]{:S(2)}) collective-permute-start(bf16[4,128,768]{2,1,0:T(8,128)(2,1)S(1)} %get-tuple-element.509), channel_id=1, source_target_pairs={{0,2},{1,3},{2,0},{3,1},{4,6},{5,7},{6,4},{7,5},{8,10},{9,11},{10,... | collective-permute-start | bytes 2359304 | tf_op jit(solution)/shard_map/ppermute | solution.py:164
  334.4 22.6 %collective-permute-start.47 = (bf16[4,128,768]{2,1,0:T(8,128)(2,1)S(1)}, bf16[4,128,768]{2,1,0:T(8,128)(2,1)S(1)}, u32[]{:S(2)}, u32[]{:S(2)}) collective-permute-start(bf16[4,128,768]{2,1,0:T(8,128)(2,1)S(1)} %get-tuple-element.507), channel_id=1, source_target_pairs={{0,16},{1,17},{2,18},{3,19},{4,20},{5,21},{6,22},{7,23},{8,24},{9,... | collective-permute-start | bytes 2359304 | tf_op jit(solution)/shard_map/ppermute | solution.py:164
  335.6 21.3 %collective-permute-start.49 = (bf16[4,96,512]{2,1,0:T(8,128)(2,1)S(1)}, bf16[4,96,512]{2,1,0:T(8,128)(2,1)S(1)}, u32[]{:S(2)}, u32[]{:S(2)}) collective-permute-start(bf16[4,96,512]{2,1,0:T(8,128)(2,1)S(1)} %add_convert_fusion.25), channel_id=1, source_target_pairs={{0,4},{1,5},{2,6},{3,7},{4,0},{5,1},{6,2},{7,3},{8,12},{9,13},{10,... | collective-permute-start | bytes 1179656 | tf_op jit(solution)/shard_map/ppermute | solution.py:164
  364.4 20.6 %collective-permute-start.51 = (bf16[2,96,1024]{2,1,0:T(8,128)(2,1)}, bf16[2,96,1024]{2,1,0:T(8,128)(2,1)S(1)}, u32[]{:S(2)}, u32[]{:S(2)}) collective-permute-start(bf16[2,96,1024]{2,1,0:T(8,128)(2,1)} %fusion.2), channel_id=1, source_target_pairs={{0,8},{1,9},{2,10},{3,11},{4,12},{5,13},{6,14},{7,15},{8,0},{9,1},... | collective-permute-start | bytes 1179656 | tf_op jit(solution)/shard_map/ppermute | solution.py:164
  367.6 17.4 %collective-permute-start.52 = (bf16[2,128,768]{2,1,0:T(8,128)(2,1)S(1)}, bf16[2,128,768]{2,1,0:T(8,128)(2,1)S(1)}, u32[]{:S(2)}, u32[]{:S(2)}) collective-permute-start(bf16[2,128,768]{2,1,0:T(8,128)(2,1)S(1)} %get-tuple-element.525), channel_id=1, source_target_pairs={{0,16},{1,17},{2,18},{3,19},{4,20},{5,21},{6,22},{7,23},{8,24},{9,... | collective-permute-start | bytes 1179656 | tf_op jit(solution)/shard_map/ppermute | solution.py:164
  369.9 15.1 %collective-permute-start.53 = (bf16[2,128,768]{2,1,0:T(8,128)(2,1)S(1)}, bf16[2,128,768]{2,1,0:T(8,128)(2,1)S(1)}, u32[]{:S(2)}, u32[]{:S(2)}) collective-permute-start(bf16[2,128,768]{2,1,0:T(8,128)(2,1)S(1)} %get-tuple-element.523), channel_id=1, source_target_pairs={{0,2},{1,3},{2,0},{3,1},{4,6},{5,7},{6,4},{7,5},{8,10},{9,11},{10,... | collective-permute-start | bytes 1179656 | tf_op jit(solution)/shard_map/ppermute | solution.py:164
  371.1 26.0 %collective-permute-start.55 = (bf16[256,1536]{1,0:T(8,128)(2,1)S(1)}, bf16[256,1536]{1,0:T(8,128)(2,1)S(1)}, u32[]{:S(2)}, u32[]{:S(2)}) collective-permute-start(bf16[256,1536]{1,0:T(8,128)(2,1)S(1)} %add_convert_fusion), channel_id=1, source_target_pairs={{0,16},{2,18},{4,20},{6,22},{9,25},{11,27},{13,29},{15,31},{17,1},... | collective-permute-start | bytes 2359304 | tf_op jit(solution)/shard_map/ppermute | solution.py:164
  385.1 11.8 %collective-permute-start.54 = (bf16[2,2,96,512]{3,2,0,1:T(8,128)(2,1)S(1)}, bf16[2,2,96,512]{3,2,0,1:T(8,128)(2,1)S(1)}, u32[]{:S(2)}, u32[]{:S(2)}) collective-permute-start(bf16[2,2,96,512]{3,2,0,1:T(8,128)(2,1)S(1)} %bitcast.200), channel_id=1, source_target_pairs={{0,2},{1,3},{2,0},{3,1},{4,6},{5,7},{6,4},{7,5},{8,10},{9,11},{10,... | collective-permute-start | bytes 1179656 | tf_op jit(solution)/shard_map/ppermute | solution.py:164
  386.7 15.5 %collective-permute-start.56 = (bf16[96,1536]{1,0:T(8,128)(2,1)S(1)}, bf16[96,1536]{1,0:T(8,128)(2,1)S(1)}, u32[]{:S(2)}, u32[]{:S(2)}) collective-permute-start(bf16[96,1536]{1,0:T(8,128)(2,1)S(1)} %shard_map.226), channel_id=1, source_target_pairs={{8,0},{9,1},{10,2},{11,3},{12,4},{13,5},{14,6},{15,7},{16,24},{17,... | collective-permute-start | bytes 884744 | tf_op jit(solution)/shard_map/ppermute | solution.py:164
  402.5 14.1 %collective-permute-start.60 = (bf16[1,128,768]{2,1,0:T(8,128)(2,1)S(1)}, bf16[1,128,768]{2,1,0:T(8,128)(2,1)S(1)}, u32[]{:S(2)}, u32[]{:S(2)}) collective-permute-start(bf16[1,128,768]{2,1,0:T(8,128)(2,1)S(1)} %get-tuple-element.541), channel_id=1, source_target_pairs={{0,4},{1,5},{2,6},{3,7},{4,0},{5,1},{6,2},{7,3},{8,12},{9,13},{10,... | collective-permute-start | bytes 589832 | tf_op jit(solution)/shard_map/ppermute | solution.py:164
  404.0 22.0 %collective-permute-start.59 = (bf16[8,96,512]{2,1,0:T(8,128)(2,1)S(1)}, bf16[8,96,512]{2,1,0:T(8,128)(2,1)S(1)}, u32[]{:S(2)}, u32[]{:S(2)}) collective-permute-start(bf16[8,96,512]{2,1,0:T(8,128)(2,1)S(1)} %bitcast.173), channel_id=1, source_target_pairs={{0,16},{1,17},{2,18},{3,19},{4,20},{5,21},{6,22},{7,23},{8,24},{9,... | collective-permute-start | bytes 2359304 | tf_op jit(solution)/shard_map/ppermute | solution.py:164
  404.2 14.3 %collective-permute-start.61 = (bf16[1,128,768]{2,1,0:T(8,128)(2,1)S(1)}, bf16[1,128,768]{2,1,0:T(8,128)(2,1)S(1)}, u32[]{:S(2)}, u32[]{:S(2)}) collective-permute-start(bf16[1,128,768]{2,1,0:T(8,128)(2,1)S(1)} %get-tuple-element.539), channel_id=1, source_target_pairs={{0,4},{1,5},{2,6},{3,7},{4,0},{5,1},{6,2},{7,3},{8,12},{9,13},{10,... | collective-permute-start | bytes 589832 | tf_op jit(solution)/shard_map/ppermute | solution.py:164
  405.3 20.7 %collective-permute-start.57 = (bf16[8,96,192]{2,1,0:T(8,128)(2,1)S(1)}, bf16[8,96,192]{2,1,0:T(8,128)(2,1)S(1)}, u32[]{:S(2)}, u32[]{:S(2)}) collective-permute-start(bf16[8,96,192]{2,1,0:T(8,128)(2,1)S(1)} %get-tuple-element.448), channel_id=1, source_target_pairs={{0,8},{1,9},{2,10},{3,11},{4,12},{5,13},{6,14},{7,15},{8,0},{9,1},... | collective-permute-start | bytes 884744 | tf_op jit(solution)/shard_map/ppermute | solution.py:164
  408.8 53.8 %collective-permute-start.73 = (bf16[96,1536]{1,0:T(8,128)(2,1)S(1)}, bf16[96,1536]{1,0:T(8,128)(2,1)S(1)}, u32[]{:S(2)}, u32[]{:S(2)}) collective-permute-start(bf16[96,1536]{1,0:T(8,128)(2,1)S(1)} %add_convert_fusion.26), channel_id=1, source_target_pairs={{0,16},{1,17},{2,18},{3,19},{4,20},{5,21},{6,22},{7,23},{24,8},{25... | collective-permute-start | bytes 884744 | tf_op jit(solution)/shard_map/ppermute | solution.py:164
  432.2 18.3 %collective-permute-start.65 = (bf16[4,128,512]{2,1,0:T(8,128)(2,1)S(1)}, bf16[4,128,512]{2,1,0:T(8,128)(2,1)S(1)}, u32[]{:S(2)}, u32[]{:S(2)}) collective-permute-start(bf16[4,128,512]{2,1,0:T(8,128)(2,1)S(1)} %get-tuple-element.515), channel_id=1, source_target_pairs={{0,4},{1,5},{2,6},{3,7},{4,0},{5,1},{6,2},{7,3},{8,12},{9,13},{10,... | collective-permute-start | bytes 1572872 | tf_op jit(solution)/shard_map/ppermute | solution.py:164
  432.6 17.9 %collective-permute-start.66 = (bf16[4,128,512]{2,1,0:T(8,128)(2,1)S(1)}, bf16[4,128,512]{2,1,0:T(8,128)(2,1)S(1)}, u32[]{:S(2)}, u32[]{:S(2)}) collective-permute-start(bf16[4,128,512]{2,1,0:T(8,128)(2,1)S(1)} %get-tuple-element.513), channel_id=1, source_target_pairs={{0,16},{1,17},{2,18},{3,19},{4,20},{5,21},{6,22},{7,23},{8,24},{9,... | collective-permute-start | bytes 1572872 | tf_op jit(solution)/shard_map/ppermute | solution.py:164
  434.0 16.6 %collective-permute-start.67 = (bf16[4,128,512]{2,1,0:T(8,128)(2,1)S(1)}, bf16[4,128,512]{2,1,0:T(8,128)(2,1)S(1)}, u32[]{:S(2)}, u32[]{:S(2)}) collective-permute-start(bf16[4,128,512]{2,1,0:T(8,128)(2,1)S(1)} %get-tuple-element.511), channel_id=1, source_target_pairs={{0,2},{1,3},{2,0},{3,1},{4,6},{5,7},{6,4},{7,5},{8,10},{9,11},{10,... | collective-permute-start | bytes 1572872 | tf_op jit(solution)/shard_map/ppermute | solution.py:164
  435.3 15.1 %collective-permute-start.68 = (bf16[2,2,96,192]{3,2,1,0:T(8,128)(2,1)S(1)}, bf16[2,2,96,192]{3,2,1,0:T(8,128)(2,1)S(1)}, u32[]{:S(2)}, u32[]{:S(2)}) collective-permute-start(bf16[2,2,96,192]{3,2,1,0:T(8,128)(2,1)S(1)} %bitcast.220), channel_id=1, source_target_pairs={{0,4},{1,5},{2,6},{3,7},{4,0},{5,1},{6,2},{7,3},{8,12},{9,13},{10,... | collective-permute-start | bytes 442376 | tf_op jit(solution)/shard_map/ppermute | solution.py:164
  450.7 11.9 %collective-permute-start.69 = (bf16[2,128,512]{2,1,0:T(8,128)(2,1)S(1)}, bf16[2,128,512]{2,1,0:T(8,128)(2,1)S(1)}, u32[]{:S(2)}, u32[]{:S(2)}) collective-permute-start(bf16[2,128,512]{2,1,0:T(8,128)(2,1)S(1)} %get-tuple-element.531), channel_id=1, source_target_pairs={{0,2},{1,3},{2,0},{3,1},{4,6},{5,7},{6,4},{7,5},{8,10},{9,11},{10,... | collective-permute-start | bytes 786440 | tf_op jit(solution)/shard_map/ppermute | solution.py:164
  451.4 11.1 %collective-permute-start.72 = (bf16[2,2,96,192]{3,2,0,1:T(8,128)(2,1)S(1)}, bf16[2,2,96,192]{3,2,0,1:T(8,128)(2,1)S(1)}, u32[]{:S(2)}, u32[]{:S(2)}) collective-permute-start(bf16[2,2,96,192]{3,2,0,1:T(8,128)(2,1)S(1)} %get-tuple-element.570), channel_id=1, source_target_pairs={{0,2},{1,3},{2,0},{3,1},{4,6},{5,7},{6,4},{7,5},{8,10},{9,11},{10,... | collective-permute-start | bytes 442376 | tf_op jit(solution)/shard_map/ppermute | solution.py:164
  453.8 8.8 %collective-permute-start.70 = (bf16[2,128,512]{2,1,0:T(8,128)(2,1)}, bf16[2,128,512]{2,1,0:T(8,128)(2,1)S(1)}, u32[]{:S(2)}, u32[]{:S(2)}) collective-permute-start(bf16[2,128,512]{2,1,0:T(8,128)(2,1)} %get-tuple-element.529), channel_id=1, source_target_pairs={{0,4},{1,5},{2,6},{3,7},{4,0},{5,1},{6,2},{7,3},{8,12},{9,13},{10,... | collective-permute-start | bytes 786440 | tf_op jit(solution)/shard_map/ppermute | solution.py:164
  454.9 7.7 %collective-permute-start.71 = (bf16[2,128,512]{2,1,0:T(8,128)(2,1)}, bf16[2,128,512]{2,1,0:T(8,128)(2,1)S(1)}, u32[]{:S(2)}, u32[]{:S(2)}) collective-permute-start(bf16[2,128,512]{2,1,0:T(8,128)(2,1)} %get-tuple-element.527), channel_id=1, source_target_pairs={{0,16},{1,17},{2,18},{3,19},{4,20},{5,21},{6,22},{7,23},{8,24},{9,... | collective-permute-start | bytes 786440 | tf_op jit(solution)/shard_map/ppermute | solution.py:164
  465.4 6.0 %collective-permute-start.76 = (bf16[1,128,512]{2,1,0:T(8,128)(2,1)S(1)}, bf16[1,128,512]{2,1,0:T(8,128)(2,1)S(1)}, u32[]{:S(2)}, u32[]{:S(2)}) collective-permute-start(bf16[1,128,512]{2,1,0:T(8,128)(2,1)S(1)} %get-tuple-element.555), channel_id=1, source_target_pairs={{0,4},{1,5},{2,6},{3,7},{4,0},{5,1},{6,2},{7,3},{8,12},{9,13},{10,... | collective-permute-start | bytes 393224 | tf_op jit(solution)/shard_map/ppermute | solution.py:164
  466.8 11.2 %collective-permute-start.78 = (bf16[8,96,192]{2,1,0:T(8,128)(2,1)S(1)}, bf16[8,96,192]{2,1,0:T(8,128)(2,1)S(1)}, u32[]{:S(2)}, u32[]{:S(2)}) collective-permute-start(bf16[8,96,192]{2,1,0:T(8,128)(2,1)S(1)} %bitcast.178), channel_id=1, source_target_pairs={{0,16},{1,17},{2,18},{3,19},{4,20},{5,21},{6,22},{7,23},{8,24},{9,... | collective-permute-start | bytes 884744 | tf_op jit(solution)/shard_map/ppermute | solution.py:164
  (119 other events, 890.5 us)
Sparse Core Ops, SparseCore 0:
  10.6 64.6 all-gather.4
  78.3 48.8 all-gather.6
  167.1 49.9 all-gather.8
  276.5 59.7 all-gather.10
